TPU v7x, 32 devices: a whole 2x2x4 slice. The times are simulated.
32 devices in a mesh: sensor: 4 (over x, core), space: 8 (over z, y).
Axes of the slice: x: 2, y: 2, z: 4, core: 2. Of those that a mesh axis runs over, the one named last changes fastest.
Arguments:
- forward_map: bfloat16 [16, 2, 1024, 2048], P(None, None, 'sensor', 'space'), may hold values from -1 to 1
- observed: float32 [16, 2, 1024, 128], P(None, None, 'sensor'), may hold values from -6 to 6
- noise_var: float32 [1024], P('sensor'), may hold values from 0.3 to 1.5
- prior_rows: bfloat16 [2048, 512], P('space'), may hold values from -2 to 14, as said below
- prior_scale: float32 [16], replicated, may hold values from 0.6 to 1.2
Outputs:
- multiplier: float32 [16, 2, 1024, 128], P(None, None, 'sensor')
- posterior: float32 [16, 2048, 2, 128], P('sensor', 'space')
Inputs may be any that keep to these rules, and one draw needn't show every extreme that they name: `prior_rows`: each block of 512 rows is a symmetric matrix.
All inputs are finite; a program needn't handle non-finite values.
Results may differ from a plain program's by a relative error of at most 0.03.
Values may be sent and summed in bfloat16 or wider, within the bound.
No kernel may reach another device: no remote copies, remote signals or barrier semaphores. Data moves between devices by JAX's collectives and lax.ppermute only.
A program may use at most 64 MiB of HBM per device.

v0:
```python
import jax
import jax.numpy as jnp
from jax import lax
from jax.sharding import PartitionSpec as P

ITERS = 2


relax_step = 0.25


def partner(block, axis, distance):
    count = lax.axis_size(axis)
    route = []
    for low in range(count):
        high = low | 1 << distance
        if high != low and high < count:
            route += [(low, high), (high, low)]
    return lax.ppermute(block, axis, route)


def as_sent(x):

    def short(part):
        return part.astype(jnp.bfloat16) if part.dtype == jnp.float32 else part

    return jax.tree.map(short, x)


def stack_sides(dual_b):
    real_part = dual_b[..., 0, :, :]
    imag_part = dual_b[..., 1, :, :]
    upper = jnp.concatenate([real_part, imag_part], -1)
    lower = jnp.concatenate([imag_part, -real_part], -1)
    return jnp.concatenate([upper, lower], -2)


def to_data(products, half, scenarios):
    upper = products[..., :half, :]
    lower = products[..., half:, :]
    real_part = upper[..., :scenarios] - lower[..., scenarios:]
    imag_part = upper[..., scenarios:] + lower[..., :scenarios]
    return jnp.stack([real_part, imag_part], -3)


def prior_apply(adjoint_sum, prior_rows, freq_gains):
    own_half = adjoint_sum.astype(jnp.bfloat16)
    other_half = partner(own_half, "space", 0)
    is_even = lax.axis_index("space") % 2 == 0
    joined = jnp.where(
        is_even,
        jnp.concatenate([own_half, other_half], 1),
        jnp.concatenate([other_half, own_half], 1),
    )
    prior_term = jnp.einsum("cj,fjr->fcr", prior_rows, joined, preferred_element_type=jnp.float32)
    return prior_term * freq_gains[:, None, None]


def space_total(partial_data):
    return lax.psum(partial_data.astype(jnp.bfloat16), "space").astype(jnp.float32)


def on_device(forward_map, observed, noise_var, prior_rows, prior_scale):
    frequencies, halves, sensors_here, cell_count = forward_map.shape
    scenarios = observed.shape[-1]
    groups = lax.axis_size("sensor")
    local_freqs = frequencies // groups
    freq_gains = lax.dynamic_slice_in_dim(
        prior_scale, lax.axis_index("sensor") * local_freqs, local_freqs, 0
    )
    local_map = forward_map.reshape(frequencies, 1, halves * sensors_here, cell_count)
    stacked = lax.all_to_all(local_map, "sensor", split_axis=0, concat_axis=1, tiled=True)
    laid_data = lax.all_to_all(
        observed.reshape(frequencies, 1, halves, sensors_here, scenarios).astype(jnp.bfloat16),
        "sensor",
        split_axis=0,
        concat_axis=1,
        tiled=True,
    ).astype(jnp.float32)
    every_noise = lax.all_gather(noise_var, "sensor", axis=0, tiled=True).reshape(
        groups, 1, sensors_here, 1
    )

    def adjoint(multiplier):
        right_sides = stack_sides(multiplier.astype(jnp.bfloat16))
        partial_sums = jnp.einsum(
            "fgkc,fgkr->fgcr", stacked, right_sides, preferred_element_type=jnp.float32
        )
        return jnp.sum(partial_sums.astype(jnp.bfloat16).astype(jnp.float32), axis=1)

    multiplier = relax_step * laid_data
    for iteration in range(ITERS):
        prior_term = prior_apply(adjoint(multiplier), prior_rows, freq_gains)
        products = jnp.einsum(
            "fgkc,fcr->fgkr",
            stacked,
            prior_term.astype(jnp.bfloat16),
            preferred_element_type=jnp.float32,
        )
        predicted = space_total(to_data(products, sensors_here, scenarios))
        multiplier = multiplier + relax_step * (laid_data - predicted - every_noise * multiplier)
    posterior = prior_apply(adjoint(multiplier), prior_rows, freq_gains)
    dual_out = (
        lax.all_to_all(as_sent(multiplier), "sensor", split_axis=1, concat_axis=0, tiled=True)
        .astype(multiplier.dtype)
        .reshape(frequencies, halves, sensors_here, scenarios)
    )
    return (dual_out, posterior.reshape(local_freqs, cell_count, 2, scenarios))


def solution(mesh):
    return jax.shard_map(
        on_device,
        mesh=mesh,
        in_specs=(
            P(None, None, "sensor", "space"),
            P(None, None, "sensor", None),
            P("sensor"),
            P("space", None),
            P(),
        ),
        out_specs=(P(None, None, "sensor", None), P("sensor", "space", None, None)),
        check_vma=False,
    )
```

profile of v0, /device:TPU:0, one launch (start us, length us, event | category | flops | bytes accessed | tf_op | source)
XLA Modules:
  0.0 411.6 jit_solution(5213985240164051723)
XLA Ops:
  7.2 2.5 convert_bitcast_fusion
  9.7 29.7 %all_to_all.36 = bf16[16,1,2,256,128]{4,3,2,1,0:T(8,128)(2,1)S(1)} all-to-all(bf16[16,1,2,256,128]{4,3,2,1,0:T(8,128)(2,1)S(1)} %convert_bitcast_fusion), channel_id=1, replica_groups=mesh['sensor'=4,'space'=8] {'sensor'}, dimensions={0} | all-to-all | bytes 4194304 | tf_op jit(solution)/shard_map/all_to_all | solution.py:73
  39.4 4.9 %all-to-all-start.1 = ((bf16[16,1,512,256]{3,2,1,0:T(8,128)(2,1)}), bf16[16,1,512,256]{3,2,1,0:T(8,128)(2,1)}, u32[]{:S(2)}, u32[]{:S(2)}) async-start(bf16[16,1,512,256]{3,2,1,0:T(8,128)(2,1)} %bitcast.133), calls=%async_computation.1 | async-start | bytes 8388608 | tf_op jit(solution)/shard_map/all_to_all | solution.py:72
  44.4 2.8 copy.13
  47.2 2.7 fusion.38
  50.3 42.3 %all-to-all-done.1 = bf16[16,1,512,256]{3,2,1,0:T(8,128)(2,1)} async-done(((bf16[16,1,512,256]{3,2,1,0:T(8,128)(2,1)}), bf16[16,1,512,256]{3,2,1,0:T(8,128)(2,1)}, u32[]{:S(2)}, u32[]{:S(2)}) %all-to-all-start.1) | async-done | bytes 4194336 | tf_op jit(solution)/shard_map/all_to_all | solution.py:72
  92.6 4.3 %convert_reduce_fusion.2 = bf16[4,256,256]{2,1,0:T(8,128)(2,1)} fusion(bf16[4,4,1,512,256]{4,3,1,0,2:T(8,128)(2,1)} %bitcast.9, bf16[4,4,256,128]{2,3,1,0:T(8,128)(2,1)S(1)} %fusion.120, bf16[4,4,256,128]{2,3,1,0:T(8,128)(2,1)S(1)} %get-tuple-element.17, bf16[4,4,256,128]{2,3,1,0:T(8,128)(2,1)S(1)} %get-tuple-element.16), kind=kOutput, calls=%fused_computation.64 | convolution fusion | flops 1092354048 | bytes 7864320 | tf_op jit(solution)/shard_map/fgkc,fgkr->fgcr/dot_general | solution.py:86
  96.9 1.5 collective-permute-start
  98.5 12.1 %collective-permute-done = bf16[4,256,256]{1,2,0:T(8,128)(2,1)S(1)} collective-permute-done((bf16[4,256,256]{1,2,0:T(8,128)(2,1)}, bf16[4,256,256]{1,2,0:T(8,128)(2,1)S(1)}, u32[]{:S(2)}, u32[]{:S(2)}) %collective-permute-start) | collective-permute-done | bytes 524320 | tf_op jit(solution)/shard_map/ppermute | solution.py:19
  110.6 7.7 %fusion.40 = f32[4,4,512,256]{2,3,1,0:T(8,128)} fusion(bf16[4,4,1,512,256]{4,3,1,0,2:T(8,128)(2,1)} %bitcast.9, bf16[4,256,256]{1,2,0:T(8,128)(2,1)S(1)} %collective-permute-done, bf16[4,256,256]{1,2,0:T(8,128)(2,1)} %bitcast.12, pred[]{:T(512)S(6)} %eq.9, f32[4]{0:T(128)S(1)} %dynamic_slice.3, bf16[256,512]{1,0:T(8,128)(2,1)S(1)} %copy-done), kind=kOutput, calls=%fused_computation.44 | convolution fusion | flops 1347420160 | bytes 13893649 | tf_op jit(solution)/shard_map/fgkc,fcr->fgkr/dot_general | solution.py:94
  118.3 4.3 %fusion.71 = (bf16[4,4,1,256,128]{3,4,1,0,2:T(8,128)(2,1)S(1)}, bf16[4,4,1,256,128]{3,4,1,0,2:T(8,128)(2,1)S(1)}) fusion(f32[4,4,512,256]{2,3,1,0:T(8,128)} %fusion.40), kind=kLoop, calls=%fused_computation.73 | loop fusion | flops 2097152 | bytes 10485760 | tf_op jit(solution)/shard_map/stack | solution.py:43
  122.6 1.5 pad_maximum_fusion
  124.2 5.3 %all-gather = f32[4,1,256]{2,1,0:T(1,128)S(1)} all-gather(f32[1,1,256]{2,1,0:T(1,128)S(1)} %bitcast.138), channel_id=1, replica_groups=mesh['sensor'=4,'space'=8] {'sensor'}, dimensions={0}, use_global_device_ids=true | all-gather | bytes 5120 | tf_op jit(solution)/shard_map/all_gather | solution.py:80
  129.5 97.0 %all-reduce.3.cloned.1.call-done = bf16[4,4,2,256,128]{3,4,1,0,2:T(8,128)(2,1)} async-done(((bf16[4,4,2,256,128]{3,4,1,0,2:T(8,128)(2,1)}), bf16[4,4,2,256,128]{3,4,1,0,2:T(8,128)(2,1)}) %all-reduce.3.cloned.1.call-update) | async-done | bytes 2097168 | tf_op jit(solution)/shard_map/psum | solution.py:60
  226.5 3.8 fusion.39
  230.6 3.5 convert_reduce_fusion.1
  234.0 1.5 collective-permute-start.1
  235.6 12.0 %collective-permute-done.1 = bf16[4,256,256]{1,2,0:T(8,128)(2,1)S(1)} collective-permute-done((bf16[4,256,256]{1,2,0:T(8,128)(2,1)S(1)}, bf16[4,256,256]{1,2,0:T(8,128)(2,1)S(1)}, u32[]{:S(2)}, u32[]{:S(2)}) %collective-permute-start.1) | collective-permute-done | bytes 524320 | tf_op jit(solution)/shard_map/ppermute | solution.py:19
  247.5 7.4 %fusion.43 = f32[4,4,512,256]{2,3,1,0:T(8,128)} fusion(bf16[4,4,1,512,256]{4,3,1,0,2:T(8,128)(2,1)} %bitcast.9, bf16[4,256,256]{1,2,0:T(8,128)(2,1)S(1)} %collective-permute-done.1, bf16[4,256,256]{1,2,0:T(8,128)(2,1)S(1)} %bitcast.136, pred[]{:T(512)S(6)} %eq.9, f32[4]{0:T(128)S(1)} %dynamic_slice.3, bf16[256,512]{1,0:T(8,128)(2,1)S(1)} %copy-done), kind=kOutput, calls=%fused_computation.45 | convolution fusion | flops 1347420160 | bytes 13893649 | tf_op jit(solution)/shard_map/fgkc,fcr->fgkr/dot_general | solution.py:94
  254.9 4.3 %fusion.73 = (bf16[4,4,1,256,128]{3,4,1,0,2:T(8,128)(2,1)S(1)}, bf16[4,4,1,256,128]{3,4,1,0,2:T(8,128)(2,1)S(1)}) fusion(f32[4,4,512,256]{2,3,1,0:T(8,128)} %fusion.43), kind=kLoop, calls=%fused_computation.75 | loop fusion | flops 2097152 | bytes 10485760 | tf_op jit(solution)/shard_map/stack | solution.py:43
  259.2 1.5 pad_maximum_fusion.1
  260.7 102.0 %all-reduce.5.cloned.1.call-done = bf16[4,4,2,256,128]{3,4,1,0,2:T(8,128)(2,1)} async-done(((bf16[4,4,2,256,128]{3,4,1,0,2:T(8,128)(2,1)}), bf16[4,4,2,256,128]{3,4,1,0,2:T(8,128)(2,1)}) %all-reduce.5.cloned.1.call-update) | async-done | bytes 2097168 | tf_op jit(solution)/shard_map/psum | solution.py:60
  362.7 4.7 %fusion.37 = bf16[4,4,2,256,128]{3,4,1,0,2:T(8,128)(2,1)S(1)} fusion(f32[4,4,1,2,256,128]{4,5,0,1,3,2:T(8,128)} %copy.13, bf16[4,4,2,256,128]{3,4,1,0,2:T(8,128)(2,1)} %all-reduce.5.cloned.1.call-done, bf16[4,4,2,256,128]{3,4,1,0,2:T(8,128)(2,1)S(1)} %copy-done.1, f32[4,256]{1,0:T(4,128)S(1)} %bitcast.137, f32[4,256]{1,0:T(4,128)S(1)} %broadcast_multiply_fusion), kind=kLoop, calls=%fused_computation.41 | loop fusion | flops 14680064 | bytes 10493952 | tf_op jit(solution)/shard_map/convert_element_type | solution.py:25
  367.5 1.5 copy.15
  369.1 4.5 %all-to-all-start.2 = ((bf16[4,4,2,256,128]{3,4,0,2,1:T(8,128)(2,1)}), bf16[4,4,2,256,128]{3,4,0,2,1:T(8,128)(2,1)}, u32[]{:S(2)}, u32[]{:S(2)}) async-start(bf16[4,4,2,256,128]{3,4,0,2,1:T(8,128)(2,1)} %copy.15), calls=%async_computation.2 | async-start | bytes 4194304 | tf_op jit(solution)/shard_map/all_to_all | solution.py:104
  373.5 3.5 convert_reduce_fusion
  377.0 1.5 collective-permute-start.2
  378.6 12.8 %collective-permute-done.2 = bf16[4,256,256]{1,2,0:T(8,128)(2,1)S(1)} collective-permute-done((bf16[4,256,256]{1,2,0:T(8,128)(2,1)S(1)}, bf16[4,256,256]{1,2,0:T(8,128)(2,1)S(1)}, u32[]{:S(2)}, u32[]{:S(2)}) %collective-permute-start.2) | collective-permute-done | bytes 524320 | tf_op jit(solution)/shard_map/ppermute | solution.py:19
  391.9 1.3 copy.17
  393.2 6.1 %all-to-all-done.2 = bf16[4,4,2,256,128]{3,4,0,2,1:T(8,128)(2,1)} async-done(((bf16[4,4,2,256,128]{3,4,0,2,1:T(8,128)(2,1)}), bf16[4,4,2,256,128]{3,4,0,2,1:T(8,128)(2,1)}, u32[]{:S(2)}, u32[]{:S(2)}) %all-to-all-start.2) | async-done | bytes 2097184 | tf_op jit(solution)/shard_map/all_to_all | solution.py:104
  399.3 3.0 copy.16
  402.3 2.5 bitcast_convert_fusion
  (22 shorter events, 1.4 us)
Async XLA Ops:
  7.2 103.5 %copy-start = (bf16[256,512]{1,0:T(8,128)(2,1)S(1)}, bf16[256,512]{1,0:T(8,128)(2,1)}, u32[]{:S(2)}) copy-start(bf16[256,512]{1,0:T(8,128)(2,1)} %param.8) | copy-start | bytes 786436
  39.4 53.2 %all-to-all-start.1 = ((bf16[16,1,512,256]{3,2,1,0:T(8,128)(2,1)}), bf16[16,1,512,256]{3,2,1,0:T(8,128)(2,1)}, u32[]{:S(2)}, u32[]{:S(2)}) async-start(bf16[16,1,512,256]{3,2,1,0:T(8,128)(2,1)} %bitcast.133), calls=%async_computation.1 | async-start | bytes 8388608 | tf_op jit(solution)/shard_map/all_to_all | solution.py:72
  44.4 182.1 %all-reduce.3.cloned.1.call-start = ((), (), s32[]{:S(2)}) async-start(), calls=%async_computation.3 | async-start | bytes 4194304 | tf_op jit(solution)/shard_map/psum | solution.py:60
  92.6 5.9 %copy-start.3 = (f32[16]{0:T(128)S(1)}, f32[16]{0:T(128)}, u32[]{:S(2)}) copy-start(f32[16]{0:T(128)} %param.9) | copy-start | bytes 196
  96.9 13.7 %collective-permute-start = (bf16[4,256,256]{1,2,0:T(8,128)(2,1)}, bf16[4,256,256]{1,2,0:T(8,128)(2,1)S(1)}, u32[]{:S(2)}, u32[]{:S(2)}) collective-permute-start(bf16[4,256,256]{1,2,0:T(8,128)(2,1)} %bitcast.12), channel_id=1, source_target_pairs={{0,1},{1,0},{2,3},{3,2},{4,5},{5,4},{6,7},{7,6},{8,9},{9,8},{10,11... | collective-permute-start | bytes 1572872 | tf_op jit(solution)/shard_map/ppermute | solution.py:19
  122.6 1.6 copy-start.2
  124.2 238.5 %all-reduce.5.cloned.1.call-start = ((), (), s32[]{:S(2)}) async-start(), calls=%async_computation.4 | async-start | bytes 4194304 | tf_op jit(solution)/shard_map/psum | solution.py:60
  234.0 13.5 %collective-permute-start.1 = (bf16[4,256,256]{1,2,0:T(8,128)(2,1)S(1)}, bf16[4,256,256]{1,2,0:T(8,128)(2,1)S(1)}, u32[]{:S(2)}, u32[]{:S(2)}) collective-permute-start(bf16[4,256,256]{1,2,0:T(8,128)(2,1)S(1)} %bitcast.135), channel_id=1, source_target_pairs={{0,1},{1,0},{2,3},{3,2},{4,5},{5,4},{6,7},{7,6},{8,9},{9,8},{10,11... | collective-permute-start | bytes 1572872 | tf_op jit(solution)/shard_map/ppermute | solution.py:19
  259.2 103.5 %copy-start.1 = (bf16[4,4,2,256,128]{3,4,1,0,2:T(8,128)(2,1)S(1)}, bf16[4,4,2,256,128]{3,4,1,0,2:T(8,128)(2,1)}, u32[]{:S(2)}) copy-start(bf16[4,4,2,256,128]{3,4,1,0,2:T(8,128)(2,1)} %all-reduce.3.cloned.1.call-done) | copy-start | bytes 6291460
  369.1 30.2 %all-to-all-start.2 = ((bf16[4,4,2,256,128]{3,4,0,2,1:T(8,128)(2,1)}), bf16[4,4,2,256,128]{3,4,0,2,1:T(8,128)(2,1)}, u32[]{:S(2)}, u32[]{:S(2)}) async-start(bf16[4,4,2,256,128]{3,4,0,2,1:T(8,128)(2,1)} %copy.15), calls=%async_computation.2 | async-start | bytes 4194304 | tf_op jit(solution)/shard_map/all_to_all | solution.py:104
  377.0 14.3 %collective-permute-start.2 = (bf16[4,256,256]{1,2,0:T(8,128)(2,1)S(1)}, bf16[4,256,256]{1,2,0:T(8,128)(2,1)S(1)}, u32[]{:S(2)}, u32[]{:S(2)}) collective-permute-start(bf16[4,256,256]{1,2,0:T(8,128)(2,1)S(1)} %bitcast.139), channel_id=1, source_target_pairs={{0,1},{1,0},{2,3},{3,2},{4,5},{5,4},{6,7},{7,6},{8,9},{9,8},{10,11... | collective-permute-start | bytes 1572872 | tf_op jit(solution)/shard_map/ppermute | solution.py:19
Sparse Core Ops, SparseCore 0:
  124.3 102.1 all-reduce.2
  260.8 101.8 all-reduce.4
where the time goes:
time: 412 us
  waiting for transfers between devices  284 us (69%)
  blocking collectives  35 us (8%)
  other arithmetic  28.1 us (7%)
  matrix products  26.9 us (7%)
  between operations  14.2 us (3%)
  starting transfers between devices  14.1 us (3%)
  local copies, waits for them, and re-layouts  9.13 us (2%)
    psum x2, waiting for transfers between devices, space_total(): lax.psum(partial_data.astype(jnp.bfloat16), 'space').astype(jnp.float32)  199 us
    all_to_all x1, waiting for transfers between devices, on_device(): lax.all_to_all(local_map, 'sensor', split_axis=0, concat_axis=1, tiled=True)  42.3 us
    ppermute x3, waiting for transfers between devices, partner(): return lax.ppermute(block, axis, route)  36.8 us
    all_to_all x1, blocking collectives, on_device(): lax.all_to_all(observed.reshape(frequencies, 1, halves, sensors_here, sce...  29.7 us
    dot_general x2, matrix products, on_device(): jnp.einsum('fgkc,fcr->fgkr', stacked, prior_term.astype(jnp.bfloat16), pr...  15.1 us
    another operation x4, other arithmetic, to_data(): return jnp.stack([real_part, imag_part], -3)  11.5 us
    dot_general x3, matrix products, adjoint(): jnp.einsum('fgkc,fgkr->fgcr', stacked, right_sides, preferred_element_typ...  11.3 us
  transfers between devices with their start and end apart: 7, of which 7 were waited for; matrix products, arithmetic and copies ran while one was open for 3% of the time, Pallas kernels for 0%

commit v1 on v0

v1 whole, which is shorter than its diff:
```python
import functools

import jax
import jax.numpy as jnp
from jax import lax
from jax.experimental import pallas as pl
from jax.experimental.pallas import tpu as pltpu
from jax.sharding import Mesh, PartitionSpec as P

ITERS = 2
relax_step = 0.25
LANES = 128
VMEM_LIMIT = 48 * 2**20


def turned(z):
    return jnp.concatenate([z[:, LANES:], -z[:, :LANES]], 1)


def turned_back(v):
    return jnp.concatenate([-v[:, LANES:], v[:, :LANES]], 1)


def dot(a, b):
    return jnp.dot(a, b, preferred_element_type=jnp.float32)


def dot_t(a, b):
    return lax.dot_general(a, b, (((0,), (0,)), ((), ())), preferred_element_type=jnp.float32)


class Rows:
    def __init__(self, sensors, cells, groups, quads, prior_width):
        sizes = {
            "map": 2 * sensors,
            "obs": sensors // quads,
            "prior": cells // groups * (prior_width // cells),
            "noise": 16,
        }
        self.size, self.at, total = sizes, {}, 0
        for name in sorted(sizes, key=lambda n: -sizes[n]):
            self.at[name] = total
            total += sizes[name]
        self.total = total

    def span(self, name):
        return slice(self.at[name], self.at[name] + self.size[name])


def pack_kernel(rows, place_ref, map_ref, obs_ref, prior_ref, noise_ref, out_ref):
    out_ref[0, rows.span("map"), :] = map_ref[0]
    obs = obs_ref[0].astype(jnp.bfloat16)
    out_ref[0, rows.span("obs"), :LANES] = obs[0]
    out_ref[0, rows.span("obs"), LANES:] = obs[1]
    share, width = prior_ref.shape
    cells = out_ref.shape[2]
    for part in range(width // cells):
        first = rows.at["prior"] + part * share
        out_ref[0, first:first + share, :] = prior_ref[:, part * cells:(part + 1) * cells]
    noise = noise_ref[...]
    high = noise.astype(jnp.bfloat16)
    low = (noise - high.astype(jnp.float32)).astype(jnp.bfloat16)
    out_ref[0, rows.span("noise"), :] = jnp.concatenate(
        [jnp.broadcast_to(high, (8, cells)), jnp.broadcast_to(low, (8, cells))], 0
    )


def pack(rows, forward_map, observed, noise_var, prior_rows, place, groups, quads):
    frequencies, halves, sensors, cells = forward_map.shape
    return pl.pallas_call(
        functools.partial(pack_kernel, rows),
        grid_spec=pltpu.PrefetchScalarGridSpec(
            num_scalar_prefetch=1,
            grid=(frequencies,),
            in_specs=[
                pl.BlockSpec((1, halves * sensors, cells), lambda f, place: (f, 0, 0)),
                pl.BlockSpec((1, halves, sensors // quads, LANES), lambda f, place: (f, 0, place[1], 0)),
                pl.BlockSpec((cells // groups, prior_rows.shape[1]), lambda f, place: (place[0], 0)),
                pl.BlockSpec((1, sensors), lambda f, place: (0, 0)),
            ],
            out_specs=pl.BlockSpec((1, rows.total, cells), lambda f, place: (f, 0, 0)),
        ),
        out_shape=jax.ShapeDtypeStruct((frequencies, rows.total, cells), jnp.bfloat16),
    )(place, forward_map.reshape(frequencies, halves * sensors, cells), observed, prior_rows, noise_var.reshape(1, sensors))


def step_kernel(stage, n_pred, sensors, scale_ref, map_ref, prior_ref, obs_ref, noise_ref, *rest):
    groups, per_block = map_ref.shape[:2]
    cells = map_ref.shape[3]
    quads = obs_ref.shape[1]
    share = prior_ref.shape[2] // per_block
    last = stage == ITERS
    preds, rest = rest[:n_pred], rest[n_pred:]
    held_ref = None
    if stage > 1:
        held_ref, rest = rest[0], rest[1:]
    if last:
        dual_ref, post_ref, z_ref = rest
    elif stage > 0:
        out_ref, next_ref, z_ref, total_ref = rest
    else:
        out_ref, z_ref, total_ref = rest
    block = pl.program_id(0)

    @pl.when(block == 0)
    def _():
        for g in range(groups):
            span = slice(g * sensors, (g + 1) * sensors)
            obs = jnp.concatenate([obs_ref[g, q] for q in range(quads)], 0).astype(jnp.float32)
            now = relax_step * obs if stage < 2 else held_ref[span, :]
            if stage > 0:
                both = noise_ref[g, 0].astype(jnp.float32)
                noise_row = both[0:1, :] + both[8:9, :]
                row = lax.broadcasted_iota(jnp.int32, (sensors, sensors), 0)
                col = lax.broadcasted_iota(jnp.int32, (sensors, sensors), 1)
                noise = jnp.sum(jnp.where(row == col, noise_row, 0.0), 1, keepdims=True)
                predicted = sum(p[span, :].astype(jnp.float32) for p in preds)
                now = now + relax_step * (obs - predicted - noise * now)
                if last:
                    dual_ref[span, :] = now.astype(jnp.bfloat16)
                elif stage > 0:
                    next_ref[span, :] = now
            z = now.astype(jnp.bfloat16)
            z_ref[0, span, :] = z
            z_ref[1, span, :] = turned(z)

    parts = []
    for q in range(per_block):
        u = jnp.zeros((cells, 2 * LANES), jnp.float32)
        for g in range(groups):
            span = slice(g * sensors, (g + 1) * sensors)
            u += dot_t(map_ref[g, q, :sensors, :], z_ref[0, span, :])
            u += dot_t(map_ref[g, q, sensors:, :], z_ref[1, span, :])
        parts.append(u.astype(jnp.bfloat16))
    ub = jnp.concatenate(parts, 0)
    scale = scale_ref[0]
    for q in range(per_block):
        row_blocks = [
            jnp.concatenate([prior_ref[g, q, p * share:(p + 1) * share, :] for p in range(per_block)], 1)
            for g in range(groups)
        ]
        term = dot(jnp.concatenate(row_blocks, 0), ub) * scale
        v = term.astype(jnp.bfloat16)
        if last:
            post_ref[q] = v
            continue
        w = turned_back(v)
        for g in range(groups):
            span = slice(g * sensors, (g + 1) * sensors)
            add = dot(map_ref[g, q, :sensors, :], v) + dot(map_ref[g, q, sensors:, :], w)
            if q == 0:
                total_ref[span, :] = jnp.where(block == 0, add, total_ref[span, :] + add)
            else:
                total_ref[span, :] += add
    if not last:

        @pl.when(block == pl.num_programs(0) - 1)
        def _():
            out_ref[...] = total_ref[...].astype(jnp.bfloat16)


def step(stage, rows, held, preds, multiplier, scale, sensors, per_block):
    groups, quads, _, cells = held.shape
    width = 2 * LANES
    whole = groups * sensors
    blocks = quads // per_block
    last = stage == ITERS

    def piece(name, inner):
        place = rows.at[name] // rows.size[name]
        if inner:
            return pl.BlockSpec((groups, per_block, rows.size[name], cells), lambda b: (0, b, place, 0))
        return pl.BlockSpec((groups, quads, rows.size[name], cells), lambda b: (0, 0, place, 0))

    fixed = pl.BlockSpec((whole, width), lambda b: (0, 0))
    operands = [scale, held, held, held, held] + list(preds)
    in_specs = [
        pl.BlockSpec(memory_space=pltpu.SMEM),
        piece("map", True),
        piece("prior", True),
        piece("obs", False),
        piece("noise", False),
    ] + [fixed] * len(preds)
    if stage > 1:
        operands.append(multiplier)
        in_specs.append(fixed)
    scratch = [pltpu.VMEM((2, whole, width), jnp.bfloat16)]
    narrow = jax.ShapeDtypeStruct((whole, width), jnp.bfloat16)
    if last:
        out_shape = [narrow, jax.ShapeDtypeStruct((quads, cells, width), jnp.bfloat16)]
        out_specs = [fixed, pl.BlockSpec((per_block, cells, width), lambda b: (b, 0, 0))]
    else:
        out_shape, out_specs = [narrow], [fixed]
        if stage > 0:
            out_shape.append(jax.ShapeDtypeStruct((whole, width), jnp.float32))
            out_specs.append(fixed)
        scratch.append(pltpu.VMEM((whole, width), jnp.float32))
    return pl.pallas_call(
        functools.partial(step_kernel, stage, len(preds), sensors),
        grid=(blocks,),
        in_specs=in_specs,
        out_specs=out_specs,
        out_shape=out_shape,
        scratch_shapes=scratch,
        compiler_params=pltpu.CompilerParams(vmem_limit_bytes=VMEM_LIMIT),
    )(*operands)


def on_device(forward_map, observed, noise_var, prior_rows, prior_scale):
    frequencies, halves, sensors, cells = forward_map.shape
    groups, quads, sides = (lax.axis_size(a) for a in ("sensor", "quad", "side"))
    per_block = prior_rows.shape[1] // cells
    g, q = lax.axis_index("sensor"), lax.axis_index("quad")
    rows = Rows(sensors, cells, groups, quads, prior_rows.shape[1])
    place = jnp.stack([g, q]).astype(jnp.int32)
    scale = lax.dynamic_slice_in_dim(prior_scale, g * quads + q, 1, 0)

    packed = pack(rows, forward_map, observed, noise_var, prior_rows, place, groups, quads)
    held = lax.all_to_all(packed, ("sensor", "quad"), split_axis=0, concat_axis=0, tiled=True)
    held = held.reshape(groups, quads, rows.total, cells)

    def over_sides(partial):
        if sides == 2:
            return [partial, lax.ppermute(partial, "side", [(0, 1), (1, 0)])]
        return [lax.psum(partial, "side")]

    run = functools.partial(step, rows=rows, held=held, scale=scale, sensors=sensors, per_block=per_block)
    preds, multiplier = [], None
    for stage in range(ITERS):
        outs = run(stage, preds=preds, multiplier=multiplier)
        preds = over_sides(outs[0])
        if stage > 0:
            multiplier = outs[1]
    dual, post = run(ITERS, preds=preds, multiplier=multiplier)

    post = lax.all_to_all(post, "quad", split_axis=0, concat_axis=0, tiled=True)
    posterior = post.astype(jnp.float32).reshape(quads, cells, 2, LANES)
    dual = jnp.broadcast_to(dual.reshape(groups, 1, sensors, 2 * LANES), (groups, quads, sensors, 2 * LANES))
    dual = lax.all_to_all(
        dual.reshape(frequencies, sensors, 2 * LANES), ("sensor", "quad"), split_axis=0, concat_axis=0, tiled=True
    )
    dual_out = jnp.stack([dual[:, :, :LANES], dual[:, :, LANES:]], 1).astype(jnp.float32)
    return dual_out, posterior


def solution(mesh):
    groups, space = mesh.devices.shape

    def run(forward_map, observed, noise_var, prior_rows, prior_scale):
        quads = forward_map.shape[0] // groups
        split = Mesh(mesh.devices.reshape(groups, space // quads, quads), ("sensor", "side", "quad"))
        return jax.shard_map(
            on_device,
            mesh=split,
            in_specs=(
                P(None, None, "sensor", ("side", "quad")),
                P(None, None, "sensor", None),
                P("sensor"),
                P(("side", "quad"), None),
                P(),
            ),
            out_specs=(P(None, None, "sensor", None), P("sensor", ("side", "quad"), None, None)),
            check_vma=False,
        )(forward_map, observed, noise_var, prior_rows, prior_scale)

    return run
```

time: 412 us -> 213 us (0.52)
  waiting for transfers between devices: 284 us -> 149 us
  Pallas kernels: 0 us -> 29.8 us
  matrix products: 26.9 us -> 0 us
  other arithmetic: 28.1 us -> 2.87 us
  blocking collectives: 35 us -> 11.8 us
  between operations: 14.2 us -> 0.71 us
  local copies, waits for them, and re-layouts: 9.13 us -> 4.17 us
    psum x2 -> x0, waiting for transfers between devices: 199 us -> none  [space_total(): lax.psum(partial_data.astype(jnp.bfloat16), 'space').astype(jnp.float32)]
    all_to_all x2, waiting for transfers between devices: 48.4 us -> 102 us  [the longest x1 75.4 us: on_device(): lax.all_to_all(packed, ('sensor', 'quad'), split_axis=0, concat_axis=0, t...]
    pallas_call x0 -> x4, Pallas kernels: none -> 29.8 us  [the longest x3 18.5 us: step(): pl.pallas_call(functools.partial(step_kernel, stage, len(preds), sensors)...]
    dot_general x6 -> x0, matrix products: 26.9 us -> none  [the longest x2 15.1 us: on_device(): jnp.einsum('fgkc,fcr->fgkr', stacked, prior_term.astype(jnp.bfloat16), pr...]
    all_to_all x1, blocking collectives: 29.7 us -> 11.8 us  [on_device(): post = lax.all_to_all(post, 'quad', split_axis=0, concat_axis=0, tiled=True)]
    convert_element_type x5 -> x1, other arithmetic: 16.3 us -> 2.29 us  [on_device(): jnp.stack([dual[:, :, :LANES], dual[:, :, LANES:]], 1).astype(jnp.float32)]
    another operation x4 -> x1, other arithmetic: 11.5 us -> 0.58 us  [on_device(): place = jnp.stack([g, q]).astype(jnp.int32)]
    ppermute x3 -> x2, waiting for transfers between devices: 36.8 us -> 46.8 us  [over_sides(): return [partial, lax.ppermute(partial, 'side', [(0, 1), (1, 0)])]]
  transfers between devices with their start and end apart: 7 -> 4, of which waited for: 7 -> 4; matrix products, arithmetic and copies ran while one was open for 3% -> 1% of each run, Pallas kernels for 0% -> 0%
where the time goes in v1:
time: 213 us; the launch traced here: 211 us
  waiting for transfers between devices  149 us (70%)
  Pallas kernels  29.8 us (14%)
  starting transfers between devices  12.9 us (6%)
  blocking collectives  11.8 us (6%)
  local copies, waits for them, and re-layouts  4.17 us (2%)
  other arithmetic  2.87 us (1%)
    all_to_all x1, waiting for transfers between devices, on_device(): lax.all_to_all(packed, ('sensor', 'quad'), split_axis=0, concat_axis=0, t...  75.4 us
    ppermute x2, waiting for transfers between devices, over_sides(): return [partial, lax.ppermute(partial, 'side', [(0, 1), (1, 0)])]  46.8 us
    all_to_all x1, waiting for transfers between devices, on_device(): lax.all_to_all(dual.reshape(frequencies, sensors, 2 * LANES), ('sensor',...  26.4 us
    pallas_call x3, Pallas kernels, step(): pl.pallas_call(functools.partial(step_kernel, stage, len(preds), sensors)...  18.5 us
    all_to_all x1, blocking collectives, on_device(): post = lax.all_to_all(post, 'quad', split_axis=0, concat_axis=0, tiled=True)  11.8 us
    pallas_call x1, Pallas kernels, pack(): pl.pallas_call(functools.partial(pack_kernel, rows), grid_spec=pltpu.Pref...  11.3 us
    all_to_all x1, starting transfers between devices, on_device(): lax.all_to_all(packed, ('sensor', 'quad'), split_axis=0, concat_axis=0, t...  6.46 us
  transfers between devices with their start and end apart: 4, of which 4 were waited for; matrix products, arithmetic and copies ran while one was open for 1% of the time, Pallas kernels for 0%

profile of v1, /device:TPU:0, one launch (start us, length us, event | category | flops | bytes accessed | tf_op | source)
XLA Modules:
  0.0 210.9 jit_solution(14238538122767911005)
XLA Ops:
  0.6 0.6 pad_add_fusion.place_ref
  1.2 11.3 %shard_map.68 = bf16[16,720,256]{2,1,0:T(8,128)(2,1)} custom-call(s32[2]{0:T(128)} %pad_add_fusion.place_ref, bf16[16,512,256]{2,1,0:T(8,128)(2,1)} %bitcast.14, f32[16,2,256,128]{3,2,1,0:T(8,128)} %obs_ref.1, bf16[256,512]{1,0:T(8,128)(2,1)} %prior_ref.1, f32[1,256]{1,0:T(1,128)} %bitcast.15), custom_call_target="tpu_custom_call" | custom-call | tf_op jit(solution)/shard_map/pallas_call | solution.py:70
  12.5 0.0 copy-start
  12.5 6.5 %all-to-all-start = ((bf16[16,720,256]{2,1,0:T(8,128)(2,1)}), bf16[16,720,256]{2,1,0:T(8,128)(2,1)}, u32[]{:S(2)}, u32[]{:S(2)}) async-start(bf16[16,720,256]{2,1,0:T(8,128)(2,1)} %shard_map.68), calls=%async_computation | async-start | bytes 11796480 | tf_op jit(solution)/shard_map/all_to_all | solution.py:219
  19.0 0.0 copy-done
  19.0 0.6 dynamic_slice.3.scale_ref
  19.6 75.4 %all-to-all-done = bf16[16,720,256]{2,1,0:T(8,128)(2,1)} async-done(((bf16[16,720,256]{2,1,0:T(8,128)(2,1)}), bf16[16,720,256]{2,1,0:T(8,128)(2,1)}, u32[]{:S(2)}, u32[]{:S(2)}) %all-to-all-start) | async-done | bytes 5898272 | tf_op jit(solution)/shard_map/all_to_all | solution.py:219
  95.0 6.6 %shard_map.69.rest_0_ = bf16[1024,256]{1,0:T(8,128)(2,1)S(1)} custom-call(f32[1]{0:T(128)} %dynamic_slice.3.scale_ref, bf16[4,4,720,256]{3,2,1,0:T(8,128)(2,1)} %bitcast.4.map_ref.prior_ref.obs_ref.noise_ref, bf16[4,4,720,256]{3,2,1,0:T(8,128)(2,1)} %bitcast.4.map_ref.prior_ref.obs_ref.noise_ref, ...), custom_call_target="tpu_custom_call" | custom-call | tf_op jit(solution)/shard_map/pallas_call | solution.py:198
  101.6 2.7 %collective-permute-start = (bf16[1024,256]{1,0:T(8,128)(2,1)S(1)}, bf16[1024,256]{1,0:T(8,128)(2,1)S(1)}, u32[]{:S(2)}, u32[]{:S(2)}) collective-permute-start(bf16[1024,256]{1,0:T(8,128)(2,1)S(1)} %shard_map.69.rest_0_), channel_id=1, source_target_pairs={{0,4},{4,0},{1,5},{5,1},{2,6},{6,2},{3,7},{7,3},{8,12},{12,8},{9,1... | collective-permute-start | bytes 1572872 | tf_op jit(solution)/shard_map/ppermute | solution.py:224
  104.3 21.4 %collective-permute-done.rest_1_ = bf16[1024,256]{1,0:T(8,128)(2,1)S(1)} collective-permute-done((bf16[1024,256]{1,0:T(8,128)(2,1)S(1)}, bf16[1024,256]{1,0:T(8,128)(2,1)S(1)}, u32[]{:S(2)}, u32[]{:S(2)}) %collective-permute-start) | collective-permute-done | bytes 524320 | tf_op jit(solution)/shard_map/ppermute | solution.py:224
  125.7 6.9 %shard_map.70 = (bf16[1024,256]{1,0:T(8,128)(2,1)S(1)}, f32[1024,256]{1,0:T(8,128)S(1)}) custom-call(f32[1]{0:T(128)} %dynamic_slice.3.scale_ref, bf16[4,4,720,256]{3,2,1,0:T(8,128)(2,1)} %bitcast.4.map_ref.prior_ref.obs_ref.noise_ref, bf16[4,4,720,256]{3,2,1,0:T(8,128)(2,1)} %bitcast.4.map_ref.prior_ref.obs_ref.noise_ref, ...), custom_call_target="tpu_custom_call" | custom-call | tf_op jit(solution)/shard_map/pallas_call | solution.py:198
  132.6 0.1 collective-permute-start.1
  132.7 25.4 %collective-permute-done.1.rest_1_ = bf16[1024,256]{1,0:T(8,128)(2,1)S(1)} collective-permute-done((bf16[1024,256]{1,0:T(8,128)(2,1)S(1)}, bf16[1024,256]{1,0:T(8,128)(2,1)S(1)}, u32[]{:S(2)}, u32[]{:S(2)}) %collective-permute-start.1) | collective-permute-done | bytes 524320 | tf_op jit(solution)/shard_map/ppermute | solution.py:224
  158.1 5.0 %shard_map.71 = (bf16[1024,256]{1,0:T(8,128)(2,1)S(1)}, bf16[4,256,256]{2,1,0:T(8,128)(2,1)S(1)}) custom-call(f32[1]{0:T(128)} %dynamic_slice.3.scale_ref, bf16[4,4,720,256]{3,2,1,0:T(8,128)(2,1)} %bitcast.4.map_ref.prior_ref.obs_ref.noise_ref, bf16[4,4,720,256]{3,2,1,0:T(8,128)(2,1)} %bitcast.4.map_ref.prior_ref.obs_ref.noise_ref, ...), custom_call_target="tpu_custom_call" | custom-call | tf_op jit(solution)/shard_map/pallas_call | solution.py:198
  163.1 11.8 %all_to_all.15 = bf16[4,256,256]{2,1,0:T(8,128)(2,1)S(1)} all-to-all(bf16[4,256,256]{2,1,0:T(8,128)(2,1)S(1)} %get-tuple-element.9), channel_id=1, replica_groups=mesh['sensor'=4,'side'=2,'quad'=4] {'quad'}, dimensions={0} | all-to-all | bytes 1048576 | tf_op jit(solution)/shard_map/all_to_all | solution.py:236
  174.9 1.5 broadcast_in_dim.8
  176.4 3.7 %all-to-all-start.1 = ((bf16[16,256,256]{2,1,0:T(8,128)(2,1)}), bf16[16,256,256]{2,1,0:T(8,128)(2,1)S(1)}, u32[]{:S(2)}, u32[]{:S(2)}) async-start(bf16[16,256,256]{2,1,0:T(8,128)(2,1)} %bitcast.6), calls=%async_computation.1 | async-start | bytes 4194304 | tf_op jit(solution)/shard_map/all_to_all | solution.py:239
  180.2 1.5 reshape.31
  181.6 26.4 %all-to-all-done.1 = bf16[16,256,256]{2,1,0:T(8,128)(2,1)S(1)} async-done(((bf16[16,256,256]{2,1,0:T(8,128)(2,1)}), bf16[16,256,256]{2,1,0:T(8,128)(2,1)S(1)}, u32[]{:S(2)}, u32[]{:S(2)}) %all-to-all-start.1) | async-done | bytes 2097184 | tf_op jit(solution)/shard_map/all_to_all | solution.py:239
  208.1 0.6 slice_bitcast_fusion.1
  208.6 2.3 %maximum_convert_fusion = f32[16,2,256,128]{3,2,1,0:T(8,128)} fusion(bf16[16,1,256,128]{3,2,1,0:T(8,128)(2,1)S(1)} %get-tuple-element.11, bf16[16,1,256,128]{3,2,1,0:T(8,128)(2,1)S(1)} %get-tuple-element.10), kind=kLoop, calls=%fused_computation | loop fusion | flops 2097152 | bytes 6291456 | tf_op jit(solution)/shard_map/convert_element_type | solution.py:242
Async XLA Ops:
  12.5 6.5 %copy-start = (f32[16]{0:T(128)S(1)}, f32[16]{0:T(128)}, u32[]{:S(2)}) copy-start(f32[16]{0:T(128)} %param.9) | copy-start | bytes 196
  12.5 82.5 %all-to-all-start = ((bf16[16,720,256]{2,1,0:T(8,128)(2,1)}), bf16[16,720,256]{2,1,0:T(8,128)(2,1)}, u32[]{:S(2)}, u32[]{:S(2)}) async-start(bf16[16,720,256]{2,1,0:T(8,128)(2,1)} %shard_map.68), calls=%async_computation | async-start | bytes 11796480 | tf_op jit(solution)/shard_map/all_to_all | solution.py:219
  101.6 24.1 %collective-permute-start = (bf16[1024,256]{1,0:T(8,128)(2,1)S(1)}, bf16[1024,256]{1,0:T(8,128)(2,1)S(1)}, u32[]{:S(2)}, u32[]{:S(2)}) collective-permute-start(bf16[1024,256]{1,0:T(8,128)(2,1)S(1)} %shard_map.69.rest_0_), channel_id=1, source_target_pairs={{0,4},{4,0},{1,5},{5,1},{2,6},{6,2},{3,7},{7,3},{8,12},{12,8},{9,1... | collective-permute-start | bytes 1572872 | tf_op jit(solution)/shard_map/ppermute | solution.py:224
  132.6 25.5 %collective-permute-start.1 = (bf16[1024,256]{1,0:T(8,128)(2,1)S(1)}, bf16[1024,256]{1,0:T(8,128)(2,1)S(1)}, u32[]{:S(2)}, u32[]{:S(2)}) collective-permute-start(bf16[1024,256]{1,0:T(8,128)(2,1)S(1)} %get-tuple-element.6.rest_0_), channel_id=1, source_target_pairs={{0,4},{4,0},{1,5},{5,1},{2,6},{6,2},{3,7},{7,3},{8,12},{12,8},{9,1... | collective-permute-start | bytes 1572872 | tf_op jit(solution)/shard_map/ppermute | solution.py:224
  176.4 31.6 %all-to-all-start.1 = ((bf16[16,256,256]{2,1,0:T(8,128)(2,1)}), bf16[16,256,256]{2,1,0:T(8,128)(2,1)S(1)}, u32[]{:S(2)}, u32[]{:S(2)}) async-start(bf16[16,256,256]{2,1,0:T(8,128)(2,1)} %bitcast.6), calls=%async_computation.1 | async-start | bytes 4194304 | tf_op jit(solution)/shard_map/all_to_all | solution.py:239

commit v2 on v0

v2 whole, which is shorter than its diff:
```python
import functools

import jax
import jax.numpy as jnp
from jax import lax
from jax.experimental import pallas as pl
from jax.experimental.pallas import tpu as pltpu
from jax.sharding import Mesh, PartitionSpec as P

ITERS = 2
relax_step = 0.25
STREAMS = 2
LANES = 128
HALF = LANES // 2
VMEM_LIMIT = 32 * 2**20
VMEM = pl.BlockSpec(memory_space=pltpu.VMEM)
SMEM = pl.BlockSpec(memory_space=pltpu.SMEM)
ANY = pl.BlockSpec(memory_space=pl.ANY)
bf16, f32 = jnp.bfloat16, jnp.float32


def shape(dims, dtype):
    return jax.ShapeDtypeStruct(dims, dtype)


def call(kernel, in_specs, out_shape, scratch=(), flops=0, moved=0):
    return pl.pallas_call(
        kernel,
        in_specs=in_specs,
        out_specs=[VMEM] * len(out_shape),
        out_shape=out_shape,
        scratch_shapes=list(scratch),
        cost_estimate=pl.CostEstimate(flops=flops, bytes_accessed=moved, transcendentals=0),
        compiler_params=pltpu.CompilerParams(vmem_limit_bytes=VMEM_LIMIT),
    )


def swap(x, axes, distance):
    count = lax.axis_size(axes)
    return lax.ppermute(x, axes, [(i, i ^ distance) for i in range(count)])


def dot(a, b):
    return jnp.dot(a, b, preferred_element_type=f32)


def dot_t(a, b):
    return lax.dot_general(a, b, (((0,), (0,)), ((), ())), preferred_element_type=f32)


def data_kernel(groups, quads, place_ref, obs_ref, noise_ref, *refs):
    outs, (held, sems) = refs[:groups], refs[groups:]
    sensors = obs_ref.shape[2]
    copies = []
    for d in range(groups):
        freq = (place_ref[0] ^ d) * quads + place_ref[1]
        copies.append(pltpu.make_async_copy(obs_ref.at[freq], held.at[d], sems.at[d]))
        copies[-1].start()
    noise = noise_ref[...]
    high = noise.astype(bf16)
    low = (noise - high.astype(f32)).astype(bf16)
    tail = jnp.concatenate([jnp.broadcast_to(high, (8, sensors)), jnp.broadcast_to(low, (8, sensors))], 0)
    for d in range(groups):
        copies[d].wait()
        re, im = held[d, 0], held[d, 1]
        for s in range(STREAMS):
            part = slice(s * HALF, (s + 1) * HALF)
            outs[d][:sensors, s * LANES:(s + 1) * LANES] = jnp.concatenate([re[:, part], im[:, part]], 1).astype(bf16)
        outs[d][sensors:, :] = tail


def gather_kernel(groups, quads, place_ref, own_ref, *refs):
    halves, other, data = refs[:quads - 1], refs[quads - 1:2 * quads - 2], refs[2 * quads - 2:2 * quads - 2 + groups]
    prior_ref, noise_ref, *streams = refs[2 * quads - 2 + groups:]
    me, quad = place_ref[0], place_ref[1]
    core = me & 1
    sensors = streams[0].shape[1]
    prior_ref[quad] = own_ref[...]
    rows = own_ref.shape[0] // 2
    mine = pl.ds(pl.multiple_of(core * rows, rows), rows)
    theirs = pl.ds(pl.multiple_of((1 - core) * rows, rows), rows)
    for d in range(1, quads):
        prior_ref[quad ^ d, mine, :] = halves[d - 1][...]
        prior_ref[quad ^ d, theirs, :] = other[d - 1][...]
    row = lax.broadcasted_iota(jnp.int32, (sensors, sensors), 0)
    col = lax.broadcasted_iota(jnp.int32, (sensors, sensors), 1)
    for d in range(groups):
        for s in range(STREAMS):
            streams[s][me ^ d] = data[d][:sensors, s * LANES:(s + 1) * LANES]
        both = data[d][sensors:, :].astype(f32)
        noise_row = both[0:1, :] + both[8:9, :]
        noise = jnp.sum(jnp.where(row == col, noise_row, 0.0), 1, keepdims=True)
        noise_ref[me ^ d] = jnp.broadcast_to(noise, (sensors, LANES))


def step_kernel(stage, n_pred, per_block, place_ref, scale_ref, map_ref, prior_ref, obs_ref, noise_ref, *rest):
    groups, quads, double, cells = map_ref.shape
    sensors = double // 2
    last = stage == ITERS
    preds, rest = rest[:n_pred], rest[n_pred:]
    if stage > 1:
        held_ref, rest = rest[0], rest[1:]
    if last:
        keep_ref, give_ref, post_ref, z_ref, dual_ref = rest
    elif stage > 0:
        out_ref, next_ref, z_ref = rest
    else:
        out_ref, z_ref = rest

    for g in range(groups):
        obs = obs_ref[g].astype(f32)
        now = relax_step * obs if stage < 2 else held_ref[g]
        if stage > 0:
            predicted = sum(p[g].astype(f32) for p in preds)
            now = now + relax_step * (obs - predicted - noise_ref[g] * now)
            if not last:
                next_ref[g] = now
        z = now.astype(bf16)
        z_ref[g, :sensors, :] = z
        z_ref[g, sensors:, :] = jnp.concatenate([z[:, HALF:], -z[:, :HALF]], 1)
        if last:
            dual_ref[g] = z
    if last:
        core = place_ref[0] & 1
        for pair in range(groups // 2):
            keep_ref[pair] = dual_ref[2 * pair + core]
            give_ref[pair] = dual_ref[2 * pair + 1 - core]

    scale = scale_ref[0]
    sources = []
    for block in range(quads // per_block):
        parts = []
        for q in range(block * per_block, (block + 1) * per_block):
            u = jnp.zeros((cells, LANES), f32)
            for g in range(groups):
                u += dot_t(map_ref[g, q], z_ref[g])
            parts.append(u.astype(bf16))
        ub = jnp.concatenate(parts, 0)
        for q in range(block * per_block, (block + 1) * per_block):
            v = (dot(prior_ref[q], ub) * scale).astype(bf16)
            if last:
                post_ref[q] = v
            else:
                sources.append((v, jnp.concatenate([-v[:, HALF:], v[:, :HALF]], 1)))
    if not last:
        for g in range(groups):
            total = jnp.zeros((sensors, LANES), f32)
            for q, (v, w) in enumerate(sources):
                total += dot(map_ref[g, q, :sensors, :], v) + dot(map_ref[g, q, sensors:, :], w)
            out_ref[g] = total.astype(bf16)


def send_kernel(groups, quads, place_ref, keep_ref, got_ref, post_ref, *outs):
    sensors = keep_ref.shape[1]
    pair, quad = place_ref[0] // 2, place_ref[1]
    for e in range(groups // 2):
        for d in range(quads if e == 0 else 1):
            out = outs[d] if e == 0 else outs[quads + e - 1]
            out[:sensors] = keep_ref[pair ^ e]
            out[sensors:2 * sensors] = got_ref[pair ^ e]
            if e == 0:
                out[2 * sensors:] = post_ref[quad ^ d]


def end_kernel(groups, quads, place_ref, *refs):
    count = groups // 2 * quads
    first, second, (dual_ref, post_ref) = refs[:count], refs[count:2 * count], refs[2 * count:]
    sensors = dual_ref.shape[2]
    cells = post_ref.shape[1] // 2
    me, quad = place_ref[0], place_ref[1]
    for e in range(groups // 2):
        for d in range(quads):
            a, b = first[e * quads + d], second[e * quads + d]
            for sibling in range(2):
                freq = (me ^ (2 * e + sibling)) * quads + (quad ^ d)
                span = slice(sibling * sensors, (sibling + 1) * sensors)
                x, y = a[span, :].astype(f32), b[span, :].astype(f32)
                dual_ref[freq, 0] = jnp.concatenate([x[:, :HALF], y[:, :HALF]], 1)
                dual_ref[freq, 1] = jnp.concatenate([x[:, HALF:], y[:, HALF:]], 1)
            if e == 0:
                x, y = a[2 * sensors:, :].astype(f32), b[2 * sensors:, :].astype(f32)
                post_ref[quad ^ d, pl.ds(0, cells, stride=2), :] = jnp.concatenate([x[:, :HALF], y[:, :HALF]], 1)
                post_ref[quad ^ d, pl.ds(1, cells, stride=2), :] = jnp.concatenate([x[:, HALF:], y[:, HALF:]], 1)


def spread(count):
    order = []
    for d in sorted(range(1, count), key=lambda d: -bin(d).count("1")):
        for x in (d, count - 1 - d):
            if x and x not in order:
                order.append(x)
    return order


def on_device(forward_map, observed, noise_var, prior_rows, prior_scale):
    frequencies, halves, sensors, cells = forward_map.shape
    groups, quads, sides = (lax.axis_size(a) for a in ("sensor", "quad", "side"))
    width = prior_rows.shape[1]
    per_block = width // cells
    me, quad = lax.axis_index("sensor"), lax.axis_index("quad")
    place = jnp.stack([me, quad]).astype(jnp.int32)
    scale = lax.dynamic_slice_in_dim(prior_scale, me * quads + quad, 1, 0)
    both = ("sensor", "quad")

    held = lax.all_to_all(
        forward_map.reshape(frequencies, halves * sensors, cells), both, split_axis=0, concat_axis=0, tiled=True
    ).reshape(groups, quads, halves * sensors, cells)

    data = call(
        functools.partial(data_kernel, groups, quads),
        [SMEM, ANY, VMEM],
        [shape((sensors + 16, STREAMS * LANES), bf16)] * groups,
        [pltpu.VMEM((groups, halves, sensors, LANES), f32), pltpu.SemaphoreType.DMA((groups,))],
        moved=groups * sensors * LANES * 12,
    )(place, observed, noise_var.reshape(1, sensors))
    data = [data[0]] + [swap(data[d], "sensor", d) for d in range(1, groups)]
    own_half = lax.dynamic_slice_in_dim(prior_rows, (me % 2) * (cells // 2), cells // 2, 0)
    came = [swap(own_half, "quad", d) for d in range(1, quads)]
    other = [swap(x, "sensor", 1) for x in came]
    prior, noise, *streams = call(
        functools.partial(gather_kernel, groups, quads),
        [SMEM] + [VMEM] * (1 + 2 * (quads - 1) + groups),
        [shape((quads, cells, width), bf16), shape((groups, sensors, LANES), f32)]
        + [shape((groups, sensors, LANES), bf16)] * STREAMS,
        moved=8 * 2**20,
    )(place, prior_rows, *came, *other, *data)

    def over_sides(partial):
        if sides == 2:
            return [partial, swap(partial, "side", 1)]
        return [lax.psum(partial, "side")]

    wide, narrow = shape((groups, sensors, LANES), f32), shape((groups, sensors, LANES), bf16)
    pairs = shape((groups // 2, sensors, LANES), bf16)

    def step(stage, obs, preds, multiplier):
        operands = [place, scale, held, prior, obs, noise] + preds + ([multiplier] if stage > 1 else [])
        out = [pairs, pairs, shape((quads, cells, LANES), bf16)] if stage == ITERS else [narrow] + [wide] * (stage > 0)
        scratch = [pltpu.VMEM((groups, halves * sensors, LANES), bf16)]
        if stage == ITERS:
            scratch.append(pltpu.VMEM((groups, sensors, LANES), bf16))
        return call(
            functools.partial(step_kernel, stage, len(preds), per_block),
            [SMEM, SMEM] + [VMEM] * (len(operands) - 2),
            out,
            scratch,
            flops=2 * 2**30,
            moved=8 * 2**20,
        )(*operands)

    preds, multiplier = [[]] * STREAMS, [None] * STREAMS
    for stage in range(ITERS):
        for s in range(STREAMS):
            outs = step(stage, streams[s], preds[s], multiplier[s])
            preds = preds[:s] + [over_sides(outs[0])] + preds[s + 1:]
            if stage > 0:
                multiplier[s] = outs[1]

    arrived = []
    for s in range(STREAMS):
        keep, give, post = step(ITERS, streams[s], preds[s], multiplier[s])
        messages = call(
            functools.partial(send_kernel, groups, quads),
            [SMEM] + [VMEM] * 3,
            [shape((2 * sensors + cells, LANES), bf16)] * quads
            + [shape((2 * sensors, LANES), bf16)] * (groups // 2 - 1),
            moved=4 * 2**20,
        )(place, keep, swap(give, "sensor", 1), post)
        got = {0: messages[0]}
        for distance in spread(groups // 2 * quads):
            e, d = divmod(distance, quads)
            out = messages[d] if e == 0 else messages[quads + e - 1]
            got[distance] = swap(out, both, 2 * e * quads + d)
        arrived += [got[i] for i in range(groups // 2 * quads)]
    dual, posterior = call(
        functools.partial(end_kernel, groups, quads),
        [SMEM] + [VMEM] * len(arrived),
        [shape((frequencies, halves, sensors, LANES), f32), shape((quads, cells * 2, LANES), f32)],
        moved=8 * 2**20,
    )(place, *arrived)
    return dual, posterior.reshape(quads, cells, 2, LANES)


def solution(mesh):
    groups, space = mesh.devices.shape

    def run(forward_map, observed, noise_var, prior_rows, prior_scale):
        quads = forward_map.shape[0] // groups
        split = Mesh(mesh.devices.reshape(groups, space // quads, quads), ("sensor", "side", "quad"))
        return jax.shard_map(
            on_device,
            mesh=split,
            in_specs=(
                P(None, None, "sensor", ("side", "quad")),
                P(None, None, "sensor", None),
                P("sensor"),
                P(("side", "quad"), None),
                P(),
            ),
            out_specs=(P(None, None, "sensor", None), P("sensor", ("side", "quad"), None, None)),
            check_vma=False,
        )(forward_map, observed, noise_var, prior_rows, prior_scale)

    return run
```

time: 412 us -> 182 us (0.44)
  waiting for transfers between devices: 284 us -> 97.9 us
  Pallas kernels: 0 us -> 40.9 us
  blocking collectives: 35 us -> 0 us
  other arithmetic: 28.1 us -> 0.07 us
  matrix products: 26.9 us -> 0 us
  starting transfers between devices: 14.1 us -> 37.5 us
  between operations: 14.2 us -> 0.83 us
  local copies, waits for them, and re-layouts: 9.13 us -> 4.45 us
    psum x2 -> x0, waiting for transfers between devices: 199 us -> none  [space_total(): lax.psum(partial_data.astype(jnp.bfloat16), 'space').astype(jnp.float32)]
    ppermute x3 -> x29, waiting for transfers between devices: 36.8 us -> 97.9 us  [swap(): return lax.ppermute(x, axes, [(i, i ^ distance) for i in range(count)])]
    all_to_all x2 -> x1, waiting for transfers between devices: 48.4 us -> 0.01 us  [on_device(): lax.all_to_all(forward_map.reshape(frequencies, halves * sensors, cells),...]
    pallas_call x0 -> x11, Pallas kernels: none -> 40.9 us  [the longest x6 34 us: step(): call(functools.partial(step_kernel, stage, len(preds), per_block), [SMEM,...]
    all_to_all x1 -> x0, blocking collectives: 29.7 us -> none  [on_device(): lax.all_to_all(observed.reshape(frequencies, 1, halves, sensors_here, sce...]
    dot_general x6 -> x0, matrix products: 26.9 us -> none  [the longest x2 15.1 us: on_device(): jnp.einsum('fgkc,fcr->fgkr', stacked, prior_term.astype(jnp.bfloat16), pr...]
    ppermute x3 -> x29, starting transfers between devices: 4.6 us -> 31 us  [swap(): return lax.ppermute(x, axes, [(i, i ^ distance) for i in range(count)])]
    convert_element_type x5 -> x0, other arithmetic: 16.3 us -> none  [the longest x2 6.57 us: adjoint(): right_sides = stack_sides(multiplier.astype(jnp.bfloat16))]
  transfers between devices with their start and end apart: 7 -> 30, of which waited for: 7 -> 16; matrix products, arithmetic and copies ran while one was open for 3% -> 0% of each run, Pallas kernels for 0% -> 17%
where the time goes in v2:
time: 182 us
  waiting for transfers between devices  97.9 us (54%)
  Pallas kernels  40.9 us (22%)
  starting transfers between devices  37.5 us (21%)
  local copies, waits for them, and re-layouts  4.45 us (2%)
    ppermute x29, waiting for transfers between devices, swap(): return lax.ppermute(x, axes, [(i, i ^ distance) for i in range(count)])  97.9 us
    pallas_call x6, Pallas kernels, step(): call(functools.partial(step_kernel, stage, len(preds), per_block), [SMEM,...  34 us
    ppermute x29, starting transfers between devices, swap(): return lax.ppermute(x, axes, [(i, i ^ distance) for i in range(count)])  31 us
    all_to_all x1, starting transfers between devices, on_device(): lax.all_to_all(forward_map.reshape(frequencies, halves * sensors, cells),...  6.48 us
    unnamed x12, local copies, waits for them, and re-layouts  3.85 us
    pallas_call x1, Pallas kernels, on_device(): call(functools.partial(end_kernel, groups, quads), [SMEM] + [VMEM] * len(...  3.66 us
  transfers between devices with their start and end apart: 30, of which 16 were waited for; matrix products, arithmetic and copies ran while one was open for 0% of the time, Pallas kernels for 17%

profile of v2, /device:TPU:0, one launch (start us, length us, event | category | flops | bytes accessed | tf_op | source)
XLA Modules:
  0.0 181.5 jit_solution(1787288360638214224)
XLA Ops:
  0.6 6.5 %all-to-all-start = ((bf16[16,512,256]{2,1,0:T(8,128)(2,1)}), bf16[16,512,256]{2,1,0:T(8,128)(2,1)}, u32[]{:S(2)}, u32[]{:S(2)}) async-start(bf16[16,512,256]{2,1,0:T(8,128)(2,1)} %bitcast.7), calls=%async_computation | async-start | bytes 8388608 | tf_op jit(solution)/shard_map/all_to_all | solution.py:205
  7.2 2.8 %collective-permute-start.2 = (bf16[128,512]{1,0:T(8,128)(2,1)S(1)}, bf16[128,512]{1,0:T(8,128)(2,1)S(1)}, u32[]{:S(2)}, u32[]{:S(2)}) collective-permute-start(bf16[128,512]{1,0:T(8,128)(2,1)S(1)} %constant_dynamic-slice_fusion), channel_id=1, source_target_pairs={{0,3},{1,2},{2,1},{3,0},{4,7},{5,6},{6,5},{7,4},{8,11},{9,10},{10,... | collective-permute-start | bytes 393224 | tf_op jit(solution)/shard_map/ppermute | solution.py:40
  10.1 2.2 %copy-done = f32[16,2,256,128]{3,2,1,0:T(8,128)S(1)} copy-done((f32[16,2,256,128]{3,2,1,0:T(8,128)S(1)}, f32[16,2,256,128]{3,2,1,0:T(8,128)}, u32[]{:S(2)}) %copy-start) | copy-done | bytes 4194328
  12.3 1.1 shard_map.68
  14.3 1.9 %collective-permute-start.7 = (bf16[272,256]{1,0:T(8,128)(2,1)S(1)}, bf16[272,256]{1,0:T(8,128)(2,1)S(1)}, u32[]{:S(2)}, u32[]{:S(2)}) collective-permute-start(bf16[272,256]{1,0:T(8,128)(2,1)S(1)} %get-tuple-element.34), channel_id=1, source_target_pairs={{0,16},{8,24},{16,0},{24,8},{1,17},{9,25},{17,1},{25,9},{2,18},{10... | collective-permute-start | bytes 417800 | tf_op jit(solution)/shard_map/ppermute | solution.py:40
  16.2 50.2 %collective-permute-done.2.refs_2_ = bf16[128,512]{1,0:T(8,128)(2,1)S(1)} collective-permute-done((bf16[128,512]{1,0:T(8,128)(2,1)S(1)}, bf16[128,512]{1,0:T(8,128)(2,1)S(1)}, u32[]{:S(2)}, u32[]{:S(2)}) %collective-permute-start.2) | collective-permute-done | bytes 131104 | tf_op jit(solution)/shard_map/ppermute | solution.py:40
  68.6 3.3 %collective-permute-done.8.refs_9_ = bf16[272,256]{1,0:T(8,128)(2,1)S(1)} collective-permute-done((bf16[272,256]{1,0:T(8,128)(2,1)S(1)}, bf16[272,256]{1,0:T(8,128)(2,1)S(1)}, u32[]{:S(2)}, u32[]{:S(2)}) %collective-permute-start.8) | collective-permute-done | bytes 139296 | tf_op jit(solution)/shard_map/ppermute | solution.py:40
  74.4 5.9 %shard_map.70.rest_0_ = bf16[4,256,128]{2,1,0:T(8,128)(2,1)S(1)} custom-call(s32[2]{0:T(128)S(1)} %pad_add_fusion.place_ref, f32[1]{0:T(128)} %dynamic_slice.6.scale_ref, bf16[4,4,512,256]{3,2,1,0:T(8,128)(2,1)} %bitcast.3.map_ref, bf16[4,256,512]{2,1,0:T(8,128)(2,1)S(1)} %get-tuple-element.36.prior_ref, bf16[4,256,128]{2,1,0:T(8,128)(2,1)S(1)} %copy-done.4, ...), custom_call_target="tpu_custom_call" | custom-call | flops 2147483648 | bytes 8388608 | tf_op jit(solution)/shard_map/pallas_call | solution.py:242
  80.4 2.7 %collective-permute-start.9 = (bf16[4,256,128]{2,1,0:T(8,128)(2,1)S(1)}, bf16[4,256,128]{2,1,0:T(8,128)(2,1)S(1)}, u32[]{:S(2)}, u32[]{:S(2)}) collective-permute-start(bf16[4,256,128]{2,1,0:T(8,128)(2,1)S(1)} %shard_map.70.rest_0_), channel_id=1, source_target_pairs={{0,4},{4,0},{1,5},{5,1},{2,6},{6,2},{3,7},{7,3},{8,12},{12,8},{9,1... | collective-permute-start | bytes 786440 | tf_op jit(solution)/shard_map/ppermute | solution.py:40
  83.0 5.9 %shard_map.74.rest_0_ = bf16[4,256,128]{2,1,0:T(8,128)(2,1)S(1)} custom-call(s32[2]{0:T(128)S(1)} %pad_add_fusion.place_ref, f32[1]{0:T(128)} %dynamic_slice.6.scale_ref, bf16[4,4,512,256]{3,2,1,0:T(8,128)(2,1)} %bitcast.3.map_ref, bf16[4,256,512]{2,1,0:T(8,128)(2,1)S(1)} %get-tuple-element.36.prior_ref, bf16[4,256,128]{2,1,0:T(8,128)(2,1)S(1)} %get-tuple-element.49.obs_ref, ...), custom_call_target="tpu_custom_call" | custom-call | flops 2147483648 | bytes 8388608 | tf_op jit(solution)/shard_map/pallas_call | solution.py:242
  89.4 9.3 %collective-permute-done.9.rest_1_ = bf16[4,256,128]{2,1,0:T(8,128)(2,1)S(1)} collective-permute-done((bf16[4,256,128]{2,1,0:T(8,128)(2,1)S(1)}, bf16[4,256,128]{2,1,0:T(8,128)(2,1)S(1)}, u32[]{:S(2)}, u32[]{:S(2)}) %collective-permute-start.9) | collective-permute-done | bytes 262176 | tf_op jit(solution)/shard_map/ppermute | solution.py:40
  98.7 6.0 %shard_map.71 = (bf16[4,256,128]{2,1,0:T(8,128)(2,1)S(1)}, f32[4,256,128]{2,1,0:T(8,128)S(1)}) custom-call(s32[2]{0:T(128)S(1)} %pad_add_fusion.place_ref, f32[1]{0:T(128)} %dynamic_slice.6.scale_ref, bf16[4,4,512,256]{3,2,1,0:T(8,128)(2,1)} %bitcast.3.map_ref, bf16[4,256,512]{2,1,0:T(8,128)(2,1)S(1)} %get-tuple-element.36.prior_ref, ...), custom_call_target="tpu_custom_call" | custom-call | flops 2147483648 | bytes 8388608 | tf_op jit(solution)/shard_map/pallas_call | solution.py:242
  104.8 6.2 %shard_map.75 = (bf16[4,256,128]{2,1,0:T(8,128)(2,1)S(1)}, f32[4,256,128]{2,1,0:T(8,128)S(1)}) custom-call(s32[2]{0:T(128)S(1)} %pad_add_fusion.place_ref, f32[1]{0:T(128)} %dynamic_slice.6.scale_ref, bf16[4,4,512,256]{3,2,1,0:T(8,128)(2,1)} %bitcast.3.map_ref, bf16[4,256,512]{2,1,0:T(8,128)(2,1)S(1)} %get-tuple-element.36.prior_ref, ...), custom_call_target="tpu_custom_call" | custom-call | flops 2147483648 | bytes 8388608 | tf_op jit(solution)/shard_map/pallas_call | solution.py:242
  111.0 3.0 %collective-permute-start.20 = (bf16[4,256,128]{2,1,0:T(8,128)(2,1)S(1)}, bf16[4,256,128]{2,1,0:T(8,128)(2,1)S(1)}, u32[]{:S(2)}, u32[]{:S(2)}) collective-permute-start(bf16[4,256,128]{2,1,0:T(8,128)(2,1)S(1)} %get-tuple-element.50.rest_0_), channel_id=1, source_target_pairs={{0,4},{4,0},{1,5},{5,1},{2,6},{6,2},{3,7},{7,3},{8,12},{12,8},{9,1... | collective-permute-start | bytes 786440 | tf_op jit(solution)/shard_map/ppermute | solution.py:40
  114.0 10.2 %collective-permute-done.10.rest_1_ = bf16[4,256,128]{2,1,0:T(8,128)(2,1)S(1)} collective-permute-done((bf16[4,256,128]{2,1,0:T(8,128)(2,1)S(1)}, bf16[4,256,128]{2,1,0:T(8,128)(2,1)S(1)}, u32[]{:S(2)}, u32[]{:S(2)}) %collective-permute-start.10) | collective-permute-done | bytes 262176 | tf_op jit(solution)/shard_map/ppermute | solution.py:40
  124.2 4.9 %shard_map.72 = (bf16[2,256,128]{2,1,0:T(8,128)(2,1)S(1)}, bf16[2,256,128]{2,1,0:T(8,128)(2,1)S(1)}, bf16[4,256,128]{2,1,0:T(8,128)(2,1)S(1)}) custom-call(s32[2]{0:T(128)S(1)} %pad_add_fusion.place_ref, f32[1]{0:T(128)} %dynamic_slice.6.scale_ref, bf16[4,4,512,256]{3,2,1,0:T(8,128)(2,1)} %bitcast.3.map_ref, ...), custom_call_target="tpu_custom_call" | custom-call | flops 2147483648 | bytes 8388608 | tf_op jit(solution)/shard_map/pallas_call | solution.py:242
  129.7 4.9 %shard_map.76 = (bf16[2,256,128]{2,1,0:T(8,128)(2,1)S(1)}, bf16[2,256,128]{2,1,0:T(8,128)(2,1)S(1)}, bf16[4,256,128]{2,1,0:T(8,128)(2,1)S(1)}) custom-call(s32[2]{0:T(128)S(1)} %pad_add_fusion.place_ref, f32[1]{0:T(128)} %dynamic_slice.6.scale_ref, bf16[4,4,512,256]{3,2,1,0:T(8,128)(2,1)} %bitcast.3.map_ref, ...), custom_call_target="tpu_custom_call" | custom-call | flops 2147483648 | bytes 8388608 | tf_op jit(solution)/shard_map/pallas_call | solution.py:242
  135.4 1.0 collective-permute-start.18
  136.4 3.3 %collective-permute-start.17 = (bf16[512,128]{1,0:T(8,128)(2,1)S(1)}, bf16[512,128]{1,0:T(8,128)(2,1)S(1)}, u32[]{:S(2)}, u32[]{:S(2)}) collective-permute-start(bf16[512,128]{1,0:T(8,128)(2,1)S(1)} %get-tuple-element.48), channel_id=1, source_target_pairs={{0,18},{1,19},{2,16},{3,17},{8,26},{9,27},{10,24},{11,25},{16,2},{... | collective-permute-start | bytes 393224 | tf_op jit(solution)/shard_map/ppermute | solution.py:40
  141.3 1.9 %collective-permute-start.12 = (bf16[768,128]{1,0:T(8,128)(2,1)S(1)}, bf16[768,128]{1,0:T(8,128)(2,1)S(1)}, u32[]{:S(2)}, u32[]{:S(2)}) collective-permute-start(bf16[768,128]{1,0:T(8,128)(2,1)S(1)} %get-tuple-element.45), channel_id=1, source_target_pairs={{0,1},{1,0},{2,3},{3,2},{8,9},{9,8},{10,11},{11,10},{16,17},{17,16... | collective-permute-start | bytes 589832 | tf_op jit(solution)/shard_map/ppermute | solution.py:40
  144.2 2.3 %collective-permute-done.17.refs_6_ = bf16[512,128]{1,0:T(8,128)(2,1)S(1)} collective-permute-done((bf16[512,128]{1,0:T(8,128)(2,1)S(1)}, bf16[512,128]{1,0:T(8,128)(2,1)S(1)}, u32[]{:S(2)}, u32[]{:S(2)}) %collective-permute-start.17) | collective-permute-done | bytes 131104 | tf_op jit(solution)/shard_map/ppermute | solution.py:40
  146.5 1.4 collective-permute-start.27
  147.9 6.6 %collective-permute-done.16.refs_5_ = bf16[512,128]{1,0:T(8,128)(2,1)S(1)} collective-permute-done((bf16[512,128]{1,0:T(8,128)(2,1)S(1)}, bf16[512,128]{1,0:T(8,128)(2,1)S(1)}, u32[]{:S(2)}, u32[]{:S(2)}) %collective-permute-start.16) | collective-permute-done | bytes 131104 | tf_op jit(solution)/shard_map/ppermute | solution.py:40
  154.5 2.4 %collective-permute-start.26 = (bf16[512,128]{1,0:T(8,128)(2,1)S(1)}, bf16[512,128]{1,0:T(8,128)(2,1)S(1)}, u32[]{:S(2)}, u32[]{:S(2)}) collective-permute-start(bf16[512,128]{1,0:T(8,128)(2,1)S(1)} %get-tuple-element.59), channel_id=1, source_target_pairs={{0,17},{1,16},{2,19},{3,18},{8,25},{9,24},{10,27},{11,26},{16,1},{... | collective-permute-start | bytes 393224 | tf_op jit(solution)/shard_map/ppermute | solution.py:40
  157.7 1.0 collective-permute-start.25
  158.7 2.0 %collective-permute-start.14 = (bf16[768,128]{1,0:T(8,128)(2,1)S(1)}, bf16[768,128]{1,0:T(8,128)(2,1)S(1)}, u32[]{:S(2)}, u32[]{:S(2)}) collective-permute-start(bf16[768,128]{1,0:T(8,128)(2,1)S(1)} %get-tuple-element.47), channel_id=1, source_target_pairs={{0,3},{1,2},{2,1},{3,0},{8,11},{9,10},{10,9},{11,8},{16,19},{17,18... | collective-permute-start | bytes 589832 | tf_op jit(solution)/shard_map/ppermute | solution.py:40
  161.7 1.9 %collective-permute-start.22 = (bf16[768,128]{1,0:T(8,128)(2,1)S(1)}, bf16[768,128]{1,0:T(8,128)(2,1)S(1)}, u32[]{:S(2)}, u32[]{:S(2)}) collective-permute-start(bf16[768,128]{1,0:T(8,128)(2,1)S(1)} %get-tuple-element.56), channel_id=1, source_target_pairs={{0,1},{1,0},{2,3},{3,2},{8,9},{9,8},{10,11},{11,10},{16,17},{17,16... | collective-permute-start | bytes 589832 | tf_op jit(solution)/shard_map/ppermute | solution.py:40
  164.0 1.6 collective-permute-start.24
  166.5 4.2 %collective-permute-done.14.refs_3_ = bf16[768,128]{1,0:T(8,128)(2,1)S(1)} collective-permute-done((bf16[768,128]{1,0:T(8,128)(2,1)S(1)}, bf16[768,128]{1,0:T(8,128)(2,1)S(1)}, u32[]{:S(2)}, u32[]{:S(2)}) %collective-permute-start.14) | collective-permute-done | bytes 196640 | tf_op jit(solution)/shard_map/ppermute | solution.py:40
  171.0 4.0 %collective-permute-done.23.refs_10_ = bf16[768,128]{1,0:T(8,128)(2,1)S(1)} collective-permute-done((bf16[768,128]{1,0:T(8,128)(2,1)S(1)}, bf16[768,128]{1,0:T(8,128)(2,1)S(1)}, u32[]{:S(2)}, u32[]{:S(2)}) %collective-permute-start.23) | collective-permute-done | bytes 196640 | tf_op jit(solution)/shard_map/ppermute | solution.py:40
  175.0 2.9 %collective-permute-done.24.refs_11_ = bf16[768,128]{1,0:T(8,128)(2,1)S(1)} collective-permute-done((bf16[768,128]{1,0:T(8,128)(2,1)S(1)}, bf16[768,128]{1,0:T(8,128)(2,1)S(1)}, u32[]{:S(2)}, u32[]{:S(2)}) %collective-permute-start.24) | collective-permute-done | bytes 196640 | tf_op jit(solution)/shard_map/ppermute | solution.py:40
  177.9 3.7 %shard_map.78 = (f32[16,2,256,128]{3,2,1,0:T(8,128)}, f32[4,512,128]{2,1,0:T(8,128)}) custom-call(s32[2]{0:T(128)S(1)} %pad_add_fusion.place_ref, bf16[768,128]{1,0:T(8,128)(2,1)S(1)} %get-tuple-element.44.refs_0_, bf16[768,128]{1,0:T(8,128)(2,1)S(1)} %collective-permute-done.12.refs_1_, bf16[768,128]{1,0:T(8,128)(2,1)S(1)} %collective-permute-done.13.refs_2_, ...), custom_call_target="tpu_custom_call" | custom-call | bytes 8388608 | tf_op jit(solution)/shard_map/pallas_call | solution.py:275
  (54 shorter events, 13.4 us)
Async XLA Ops:
  0.6 9.5 %copy-start.2 = (f32[256]{0:T(256)S(1)}, f32[256]{0:T(256)}, u32[]{:S(2)}) copy-start(f32[256]{0:T(256)} %param.7) | copy-start | bytes 3076
  0.6 72.8 %all-to-all-start = ((bf16[16,512,256]{2,1,0:T(8,128)(2,1)}), bf16[16,512,256]{2,1,0:T(8,128)(2,1)}, u32[]{:S(2)}, u32[]{:S(2)}) async-start(bf16[16,512,256]{2,1,0:T(8,128)(2,1)} %bitcast.7), calls=%async_computation | async-start | bytes 8388608 | tf_op jit(solution)/shard_map/all_to_all | solution.py:205
  7.1 60.8 %copy-start.5 = (f32[16]{0:T(128)S(1)}, f32[16]{0:T(128)}, u32[]{:S(2)}) copy-start(f32[16]{0:T(128)} %param.9) | copy-start | bytes 196
  7.2 59.1 %collective-permute-start.2 = (bf16[128,512]{1,0:T(8,128)(2,1)S(1)}, bf16[128,512]{1,0:T(8,128)(2,1)S(1)}, u32[]{:S(2)}, u32[]{:S(2)}) collective-permute-start(bf16[128,512]{1,0:T(8,128)(2,1)S(1)} %constant_dynamic-slice_fusion), channel_id=1, source_target_pairs={{0,3},{1,2},{2,1},{3,0},{4,7},{5,6},{6,5},{7,4},{8,11},{9,10},{10,... | collective-permute-start | bytes 393224 | tf_op jit(solution)/shard_map/ppermute | solution.py:40
  13.4 54.3 %collective-permute-start.6 = (bf16[272,256]{1,0:T(8,128)(2,1)S(1)}, bf16[272,256]{1,0:T(8,128)(2,1)S(1)}, u32[]{:S(2)}, u32[]{:S(2)}) collective-permute-start(bf16[272,256]{1,0:T(8,128)(2,1)S(1)} %get-tuple-element.33), channel_id=1, source_target_pairs={{0,8},{8,0},{16,24},{24,16},{1,9},{9,1},{17,25},{25,17},{2,10},{10... | collective-permute-start | bytes 417800 | tf_op jit(solution)/shard_map/ppermute | solution.py:40
  13.5 53.7 %collective-permute-start.1 = (bf16[128,512]{1,0:T(8,128)(2,1)S(1)}, bf16[128,512]{1,0:T(8,128)(2,1)S(1)}, u32[]{:S(2)}, u32[]{:S(2)}) collective-permute-start(bf16[128,512]{1,0:T(8,128)(2,1)S(1)} %constant_dynamic-slice_fusion), channel_id=1, source_target_pairs={{0,2},{1,3},{2,0},{3,1},{4,6},{5,7},{6,4},{7,5},{8,10},{9,11},{10,... | collective-permute-start | bytes 393224 | tf_op jit(solution)/shard_map/ppermute | solution.py:40
  14.1 53.3 %collective-permute-start = (bf16[128,512]{1,0:T(8,128)(2,1)S(1)}, bf16[128,512]{1,0:T(8,128)(2,1)S(1)}, u32[]{:S(2)}, u32[]{:S(2)}) collective-permute-start(bf16[128,512]{1,0:T(8,128)(2,1)S(1)} %constant_dynamic-slice_fusion), channel_id=1, source_target_pairs={{0,1},{1,0},{2,3},{3,2},{4,5},{5,4},{6,7},{7,6},{8,9},{9,8},{10,11... | collective-permute-start | bytes 393224 | tf_op jit(solution)/shard_map/ppermute | solution.py:40
  14.3 54.3 %collective-permute-start.7 = (bf16[272,256]{1,0:T(8,128)(2,1)S(1)}, bf16[272,256]{1,0:T(8,128)(2,1)S(1)}, u32[]{:S(2)}, u32[]{:S(2)}) collective-permute-start(bf16[272,256]{1,0:T(8,128)(2,1)S(1)} %get-tuple-element.34), channel_id=1, source_target_pairs={{0,16},{8,24},{16,0},{24,8},{1,17},{9,25},{17,1},{25,9},{2,18},{10... | collective-permute-start | bytes 417800 | tf_op jit(solution)/shard_map/ppermute | solution.py:40
  66.3 5.5 %collective-permute-start.8 = (bf16[272,256]{1,0:T(8,128)(2,1)S(1)}, bf16[272,256]{1,0:T(8,128)(2,1)S(1)}, u32[]{:S(2)}, u32[]{:S(2)}) collective-permute-start(bf16[272,256]{1,0:T(8,128)(2,1)S(1)} %get-tuple-element.35), channel_id=1, source_target_pairs={{0,24},{8,16},{16,8},{24,0},{1,25},{9,17},{17,9},{25,1},{2,26},{10... | collective-permute-start | bytes 417800 | tf_op jit(solution)/shard_map/ppermute | solution.py:40
  67.2 4.7 %collective-permute-start.5 = (bf16[128,512]{1,0:T(8,128)(2,1)S(1)}, bf16[128,512]{1,0:T(8,128)(2,1)S(1)}, u32[]{:S(2)}, u32[]{:S(2)}) collective-permute-start(bf16[128,512]{1,0:T(8,128)(2,1)S(1)} %collective-permute-done.2.refs_2_), channel_id=1, source_target_pairs={{0,8},{8,0},{16,24},{24,16},{1,9},{9,1},{17,25},{25,17},{2,10},{10... | collective-permute-start | bytes 393224 | tf_op jit(solution)/shard_map/ppermute | solution.py:40
  67.5 4.4 %collective-permute-start.4 = (bf16[128,512]{1,0:T(8,128)(2,1)S(1)}, bf16[128,512]{1,0:T(8,128)(2,1)S(1)}, u32[]{:S(2)}, u32[]{:S(2)}) collective-permute-start(bf16[128,512]{1,0:T(8,128)(2,1)S(1)} %collective-permute-done.1.refs_1_), channel_id=1, source_target_pairs={{0,8},{8,0},{16,24},{24,16},{1,9},{9,1},{17,25},{25,17},{2,10},{10... | collective-permute-start | bytes 393224 | tf_op jit(solution)/shard_map/ppermute | solution.py:40
  67.7 4.2 %collective-permute-start.3 = (bf16[128,512]{1,0:T(8,128)(2,1)S(1)}, bf16[128,512]{1,0:T(8,128)(2,1)S(1)}, u32[]{:S(2)}, u32[]{:S(2)}) collective-permute-start(bf16[128,512]{1,0:T(8,128)(2,1)S(1)} %collective-permute-done.refs_0_), channel_id=1, source_target_pairs={{0,8},{8,0},{16,24},{24,16},{1,9},{9,1},{17,25},{25,17},{2,10},{10... | collective-permute-start | bytes 393224 | tf_op jit(solution)/shard_map/ppermute | solution.py:40
  80.4 18.3 %collective-permute-start.9 = (bf16[4,256,128]{2,1,0:T(8,128)(2,1)S(1)}, bf16[4,256,128]{2,1,0:T(8,128)(2,1)S(1)}, u32[]{:S(2)}, u32[]{:S(2)}) collective-permute-start(bf16[4,256,128]{2,1,0:T(8,128)(2,1)S(1)} %shard_map.70.rest_0_), channel_id=1, source_target_pairs={{0,4},{4,0},{1,5},{5,1},{2,6},{6,2},{3,7},{7,3},{8,12},{12,8},{9,1... | collective-permute-start | bytes 786440 | tf_op jit(solution)/shard_map/ppermute | solution.py:40
  89.0 15.8 %collective-permute-start.19 = (bf16[4,256,128]{2,1,0:T(8,128)(2,1)S(1)}, bf16[4,256,128]{2,1,0:T(8,128)(2,1)S(1)}, u32[]{:S(2)}, u32[]{:S(2)}) collective-permute-start(bf16[4,256,128]{2,1,0:T(8,128)(2,1)S(1)} %shard_map.74.rest_0_), channel_id=1, source_target_pairs={{0,4},{4,0},{1,5},{5,1},{2,6},{6,2},{3,7},{7,3},{8,12},{12,8},{9,1... | collective-permute-start | bytes 786440 | tf_op jit(solution)/shard_map/ppermute | solution.py:40
  104.7 19.5 %collective-permute-start.10 = (bf16[4,256,128]{2,1,0:T(8,128)(2,1)S(1)}, bf16[4,256,128]{2,1,0:T(8,128)(2,1)S(1)}, u32[]{:S(2)}, u32[]{:S(2)}) collective-permute-start(bf16[4,256,128]{2,1,0:T(8,128)(2,1)S(1)} %get-tuple-element.39.rest_0_), channel_id=1, source_target_pairs={{0,4},{4,0},{1,5},{5,1},{2,6},{6,2},{3,7},{7,3},{8,12},{12,8},{9,1... | collective-permute-start | bytes 786440 | tf_op jit(solution)/shard_map/ppermute | solution.py:40
  111.0 18.7 %collective-permute-start.20 = (bf16[4,256,128]{2,1,0:T(8,128)(2,1)S(1)}, bf16[4,256,128]{2,1,0:T(8,128)(2,1)S(1)}, u32[]{:S(2)}, u32[]{:S(2)}) collective-permute-start(bf16[4,256,128]{2,1,0:T(8,128)(2,1)S(1)} %get-tuple-element.50.rest_0_), channel_id=1, source_target_pairs={{0,4},{4,0},{1,5},{5,1},{2,6},{6,2},{3,7},{7,3},{8,12},{12,8},{9,1... | collective-permute-start | bytes 786440 | tf_op jit(solution)/shard_map/ppermute | solution.py:40
  129.1 5.6 %collective-permute-start.11 = (bf16[2,256,128]{2,1,0:T(8,128)(2,1)S(1)}, bf16[2,256,128]{2,1,0:T(8,128)(2,1)S(1)}, u32[]{:S(2)}, u32[]{:S(2)}) collective-permute-start(bf16[2,256,128]{2,1,0:T(8,128)(2,1)S(1)} %get-tuple-element.42), channel_id=1, source_target_pairs={{0,8},{8,0},{16,24},{24,16},{1,9},{9,1},{17,25},{25,17},{2,10},{10... | collective-permute-start | bytes 393224 | tf_op jit(solution)/shard_map/ppermute | solution.py:40
  134.7 6.7 %collective-permute-start.21 = (bf16[2,256,128]{2,1,0:T(8,128)(2,1)S(1)}, bf16[2,256,128]{2,1,0:T(8,128)(2,1)S(1)}, u32[]{:S(2)}, u32[]{:S(2)}) collective-permute-start(bf16[2,256,128]{2,1,0:T(8,128)(2,1)S(1)} %get-tuple-element.53), channel_id=1, source_target_pairs={{0,8},{8,0},{16,24},{24,16},{1,9},{9,1},{17,25},{25,17},{2,10},{10... | collective-permute-start | bytes 393224 | tf_op jit(solution)/shard_map/ppermute | solution.py:40
  135.4 8.5 %collective-permute-start.18 = (bf16[512,128]{1,0:T(8,128)(2,1)S(1)}, bf16[512,128]{1,0:T(8,128)(2,1)S(1)}, u32[]{:S(2)}, u32[]{:S(2)}) collective-permute-start(bf16[512,128]{1,0:T(8,128)(2,1)S(1)} %get-tuple-element.48), channel_id=1, source_target_pairs={{0,19},{1,18},{2,17},{3,16},{8,27},{9,26},{10,25},{11,24},{16,3},{... | collective-permute-start | bytes 393224 | tf_op jit(solution)/shard_map/ppermute | solution.py:40
  136.4 10.1 %collective-permute-start.17 = (bf16[512,128]{1,0:T(8,128)(2,1)S(1)}, bf16[512,128]{1,0:T(8,128)(2,1)S(1)}, u32[]{:S(2)}, u32[]{:S(2)}) collective-permute-start(bf16[512,128]{1,0:T(8,128)(2,1)S(1)} %get-tuple-element.48), channel_id=1, source_target_pairs={{0,18},{1,19},{2,16},{3,17},{8,26},{9,27},{10,24},{11,25},{16,2},{... | collective-permute-start | bytes 393224 | tf_op jit(solution)/shard_map/ppermute | solution.py:40
  139.7 14.8 %collective-permute-start.16 = (bf16[512,128]{1,0:T(8,128)(2,1)S(1)}, bf16[512,128]{1,0:T(8,128)(2,1)S(1)}, u32[]{:S(2)}, u32[]{:S(2)}) collective-permute-start(bf16[512,128]{1,0:T(8,128)(2,1)S(1)} %get-tuple-element.48), channel_id=1, source_target_pairs={{0,17},{1,16},{2,19},{3,18},{8,25},{9,24},{10,27},{11,26},{16,1},{... | collective-permute-start | bytes 393224 | tf_op jit(solution)/shard_map/ppermute | solution.py:40
  140.7 17.0 %collective-permute-start.15 = (bf16[512,128]{1,0:T(8,128)(2,1)S(1)}, bf16[512,128]{1,0:T(8,128)(2,1)S(1)}, u32[]{:S(2)}, u32[]{:S(2)}) collective-permute-start(bf16[512,128]{1,0:T(8,128)(2,1)S(1)} %get-tuple-element.48), channel_id=1, source_target_pairs={{0,16},{1,17},{2,18},{3,19},{8,24},{9,25},{10,26},{11,27},{16,0},{... | collective-permute-start | bytes 393224 | tf_op jit(solution)/shard_map/ppermute | solution.py:40
  141.3 22.7 %collective-permute-start.12 = (bf16[768,128]{1,0:T(8,128)(2,1)S(1)}, bf16[768,128]{1,0:T(8,128)(2,1)S(1)}, u32[]{:S(2)}, u32[]{:S(2)}) collective-permute-start(bf16[768,128]{1,0:T(8,128)(2,1)S(1)} %get-tuple-element.45), channel_id=1, source_target_pairs={{0,1},{1,0},{2,3},{3,2},{8,9},{9,8},{10,11},{11,10},{16,17},{17,16... | collective-permute-start | bytes 589832 | tf_op jit(solution)/shard_map/ppermute | solution.py:40
  143.9 14.8 %collective-permute-start.28 = (bf16[512,128]{1,0:T(8,128)(2,1)S(1)}, bf16[512,128]{1,0:T(8,128)(2,1)S(1)}, u32[]{:S(2)}, u32[]{:S(2)}) collective-permute-start(bf16[512,128]{1,0:T(8,128)(2,1)S(1)} %get-tuple-element.59), channel_id=1, source_target_pairs={{0,19},{1,18},{2,17},{3,16},{8,27},{9,26},{10,25},{11,24},{16,3},{... | collective-permute-start | bytes 393224 | tf_op jit(solution)/shard_map/ppermute | solution.py:40
  146.5 12.2 %collective-permute-start.27 = (bf16[512,128]{1,0:T(8,128)(2,1)S(1)}, bf16[512,128]{1,0:T(8,128)(2,1)S(1)}, u32[]{:S(2)}, u32[]{:S(2)}) collective-permute-start(bf16[512,128]{1,0:T(8,128)(2,1)S(1)} %get-tuple-element.59), channel_id=1, source_target_pairs={{0,18},{1,19},{2,16},{3,17},{8,26},{9,27},{10,24},{11,25},{16,2},{... | collective-permute-start | bytes 393224 | tf_op jit(solution)/shard_map/ppermute | solution.py:40
  154.5 7.1 %collective-permute-start.26 = (bf16[512,128]{1,0:T(8,128)(2,1)S(1)}, bf16[512,128]{1,0:T(8,128)(2,1)S(1)}, u32[]{:S(2)}, u32[]{:S(2)}) collective-permute-start(bf16[512,128]{1,0:T(8,128)(2,1)S(1)} %get-tuple-element.59), channel_id=1, source_target_pairs={{0,17},{1,16},{2,19},{3,18},{8,25},{9,24},{10,27},{11,26},{16,1},{... | collective-permute-start | bytes 393224 | tf_op jit(solution)/shard_map/ppermute | solution.py:40
  157.7 6.3 %collective-permute-start.25 = (bf16[512,128]{1,0:T(8,128)(2,1)S(1)}, bf16[512,128]{1,0:T(8,128)(2,1)S(1)}, u32[]{:S(2)}, u32[]{:S(2)}) collective-permute-start(bf16[512,128]{1,0:T(8,128)(2,1)S(1)} %get-tuple-element.59), channel_id=1, source_target_pairs={{0,16},{1,17},{2,18},{3,19},{8,24},{9,25},{10,26},{11,27},{16,0},{... | collective-permute-start | bytes 393224 | tf_op jit(solution)/shard_map/ppermute | solution.py:40
  158.7 7.8 %collective-permute-start.13 = (bf16[768,128]{1,0:T(8,128)(2,1)S(1)}, bf16[768,128]{1,0:T(8,128)(2,1)S(1)}, u32[]{:S(2)}, u32[]{:S(2)}) collective-permute-start(bf16[768,128]{1,0:T(8,128)(2,1)S(1)} %get-tuple-element.46), channel_id=1, source_target_pairs={{0,2},{1,3},{2,0},{3,1},{8,10},{9,11},{10,8},{11,9},{16,18},{17,19... | collective-permute-start | bytes 589832 | tf_op jit(solution)/shard_map/ppermute | solution.py:40
  158.7 12.0 %collective-permute-start.14 = (bf16[768,128]{1,0:T(8,128)(2,1)S(1)}, bf16[768,128]{1,0:T(8,128)(2,1)S(1)}, u32[]{:S(2)}, u32[]{:S(2)}) collective-permute-start(bf16[768,128]{1,0:T(8,128)(2,1)S(1)} %get-tuple-element.47), channel_id=1, source_target_pairs={{0,3},{1,2},{2,1},{3,0},{8,11},{9,10},{10,9},{11,8},{16,19},{17,18... | collective-permute-start | bytes 589832 | tf_op jit(solution)/shard_map/ppermute | solution.py:40
  161.7 9.3 %collective-permute-start.22 = (bf16[768,128]{1,0:T(8,128)(2,1)S(1)}, bf16[768,128]{1,0:T(8,128)(2,1)S(1)}, u32[]{:S(2)}, u32[]{:S(2)}) collective-permute-start(bf16[768,128]{1,0:T(8,128)(2,1)S(1)} %get-tuple-element.56), channel_id=1, source_target_pairs={{0,1},{1,0},{2,3},{3,2},{8,9},{9,8},{10,11},{11,10},{16,17},{17,16... | collective-permute-start | bytes 589832 | tf_op jit(solution)/shard_map/ppermute | solution.py:40
  164.0 11.0 %collective-permute-start.23 = (bf16[768,128]{1,0:T(8,128)(2,1)S(1)}, bf16[768,128]{1,0:T(8,128)(2,1)S(1)}, u32[]{:S(2)}, u32[]{:S(2)}) collective-permute-start(bf16[768,128]{1,0:T(8,128)(2,1)S(1)} %get-tuple-element.57), channel_id=1, source_target_pairs={{0,2},{1,3},{2,0},{3,1},{8,10},{9,11},{10,8},{11,9},{16,18},{17,19... | collective-permute-start | bytes 589832 | tf_op jit(solution)/shard_map/ppermute | solution.py:40
  164.0 13.9 %collective-permute-start.24 = (bf16[768,128]{1,0:T(8,128)(2,1)S(1)}, bf16[768,128]{1,0:T(8,128)(2,1)S(1)}, u32[]{:S(2)}, u32[]{:S(2)}) collective-permute-start(bf16[768,128]{1,0:T(8,128)(2,1)S(1)} %get-tuple-element.58), channel_id=1, source_target_pairs={{0,3},{1,2},{2,1},{3,0},{8,11},{9,10},{10,9},{11,8},{16,19},{17,18... | collective-permute-start | bytes 589832 | tf_op jit(solution)/shard_map/ppermute | solution.py:40
  (4 other events, 10.4 us)

commit v3 on v0

v3 whole, which is shorter than its diff:
```python
import functools

import jax
import jax.numpy as jnp
from jax import lax
from jax.experimental import pallas as pl
from jax.experimental.pallas import tpu as pltpu
from jax.sharding import Mesh, PartitionSpec as P

ITERS = 2
relax_step = 0.25
CORES = 2
LANES = 128
HALF = LANES // CORES
BATCHES = ((0, 1),)
VMEM_LIMIT = 32 * 2**20
VMEM = pl.BlockSpec(memory_space=pltpu.VMEM)
SMEM = pl.BlockSpec(memory_space=pltpu.SMEM)
ANY = pl.BlockSpec(memory_space=pl.ANY)
bf16, f32 = jnp.bfloat16, jnp.float32


def shape(dims, dtype):
    return jax.ShapeDtypeStruct(dims, dtype)


def call(kernel, in_specs, out_shape, scratch=(), out_specs=None, flops=0, moved=0):
    return pl.pallas_call(
        kernel,
        in_specs=in_specs,
        out_specs=out_specs or [VMEM] * len(out_shape),
        out_shape=out_shape,
        scratch_shapes=list(scratch),
        cost_estimate=pl.CostEstimate(flops=flops, bytes_accessed=moved, transcendentals=0),
        compiler_params=pltpu.CompilerParams(vmem_limit_bytes=VMEM_LIMIT),
    )


def dot(a, b):
    return jnp.dot(a, b, preferred_element_type=f32)


def dot_nt(a, b):
    return lax.dot_general(a, b, (((1,), (1,)), ((), ())), preferred_element_type=f32)


class Plan:
    def __init__(self, groups, quads, sensors, cells, width):
        self.groups, self.quads, self.sensors, self.cells, self.width = groups, quads, sensors, cells, width
        self.pairs = groups // CORES
        self.chips = self.pairs * quads
        self.per_block = width // cells
        self.map_rows = 2 * sensors
        self.share = cells // CORES

    def extra(self, batch, d):
        e, dq = divmod(d, self.quads)
        if batch > 0:
            return 0
        if dq == 0:
            return CORES * self.sensors + 16
        return self.share * self.per_block if e == 0 else 0

    def rows(self, batch, d):
        return len(BATCHES[batch]) * self.map_rows + self.extra(batch, d)

    def order(self):
        order = []
        for d in sorted(range(1, self.chips), key=lambda d: -bin(d).count("1")):
            for x in (d, self.chips - 1 - d):
                if x and x not in order:
                    order.append(x)
        return order


def pack_kernel(plan, batch, place_ref, map_ref, obs_ref, prior_ref, noise_ref, *refs):
    outs, (held, lines, sems) = refs[:plan.chips], refs[plan.chips:]
    pair, quad, core = place_ref[0], place_ref[1], place_ref[2]
    chip = pair * plan.quads + quad
    copies = []
    first, count = BATCHES[batch][0], len(BATCHES[batch])
    for d in range(plan.chips):
        freq = CORES * (chip ^ d) + first
        for j in range(count):
            to = outs[d].at[pl.ds(j * plan.map_rows, plan.map_rows)]
            copies.append(pltpu.make_async_copy(map_ref.at[freq + j], to, sems.at[d, j]))
            copies[-1].start()
    if batch == 0:
        at = count * plan.map_rows
        noise = noise_ref[...]
        high = noise.astype(bf16)
        low = (noise - high.astype(f32)).astype(bf16)
        wide = (8, plan.sensors)
        tail = jnp.concatenate([jnp.broadcast_to(high, wide), jnp.broadcast_to(low, wide)], 0)
        loads = []
        for e in range(plan.pairs):
            freq = CORES * (chip ^ (e * plan.quads))
            loads.append(pltpu.make_async_copy(obs_ref.at[pl.ds(freq, CORES)], held.at[e], sems.at[plan.chips, e]))
            loads[-1].start()
        half = prior_ref[pl.ds(pl.multiple_of(core * plan.share, plan.share), plan.share), :]
        for k in range(plan.per_block):
            lines[0, k * plan.share:(k + 1) * plan.share, :] = half[:, k * plan.cells:(k + 1) * plan.cells]
        stores = []
        for dq in range(1, plan.quads):
            size = plan.share * plan.per_block
            to = outs[dq].at[pl.ds(at, size)]
            stores.append(pltpu.make_async_copy(lines.at[0, pl.ds(0, size)], to, sems.at[plan.chips + 1, dq]))
            stores[-1].start()
        for e in range(plan.pairs):
            loads[e].wait()
            slot = 1 + e
            for j in range(CORES):
                re, im = held[e, j, 0], held[e, j, 1]
                for s in range(CORES):
                    part = slice(s * HALF, (s + 1) * HALF)
                    lines[slot, j * plan.sensors:(j + 1) * plan.sensors, s * LANES:(s + 1) * LANES] = (
                        jnp.concatenate([re[:, part], im[:, part]], 1).astype(bf16)
                    )
            size = plan.extra(0, 0)
            lines[slot, size - 16:size, :] = tail
            to = outs[e * plan.quads].at[pl.ds(at, size)]
            stores.append(pltpu.make_async_copy(lines.at[slot, pl.ds(0, size)], to, sems.at[plan.chips + 2, e]))
            stores[-1].start()
        for copy in stores:
            copy.wait()
    for copy in copies:
        copy.wait()


def gather_kernel(plan, place_ref, own_ref, *refs):
    mine, theirs = refs[:plan.chips], refs[plan.chips:2 * plan.chips]
    prior_ref, noise_ref, *streams = refs[2 * plan.chips:]
    quad, core = place_ref[1], place_ref[2]
    at = len(BATCHES[0]) * plan.map_rows
    share, cells, sensors = plan.share, plan.cells, plan.sensors
    for k in range(plan.per_block):
        column = k ^ (quad & (plan.per_block - 1))
        to = slice(k * cells, (k + 1) * cells)
        prior_ref[0, :, to] = own_ref[:, pl.ds(pl.multiple_of(column * cells, cells), cells)]
        for dq in range(1, plan.quads):
            span = pl.ds(pl.multiple_of(at + column * share, share), share)
            for part, ref in ((core, mine[dq]), (1 - core, theirs[dq])):
                prior_ref[dq, pl.ds(pl.multiple_of(part * share, share), share), to] = ref[span, :]
    row = lax.broadcasted_iota(jnp.int32, (sensors, sensors), 0)
    col = lax.broadcasted_iota(jnp.int32, (sensors, sensors), 1)
    lanes = pl.ds(pl.multiple_of(core * LANES, LANES), LANES)
    for e in range(plan.pairs):
        for s, refs_s in enumerate((mine, theirs)):
            ref, r = refs_s[e * plan.quads], CORES * e + s
            for j in range(CORES):
                streams[j][r] = ref[at + j * sensors:at + (j + 1) * sensors, lanes]
            both = ref[at + CORES * sensors:, :].astype(f32)
            noise_row = both[0:1, :] + both[8:9, :]
            noise = jnp.sum(jnp.where(row == col, noise_row, 0.0), 1, keepdims=True)
            noise_ref[r] = jnp.broadcast_to(noise, (sensors, LANES))


def sides(z):
    return jnp.concatenate([z, jnp.concatenate([z[:, HALF:], -z[:, :HALF]], 1)], 0).T


def source(plan, chunk, sides_ref, prior_ref, scale):
    out = []
    for block in range(plan.quads // plan.per_block):
        quads = range(block * plan.per_block, (block + 1) * plan.per_block)
        parts = []
        for dq in quads:
            u = jnp.zeros((LANES, plan.cells), f32)
            for r in range(plan.groups):
                u += dot(sides_ref[r], chunk(r, dq)[...])
            parts.append(u.astype(bf16))
        ub = jnp.concatenate(parts, 1)
        out += [(dot_nt(prior_ref[dq], ub) * scale).astype(bf16) for dq in quads]
    return out


def chunks(plan, refs, start):
    rows = pl.ds(start, plan.map_rows)
    return lambda r, dq: refs[(r % CORES) * plan.chips + r // CORES * plan.quads + dq].at[rows]


def step_kernel(plan, stage, start, n_pred, scale_ref, prior_ref, obs_ref, noise_ref, *refs):
    chunk, refs = chunks(plan, refs, start), refs[2 * plan.chips:]
    preds, refs = refs[:n_pred], refs[n_pred:]
    if stage > 0:
        next_ref, refs = refs[0], refs[1:]
    outs, sides_ref = refs[:-1], refs[-1]
    for r in range(plan.groups):
        obs = obs_ref[r].astype(f32)
        now = relax_step * obs
        if stage > 0:
            predicted = sum(p[r].astype(f32) for p in preds)
            now = now + relax_step * (obs - predicted - noise_ref[r] * now)
            next_ref[r] = now
        sides_ref[r] = sides(now.astype(bf16))
    sources = source(plan, chunk, sides_ref, prior_ref, scale_ref[0])
    turned = [jnp.concatenate([-v[:, HALF:], v[:, :HALF]], 1) for v in sources]
    for r in reversed(range(plan.groups)):
        total = jnp.zeros((plan.sensors, LANES), f32)
        for dq in range(plan.quads):
            block = chunk(r, dq)
            total += dot(block[:plan.sensors, :], sources[dq]) + dot(block[plan.sensors:, :], turned[dq])
        if len(outs) == 1:
            outs[0][r] = total.astype(bf16)
        else:
            outs[r // CORES][r % CORES] = total.astype(bf16)


def last_kernel(plan, e, n_pred, noise_ref, *refs):
    obs, held, refs = refs[:CORES], refs[CORES:2 * CORES], refs[2 * CORES:]
    preds, (keep_ref, give_ref) = refs[:CORES * n_pred], refs[CORES * n_pred:]
    for j in range(CORES):
        for s, out in ((1, give_ref), (0, keep_ref)):
            r = CORES * e + s
            now = held[j][r]
            predicted = sum(p[s].astype(f32) for p in preds[j * n_pred:(j + 1) * n_pred])
            now = now + relax_step * (obs[j][r].astype(f32) - predicted - noise_ref[r] * now)
            out[j] = now.astype(bf16)


def merge(flag, mine, theirs):
    low, high = jnp.where(flag, theirs, mine), jnp.where(flag, mine, theirs)
    re = jnp.concatenate([low[:, :HALF], high[:, :HALF]], 1)
    im = jnp.concatenate([low[:, HALF:], high[:, HALF:]], 1)
    return re, im


def send_kernel(place_ref, keep_ref, got_ref, out_ref):
    for j in range(CORES):
        re, im = merge(place_ref[2] == 1, keep_ref[j].astype(f32), got_ref[j].astype(f32))
        out_ref[j, :, :LANES] = re.astype(bf16)
        out_ref[j, :, LANES:] = im.astype(bf16)


def post_kernel(plan, starts, place_ref, scale_ref, prior_ref, *refs):
    maps, refs = refs[:2 * plan.chips * len(BATCHES)], refs[2 * plan.chips * len(BATCHES):]
    keeps, gives, refs = refs[:plan.pairs], refs[plan.pairs:2 * plan.pairs], refs[2 * plan.pairs:]
    outs, (sides_ref, held_ref) = refs[:plan.quads], refs[plan.quads:]
    quad, core = place_ref[1], place_ref[2]
    for j in range(CORES):
        batch, start = starts[j]
        chunk = chunks(plan, maps[2 * plan.chips * batch:], start)
        for r in range(plan.groups):
            sides_ref[r] = sides((gives if r % CORES else keeps)[r // CORES][j])
        for dq, v in enumerate(source(plan, chunk, sides_ref, prior_ref, scale_ref[j])):
            held_ref[dq, j] = v
    wide = plan.quads // CORES
    for flip in range(CORES):
        for step in range(wide):
            to = (core ^ flip) * wide + ((quad & (wide - 1)) ^ step)
            outs[flip * wide + step][...] = held_ref[to ^ quad]


def post_route(groups, quads, flip, step):
    wide, route = quads // CORES, []
    for g in range(groups):
        for q in range(quads):
            core = g % CORES
            to_quad = (core ^ flip) * wide + ((q % wide) ^ step)
            route.append((g * quads + q, (g - core + q // wide) * quads + to_quad))
    return route


def end_kernel(plan, place_ref, *refs):
    duals, posts = refs[:plan.chips], refs[plan.chips:plan.chips + plan.quads]
    dual_ref, post_ref = refs[plan.chips + plan.quads:]
    pair, quad = place_ref[0], place_ref[1]
    chip = pair * plan.quads + quad
    for d in range(plan.chips):
        for j in range(CORES):
            freq = CORES * (chip ^ d) + j
            dual_ref[freq, 0] = duals[d][j, :, :LANES].astype(f32)
            dual_ref[freq, 1] = duals[d][j, :, LANES:].astype(f32)
    wide = plan.quads // CORES
    for step in range(wide):
        for j in range(CORES):
            re, im = merge(quad // wide == 1, posts[step][j].astype(f32), posts[wide + step][j].astype(f32))
            freq = CORES * ((quad & (wide - 1)) ^ step) + j
            post_ref[freq, pl.ds(0, plan.cells, stride=2), :] = re
            post_ref[freq, pl.ds(1, plan.cells, stride=2), :] = im


def on_device(forward_map, observed, noise_var, prior_rows, prior_scale):
    frequencies, halves, sensors, cells = forward_map.shape
    groups, quads, count = (lax.axis_size(a) for a in ("sensor", "quad", "side"))
    plan = Plan(groups, quads, sensors, cells, prior_rows.shape[1])
    me, quad = lax.axis_index("sensor"), lax.axis_index("quad")
    pair, core = me // CORES, me % CORES
    place = jnp.stack([pair, quad, core]).astype(jnp.int32)
    scales = lax.dynamic_slice_in_dim(prior_scale, CORES * (pair * quads + quad), CORES, 0)
    both = ("sensor", "quad")

    def swap(x, axes, distance):
        return lax.ppermute(x, axes, [(i, i ^ distance) for i in range(lax.axis_size(axes))])

    def to_chip(x, d):
        e, dq = divmod(d, quads)
        return swap(x, both, CORES * e * quads + dq)

    def to_sibling(x):
        return swap(x, "sensor", 1)

    flat = forward_map.reshape(frequencies, halves * sensors, cells)
    maps = []
    for batch in range(len(BATCHES)):
        line = max(plan.extra(0, d) for d in range(plan.chips))
        messages = call(
            functools.partial(pack_kernel, plan, batch),
            [SMEM, ANY, ANY, VMEM, VMEM],
            [shape((plan.rows(batch, d), cells), bf16) for d in range(plan.chips)],
            [
                pltpu.VMEM((plan.pairs, CORES, halves, sensors, LANES), f32),
                pltpu.VMEM((1 + plan.pairs, line, cells), bf16),
                pltpu.SemaphoreType.DMA((plan.chips + 3, max(plan.chips, quads, CORES))),
            ],
            [ANY] * plan.chips,
            moved=10 * 2**20,
        )(place, flat, observed, prior_rows, noise_var.reshape(1, sensors))
        mine = [messages[0]] + [None] * (plan.chips - 1)
        for d in plan.order():
            mine[d] = to_chip(messages[d], d)
        maps.append(mine + [to_sibling(x) for x in mine])
    starts = {}
    for batch, held in enumerate(BATCHES):
        for i, j in enumerate(held):
            starts[j] = (batch, i * plan.map_rows)

    prior, noise, *streams = call(
        functools.partial(gather_kernel, plan),
        [SMEM] + [VMEM] * (1 + 2 * plan.chips),
        [shape((quads, cells, plan.width), bf16), shape((groups, sensors, LANES), f32)]
        + [shape((groups, sensors, LANES), bf16)] * CORES,
        moved=4 * 2**20,
    )(place, prior_rows, *maps[0])

    def over_sides(partial):
        if count == 2:
            return [partial, swap(partial, "side", 1)]
        return [lax.psum(partial, "side")]

    wide, narrow = shape((groups, sensors, LANES), f32), shape((groups, sensors, LANES), bf16)
    couple = shape((CORES, sensors, LANES), bf16)
    sides_scratch = pltpu.VMEM((groups, LANES, halves * sensors), bf16)

    def step(stage, j, preds):
        batch, start = starts[j]
        operands = [scales[j:j + 1], prior, streams[j], noise] + maps[batch] + preds
        return call(
            functools.partial(step_kernel, plan, stage, start, len(preds)),
            [SMEM] + [VMEM] * (len(operands) - 1),
            [narrow] if stage == 0 else [wide] + [couple] * plan.pairs,
            [sides_scratch],
            flops=2**31,
            moved=8 * 2**20,
        )(*operands)

    first = [over_sides(step(0, j, [])[0]) for j in range(CORES)]
    multiplier, partials = [], []
    for j in range(CORES):
        held, *parts = step(1, j, first[j])
        multiplier.append(held)
        partials.append(parts)
    keeps, gives = [None] * plan.pairs, [None] * plan.pairs
    duals = [None] * plan.chips
    for e in reversed(range(plan.pairs)):
        preds = [over_sides(partials[j][e]) for j in range(CORES)]
        preds = preds[0] + preds[1]
        keeps[e], gives[e] = call(
            functools.partial(last_kernel, plan, e, len(preds) // CORES),
            [VMEM] * (1 + 2 * CORES + len(preds)),
            [couple, couple],
            moved=2 * 2**20,
        )(noise, *streams, *multiplier, *preds)
        message = call(
            send_kernel,
            [SMEM, VMEM, VMEM],
            [shape((CORES, sensors, 2 * LANES), bf16)],
            moved=2**20,
        )(place, keeps[e], to_sibling(gives[e]))[0]
        for dq in reversed(range(quads)):
            d = e * quads + dq
            duals[d] = to_chip(message, d) if d else message

    posts = call(
        functools.partial(post_kernel, plan, starts),
        [SMEM, SMEM] + [VMEM] * (1 + sum(len(m) for m in maps) + 2 * plan.pairs),
        [shape((CORES, cells, LANES), bf16)] * quads,
        [sides_scratch, pltpu.VMEM((quads, CORES, cells, LANES), bf16)],
        flops=2**31,
        moved=16 * 2**20,
    )(place, scales, prior, *[x for m in maps for x in m], *keeps, *gives)
    half = quads // CORES
    posts = [lax.ppermute(posts[i], both, post_route(groups, quads, *divmod(i, half))) for i in range(quads)]
    dual, posterior = call(
        functools.partial(end_kernel, plan),
        [SMEM] + [VMEM] * (plan.chips + quads),
        [shape((frequencies, halves, sensors, LANES), f32), shape((quads, cells * 2, LANES), f32)],
        moved=8 * 2**20,
    )(place, *duals, *posts)
    return dual, posterior.reshape(quads, cells, 2, LANES)


def solution(mesh):
    groups, space = mesh.devices.shape

    def run(forward_map, observed, noise_var, prior_rows, prior_scale):
        quads = forward_map.shape[0] // groups
        split = Mesh(mesh.devices.reshape(groups, space // quads, quads), ("sensor", "side", "quad"))
        return jax.shard_map(
            on_device,
            mesh=split,
            in_specs=(
                P(None, None, "sensor", ("side", "quad")),
                P(None, None, "sensor", None),
                P("sensor"),
                P(("side", "quad"), None),
                P(),
            ),
            out_specs=(P(None, None, "sensor", None), P("sensor", ("side", "quad"), None, None)),
            check_vma=False,
        )(forward_map, observed, noise_var, prior_rows, prior_scale)

    return run
```

time: 412 us -> 195 us (0.47)
  waiting for transfers between devices: 284 us -> 105 us
  Pallas kernels: 0 us -> 38.7 us
  blocking collectives: 35 us -> 0 us
  other arithmetic: 28.1 us -> 0.08 us
  matrix products: 26.9 us -> 0 us
  starting transfers between devices: 14.1 us -> 36 us
  between operations: 14.2 us -> 0.84 us
  local copies, waits for them, and re-layouts: 9.13 us -> 14 us
    psum x2 -> x0, waiting for transfers between devices: 199 us -> none  [space_total(): lax.psum(partial_data.astype(jnp.bfloat16), 'space').astype(jnp.float32)]
    ppermute x3 -> x34, waiting for transfers between devices: 36.8 us -> 105 us  [the longest x30 96.3 us: swap(): lax.ppermute(x, axes, [(i, i ^ distance) for i in range(lax.axis_size(axe...]
    all_to_all x2 -> x0, waiting for transfers between devices: 48.4 us -> none  [the longest x1 42.3 us: on_device(): lax.all_to_all(local_map, 'sensor', split_axis=0, concat_axis=1, tiled=True)]
    pallas_call x0 -> x12, Pallas kernels: none -> 38.7 us  [the longest x4 23.1 us: step(): call(functools.partial(step_kernel, plan, stage, start, len(preds)), [SME...]
    ppermute x3 -> x34, starting transfers between devices: 4.6 us -> 36 us  [the longest x30 33.2 us: swap(): lax.ppermute(x, axes, [(i, i ^ distance) for i in range(lax.axis_size(axe...]
    all_to_all x1 -> x0, blocking collectives: 29.7 us -> none  [on_device(): lax.all_to_all(observed.reshape(frequencies, 1, halves, sensors_here, sce...]
    dot_general x6 -> x0, matrix products: 26.9 us -> none  [the longest x2 15.1 us: on_device(): jnp.einsum('fgkc,fcr->fgkr', stacked, prior_term.astype(jnp.bfloat16), pr...]
    convert_element_type x5 -> x0, other arithmetic: 16.3 us -> none  [the longest x2 6.57 us: adjoint(): right_sides = stack_sides(multiplier.astype(jnp.bfloat16))]
  transfers between devices with their start and end apart: 7 -> 34, of which waited for: 7 -> 13; matrix products, arithmetic and copies ran while one was open for 3% -> 0% of each run, Pallas kernels for 0% -> 13%
where the time goes in v3:
time: 195 us
  waiting for transfers between devices  105 us (54%)
  Pallas kernels  38.7 us (20%)
  starting transfers between devices  36 us (18%)
  local copies, waits for them, and re-layouts  14 us (7%)
    ppermute x30, waiting for transfers between devices, swap(): lax.ppermute(x, axes, [(i, i ^ distance) for i in range(lax.axis_size(axe...  96.3 us
    ppermute x30, starting transfers between devices, swap(): lax.ppermute(x, axes, [(i, i ^ distance) for i in range(lax.axis_size(axe...  33.2 us
    pallas_call x4, Pallas kernels, step(): call(functools.partial(step_kernel, plan, stage, start, len(preds)), [SME...  23.1 us
    unnamed x34, local copies, waits for them, and re-layouts  13.4 us
    ppermute x4, waiting for transfers between devices, on_device(): lax.ppermute(posts[i], both, post_route(groups, quads, *divmod(i, half)))  8.76 us
    pallas_call x1, Pallas kernels, on_device(): call(functools.partial(post_kernel, plan, starts), [SMEM, SMEM] + [VMEM]...  5.33 us
  transfers between devices with their start and end apart: 34, of which 13 were waited for; matrix products, arithmetic and copies ran while one was open for 0% of the time, Pallas kernels for 13%

profile of v3, /device:TPU:0, one launch (start us, length us, event | category | flops | bytes accessed | tf_op | source)
XLA Modules:
  0.0 194.7 jit_solution(25997739284642174)
XLA Ops:
  0.7 2.2 %copy-done.11 = bf16[16,2,256,256]{3,2,1,0:T(8,128)(2,1)S(1)} copy-done((bf16[16,2,256,256]{3,2,1,0:T(8,128)(2,1)S(1)}, bf16[16,2,256,256]{3,2,1,0:T(8,128)(2,1)}, u32[]{:S(2)}) %copy-start.11) | copy-done | bytes 4194328
  2.9 2.2 %copy-done.12 = f32[16,2,256,128]{3,2,1,0:T(8,128)S(1)} copy-done((f32[16,2,256,128]{3,2,1,0:T(8,128)S(1)}, f32[16,2,256,128]{3,2,1,0:T(8,128)}, u32[]{:S(2)}) %copy-start.12) | copy-done | bytes 4194328
  6.7 2.6 %shard_map.68 = (bf16[1552,256]{1,0:T(8,128)(2,1)S(1)}, bf16[1280,256]{1,0:T(8,128)(2,1)S(1)}, bf16[1280,256]{1,0:T(8,128)(2,1)S(1)}, bf16[1280,256]{1,0:T(8,128...) custom-call(s32[3]{0:T(128)S(1)} %pad_add_fusion.place_ref, ...), custom_call_target="tpu_custom_call" | custom-call | bytes 10485760 | tf_op jit(solution)/shard_map/pallas_call | solution.py:307
  9.3 4.0 %collective-permute-start.4 = (bf16[1024,256]{1,0:T(8,128)(2,1)S(1)}, bf16[1024,256]{1,0:T(8,128)(2,1)S(1)}, u32[]{:S(2)}, u32[]{:S(2)}) collective-permute-start(bf16[1024,256]{1,0:T(8,128)(2,1)S(1)} %get-tuple-element.35), channel_id=1, source_target_pairs={{0,17},{1,16},{2,19},{3,18},{8,25},{9,24},{10,27},{11,26},{16,1},{... | collective-permute-start | bytes 1572872 | tf_op jit(solution)/shard_map/ppermute | solution.py:294
  13.3 1.5 collective-permute-start.5
  16.2 2.5 %collective-permute-start.2 = (bf16[1280,256]{1,0:T(8,128)(2,1)S(1)}, bf16[1280,256]{1,0:T(8,128)(2,1)}, u32[]{:S(2)}, u32[]{:S(2)}) collective-permute-start(bf16[1280,256]{1,0:T(8,128)(2,1)S(1)} %get-tuple-element.33), channel_id=1, source_target_pairs={{0,3},{1,2},{2,1},{3,0},{8,11},{9,10},{10,9},{11,8},{16,19},{17,18... | collective-permute-start | bytes 1966088 | tf_op jit(solution)/shard_map/ppermute | solution.py:294
  19.2 39.0 %collective-permute-done.4.refs_5_ = bf16[1024,256]{1,0:T(8,128)(2,1)S(1)} collective-permute-done((bf16[1024,256]{1,0:T(8,128)(2,1)S(1)}, bf16[1024,256]{1,0:T(8,128)(2,1)S(1)}, u32[]{:S(2)}, u32[]{:S(2)}) %collective-permute-start.4) | collective-permute-done | bytes 524320 | tf_op jit(solution)/shard_map/ppermute | solution.py:294
  58.2 2.0 %collective-permute-start.3 = (bf16[1552,256]{1,0:T(8,128)(2,1)S(1)}, bf16[1552,256]{1,0:T(8,128)(2,1)S(1)}, u32[]{:S(2)}, u32[]{:S(2)}) collective-permute-start(bf16[1552,256]{1,0:T(8,128)(2,1)S(1)} %get-tuple-element.34), channel_id=1, source_target_pairs={{0,16},{1,17},{2,18},{3,19},{8,24},{9,25},{10,26},{11,27},{16,0},{... | collective-permute-start | bytes 2383880 | tf_op jit(solution)/shard_map/ppermute | solution.py:294
  60.2 1.6 collective-permute-start.1
  62.8 5.5 %collective-permute-done.refs_1_ = bf16[1280,256]{1,0:T(8,128)(2,1)} collective-permute-done((bf16[1280,256]{1,0:T(8,128)(2,1)S(1)}, bf16[1280,256]{1,0:T(8,128)(2,1)}, u32[]{:S(2)}, u32[]{:S(2)}) %collective-permute-start) | collective-permute-done | bytes 655392 | tf_op jit(solution)/shard_map/ppermute | solution.py:294
  69.1 6.9 %collective-permute-done.3.refs_4_ = bf16[1552,256]{1,0:T(8,128)(2,1)S(1)} collective-permute-done((bf16[1552,256]{1,0:T(8,128)(2,1)S(1)}, bf16[1552,256]{1,0:T(8,128)(2,1)S(1)}, u32[]{:S(2)}, u32[]{:S(2)}) %collective-permute-start.3) | collective-permute-done | bytes 794656 | tf_op jit(solution)/shard_map/ppermute | solution.py:294
  76.0 1.5 collective-permute-done.1.refs_2_
  80.7 1.8 collective-permute-done.14.refs_15_
  86.7 2.7 %shard_map.69 = (bf16[4,256,512]{2,1,0:T(8,128)(2,1)S(1)}, f32[4,256,128]{2,1,0:T(8,128)S(1)}, bf16[4,256,128]{2,1,0:T(8,128)(2,1)S(1)}, bf16[4,256,128]{2,1,0:T(8,128)(2,1)S(1)}) custom-call(s32[3]{0:T(128)S(1)} %pad_add_fusion.place_ref, bf16[256,512]{1,0:T(8,128)(2,1)S(1)} %copy-done.14, bf16[1552,256]{1,0:T(8,128)(2,1)S(1)} %get-tuple-element.30.refs_0_, ...), custom_call_target="tpu_custom_call" | custom-call | bytes 4194304 | tf_op jit(solution)/shard_map/pallas_call | solution.py:328
  89.4 5.7 %shard_map.72.refs_16_ = bf16[4,256,128]{2,1,0:T(8,128)(2,1)S(1)} custom-call(f32[1]{0:T(128)} %get-tuple-element.58.scale_ref, bf16[4,256,512]{2,1,0:T(8,128)(2,1)S(1)} %get-tuple-element.41.prior_ref, bf16[4,256,128]{2,1,0:T(8,128)(2,1)S(1)} %get-tuple-element.40.obs_ref.refs_1_, f32[4,256,128]{2,1,0:T(8,128)S(1)} %get-tuple-element.38.noise_ref, ...), custom_call_target="tpu_custom_call" | custom-call | flops 2147483648 | bytes 8388608 | tf_op jit(solution)/shard_map/pallas_call | solution.py:348
  95.2 2.6 %collective-permute-start.16 = (bf16[4,256,128]{2,1,0:T(8,128)(2,1)S(1)}, bf16[4,256,128]{2,1,0:T(8,128)(2,1)S(1)}, u32[]{:S(2)}, u32[]{:S(2)}) collective-permute-start(bf16[4,256,128]{2,1,0:T(8,128)(2,1)S(1)} %shard_map.72.refs_16_), channel_id=1, source_target_pairs={{0,4},{4,0},{1,5},{5,1},{2,6},{6,2},{3,7},{7,3},{8,12},{12,8},{9,1... | collective-permute-start | bytes 786440 | tf_op jit(solution)/shard_map/ppermute | solution.py:294
  97.8 5.8 %shard_map.70.refs_16_ = bf16[4,256,128]{2,1,0:T(8,128)(2,1)S(1)} custom-call(f32[1]{0:T(128)} %get-tuple-element.59.scale_ref, bf16[4,256,512]{2,1,0:T(8,128)(2,1)S(1)} %get-tuple-element.41.prior_ref, bf16[4,256,128]{2,1,0:T(8,128)(2,1)S(1)} %get-tuple-element.39.obs_ref.refs_0_, f32[4,256,128]{2,1,0:T(8,128)S(1)} %get-tuple-element.38.noise_ref, ...), custom_call_target="tpu_custom_call" | custom-call | flops 2147483648 | bytes 8388608 | tf_op jit(solution)/shard_map/pallas_call | solution.py:348
  104.1 12.5 %collective-permute-done.16.refs_17_ = bf16[4,256,128]{2,1,0:T(8,128)(2,1)S(1)} collective-permute-done((bf16[4,256,128]{2,1,0:T(8,128)(2,1)S(1)}, bf16[4,256,128]{2,1,0:T(8,128)(2,1)S(1)}, u32[]{:S(2)}, u32[]{:S(2)}) %collective-permute-start.16) | collective-permute-done | bytes 262176 | tf_op jit(solution)/shard_map/ppermute | solution.py:294
  116.5 5.7 %shard_map.73 = (f32[4,256,128]{2,1,0:T(8,128)S(1)}, bf16[2,256,128]{2,1,0:T(8,128)(2,1)S(1)}, bf16[2,256,128]{2,1,0:T(8,128)(2,1)S(1)}) custom-call(f32[1]{0:T(128)} %get-tuple-element.58.scale_ref, bf16[4,256,512]{2,1,0:T(8,128)(2,1)S(1)} %get-tuple-element.41.prior_ref, bf16[4,256,128]{2,1,0:T(8,128)(2,1)S(1)} %get-tuple-element.40.obs_ref.refs_1_, ...), custom_call_target="tpu_custom_call" | custom-call | flops 2147483648 | bytes 8388608 | tf_op jit(solution)/shard_map/pallas_call | solution.py:348
  122.4 5.8 %shard_map.71 = (f32[4,256,128]{2,1,0:T(8,128)S(1)}, bf16[2,256,128]{2,1,0:T(8,128)(2,1)S(1)}, bf16[2,256,128]{2,1,0:T(8,128)(2,1)S(1)}) custom-call(f32[1]{0:T(128)} %get-tuple-element.59.scale_ref, bf16[4,256,512]{2,1,0:T(8,128)(2,1)S(1)} %get-tuple-element.41.prior_ref, bf16[4,256,128]{2,1,0:T(8,128)(2,1)S(1)} %get-tuple-element.39.obs_ref.refs_0_, ...), custom_call_target="tpu_custom_call" | custom-call | flops 2147483648 | bytes 8388608 | tf_op jit(solution)/shard_map/pallas_call | solution.py:348
  128.2 3.0 %collective-permute-start.23 = (bf16[2,256,128]{2,1,0:T(8,128)(2,1)S(1)}, bf16[2,256,128]{2,1,0:T(8,128)(2,1)S(1)}, u32[]{:S(2)}, u32[]{:S(2)}) collective-permute-start(bf16[2,256,128]{2,1,0:T(8,128)(2,1)S(1)} %get-tuple-element.48.refs_4_), channel_id=1, source_target_pairs={{0,4},{4,0},{1,5},{5,1},{2,6},{6,2},{3,7},{7,3},{8,12},{12,8},{9,1... | collective-permute-start | bytes 393224 | tf_op jit(solution)/shard_map/ppermute | solution.py:294
  131.2 2.8 %collective-permute-start.17 = (bf16[2,256,128]{2,1,0:T(8,128)(2,1)S(1)}, bf16[2,256,128]{2,1,0:T(8,128)(2,1)S(1)}, u32[]{:S(2)}, u32[]{:S(2)}) collective-permute-start(bf16[2,256,128]{2,1,0:T(8,128)(2,1)S(1)} %get-tuple-element.44.refs_4_), channel_id=1, source_target_pairs={{0,4},{4,0},{1,5},{5,1},{2,6},{6,2},{3,7},{7,3},{8,12},{12,8},{9,1... | collective-permute-start | bytes 393224 | tf_op jit(solution)/shard_map/ppermute | solution.py:294
  134.1 9.9 %collective-permute-done.23.refs_5_ = bf16[2,256,128]{2,1,0:T(8,128)(2,1)S(1)} collective-permute-done((bf16[2,256,128]{2,1,0:T(8,128)(2,1)S(1)}, bf16[2,256,128]{2,1,0:T(8,128)(2,1)S(1)}, u32[]{:S(2)}, u32[]{:S(2)}) %collective-permute-start.23) | collective-permute-done | bytes 131104 | tf_op jit(solution)/shard_map/ppermute | solution.py:294
  144.2 2.4 %collective-permute-done.18.refs_7_ = bf16[2,256,128]{2,1,0:T(8,128)(2,1)S(1)} collective-permute-done((bf16[2,256,128]{2,1,0:T(8,128)(2,1)S(1)}, bf16[2,256,128]{2,1,0:T(8,128)(2,1)S(1)}, u32[]{:S(2)}, u32[]{:S(2)}) %collective-permute-start.18) | collective-permute-done | bytes 131104 | tf_op jit(solution)/shard_map/ppermute | solution.py:294
  146.6 1.4 collective-permute-done.17.refs_5_
  148.2 5.3 %shard_map.78 = (bf16[2,256,128]{2,1,0:T(8,128)(2,1)S(1)}, bf16[2,256,128]{2,1,0:T(8,128)(2,1)S(1)}, bf16[2,256,128]{2,1,0:T(8,128)(2,1)S(1)}, bf16[2,256,128]{2,1,0:T(8,128)(2,1)S(1)}) custom-call(s32[3]{0:T(128)S(1)} %pad_add_fusion.place_ref, f32[2]{0:T(128)S(1)} %dynamic_slice.3.scale_ref, bf16[4,256,512]{2,1,0:T(8,128)(2,1)S(1)} %get-tuple-element.41.prior_ref, ...), custom_call_target="tpu_custom_call" | custom-call | flops 2147483648 | bytes 16777216 | tf_op jit(solution)/shard_map/pallas_call | solution.py:384
  157.3 1.9 collective-permute-start.27
  161.9 8.8 %collective-permute-done.31.refs_9_ = bf16[2,256,128]{2,1,0:T(8,128)(2,1)S(1)} collective-permute-done((bf16[2,256,128]{2,1,0:T(8,128)(2,1)S(1)}, bf16[2,256,128]{2,1,0:T(8,128)(2,1)S(1)}, u32[]{:S(2)}, u32[]{:S(2)}) %collective-permute-start.31) | collective-permute-done | bytes 131104 | tf_op jit(solution)/shard_map/ppermute | solution.py:393
  170.7 3.1 %collective-permute-start.29 = (bf16[2,256,256]{2,1,0:T(8,128)(2,1)S(1)}, bf16[2,256,256]{2,1,0:T(8,128)(2,1)S(1)}, u32[]{:S(2)}, u32[]{:S(2)}) collective-permute-start(bf16[2,256,256]{2,1,0:T(8,128)(2,1)S(1)} %shard_map.77), channel_id=1, source_target_pairs={{0,19},{1,18},{2,17},{3,16},{8,27},{9,26},{10,25},{11,24},{16,3},{... | collective-permute-start | bytes 786440 | tf_op jit(solution)/shard_map/ppermute | solution.py:294
  175.1 8.0 %collective-permute-done.27.refs_5_ = bf16[2,256,256]{2,1,0:T(8,128)(2,1)S(1)} collective-permute-done((bf16[2,256,256]{2,1,0:T(8,128)(2,1)S(1)}, bf16[2,256,256]{2,1,0:T(8,128)(2,1)S(1)}, u32[]{:S(2)}, u32[]{:S(2)}) %collective-permute-start.27) | collective-permute-done | bytes 262176 | tf_op jit(solution)/shard_map/ppermute | solution.py:294
  184.1 7.3 %collective-permute-done.20.refs_1_ = bf16[2,256,256]{2,1,0:T(8,128)(2,1)S(1)} collective-permute-done((bf16[2,256,256]{2,1,0:T(8,128)(2,1)S(1)}, bf16[2,256,256]{2,1,0:T(8,128)(2,1)S(1)}, u32[]{:S(2)}, u32[]{:S(2)}) %collective-permute-start.20) | collective-permute-done | bytes 262176 | tf_op jit(solution)/shard_map/ppermute | solution.py:294
  191.4 3.3 %shard_map.79 = (f32[16,2,256,128]{3,2,1,0:T(8,128)}, f32[4,512,128]{2,1,0:T(8,128)}) custom-call(s32[3]{0:T(128)S(1)} %pad_add_fusion.place_ref, bf16[2,256,256]{2,1,0:T(8,128)(2,1)S(1)} %shard_map.75.refs_0_, bf16[2,256,256]{2,1,0:T(8,128)(2,1)S(1)} %collective-permute-done.20.refs_1_, bf16[2,256,256]{2,1,0:T(8,128)(2,1)S(1)} %collective-permute-done.21.refs_2_, ...), custom_call_target="tpu_custom_call" | custom-call | bytes 8388608 | tf_op jit(solution)/shard_map/pallas_call | solution.py:394
  (85 shorter events, 22.4 us)
Async XLA Ops:
  9.3 48.9 %collective-permute-start.4 = (bf16[1024,256]{1,0:T(8,128)(2,1)S(1)}, bf16[1024,256]{1,0:T(8,128)(2,1)S(1)}, u32[]{:S(2)}, u32[]{:S(2)}) collective-permute-start(bf16[1024,256]{1,0:T(8,128)(2,1)S(1)} %get-tuple-element.35), channel_id=1, source_target_pairs={{0,17},{1,16},{2,19},{3,18},{8,25},{9,24},{10,27},{11,26},{16,1},{... | collective-permute-start | bytes 1572872 | tf_op jit(solution)/shard_map/ppermute | solution.py:294
  13.3 46.9 %collective-permute-start.5 = (bf16[1024,256]{1,0:T(8,128)(2,1)S(1)}, bf16[1024,256]{1,0:T(8,128)(2,1)S(1)}, u32[]{:S(2)}, u32[]{:S(2)}) collective-permute-start(bf16[1024,256]{1,0:T(8,128)(2,1)S(1)} %get-tuple-element.36), channel_id=1, source_target_pairs={{0,18},{1,19},{2,16},{3,17},{8,26},{9,27},{10,24},{11,25},{16,2},{... | collective-permute-start | bytes 1572872 | tf_op jit(solution)/shard_map/ppermute | solution.py:294
  14.8 45.4 %collective-permute-start.6 = (bf16[1024,256]{1,0:T(8,128)(2,1)S(1)}, bf16[1024,256]{1,0:T(8,128)(2,1)}, u32[]{:S(2)}, u32[]{:S(2)}) collective-permute-start(bf16[1024,256]{1,0:T(8,128)(2,1)S(1)} %get-tuple-element.37), channel_id=1, source_target_pairs={{0,19},{1,18},{2,17},{3,16},{8,27},{9,26},{10,25},{11,24},{16,3},{... | collective-permute-start | bytes 1572872 | tf_op jit(solution)/shard_map/ppermute | solution.py:294
  16.2 45.8 %collective-permute-start.2 = (bf16[1280,256]{1,0:T(8,128)(2,1)S(1)}, bf16[1280,256]{1,0:T(8,128)(2,1)}, u32[]{:S(2)}, u32[]{:S(2)}) collective-permute-start(bf16[1280,256]{1,0:T(8,128)(2,1)S(1)} %get-tuple-element.33), channel_id=1, source_target_pairs={{0,3},{1,2},{2,1},{3,0},{8,11},{9,10},{10,9},{11,8},{16,19},{17,18... | collective-permute-start | bytes 1966088 | tf_op jit(solution)/shard_map/ppermute | solution.py:294
  18.7 49.6 %collective-permute-start = (bf16[1280,256]{1,0:T(8,128)(2,1)S(1)}, bf16[1280,256]{1,0:T(8,128)(2,1)}, u32[]{:S(2)}, u32[]{:S(2)}) collective-permute-start(bf16[1280,256]{1,0:T(8,128)(2,1)S(1)} %get-tuple-element.31), channel_id=1, source_target_pairs={{0,1},{1,0},{2,3},{3,2},{8,9},{9,8},{10,11},{11,10},{16,17},{17,16... | collective-permute-start | bytes 1966088 | tf_op jit(solution)/shard_map/ppermute | solution.py:294
  58.2 17.7 %collective-permute-start.3 = (bf16[1552,256]{1,0:T(8,128)(2,1)S(1)}, bf16[1552,256]{1,0:T(8,128)(2,1)S(1)}, u32[]{:S(2)}, u32[]{:S(2)}) collective-permute-start(bf16[1552,256]{1,0:T(8,128)(2,1)S(1)} %get-tuple-element.34), channel_id=1, source_target_pairs={{0,16},{1,17},{2,18},{3,19},{8,24},{9,25},{10,26},{11,27},{16,0},{... | collective-permute-start | bytes 2383880 | tf_op jit(solution)/shard_map/ppermute | solution.py:294
  60.2 17.3 %collective-permute-start.7 = (bf16[1552,256]{1,0:T(8,128)(2,1)S(1)}, bf16[1552,256]{1,0:T(8,128)(2,1)S(1)}, u32[]{:S(2)}, u32[]{:S(2)}) collective-permute-start(bf16[1552,256]{1,0:T(8,128)(2,1)S(1)} %get-tuple-element.30.refs_0_), channel_id=1, source_target_pairs={{0,8},{8,0},{16,24},{24,16},{1,9},{9,1},{17,25},{25,17},{2,10},{10... | collective-permute-start | bytes 2383880 | tf_op jit(solution)/shard_map/ppermute | solution.py:294
  60.2 17.2 %collective-permute-start.1 = (bf16[1280,256]{1,0:T(8,128)(2,1)S(1)}, bf16[1280,256]{1,0:T(8,128)(2,1)}, u32[]{:S(2)}, u32[]{:S(2)}) collective-permute-start(bf16[1280,256]{1,0:T(8,128)(2,1)S(1)} %get-tuple-element.32), channel_id=1, source_target_pairs={{0,2},{1,3},{2,0},{3,1},{8,10},{9,11},{10,8},{11,9},{16,18},{17,19... | collective-permute-start | bytes 1966088 | tf_op jit(solution)/shard_map/ppermute | solution.py:294
  62.0 16.0 %collective-permute-start.12 = (bf16[1024,256]{1,0:T(8,128)(2,1)S(1)}, bf16[1024,256]{1,0:T(8,128)(2,1)S(1)}, u32[]{:S(2)}, u32[]{:S(2)}) collective-permute-start(bf16[1024,256]{1,0:T(8,128)(2,1)S(1)} %collective-permute-done.4.refs_5_), channel_id=1, source_target_pairs={{0,8},{8,0},{16,24},{24,16},{1,9},{9,1},{17,25},{25,17},{2,10},{10... | collective-permute-start | bytes 1572872 | tf_op jit(solution)/shard_map/ppermute | solution.py:294
  68.3 10.5 %collective-permute-start.13 = (bf16[1024,256]{1,0:T(8,128)(2,1)S(1)}, bf16[1024,256]{1,0:T(8,128)(2,1)S(1)}, u32[]{:S(2)}, u32[]{:S(2)}) collective-permute-start(bf16[1024,256]{1,0:T(8,128)(2,1)S(1)} %collective-permute-done.5.refs_6_), channel_id=1, source_target_pairs={{0,8},{8,0},{16,24},{24,16},{1,9},{9,1},{17,25},{25,17},{2,10},{10... | collective-permute-start | bytes 1572872 | tf_op jit(solution)/shard_map/ppermute | solution.py:294
  76.0 6.6 %collective-permute-start.11 = (bf16[1552,256]{1,0:T(8,128)(2,1)S(1)}, bf16[1552,256]{1,0:T(8,128)(2,1)S(1)}, u32[]{:S(2)}, u32[]{:S(2)}) collective-permute-start(bf16[1552,256]{1,0:T(8,128)(2,1)S(1)} %collective-permute-done.3.refs_4_), channel_id=1, source_target_pairs={{0,8},{8,0},{16,24},{24,16},{1,9},{9,1},{17,25},{25,17},{2,10},{10... | collective-permute-start | bytes 2383880 | tf_op jit(solution)/shard_map/ppermute | solution.py:294
  77.5 5.1 %collective-permute-start.10 = (bf16[1280,256]{1,0:T(8,128)(2,1)}, bf16[1280,256]{1,0:T(8,128)(2,1)}, u32[]{:S(2)}, u32[]{:S(2)}) collective-permute-start(bf16[1280,256]{1,0:T(8,128)(2,1)} %collective-permute-done.2.refs_3_), channel_id=1, source_target_pairs={{0,8},{8,0},{16,24},{24,16},{1,9},{9,1},{17,25},{25,17},{2,10},{10... | collective-permute-start | bytes 1966088 | tf_op jit(solution)/shard_map/ppermute | solution.py:294
  77.5 5.1 %collective-permute-start.8 = (bf16[1280,256]{1,0:T(8,128)(2,1)}, bf16[1280,256]{1,0:T(8,128)(2,1)}, u32[]{:S(2)}, u32[]{:S(2)}) collective-permute-start(bf16[1280,256]{1,0:T(8,128)(2,1)} %collective-permute-done.refs_1_), channel_id=1, source_target_pairs={{0,8},{8,0},{16,24},{24,16},{1,9},{9,1},{17,25},{25,17},{2,10},{10... | collective-permute-start | bytes 1966088 | tf_op jit(solution)/shard_map/ppermute | solution.py:294
  95.2 21.4 %collective-permute-start.16 = (bf16[4,256,128]{2,1,0:T(8,128)(2,1)S(1)}, bf16[4,256,128]{2,1,0:T(8,128)(2,1)S(1)}, u32[]{:S(2)}, u32[]{:S(2)}) collective-permute-start(bf16[4,256,128]{2,1,0:T(8,128)(2,1)S(1)} %shard_map.72.refs_16_), channel_id=1, source_target_pairs={{0,4},{4,0},{1,5},{5,1},{2,6},{6,2},{3,7},{7,3},{8,12},{12,8},{9,1... | collective-permute-start | bytes 786440 | tf_op jit(solution)/shard_map/ppermute | solution.py:294
  103.7 18.7 %collective-permute-start.15 = (bf16[4,256,128]{2,1,0:T(8,128)(2,1)S(1)}, bf16[4,256,128]{2,1,0:T(8,128)(2,1)S(1)}, u32[]{:S(2)}, u32[]{:S(2)}) collective-permute-start(bf16[4,256,128]{2,1,0:T(8,128)(2,1)S(1)} %shard_map.70.refs_16_), channel_id=1, source_target_pairs={{0,4},{4,0},{1,5},{5,1},{2,6},{6,2},{3,7},{7,3},{8,12},{12,8},{9,1... | collective-permute-start | bytes 786440 | tf_op jit(solution)/shard_map/ppermute | solution.py:294
  122.3 11.8 %collective-permute-start.24 = (bf16[2,256,128]{2,1,0:T(8,128)(2,1)S(1)}, bf16[2,256,128]{2,1,0:T(8,128)(2,1)S(1)}, u32[]{:S(2)}, u32[]{:S(2)}) collective-permute-start(bf16[2,256,128]{2,1,0:T(8,128)(2,1)S(1)} %get-tuple-element.49.refs_6_), channel_id=1, source_target_pairs={{0,4},{4,0},{1,5},{5,1},{2,6},{6,2},{3,7},{7,3},{8,12},{12,8},{9,1... | collective-permute-start | bytes 393224 | tf_op jit(solution)/shard_map/ppermute | solution.py:294
  128.2 15.8 %collective-permute-start.23 = (bf16[2,256,128]{2,1,0:T(8,128)(2,1)S(1)}, bf16[2,256,128]{2,1,0:T(8,128)(2,1)S(1)}, u32[]{:S(2)}, u32[]{:S(2)}) collective-permute-start(bf16[2,256,128]{2,1,0:T(8,128)(2,1)S(1)} %get-tuple-element.48.refs_4_), channel_id=1, source_target_pairs={{0,4},{4,0},{1,5},{5,1},{2,6},{6,2},{3,7},{7,3},{8,12},{12,8},{9,1... | collective-permute-start | bytes 393224 | tf_op jit(solution)/shard_map/ppermute | solution.py:294
  131.1 15.5 %collective-permute-start.18 = (bf16[2,256,128]{2,1,0:T(8,128)(2,1)S(1)}, bf16[2,256,128]{2,1,0:T(8,128)(2,1)S(1)}, u32[]{:S(2)}, u32[]{:S(2)}) collective-permute-start(bf16[2,256,128]{2,1,0:T(8,128)(2,1)S(1)} %get-tuple-element.45.refs_6_), channel_id=1, source_target_pairs={{0,4},{4,0},{1,5},{5,1},{2,6},{6,2},{3,7},{7,3},{8,12},{12,8},{9,1... | collective-permute-start | bytes 393224 | tf_op jit(solution)/shard_map/ppermute | solution.py:294
  131.2 16.8 %collective-permute-start.17 = (bf16[2,256,128]{2,1,0:T(8,128)(2,1)S(1)}, bf16[2,256,128]{2,1,0:T(8,128)(2,1)S(1)}, u32[]{:S(2)}, u32[]{:S(2)}) collective-permute-start(bf16[2,256,128]{2,1,0:T(8,128)(2,1)S(1)} %get-tuple-element.44.refs_4_), channel_id=1, source_target_pairs={{0,4},{4,0},{1,5},{5,1},{2,6},{6,2},{3,7},{7,3},{8,12},{12,8},{9,1... | collective-permute-start | bytes 393224 | tf_op jit(solution)/shard_map/ppermute | solution.py:294
  144.1 11.3 %collective-permute-start.25 = (bf16[2,256,128]{2,1,0:T(8,128)(2,1)S(1)}, bf16[2,256,128]{2,1,0:T(8,128)(2,1)S(1)}, u32[]{:S(2)}, u32[]{:S(2)}) collective-permute-start(bf16[2,256,128]{2,1,0:T(8,128)(2,1)S(1)} %get-tuple-element.51.refs_19_), channel_id=1, source_target_pairs={{0,8},{8,0},{16,24},{24,16},{1,9},{9,1},{17,25},{25,17},{2,10},{10... | collective-permute-start | bytes 393224 | tf_op jit(solution)/shard_map/ppermute | solution.py:294
  153.6 6.1 %collective-permute-start.30 = (bf16[2,256,128]{2,1,0:T(8,128)(2,1)S(1)}, bf16[2,256,128]{2,1,0:T(8,128)(2,1)S(1)}, u32[]{:S(2)}, u32[]{:S(2)}) collective-permute-start(bf16[2,256,128]{2,1,0:T(8,128)(2,1)S(1)} %get-tuple-element.52), channel_id=1, source_target_pairs={{0,0},{1,1},{2,8},{3,9},{8,2},{9,3},{10,10},{11,11},{16,16},{17,17... | collective-permute-start | bytes 393224 | tf_op jit(solution)/shard_map/ppermute | solution.py:393
  154.2 6.0 %collective-permute-start.19 = (bf16[2,256,128]{2,1,0:T(8,128)(2,1)S(1)}, bf16[2,256,128]{2,1,0:T(8,128)(2,1)S(1)}, u32[]{:S(2)}, u32[]{:S(2)}) collective-permute-start(bf16[2,256,128]{2,1,0:T(8,128)(2,1)S(1)} %get-tuple-element.47.refs_18_), channel_id=1, source_target_pairs={{0,8},{8,0},{16,24},{24,16},{1,9},{9,1},{17,25},{25,17},{2,10},{10... | collective-permute-start | bytes 393224 | tf_op jit(solution)/shard_map/ppermute | solution.py:294
  156.1 18.9 %collective-permute-start.26 = (bf16[2,256,256]{2,1,0:T(8,128)(2,1)S(1)}, bf16[2,256,256]{2,1,0:T(8,128)(2,1)S(1)}, u32[]{:S(2)}, u32[]{:S(2)}) collective-permute-start(bf16[2,256,256]{2,1,0:T(8,128)(2,1)S(1)} %shard_map.77), channel_id=1, source_target_pairs={{0,16},{1,17},{2,18},{3,19},{8,24},{9,25},{10,26},{11,27},{16,0},{... | collective-permute-start | bytes 786440 | tf_op jit(solution)/shard_map/ppermute | solution.py:294
  157.3 25.8 %collective-permute-start.27 = (bf16[2,256,256]{2,1,0:T(8,128)(2,1)S(1)}, bf16[2,256,256]{2,1,0:T(8,128)(2,1)S(1)}, u32[]{:S(2)}, u32[]{:S(2)}) collective-permute-start(bf16[2,256,256]{2,1,0:T(8,128)(2,1)S(1)} %shard_map.77), channel_id=1, source_target_pairs={{0,17},{1,16},{2,19},{3,18},{8,25},{9,24},{10,27},{11,26},{16,1},{... | collective-permute-start | bytes 786440 | tf_op jit(solution)/shard_map/ppermute | solution.py:294
  159.2 11.5 %collective-permute-start.31 = (bf16[2,256,128]{2,1,0:T(8,128)(2,1)S(1)}, bf16[2,256,128]{2,1,0:T(8,128)(2,1)S(1)}, u32[]{:S(2)}, u32[]{:S(2)}) collective-permute-start(bf16[2,256,128]{2,1,0:T(8,128)(2,1)S(1)} %get-tuple-element.53), channel_id=1, source_target_pairs={{0,1},{1,0},{2,9},{3,8},{8,3},{9,2},{10,11},{11,10},{16,17},{17,16... | collective-permute-start | bytes 393224 | tf_op jit(solution)/shard_map/ppermute | solution.py:393
  159.7 11.0 %collective-permute-start.32 = (bf16[2,256,128]{2,1,0:T(8,128)(2,1)S(1)}, bf16[2,256,128]{2,1,0:T(8,128)(2,1)S(1)}, u32[]{:S(2)}, u32[]{:S(2)}) collective-permute-start(bf16[2,256,128]{2,1,0:T(8,128)(2,1)S(1)} %get-tuple-element.54), channel_id=1, source_target_pairs={{0,2},{1,3},{2,10},{3,11},{8,0},{9,1},{10,8},{11,9},{16,18},{17,19... | collective-permute-start | bytes 393224 | tf_op jit(solution)/shard_map/ppermute | solution.py:393
  160.2 13.6 %collective-permute-start.33 = (bf16[2,256,128]{2,1,0:T(8,128)(2,1)S(1)}, bf16[2,256,128]{2,1,0:T(8,128)(2,1)S(1)}, u32[]{:S(2)}, u32[]{:S(2)}) collective-permute-start(bf16[2,256,128]{2,1,0:T(8,128)(2,1)S(1)} %get-tuple-element.55), channel_id=1, source_target_pairs={{0,3},{1,2},{2,11},{3,10},{8,1},{9,0},{10,9},{11,8},{16,19},{17,18... | collective-permute-start | bytes 393224 | tf_op jit(solution)/shard_map/ppermute | solution.py:393
  170.7 13.4 %collective-permute-start.28 = (bf16[2,256,256]{2,1,0:T(8,128)(2,1)S(1)}, bf16[2,256,256]{2,1,0:T(8,128)(2,1)S(1)}, u32[]{:S(2)}, u32[]{:S(2)}) collective-permute-start(bf16[2,256,256]{2,1,0:T(8,128)(2,1)S(1)} %shard_map.77), channel_id=1, source_target_pairs={{0,18},{1,19},{2,16},{3,17},{8,26},{9,27},{10,24},{11,25},{16,2},{... | collective-permute-start | bytes 786440 | tf_op jit(solution)/shard_map/ppermute | solution.py:294
  170.7 13.4 %collective-permute-start.29 = (bf16[2,256,256]{2,1,0:T(8,128)(2,1)S(1)}, bf16[2,256,256]{2,1,0:T(8,128)(2,1)S(1)}, u32[]{:S(2)}, u32[]{:S(2)}) collective-permute-start(bf16[2,256,256]{2,1,0:T(8,128)(2,1)S(1)} %shard_map.77), channel_id=1, source_target_pairs={{0,19},{1,18},{2,17},{3,16},{8,27},{9,26},{10,25},{11,24},{16,3},{... | collective-permute-start | bytes 786440 | tf_op jit(solution)/shard_map/ppermute | solution.py:294
  173.8 17.6 %collective-permute-start.20 = (bf16[2,256,256]{2,1,0:T(8,128)(2,1)S(1)}, bf16[2,256,256]{2,1,0:T(8,128)(2,1)S(1)}, u32[]{:S(2)}, u32[]{:S(2)}) collective-permute-start(bf16[2,256,256]{2,1,0:T(8,128)(2,1)S(1)} %shard_map.75.refs_0_), channel_id=1, source_target_pairs={{0,1},{1,0},{2,3},{3,2},{8,9},{9,8},{10,11},{11,10},{16,17},{17,16... | collective-permute-start | bytes 786440 | tf_op jit(solution)/shard_map/ppermute | solution.py:294
  175.1 16.3 %collective-permute-start.21 = (bf16[2,256,256]{2,1,0:T(8,128)(2,1)S(1)}, bf16[2,256,256]{2,1,0:T(8,128)(2,1)S(1)}, u32[]{:S(2)}, u32[]{:S(2)}) collective-permute-start(bf16[2,256,256]{2,1,0:T(8,128)(2,1)S(1)} %shard_map.75.refs_0_), channel_id=1, source_target_pairs={{0,2},{1,3},{2,0},{3,1},{8,10},{9,11},{10,8},{11,9},{16,18},{17,19... | collective-permute-start | bytes 786440 | tf_op jit(solution)/shard_map/ppermute | solution.py:294
  183.1 8.3 %collective-permute-start.22 = (bf16[2,256,256]{2,1,0:T(8,128)(2,1)S(1)}, bf16[2,256,256]{2,1,0:T(8,128)(2,1)S(1)}, u32[]{:S(2)}, u32[]{:S(2)}) collective-permute-start(bf16[2,256,256]{2,1,0:T(8,128)(2,1)S(1)} %shard_map.75.refs_0_), channel_id=1, source_target_pairs={{0,3},{1,2},{2,1},{3,0},{8,11},{9,10},{10,9},{11,8},{16,19},{17,18... | collective-permute-start | bytes 786440 | tf_op jit(solution)/shard_map/ppermute | solution.py:294
  (19 other events, 216.4 us)

commit v4 on v3

v4 whole, which is shorter than its diff:
```python
import functools

import jax
import jax.numpy as jnp
from jax import lax
from jax.experimental import pallas as pl
from jax.experimental.pallas import tpu as pltpu
from jax.sharding import Mesh, PartitionSpec as P

ITERS = 2
relax_step = 0.25
CORES = 2
LANES = 128
HALF = LANES // CORES
BATCHES = ((0,), (1,))
VMEM_LIMIT = 16 * 2**20
VMEM = pl.BlockSpec(memory_space=pltpu.VMEM)
SMEM = pl.BlockSpec(memory_space=pltpu.SMEM)
ANY = pl.BlockSpec(memory_space=pl.ANY)
HBM = pl.BlockSpec(memory_space=pltpu.HBM)
bf16, f32 = jnp.bfloat16, jnp.float32


def shape(dims, dtype):
    return jax.ShapeDtypeStruct(dims, dtype)


def call(kernel, in_specs, out_shape, scratch=(), out_specs=None, flops=0, moved=0, aliases=None):
    return pl.pallas_call(
        kernel,
        input_output_aliases=aliases or {},
        in_specs=in_specs,
        out_specs=out_specs or [VMEM] * len(out_shape),
        out_shape=out_shape,
        scratch_shapes=list(scratch),
        cost_estimate=pl.CostEstimate(flops=flops, bytes_accessed=moved, transcendentals=0),
        compiler_params=pltpu.CompilerParams(vmem_limit_bytes=VMEM_LIMIT),
    )


def dot(a, b):
    return jnp.dot(a, b, preferred_element_type=f32)


def dot_nt(a, b):
    return lax.dot_general(a, b, (((1,), (1,)), ((), ())), preferred_element_type=f32)


class Plan:
    def __init__(self, groups, quads, sensors, cells, width):
        self.groups, self.quads, self.sensors, self.cells, self.width = groups, quads, sensors, cells, width
        self.pairs = groups // CORES
        self.chips = self.pairs * quads
        self.per_block = width // cells
        self.map_rows = 2 * sensors
        self.share = cells // CORES

    def extra(self, batch, d):
        e, dq = divmod(d, self.quads)
        if batch > 0:
            return 0
        if dq == 0:
            return CORES * self.sensors + 16
        return self.share * self.per_block if e == 0 else 0

    def rows(self, batch, d):
        return len(BATCHES[batch]) * self.map_rows + self.extra(batch, d)

    def order(self):
        far, order = self.chips - 1, []
        for d in sorted(range(1, far), key=lambda d: -bin(d).count("1")):
            for x in (d, far - d):
                if x not in order:
                    order.append(x)
        return order[:2] + [far] + order[2:]


def pack_kernel(plan, batch, place_ref, map_ref, obs_ref, prior_ref, noise_ref, *refs):
    refs = refs[batch:]
    outs, (held, lines, sems) = refs[:plan.chips], refs[plan.chips:]
    pair, quad, core = place_ref[0], place_ref[1], place_ref[2]
    chip = pair * plan.quads + quad
    copies = []
    first, count = BATCHES[batch][0], len(BATCHES[batch])
    for d in range(plan.chips):
        freq = CORES * (chip ^ d) + first
        for j in range(count):
            to = outs[d].at[pl.ds(j * plan.map_rows, plan.map_rows)]
            copies.append(pltpu.make_async_copy(map_ref.at[freq + j], to, sems.at[d, j]))
            copies[-1].start()
    if batch == 0:
        at = count * plan.map_rows
        noise = noise_ref[...]
        high = noise.astype(bf16)
        low = (noise - high.astype(f32)).astype(bf16)
        wide = (8, plan.sensors)
        tail = jnp.concatenate([jnp.broadcast_to(high, wide), jnp.broadcast_to(low, wide)], 0)
        loads = []
        for e in range(plan.pairs):
            freq = CORES * (chip ^ (e * plan.quads))
            loads.append(pltpu.make_async_copy(obs_ref.at[pl.ds(freq, CORES)], held.at[e], sems.at[plan.chips, e]))
            loads[-1].start()
        half = prior_ref[pl.ds(pl.multiple_of(core * plan.share, plan.share), plan.share), :]
        for k in range(plan.per_block):
            lines[0, k * plan.share:(k + 1) * plan.share, :] = half[:, k * plan.cells:(k + 1) * plan.cells]
        stores = []
        for dq in range(1, plan.quads):
            size = plan.share * plan.per_block
            to = outs[dq].at[pl.ds(at, size)]
            stores.append(pltpu.make_async_copy(lines.at[0, pl.ds(0, size)], to, sems.at[plan.chips + 1, dq]))
            stores[-1].start()
        for e in range(plan.pairs):
            loads[e].wait()
            slot = 1 + e
            for j in range(CORES):
                re, im = held[e, j, 0], held[e, j, 1]
                for s in range(CORES):
                    part = slice(s * HALF, (s + 1) * HALF)
                    lines[slot, j * plan.sensors:(j + 1) * plan.sensors, s * LANES:(s + 1) * LANES] = (
                        jnp.concatenate([re[:, part], im[:, part]], 1).astype(bf16)
                    )
            size = plan.extra(0, 0)
            lines[slot, size - 16:size, :] = tail
            to = outs[e * plan.quads].at[pl.ds(at, size)]
            stores.append(pltpu.make_async_copy(lines.at[slot, pl.ds(0, size)], to, sems.at[plan.chips + 2, e]))
            stores[-1].start()
        for copy in stores:
            copy.wait()
    for copy in copies:
        copy.wait()


def gather_kernel(plan, place_ref, own_ref, *refs):
    mine, theirs = refs[:plan.chips], refs[plan.chips:2 * plan.chips]
    prior_ref, noise_ref, *streams = refs[2 * plan.chips:]
    quad, core = place_ref[1], place_ref[2]
    at = len(BATCHES[0]) * plan.map_rows
    share, cells, sensors = plan.share, plan.cells, plan.sensors
    for k in range(plan.per_block):
        column = k ^ (quad & (plan.per_block - 1))
        to = slice(k * cells, (k + 1) * cells)
        prior_ref[0, :, to] = own_ref[:, pl.ds(pl.multiple_of(column * cells, cells), cells)]
        for dq in range(1, plan.quads):
            span = pl.ds(pl.multiple_of(at + column * share, share), share)
            for part, ref in ((core, mine[dq]), (1 - core, theirs[dq])):
                prior_ref[dq, pl.ds(pl.multiple_of(part * share, share), share), to] = ref[span, :]
    row = lax.broadcasted_iota(jnp.int32, (sensors, sensors), 0)
    col = lax.broadcasted_iota(jnp.int32, (sensors, sensors), 1)
    lanes = pl.ds(pl.multiple_of(core * LANES, LANES), LANES)
    for e in range(plan.pairs):
        for s, refs_s in enumerate((mine, theirs)):
            ref, r = refs_s[e * plan.quads], CORES * e + s
            for j in range(CORES):
                streams[j][r] = ref[at + j * sensors:at + (j + 1) * sensors, lanes]
            both = ref[at + CORES * sensors:, :].astype(f32)
            noise_row = both[0:1, :] + both[8:9, :]
            noise = jnp.sum(jnp.where(row == col, noise_row, 0.0), 1, keepdims=True)
            noise_ref[r] = jnp.broadcast_to(noise, (sensors, LANES))


def sides(z):
    return jnp.concatenate([z, jnp.concatenate([z[:, HALF:], -z[:, :HALF]], 1)], 0).T


def source(plan, chunk, sides_ref, prior_ref, scale):
    out = []
    for block in range(plan.quads // plan.per_block):
        quads = range(block * plan.per_block, (block + 1) * plan.per_block)
        parts = []
        for dq in quads:
            u = jnp.zeros((LANES, plan.cells), f32)
            for r in range(plan.groups):
                u += dot(sides_ref[r], chunk(r, dq)[...])
            parts.append(u.astype(bf16))
        ub = jnp.concatenate(parts, 1)
        out += [(dot_nt(prior_ref[dq], ub) * scale).astype(bf16) for dq in quads]
    return out


def chunks(plan, refs, start):
    rows = pl.ds(start, plan.map_rows)
    return lambda r, dq: refs[(r % CORES) * plan.chips + r // CORES * plan.quads + dq].at[rows]


def step_kernel(plan, stage, start, n_pred, scale_ref, prior_ref, obs_ref, noise_ref, *refs):
    chunk, refs = chunks(plan, refs, start), refs[2 * plan.chips:]
    preds, refs = refs[:n_pred], refs[n_pred:]
    if stage > 0:
        next_ref, refs = refs[0], refs[1:]
    out_ref, sides_ref = refs
    for r in range(plan.groups):
        obs = obs_ref[r].astype(f32)
        now = relax_step * obs
        if stage > 0:
            predicted = sum(p[r].astype(f32) for p in preds)
            now = now + relax_step * (obs - predicted - noise_ref[r] * now)
            next_ref[r] = now
        sides_ref[r] = sides(now.astype(bf16))
    sources = source(plan, chunk, sides_ref, prior_ref, scale_ref[0])
    turned = [jnp.concatenate([-v[:, HALF:], v[:, :HALF]], 1) for v in sources]
    for r in range(plan.groups):
        total = jnp.zeros((plan.sensors, LANES), f32)
        for dq in range(plan.quads):
            block = chunk(r, dq)
            total += dot(block[:plan.sensors, :], sources[dq]) + dot(block[plan.sensors:, :], turned[dq])
        out_ref[r] = total.astype(bf16)


def last_kernel(plan, n_pred, place_ref, noise_ref, obs_ref, held_ref, *refs):
    preds, (final_ref, out_ref) = refs[:n_pred], refs[n_pred:]
    first = CORES * place_ref[0] + place_ref[2]
    for r in range(plan.groups):
        now = held_ref[r]
        predicted = sum(p[r].astype(f32) for p in preds)
        now = now + relax_step * (obs_ref[r].astype(f32) - predicted - noise_ref[r] * now)
        now = now.astype(bf16)
        final_ref[r] = now
        for q in range(plan.quads):
            out_ref[first ^ r, q] = now


def post_kernel(plan, start, place_ref, scale_ref, prior_ref, final_ref, *refs):
    chunk, refs = chunks(plan, refs, start), refs[2 * plan.chips:]
    outs, (sides_ref, held_ref) = refs[:plan.quads], refs[plan.quads:]
    quad, core = place_ref[1], place_ref[2]
    for r in range(plan.groups):
        sides_ref[r] = sides(final_ref[r])
    for dq, v in enumerate(source(plan, chunk, sides_ref, prior_ref, scale_ref[0])):
        held_ref[dq] = v
    wide = plan.quads // CORES
    for flip in range(CORES):
        for step in range(wide):
            to = (core ^ flip) * wide + ((quad & (wide - 1)) ^ step)
            outs[flip * wide + step][...] = held_ref[to ^ quad]


def post_route(quads, flip, step):
    wide, route = quads // CORES, []
    for core in range(CORES):
        for q in range(quads):
            to_quad = (core ^ flip) * wide + ((q % wide) ^ step)
            route.append((core * quads + q, q // wide * quads + to_quad))
    return route


def end_kernel(plan, j, place_ref, dual_ref, *refs):
    posts, refs = refs[:plan.quads], refs[plan.quads + 2 * j:]
    dual_out, post_out, wide_ref, post_ref, sems = refs
    quad = place_ref[1]
    sends = []
    for chip in range(plan.chips):
        x, q = divmod(chip, plan.quads)
        low, high = dual_ref[x, 0, q].astype(f32), dual_ref[x, 1, q].astype(f32)
        wide_ref[chip, 0] = jnp.concatenate([low[:, :HALF], high[:, :HALF]], 1)
        wide_ref[chip, 1] = jnp.concatenate([low[:, HALF:], high[:, HALF:]], 1)
        sends.append(pltpu.make_async_copy(wide_ref.at[chip], dual_out.at[CORES * chip + j], sems.at[chip]))
        sends[-1].start()
    half = plan.quads // CORES
    flip = quad // half == 1
    for step in range(half):
        mine, theirs = posts[step][...].astype(f32), posts[half + step][...].astype(f32)
        low, high = jnp.where(flip, theirs, mine), jnp.where(flip, mine, theirs)
        post_ref[step, pl.ds(0, plan.cells, stride=2), :] = jnp.concatenate([low[:, :HALF], high[:, :HALF]], 1)
        post_ref[step, pl.ds(1, plan.cells, stride=2), :] = jnp.concatenate([low[:, HALF:], high[:, HALF:]], 1)
        freq = CORES * ((quad & (half - 1)) ^ step) + j
        sends.append(pltpu.make_async_copy(post_ref.at[step], post_out.at[freq], sems.at[plan.chips + step]))
        sends[-1].start()
    for copy in sends:
        copy.wait()


def on_device(forward_map, observed, noise_var, prior_rows, prior_scale):
    frequencies, halves, sensors, cells = forward_map.shape
    pairs, quads, count = (lax.axis_size(a) for a in ("pair", "quad", "side"))
    groups = pairs * CORES
    plan = Plan(groups, quads, sensors, cells, prior_rows.shape[1])
    pair, core, quad = (lax.axis_index(a) for a in ("pair", "core", "quad"))
    place = jnp.stack([pair, quad, core]).astype(jnp.int32)
    scales = lax.dynamic_slice_in_dim(prior_scale, CORES * (pair * quads + quad), CORES, 0)

    def swap(x, axes, distance):
        return lax.ppermute(x, axes, [(i, i ^ distance) for i in range(lax.axis_size(axes))])

    flat = forward_map.reshape(frequencies, halves * sensors, cells)
    line = max(plan.extra(0, d) for d in range(plan.chips))
    order, starts, maps = plan.order(), {}, []
    for batch, held in enumerate(BATCHES):
        for i, j in enumerate(held):
            starts[j] = (batch, i * plan.map_rows)
        operands = [place, flat, observed, prior_rows, noise_var.reshape(1, sensors)]
        messages = call(
            functools.partial(pack_kernel, plan, batch),
            [SMEM, HBM, HBM, VMEM, VMEM] + [ANY] * batch,
            [shape((plan.rows(batch, d), cells), bf16) for d in range(plan.chips)],
            [
                pltpu.VMEM((plan.pairs, CORES, halves, sensors, LANES), f32),
                pltpu.VMEM((1 + plan.pairs, line, cells), bf16),
                pltpu.SemaphoreType.DMA((plan.chips + 3, max(plan.chips, quads, CORES))),
            ],
            [ANY] * plan.chips,
            moved=10 * 2**20,
        )(*operands, *[maps[i][order[2]] for i in range(batch)])
        mine = [messages[0]] + [None] * (plan.chips - 1)
        for d in order:
            mine[d] = swap(messages[d], ("pair", "quad"), d)
        maps.append(mine + [swap(x, "core", 1) for x in mine])

    prior, noise, *streams = call(
        functools.partial(gather_kernel, plan),
        [SMEM] + [VMEM] * (1 + 2 * plan.chips),
        [shape((quads, cells, plan.width), bf16), shape((groups, sensors, LANES), f32)]
        + [shape((groups, sensors, LANES), bf16)] * CORES,
        moved=4 * 2**20,
    )(place, prior_rows, *maps[0])

    def over_sides(partial):
        if count == 2:
            return [partial, swap(partial, "side", 1)]
        return [lax.psum(partial, "side")]

    wide, narrow = shape((groups, sensors, LANES), f32), shape((groups, sensors, LANES), bf16)
    sides_scratch = pltpu.VMEM((groups, LANES, halves * sensors), bf16)

    def step(stage, j, preds):
        batch, start = starts[j]
        operands = [scales[j:j + 1], prior, streams[j], noise] + maps[batch] + preds
        return call(
            functools.partial(step_kernel, plan, stage, start, len(preds)),
            [SMEM] + [VMEM] * (len(operands) - 1),
            [narrow] if stage == 0 else [wide, narrow],
            [sides_scratch],
            flops=2**31,
            moved=8 * 2**20,
        )(*operands)

    outputs = []
    for j in range(CORES):
        batch, start = starts[j]
        preds = over_sides(step(0, j, [])[0])
        held, partial = step(1, j, preds)
        preds = over_sides(partial)
        final, dual = call(
            functools.partial(last_kernel, plan, len(preds)),
            [SMEM] + [VMEM] * (3 + len(preds)),
            [narrow, shape((groups, quads, sensors, LANES), bf16)],
            moved=2 * 2**20,
        )(place, noise, streams[j], held, *preds)
        dual = lax.all_to_all(
            dual.reshape(groups * quads, sensors, LANES), ("pair", "core", "quad"), split_axis=0, concat_axis=0, tiled=True
        ).reshape(pairs, CORES, quads, sensors, LANES)
        posts = call(
            functools.partial(post_kernel, plan, start),
            [SMEM, SMEM] + [VMEM] * (2 + 2 * plan.chips),
            [shape((cells, LANES), bf16)] * quads,
            [sides_scratch, pltpu.VMEM((quads, cells, LANES), bf16)],
            flops=2**31,
            moved=16 * 2**20,
        )(place, scales[j:j + 1], prior, final, *maps[batch])
        half = quads // CORES
        posts = [lax.ppermute(posts[i], ("core", "quad"), post_route(quads, *divmod(i, half))) for i in range(quads)]
        operands = [place, dual] + posts + outputs
        outputs = call(
            functools.partial(end_kernel, plan, j),
            [SMEM] + [VMEM] * (1 + quads) + [ANY] * len(outputs),
            [shape((frequencies, halves, sensors, LANES), f32), shape((quads, cells * 2, LANES), f32)],
            [
                pltpu.VMEM((plan.chips, halves, sensors, LANES), f32),
                pltpu.VMEM((half, cells * 2, LANES), f32),
                pltpu.SemaphoreType.DMA((plan.chips + half,)),
            ],
            [ANY, ANY],
            moved=8 * 2**20,
            aliases={len(operands) - 2: 0, len(operands) - 1: 1} if j else None,
        )(*operands)
        outputs = list(outputs)
    dual, posterior = outputs
    return dual, posterior.reshape(quads, cells, 2, LANES)


def solution(mesh):
    groups, space = mesh.devices.shape

    def run(forward_map, observed, noise_var, prior_rows, prior_scale):
        quads = forward_map.shape[0] // groups
        split = Mesh(
            mesh.devices.reshape(groups // CORES, CORES, space // quads, quads), ("pair", "core", "side", "quad")
        )
        return jax.shard_map(
            on_device,
            mesh=split,
            in_specs=(
                P(None, None, ("pair", "core"), ("side", "quad")),
                P(None, None, ("pair", "core"), None),
                P(("pair", "core")),
                P(("side", "quad"), None),
                P(),
            ),
            out_specs=(P(None, None, ("pair", "core"), None), P(("pair", "core"), ("side", "quad"), None, None)),
            check_vma=False,
        )(forward_map, observed, noise_var, prior_rows, prior_scale)

    return run
```

time: 195 us -> 239 us (1.23)
  local copies, waits for them, and re-layouts: 14 us -> 35.1 us
  starting transfers between devices: 36 us -> 51.1 us
  waiting for transfers between devices: 105 us -> 113 us
  Pallas kernels: 38.7 us -> 36.3 us
    unnamed x34 -> x152, local copies, waits for them, and re-layouts: 13.4 us -> 34.4 us
    ppermute x30 -> x34, waiting for transfers between devices: 96.3 us -> 113 us  [swap(): lax.ppermute(x, axes, [(i, i ^ distance) for i in range(lax.axis_size(axe...]
    ppermute x4 -> x8, starting transfers between devices: 2.73 us -> 11.7 us  [on_device(): lax.ppermute(posts[i], ('core', 'quad'), post_route(quads, *divmod(i, hal...]
    all_to_all x0 -> x2, starting transfers between devices: none -> 8.85 us  [on_device(): lax.all_to_all(dual.reshape(groups * quads, sensors, LANES), ('pair', 'co...]
    ppermute x4 -> x8, waiting for transfers between devices: 8.76 us -> 0.65 us  [on_device(): lax.ppermute(posts[i], ('core', 'quad'), post_route(quads, *divmod(i, hal...]
    pallas_call x4, Pallas kernels: 23.1 us -> 16.5 us  [step(): call(functools.partial(step_kernel, plan, stage, start, len(preds)), [SME...]
    pallas_call x7 -> x8, Pallas kernels: 12.9 us -> 18.1 us  [the longest x2 6.97 us: on_device(): call(functools.partial(post_kernel, plan, start), [SMEM, SMEM] + [VMEM] *...]
    ppermute x30 -> x34, starting transfers between devices: 33.2 us -> 30.6 us  [swap(): lax.ppermute(x, axes, [(i, i ^ distance) for i in range(lax.axis_size(axe...]
  transfers between devices with their start and end apart: 34 -> 44, of which waited for: 13 -> 16; matrix products, arithmetic and copies ran while one was open for 0% -> 0% of each run, Pallas kernels for 13% -> 8%
where the time goes in v4:
time: 239 us; the launch traced here: 238 us
  waiting for transfers between devices  113 us (47%)
  starting transfers between devices  51.1 us (21%)
  Pallas kernels  36.3 us (15%)
  local copies, waits for them, and re-layouts  35.1 us (15%)
    ppermute x34, waiting for transfers between devices, swap(): lax.ppermute(x, axes, [(i, i ^ distance) for i in range(lax.axis_size(axe...  113 us
    unnamed x152, local copies, waits for them, and re-layouts  34.4 us
    ppermute x34, starting transfers between devices, swap(): lax.ppermute(x, axes, [(i, i ^ distance) for i in range(lax.axis_size(axe...  30.6 us
    pallas_call x4, Pallas kernels, step(): call(functools.partial(step_kernel, plan, stage, start, len(preds)), [SME...  16.5 us
    ppermute x8, starting transfers between devices, on_device(): lax.ppermute(posts[i], ('core', 'quad'), post_route(quads, *divmod(i, hal...  11.7 us
    all_to_all x2, starting transfers between devices, on_device(): lax.all_to_all(dual.reshape(groups * quads, sensors, LANES), ('pair', 'co...  8.85 us
    pallas_call x2, Pallas kernels, on_device(): call(functools.partial(post_kernel, plan, start), [SMEM, SMEM] + [VMEM] *...  6.97 us
    pallas_call x2, Pallas kernels, on_device(): call(functools.partial(end_kernel, plan, j), [SMEM] + [VMEM] * (1 + quads...  5.81 us
  transfers between devices with their start and end apart: 44, of which 16 were waited for; matrix products, arithmetic and copies ran while one was open for 0% of the time, Pallas kernels for 8%

profile of v4, /device:TPU:0, one launch (start us, length us, event | category | flops | bytes accessed | tf_op | source)
XLA Modules:
  0.0 237.6 jit_solution(17365872806781598567)
XLA Ops:
  0.7 2.2 copy-done
  2.9 2.2 copy-done.2
  6.7 2.4 %shard_map.68 = (bf16[1040,256]{1,0:T(8,128)(2,1)S(1)}, bf16[768,256]{1,0:T(8,128)(2,1)S(1)}, bf16[768,256]{1,0:T(8,128)(2,1)S(1)}, bf16[768,256]{1,0:T(8,128)(2...) custom-call(s32[3]{0:T(128)S(1)} %pad_add_fusion.place_ref, ...), custom_call_target="tpu_custom_call" | custom-call | bytes 10485760 | tf_op jit(solution)/shard_map/pallas_call | solution.py:291
  9.2 5.0 %collective-permute-start.6 = (bf16[512,256]{1,0:T(8,128)(2,1)S(1)}, bf16[512,256]{1,0:T(8,128)(2,1)S(1)}, u32[]{:S(2)}, u32[]{:S(2)}) collective-permute-start(bf16[512,256]{1,0:T(8,128)(2,1)S(1)} %get-tuple-element.49), channel_id=1, source_target_pairs={{0,19},{1,18},{2,17},{3,16},{16,3},{17,2},{18,1},{19,0},{4,23},{5,... | collective-permute-start | bytes 786440 | tf_op jit(solution)/shard_map/ppermute | solution.py:282
  18.0 4.0 %collective-permute-done.6.refs_7_.refs_0_ = bf16[512,256]{1,0:T(8,128)(2,1)S(1)} collective-permute-done((bf16[512,256]{1,0:T(8,128)(2,1)S(1)}, bf16[512,256]{1,0:T(8,128)(2,1)S(1)}, u32[]{:S(2)}, u32[]{:S(2)}) %collective-permute-start.6) | collective-permute-done | bytes 262176 | tf_op jit(solution)/shard_map/ppermute | solution.py:282
  22.0 2.0 collective-permute-start.1
  24.1 8.1 %collective-permute-done.4.refs_5_ = bf16[512,256]{1,0:T(8,128)(2,1)S(1)} collective-permute-done((bf16[512,256]{1,0:T(8,128)(2,1)S(1)}, bf16[512,256]{1,0:T(8,128)(2,1)S(1)}, u32[]{:S(2)}, u32[]{:S(2)}) %collective-permute-start.4) | collective-permute-done | bytes 262176 | tf_op jit(solution)/shard_map/ppermute | solution.py:282
  32.1 3.6 %collective-permute-start.5 = (bf16[512,256]{1,0:T(8,128)(2,1)S(1)}, bf16[512,256]{1,0:T(8,128)(2,1)S(1)}, u32[]{:S(2)}, u32[]{:S(2)}) collective-permute-start(bf16[512,256]{1,0:T(8,128)(2,1)S(1)} %get-tuple-element.48), channel_id=1, source_target_pairs={{0,18},{1,19},{2,16},{3,17},{16,2},{17,3},{18,0},{19,1},{4,22},{5,... | collective-permute-start | bytes 786440 | tf_op jit(solution)/shard_map/ppermute | solution.py:282
  35.8 13.2 %collective-permute-done.5.refs_6_ = bf16[512,256]{1,0:T(8,128)(2,1)S(1)} collective-permute-done((bf16[512,256]{1,0:T(8,128)(2,1)S(1)}, bf16[512,256]{1,0:T(8,128)(2,1)S(1)}, u32[]{:S(2)}, u32[]{:S(2)}) %collective-permute-start.5) | collective-permute-done | bytes 262176 | tf_op jit(solution)/shard_map/ppermute | solution.py:282
  66.2 4.9 %shard_map.75.refs_16_ = bf16[4,256,128]{2,1,0:T(8,128)(2,1)S(1)} custom-call(f32[1]{0:T(128)} %get-tuple-element.82.scale_ref, bf16[4,256,512]{2,1,0:T(8,128)(2,1)S(1)} %get-tuple-element.52.prior_ref, bf16[4,256,128]{2,1,0:T(8,128)(2,1)S(1)} %get-tuple-element.69.obs_ref, f32[4,256,128]{2,1,0:T(8,128)S(1)} %get-tuple-element.50.noise_ref, ...), custom_call_target="tpu_custom_call" | custom-call | flops 2147483648 | bytes 8388608 | tf_op jit(solution)/shard_map/pallas_call | solution.py:327
  71.1 2.7 %collective-permute-start.36 = (bf16[4,256,128]{2,1,0:T(8,128)(2,1)S(1)}, bf16[4,256,128]{2,1,0:T(8,128)(2,1)S(1)}, u32[]{:S(2)}, u32[]{:S(2)}) collective-permute-start(bf16[4,256,128]{2,1,0:T(8,128)(2,1)S(1)} %shard_map.75.refs_16_), channel_id=1, source_target_pairs={{0,4},{4,0},{1,5},{5,1},{2,6},{6,2},{3,7},{7,3},{8,12},{12,8},{9,1... | collective-permute-start | bytes 786440 | tf_op jit(solution)/shard_map/ppermute | solution.py:282
  73.8 12.5 %collective-permute-done.36.refs_17_ = bf16[4,256,128]{2,1,0:T(8,128)(2,1)S(1)} collective-permute-done((bf16[4,256,128]{2,1,0:T(8,128)(2,1)S(1)}, bf16[4,256,128]{2,1,0:T(8,128)(2,1)S(1)}, u32[]{:S(2)}, u32[]{:S(2)}) %collective-permute-start.36) | collective-permute-done | bytes 262176 | tf_op jit(solution)/shard_map/ppermute | solution.py:282
  86.3 4.8 %shard_map.76 = (f32[4,256,128]{2,1,0:T(8,128)S(1)}, bf16[4,256,128]{2,1,0:T(8,128)(2,1)S(1)}) custom-call(f32[1]{0:T(128)} %get-tuple-element.82.scale_ref, bf16[4,256,512]{2,1,0:T(8,128)(2,1)S(1)} %get-tuple-element.52.prior_ref, bf16[4,256,128]{2,1,0:T(8,128)(2,1)S(1)} %get-tuple-element.69.obs_ref, f32[4,256,128]{2,1,0:T(8,128)S(1)} %get-tuple-element.50.noise_ref, ...), custom_call_target="tpu_custom_call" | custom-call | flops 2147483648 | bytes 8388608 | tf_op jit(solution)/shard_map/pallas_call | solution.py:327
  91.2 14.3 %collective-permute-done.37.refs_1_ = bf16[4,256,128]{2,1,0:T(8,128)(2,1)S(1)} collective-permute-done((bf16[4,256,128]{2,1,0:T(8,128)(2,1)S(1)}, bf16[4,256,128]{2,1,0:T(8,128)(2,1)S(1)}, u32[]{:S(2)}, u32[]{:S(2)}) %collective-permute-start.37) | collective-permute-done | bytes 262176 | tf_op jit(solution)/shard_map/ppermute | solution.py:282
  107.9 4.5 %all-to-all-start.1 = ((bf16[16,256,128]{2,1,0:T(8,128)(2,1)}), bf16[16,256,128]{2,1,0:T(8,128)(2,1)}, u32[]{:S(2)}, u32[]{:S(2)}) async-start(bf16[16,256,128]{2,1,0:T(8,128)(2,1)} %bitcast.12), calls=%async_computation.1 | async-start | bytes 2097152 | tf_op jit(solution)/shard_map/all_to_all | solution.py:348
  112.5 2.2 copy-done.1
  114.6 2.2 copy-done.3
  125.9 20.1 %collective-permute-done.15.refs_1_ = bf16[512,256]{1,0:T(8,128)(2,1)S(1)} collective-permute-done((bf16[512,256]{1,0:T(8,128)(2,1)S(1)}, bf16[512,256]{1,0:T(8,128)(2,1)S(1)}, u32[]{:S(2)}, u32[]{:S(2)}) %collective-permute-start.15) | collective-permute-done | bytes 262176 | tf_op jit(solution)/shard_map/ppermute | solution.py:282
  149.5 6.5 %collective-permute-done.20.refs_6_ = bf16[512,256]{1,0:T(8,128)(2,1)S(1)} collective-permute-done((bf16[512,256]{1,0:T(8,128)(2,1)S(1)}, bf16[512,256]{1,0:T(8,128)(2,1)S(1)}, u32[]{:S(2)}, u32[]{:S(2)}) %collective-permute-start.20) | collective-permute-done | bytes 262176 | tf_op jit(solution)/shard_map/ppermute | solution.py:282
  156.1 4.7 %collective-permute-done.21.refs_7_ = bf16[512,256]{1,0:T(8,128)(2,1)S(1)} collective-permute-done((bf16[512,256]{1,0:T(8,128)(2,1)S(1)}, bf16[512,256]{1,0:T(8,128)(2,1)S(1)}, u32[]{:S(2)}, u32[]{:S(2)}) %collective-permute-start.21) | collective-permute-done | bytes 262176 | tf_op jit(solution)/shard_map/ppermute | solution.py:282
  163.4 3.4 %shard_map.71.refs_16_ = bf16[4,256,128]{2,1,0:T(8,128)(2,1)S(1)} custom-call(f32[1]{0:T(128)} %get-tuple-element.83.scale_ref, bf16[4,256,512]{2,1,0:T(8,128)(2,1)S(1)} %copy-done.5, bf16[4,256,128]{2,1,0:T(8,128)(2,1)S(1)} %copy-done.36, f32[4,256,128]{2,1,0:T(8,128)S(1)} %get-tuple-element.50.noise_ref, bf16[512,256]{1,0:T(8,128)(2,1)S(1)} %get-tuple-element.53.refs_0_, ...), custom_call_target="tpu_custom_call" | custom-call | flops 2147483648 | bytes 8388608 | tf_op jit(solution)/shard_map/pallas_call | solution.py:327
  166.9 14.8 %collective-permute-done.30.refs_17_ = bf16[4,256,128]{2,1,0:T(8,128)(2,1)S(1)} collective-permute-done((bf16[4,256,128]{2,1,0:T(8,128)(2,1)S(1)}, bf16[4,256,128]{2,1,0:T(8,128)(2,1)S(1)}, u32[]{:S(2)}, u32[]{:S(2)}) %collective-permute-start.30) | collective-permute-done | bytes 262176 | tf_op jit(solution)/shard_map/ppermute | solution.py:282
  181.7 3.4 %shard_map.72 = (f32[4,256,128]{2,1,0:T(8,128)S(1)}, bf16[4,256,128]{2,1,0:T(8,128)(2,1)S(1)}) custom-call(f32[1]{0:T(128)} %get-tuple-element.83.scale_ref, bf16[4,256,512]{2,1,0:T(8,128)(2,1)S(1)} %copy-done.5, bf16[4,256,128]{2,1,0:T(8,128)(2,1)S(1)} %copy-done.36, f32[4,256,128]{2,1,0:T(8,128)S(1)} %get-tuple-element.50.noise_ref, ...), custom_call_target="tpu_custom_call" | custom-call | flops 2147483648 | bytes 8388608 | tf_op jit(solution)/shard_map/pallas_call | solution.py:327
  185.3 12.0 %collective-permute-done.31.refs_1_ = bf16[4,256,128]{2,1,0:T(8,128)(2,1)S(1)} collective-permute-done((bf16[4,256,128]{2,1,0:T(8,128)(2,1)S(1)}, bf16[4,256,128]{2,1,0:T(8,128)(2,1)S(1)}, u32[]{:S(2)}, u32[]{:S(2)}) %collective-permute-start.31) | collective-permute-done | bytes 262176 | tf_op jit(solution)/shard_map/ppermute | solution.py:282
  199.7 4.3 %all-to-all-start = ((bf16[16,256,128]{2,1,0:T(8,128)(2,1)}), bf16[16,256,128]{2,1,0:T(8,128)(2,1)}, u32[]{:S(2)}, u32[]{:S(2)}) async-start(bf16[16,256,128]{2,1,0:T(8,128)(2,1)} %bitcast.13), calls=%async_computation | async-start | bytes 2097152 | tf_op jit(solution)/shard_map/all_to_all | solution.py:348
  212.1 4.2 %shard_map.78 = (bf16[256,128]{1,0:T(8,128)(2,1)S(1)}, bf16[256,128]{1,0:T(8,128)(2,1)S(1)}, bf16[256,128]{1,0:T(8,128)(2,1)S(1)}, bf16[256,128]{1,0:T(8,128)(2,1)S(1)}) custom-call(s32[3]{0:T(128)S(1)} %pad_add_fusion.place_ref, f32[1]{0:T(128)} %get-tuple-element.82.scale_ref, bf16[4,256,512]{2,1,0:T(8,128)(2,1)S(1)} %copy-done.6, ...), custom_call_target="tpu_custom_call" | custom-call | flops 2147483648 | bytes 16777216 | tf_op jit(solution)/shard_map/pallas_call | solution.py:351
  217.0 1.8 collective-permute-start.39
  218.8 3.9 %collective-permute-start.40 = (bf16[256,128]{1,0:T(8,128)(2,1)S(1)}, bf16[256,128]{1,0:T(8,128)(2,1)S(1)}, u32[]{:S(2)}, u32[]{:S(2)}) collective-permute-start(bf16[256,128]{1,0:T(8,128)(2,1)S(1)} %get-tuple-element.76), channel_id=1, source_target_pairs={{0,2},{1,3},{2,10},{3,11},{8,0},{9,1},{10,8},{11,9},{4,6},{5,7},{6... | collective-permute-start | bytes 196616 | tf_op jit(solution)/shard_map/ppermute | solution.py:360
  222.8 2.8 %shard_map.74 = (bf16[256,128]{1,0:T(8,128)(2,1)S(1)}, bf16[256,128]{1,0:T(8,128)(2,1)S(1)}, bf16[256,128]{1,0:T(8,128)(2,1)S(1)}, bf16[256,128]{1,0:T(8,128)(2,1)S(1)}) custom-call(s32[3]{0:T(128)S(1)} %pad_add_fusion.place_ref, f32[1]{0:T(128)} %get-tuple-element.83.scale_ref, bf16[4,256,512]{2,1,0:T(8,128)(2,1)S(1)} %copy-done.6, ...), custom_call_target="tpu_custom_call" | custom-call | flops 2147483648 | bytes 16777216 | tf_op jit(solution)/shard_map/pallas_call | solution.py:351
  227.8 3.0 %collective-permute-start.34 = (bf16[256,128]{1,0:T(8,128)(2,1)S(1)}, bf16[256,128]{1,0:T(8,128)(2,1)S(1)}, u32[]{:S(2)}, u32[]{:S(2)}) collective-permute-start(bf16[256,128]{1,0:T(8,128)(2,1)S(1)} %get-tuple-element.67), channel_id=1, source_target_pairs={{0,2},{1,3},{2,10},{3,11},{8,0},{9,1},{10,8},{11,9},{4,6},{5,7},{6... | collective-permute-start | bytes 196616 | tf_op jit(solution)/shard_map/ppermute | solution.py:360
  231.0 2.9 %shard_map.79 = (f32[16,2,256,128]{3,2,1,0:T(8,128)}, f32[4,512,128]{2,1,0:T(8,128)}) custom-call(s32[3]{0:T(128)S(1)} %pad_add_fusion.place_ref, bf16[2,2,4,256,128]{4,3,2,1,0:T(8,128)(2,1)} %bitcast.8.dual_ref, bf16[256,128]{1,0:T(8,128)(2,1)S(1)} %collective-permute-done.38.refs_0_, bf16[256,128]{1,0:T(8,128)(2,1)S(1)} %collective-permute-done.39.refs_1_, ...), custom_call_target="tpu_custom_call" | custom-call | bytes 8388608 | tf_op jit(solution)/shard_map/pallas_call | solution.py:362
  234.6 2.9 %shard_map.80 = (f32[16,2,256,128]{3,2,1,0:T(8,128)}, f32[4,512,128]{2,1,0:T(8,128)}) custom-call(s32[3]{0:T(128)S(1)} %pad_add_fusion.place_ref, bf16[2,2,4,256,128]{4,3,2,1,0:T(8,128)(2,1)} %bitcast.6.dual_ref, bf16[256,128]{1,0:T(8,128)(2,1)S(1)} %collective-permute-done.32.refs_0_, ...), custom_call_target="tpu_custom_call", output_to_operand_aliasing={{0}: (6, {}), {1}: (7, {})} | custom-call | bytes 8388608 | tf_op jit(solution)/shard_map/pallas_call | solution.py:362
  (224 shorter events, 54.6 us)
Async XLA Ops:
  9.2 12.8 %collective-permute-start.6 = (bf16[512,256]{1,0:T(8,128)(2,1)S(1)}, bf16[512,256]{1,0:T(8,128)(2,1)S(1)}, u32[]{:S(2)}, u32[]{:S(2)}) collective-permute-start(bf16[512,256]{1,0:T(8,128)(2,1)S(1)} %get-tuple-element.49), channel_id=1, source_target_pairs={{0,19},{1,18},{2,17},{3,16},{16,3},{17,2},{18,1},{19,0},{4,23},{5,... | collective-permute-start | bytes 786440 | tf_op jit(solution)/shard_map/ppermute | solution.py:282
  14.1 18.0 %collective-permute-start.4 = (bf16[512,256]{1,0:T(8,128)(2,1)S(1)}, bf16[512,256]{1,0:T(8,128)(2,1)S(1)}, u32[]{:S(2)}, u32[]{:S(2)}) collective-permute-start(bf16[512,256]{1,0:T(8,128)(2,1)S(1)} %get-tuple-element.47), channel_id=1, source_target_pairs={{0,17},{1,16},{2,19},{3,18},{16,1},{17,0},{18,3},{19,2},{4,21},{5,... | collective-permute-start | bytes 786440 | tf_op jit(solution)/shard_map/ppermute | solution.py:282
  14.6 36.8 %collective-permute-start.3 = (bf16[1040,256]{1,0:T(8,128)(2,1)S(1)}, bf16[1040,256]{1,0:T(8,128)(2,1)S(1)}, u32[]{:S(2)}, u32[]{:S(2)}) collective-permute-start(bf16[1040,256]{1,0:T(8,128)(2,1)S(1)} %get-tuple-element.46), channel_id=1, source_target_pairs={{0,16},{1,17},{2,18},{3,19},{16,0},{17,1},{18,2},{19,3},{4,20},{5,... | collective-permute-start | bytes 1597448 | tf_op jit(solution)/shard_map/ppermute | solution.py:282
  16.1 32.9 %collective-permute-start.2 = (bf16[768,256]{1,0:T(8,128)(2,1)S(1)}, bf16[768,256]{1,0:T(8,128)(2,1)S(1)}, u32[]{:S(2)}, u32[]{:S(2)}) collective-permute-start(bf16[768,256]{1,0:T(8,128)(2,1)S(1)} %get-tuple-element.45), channel_id=1, source_target_pairs={{0,3},{1,2},{2,1},{3,0},{16,19},{17,18},{18,17},{19,16},{4,7},{5,6... | collective-permute-start | bytes 1179656 | tf_op jit(solution)/shard_map/ppermute | solution.py:282
  17.5 32.7 %collective-permute-start = (bf16[768,256]{1,0:T(8,128)(2,1)S(1)}, bf16[768,256]{1,0:T(8,128)(2,1)S(1)}, u32[]{:S(2)}, u32[]{:S(2)}) collective-permute-start(bf16[768,256]{1,0:T(8,128)(2,1)S(1)} %get-tuple-element.43), channel_id=1, source_target_pairs={{0,1},{1,0},{2,3},{3,2},{16,17},{17,16},{18,19},{19,18},{4,5},{5,4... | collective-permute-start | bytes 1179656 | tf_op jit(solution)/shard_map/ppermute | solution.py:282
  22.0 28.9 %collective-permute-start.1 = (bf16[768,256]{1,0:T(8,128)(2,1)S(1)}, bf16[768,256]{1,0:T(8,128)(2,1)}, u32[]{:S(2)}, u32[]{:S(2)}) collective-permute-start(bf16[768,256]{1,0:T(8,128)(2,1)S(1)} %get-tuple-element.44), channel_id=1, source_target_pairs={{0,2},{1,3},{2,0},{3,1},{16,18},{17,19},{18,16},{19,17},{4,6},{5,7... | collective-permute-start | bytes 1179656 | tf_op jit(solution)/shard_map/ppermute | solution.py:282
  32.1 16.9 %collective-permute-start.5 = (bf16[512,256]{1,0:T(8,128)(2,1)S(1)}, bf16[512,256]{1,0:T(8,128)(2,1)S(1)}, u32[]{:S(2)}, u32[]{:S(2)}) collective-permute-start(bf16[512,256]{1,0:T(8,128)(2,1)S(1)} %get-tuple-element.48), channel_id=1, source_target_pairs={{0,18},{1,19},{2,16},{3,17},{16,2},{17,3},{18,0},{19,1},{4,22},{5,... | collective-permute-start | bytes 786440 | tf_op jit(solution)/shard_map/ppermute | solution.py:282
  51.4 5.6 %collective-permute-start.11 = (bf16[1040,256]{1,0:T(8,128)(2,1)S(1)}, bf16[1040,256]{1,0:T(8,128)(2,1)S(1)}, u32[]{:S(2)}, u32[]{:S(2)}) collective-permute-start(bf16[1040,256]{1,0:T(8,128)(2,1)S(1)} %collective-permute-done.3.refs_4_), channel_id=1, source_target_pairs={{0,8},{8,0},{1,9},{9,1},{2,10},{10,2},{3,11},{11,3},{4,12},{12,4},... | collective-permute-start | bytes 1597448 | tf_op jit(solution)/shard_map/ppermute | solution.py:282
  71.1 15.2 %collective-permute-start.36 = (bf16[4,256,128]{2,1,0:T(8,128)(2,1)S(1)}, bf16[4,256,128]{2,1,0:T(8,128)(2,1)S(1)}, u32[]{:S(2)}, u32[]{:S(2)}) collective-permute-start(bf16[4,256,128]{2,1,0:T(8,128)(2,1)S(1)} %shard_map.75.refs_16_), channel_id=1, source_target_pairs={{0,4},{4,0},{1,5},{5,1},{2,6},{6,2},{3,7},{7,3},{8,12},{12,8},{9,1... | collective-permute-start | bytes 786440 | tf_op jit(solution)/shard_map/ppermute | solution.py:282
  91.1 14.4 %collective-permute-start.37 = (bf16[4,256,128]{2,1,0:T(8,128)(2,1)S(1)}, bf16[4,256,128]{2,1,0:T(8,128)(2,1)S(1)}, u32[]{:S(2)}, u32[]{:S(2)}) collective-permute-start(bf16[4,256,128]{2,1,0:T(8,128)(2,1)S(1)} %get-tuple-element.71.refs_0_), channel_id=1, source_target_pairs={{0,4},{4,0},{1,5},{5,1},{2,6},{6,2},{3,7},{7,3},{8,12},{12,8},{9,1... | collective-permute-start | bytes 786440 | tf_op jit(solution)/shard_map/ppermute | solution.py:282
  107.9 91.8 %all-to-all-start.1 = ((bf16[16,256,128]{2,1,0:T(8,128)(2,1)}), bf16[16,256,128]{2,1,0:T(8,128)(2,1)}, u32[]{:S(2)}, u32[]{:S(2)}) async-start(bf16[16,256,128]{2,1,0:T(8,128)(2,1)} %bitcast.12), calls=%async_computation.1 | async-start | bytes 2097152 | tf_op jit(solution)/shard_map/all_to_all | solution.py:348
  119.3 26.7 %collective-permute-start.15 = (bf16[512,256]{1,0:T(8,128)(2,1)S(1)}, bf16[512,256]{1,0:T(8,128)(2,1)S(1)}, u32[]{:S(2)}, u32[]{:S(2)}) collective-permute-start(bf16[512,256]{1,0:T(8,128)(2,1)S(1)} %get-tuple-element.54), channel_id=1, source_target_pairs={{0,1},{1,0},{2,3},{3,2},{16,17},{17,16},{18,19},{19,18},{4,5},{5,4... | collective-permute-start | bytes 786440 | tf_op jit(solution)/shard_map/ppermute | solution.py:282
  120.9 26.2 %collective-permute-start.16 = (bf16[512,256]{1,0:T(8,128)(2,1)S(1)}, bf16[512,256]{1,0:T(8,128)(2,1)S(1)}, u32[]{:S(2)}, u32[]{:S(2)}) collective-permute-start(bf16[512,256]{1,0:T(8,128)(2,1)S(1)} %get-tuple-element.55), channel_id=1, source_target_pairs={{0,2},{1,3},{2,0},{3,1},{16,18},{17,19},{18,16},{19,17},{4,6},{5,7... | collective-permute-start | bytes 786440 | tf_op jit(solution)/shard_map/ppermute | solution.py:282
  122.4 26.5 %collective-permute-start.17 = (bf16[512,256]{1,0:T(8,128)(2,1)S(1)}, bf16[512,256]{1,0:T(8,128)(2,1)S(1)}, u32[]{:S(2)}, u32[]{:S(2)}) collective-permute-start(bf16[512,256]{1,0:T(8,128)(2,1)S(1)} %get-tuple-element.56), channel_id=1, source_target_pairs={{0,3},{1,2},{2,1},{3,0},{16,19},{17,18},{18,17},{19,16},{4,7},{5,6... | collective-permute-start | bytes 786440 | tf_op jit(solution)/shard_map/ppermute | solution.py:282
  122.8 26.1 %collective-permute-start.18 = (bf16[512,256]{1,0:T(8,128)(2,1)S(1)}, bf16[512,256]{1,0:T(8,128)(2,1)S(1)}, u32[]{:S(2)}, u32[]{:S(2)}) collective-permute-start(bf16[512,256]{1,0:T(8,128)(2,1)S(1)} %get-tuple-element.57), channel_id=1, source_target_pairs={{0,16},{1,17},{2,18},{3,19},{16,0},{17,1},{18,2},{19,3},{4,20},{5,... | collective-permute-start | bytes 786440 | tf_op jit(solution)/shard_map/ppermute | solution.py:282
  124.5 25.0 %collective-permute-start.19 = (bf16[512,256]{1,0:T(8,128)(2,1)S(1)}, bf16[512,256]{1,0:T(8,128)(2,1)S(1)}, u32[]{:S(2)}, u32[]{:S(2)}) collective-permute-start(bf16[512,256]{1,0:T(8,128)(2,1)S(1)} %get-tuple-element.58), channel_id=1, source_target_pairs={{0,17},{1,16},{2,19},{3,18},{16,1},{17,0},{18,3},{19,2},{4,21},{5,... | collective-permute-start | bytes 786440 | tf_op jit(solution)/shard_map/ppermute | solution.py:282
  146.0 10.1 %collective-permute-start.20 = (bf16[512,256]{1,0:T(8,128)(2,1)S(1)}, bf16[512,256]{1,0:T(8,128)(2,1)S(1)}, u32[]{:S(2)}, u32[]{:S(2)}) collective-permute-start(bf16[512,256]{1,0:T(8,128)(2,1)S(1)} %get-tuple-element.59), channel_id=1, source_target_pairs={{0,18},{1,19},{2,16},{3,17},{16,2},{17,3},{18,0},{19,1},{4,22},{5,... | collective-permute-start | bytes 786440 | tf_op jit(solution)/shard_map/ppermute | solution.py:282
  147.1 13.6 %collective-permute-start.21 = (bf16[512,256]{1,0:T(8,128)(2,1)S(1)}, bf16[512,256]{1,0:T(8,128)(2,1)S(1)}, u32[]{:S(2)}, u32[]{:S(2)}) collective-permute-start(bf16[512,256]{1,0:T(8,128)(2,1)S(1)} %get-tuple-element.60), channel_id=1, source_target_pairs={{0,19},{1,18},{2,17},{3,16},{16,3},{17,2},{18,1},{19,0},{4,23},{5,... | collective-permute-start | bytes 786440 | tf_op jit(solution)/shard_map/ppermute | solution.py:282
  148.9 11.8 %collective-permute-start.22 = (bf16[512,256]{1,0:T(8,128)(2,1)S(1)}, bf16[512,256]{1,0:T(8,128)(2,1)S(1)}, u32[]{:S(2)}, u32[]{:S(2)}) collective-permute-start(bf16[512,256]{1,0:T(8,128)(2,1)S(1)} %get-tuple-element.53.refs_0_), channel_id=1, source_target_pairs={{0,8},{8,0},{1,9},{9,1},{2,10},{10,2},{3,11},{11,3},{4,12},{12,4},... | collective-permute-start | bytes 786440 | tf_op jit(solution)/shard_map/ppermute | solution.py:282
  148.9 12.3 %collective-permute-start.23 = (bf16[512,256]{1,0:T(8,128)(2,1)S(1)}, bf16[512,256]{1,0:T(8,128)(2,1)S(1)}, u32[]{:S(2)}, u32[]{:S(2)}) collective-permute-start(bf16[512,256]{1,0:T(8,128)(2,1)S(1)} %collective-permute-done.15.refs_1_), channel_id=1, source_target_pairs={{0,8},{8,0},{1,9},{9,1},{2,10},{10,2},{3,11},{11,3},{4,12},{12,4},... | collective-permute-start | bytes 786440 | tf_op jit(solution)/shard_map/ppermute | solution.py:282
  149.4 11.9 %collective-permute-start.24 = (bf16[512,256]{1,0:T(8,128)(2,1)S(1)}, bf16[512,256]{1,0:T(8,128)(2,1)S(1)}, u32[]{:S(2)}, u32[]{:S(2)}) collective-permute-start(bf16[512,256]{1,0:T(8,128)(2,1)S(1)} %collective-permute-done.16.refs_2_), channel_id=1, source_target_pairs={{0,8},{8,0},{1,9},{9,1},{2,10},{10,2},{3,11},{11,3},{4,12},{12,4},... | collective-permute-start | bytes 786440 | tf_op jit(solution)/shard_map/ppermute | solution.py:282
  156.1 5.7 %collective-permute-start.25 = (bf16[512,256]{1,0:T(8,128)(2,1)S(1)}, bf16[512,256]{1,0:T(8,128)(2,1)S(1)}, u32[]{:S(2)}, u32[]{:S(2)}) collective-permute-start(bf16[512,256]{1,0:T(8,128)(2,1)S(1)} %collective-permute-done.17.refs_3_), channel_id=1, source_target_pairs={{0,8},{8,0},{1,9},{9,1},{2,10},{10,2},{3,11},{11,3},{4,12},{12,4},... | collective-permute-start | bytes 786440 | tf_op jit(solution)/shard_map/ppermute | solution.py:282
  166.8 14.9 %collective-permute-start.30 = (bf16[4,256,128]{2,1,0:T(8,128)(2,1)S(1)}, bf16[4,256,128]{2,1,0:T(8,128)(2,1)S(1)}, u32[]{:S(2)}, u32[]{:S(2)}) collective-permute-start(bf16[4,256,128]{2,1,0:T(8,128)(2,1)S(1)} %shard_map.71.refs_16_), channel_id=1, source_target_pairs={{0,4},{4,0},{1,5},{5,1},{2,6},{6,2},{3,7},{7,3},{8,12},{12,8},{9,1... | collective-permute-start | bytes 786440 | tf_op jit(solution)/shard_map/ppermute | solution.py:282
  185.2 12.1 %collective-permute-start.31 = (bf16[4,256,128]{2,1,0:T(8,128)(2,1)S(1)}, bf16[4,256,128]{2,1,0:T(8,128)(2,1)S(1)}, u32[]{:S(2)}, u32[]{:S(2)}) collective-permute-start(bf16[4,256,128]{2,1,0:T(8,128)(2,1)S(1)} %get-tuple-element.62.refs_0_), channel_id=1, source_target_pairs={{0,4},{4,0},{1,5},{5,1},{2,6},{6,2},{3,7},{7,3},{8,12},{12,8},{9,1... | collective-permute-start | bytes 786440 | tf_op jit(solution)/shard_map/ppermute | solution.py:282
  199.7 34.9 %all-to-all-start = ((bf16[16,256,128]{2,1,0:T(8,128)(2,1)}), bf16[16,256,128]{2,1,0:T(8,128)(2,1)}, u32[]{:S(2)}, u32[]{:S(2)}) async-start(bf16[16,256,128]{2,1,0:T(8,128)(2,1)} %bitcast.13), calls=%async_computation | async-start | bytes 2097152 | tf_op jit(solution)/shard_map/all_to_all | solution.py:348
  216.3 10.0 %collective-permute-start.38 = (bf16[256,128]{1,0:T(8,128)(2,1)S(1)}, bf16[256,128]{1,0:T(8,128)(2,1)S(1)}, u32[]{:S(2)}, u32[]{:S(2)}) collective-permute-start(bf16[256,128]{1,0:T(8,128)(2,1)S(1)} %get-tuple-element.74), channel_id=1, source_target_pairs={{0,0},{1,1},{2,8},{3,9},{8,2},{9,3},{10,10},{11,11},{4,4},{5,5},{6... | collective-permute-start | bytes 196616 | tf_op jit(solution)/shard_map/ppermute | solution.py:360
  217.0 10.9 %collective-permute-start.39 = (bf16[256,128]{1,0:T(8,128)(2,1)S(1)}, bf16[256,128]{1,0:T(8,128)(2,1)S(1)}, u32[]{:S(2)}, u32[]{:S(2)}) collective-permute-start(bf16[256,128]{1,0:T(8,128)(2,1)S(1)} %get-tuple-element.75), channel_id=1, source_target_pairs={{0,1},{1,0},{2,9},{3,8},{8,3},{9,2},{10,11},{11,10},{4,5},{5,4},{6... | collective-permute-start | bytes 196616 | tf_op jit(solution)/shard_map/ppermute | solution.py:360
  218.8 12.1 %collective-permute-start.40 = (bf16[256,128]{1,0:T(8,128)(2,1)S(1)}, bf16[256,128]{1,0:T(8,128)(2,1)S(1)}, u32[]{:S(2)}, u32[]{:S(2)}) collective-permute-start(bf16[256,128]{1,0:T(8,128)(2,1)S(1)} %get-tuple-element.76), channel_id=1, source_target_pairs={{0,2},{1,3},{2,10},{3,11},{8,0},{9,1},{10,8},{11,9},{4,6},{5,7},{6... | collective-permute-start | bytes 196616 | tf_op jit(solution)/shard_map/ppermute | solution.py:360
  222.7 8.3 %collective-permute-start.41 = (bf16[256,128]{1,0:T(8,128)(2,1)S(1)}, bf16[256,128]{1,0:T(8,128)(2,1)S(1)}, u32[]{:S(2)}, u32[]{:S(2)}) collective-permute-start(bf16[256,128]{1,0:T(8,128)(2,1)S(1)} %get-tuple-element.77), channel_id=1, source_target_pairs={{0,3},{1,2},{2,11},{3,10},{8,1},{9,0},{10,9},{11,8},{4,7},{5,6},{6... | collective-permute-start | bytes 196616 | tf_op jit(solution)/shard_map/ppermute | solution.py:360
  225.6 8.3 %collective-permute-start.32 = (bf16[256,128]{1,0:T(8,128)(2,1)S(1)}, bf16[256,128]{1,0:T(8,128)(2,1)S(1)}, u32[]{:S(2)}, u32[]{:S(2)}) collective-permute-start(bf16[256,128]{1,0:T(8,128)(2,1)S(1)} %get-tuple-element.65), channel_id=1, source_target_pairs={{0,0},{1,1},{2,8},{3,9},{8,2},{9,3},{10,10},{11,11},{4,4},{5,5},{6... | collective-permute-start | bytes 196616 | tf_op jit(solution)/shard_map/ppermute | solution.py:360
  226.3 7.6 %collective-permute-start.33 = (bf16[256,128]{1,0:T(8,128)(2,1)S(1)}, bf16[256,128]{1,0:T(8,128)(2,1)S(1)}, u32[]{:S(2)}, u32[]{:S(2)}) collective-permute-start(bf16[256,128]{1,0:T(8,128)(2,1)S(1)} %get-tuple-element.66), channel_id=1, source_target_pairs={{0,1},{1,0},{2,9},{3,8},{8,3},{9,2},{10,11},{11,10},{4,5},{5,4},{6... | collective-permute-start | bytes 196616 | tf_op jit(solution)/shard_map/ppermute | solution.py:360
  227.8 6.1 %collective-permute-start.34 = (bf16[256,128]{1,0:T(8,128)(2,1)S(1)}, bf16[256,128]{1,0:T(8,128)(2,1)S(1)}, u32[]{:S(2)}, u32[]{:S(2)}) collective-permute-start(bf16[256,128]{1,0:T(8,128)(2,1)S(1)} %get-tuple-element.67), channel_id=1, source_target_pairs={{0,2},{1,3},{2,10},{3,11},{8,0},{9,1},{10,8},{11,9},{4,6},{5,7},{6... | collective-permute-start | bytes 196616 | tf_op jit(solution)/shard_map/ppermute | solution.py:360
  (88 other events, 1012.2 us)

commit v5 on v2

v5 whole, which is shorter than its diff:
```python
import functools

import jax
import jax.numpy as jnp
from jax import lax
from jax.experimental import pallas as pl
from jax.experimental.pallas import tpu as pltpu
from jax.sharding import Mesh, PartitionSpec as P

ITERS = 2
relax_step = 0.25
STREAMS = 2
CORES = 2
LANES = 128
HALF = LANES // 2
VMEM_LIMIT = 16 * 2**20
VMEM = pl.BlockSpec(memory_space=pltpu.VMEM)
SMEM = pl.BlockSpec(memory_space=pltpu.SMEM)
ANY = pl.BlockSpec(memory_space=pl.ANY)
bf16, f32 = jnp.bfloat16, jnp.float32


def shape(dims, dtype):
    return jax.ShapeDtypeStruct(dims, dtype)


def call(kernel, in_specs, out_shape, scratch=(), flops=0, moved=0):
    return pl.pallas_call(
        kernel,
        in_specs=in_specs,
        out_specs=[VMEM] * len(out_shape),
        out_shape=out_shape,
        scratch_shapes=list(scratch),
        cost_estimate=pl.CostEstimate(flops=flops, bytes_accessed=moved, transcendentals=0),
        compiler_params=pltpu.CompilerParams(vmem_limit_bytes=VMEM_LIMIT),
    )


def swap(x, axes, distance):
    count = lax.axis_size(axes)
    return lax.ppermute(x, axes, [(i, i ^ distance) for i in range(count)])


def dot(a, b):
    return jnp.dot(a, b, preferred_element_type=f32)


def dot_nt(a, b):
    return lax.dot_general(a, b, (((1,), (1,)), ((), ())), preferred_element_type=f32)


def data_kernel(groups, quads, place_ref, obs_ref, noise_ref, *refs):
    outs, (held, sems) = refs[:groups], refs[groups:]
    sensors = obs_ref.shape[2]
    copies = []
    for d in range(groups):
        freq = ((place_ref[0] * CORES + place_ref[2]) ^ d) * quads + place_ref[1]
        copies.append(pltpu.make_async_copy(obs_ref.at[freq], held.at[d], sems.at[d]))
        copies[-1].start()
    noise = noise_ref[...]
    high = noise.astype(bf16)
    low = (noise - high.astype(f32)).astype(bf16)
    tail = jnp.concatenate([jnp.broadcast_to(high, (8, sensors)), jnp.broadcast_to(low, (8, sensors))], 0)
    for d in range(groups):
        copies[d].wait()
        re, im = held[d, 0], held[d, 1]
        for s in range(STREAMS):
            part = slice(s * HALF, (s + 1) * HALF)
            outs[d][:sensors, s * LANES:(s + 1) * LANES] = jnp.concatenate([re[:, part], im[:, part]], 1).astype(bf16)
        outs[d][sensors:, :] = tail


def gather_kernel(groups, quads, place_ref, own_ref, *refs):
    came, data = refs[:quads - 1], refs[quads - 1:quads - 1 + groups]
    prior_ref, noise_ref, *streams = refs[quads - 1 + groups:]
    me, quad = place_ref[0] * CORES + place_ref[2], place_ref[1]
    sensors, cells = streams[0].shape[1], own_ref.shape[0]
    on, off = (pl.ds(pl.multiple_of(p * cells, cells), cells) for p in (quad & 1, 1 - (quad & 1)))
    for d in range(0, quads, 2):
        rows = own_ref if d == 0 else came[d - 1]
        prior_ref[quad ^ d] = rows[...]
        prior_ref[quad ^ d ^ 1, :, on] = rows[:, off].T
        prior_ref[quad ^ d ^ 1, :, off] = came[d][...]
    row = lax.broadcasted_iota(jnp.int32, (sensors, sensors), 0)
    col = lax.broadcasted_iota(jnp.int32, (sensors, sensors), 1)
    for d in range(groups):
        for s in range(STREAMS):
            streams[s][me ^ d] = data[d][:sensors, s * LANES:(s + 1) * LANES]
        both = data[d][sensors:, :].astype(f32)
        noise_row = both[0:1, :] + both[8:9, :]
        noise = jnp.sum(jnp.where(row == col, noise_row, 0.0), 1, keepdims=True)
        noise_ref[me ^ d] = jnp.broadcast_to(noise, (sensors, LANES))


def source(map_ref, sides_ref, prior_ref, scale):
    groups, quads, _, cells = map_ref.shape
    per_block = prior_ref.shape[2] // cells
    out = []
    for block in range(quads // per_block):
        members = range(block * per_block, (block + 1) * per_block)
        parts = []
        for q in members:
            u = jnp.zeros((sides_ref.shape[1], cells), f32)
            for g in range(groups):
                u += dot(sides_ref[g], map_ref[g, q])
            parts.append(u.astype(bf16))
        ub = jnp.concatenate(parts, 1)
        out += [(dot_nt(prior_ref[q], ub) * scale).astype(bf16) for q in members]
    return out


def sides(z):
    half = z.shape[1] // 2
    return jnp.concatenate([z, jnp.concatenate([z[:, half:], -z[:, :half]], 1)], 0).T


def step_kernel(stage, n_pred, place_ref, scale_ref, map_ref, prior_ref, obs_ref, noise_ref, *refs):
    groups, quads, double, _ = map_ref.shape
    sensors = double // 2
    preds, refs = refs[:n_pred], refs[n_pred:]
    if stage > 0:
        next_ref, refs = refs[0], refs[1:]
    outs, sides_ref = refs[:-1], refs[-1]
    for g in range(groups):
        obs = obs_ref[g].astype(f32)
        now = relax_step * obs
        if stage > 0:
            predicted = sum(p[g].astype(f32) for p in preds)
            now = now + relax_step * (obs - predicted - noise_ref[g] * now)
            next_ref[g] = now
        sides_ref[g] = sides(now.astype(bf16))
    sources = source(map_ref, sides_ref, prior_ref, scale_ref[0])
    turned = [jnp.concatenate([-v[:, HALF:], v[:, :HALF]], 1) for v in sources]
    for e in reversed(range(groups // CORES)):
        for core in range(CORES):
            g = CORES * (place_ref[0] ^ e) + core if stage > 0 else CORES * e + core
            total = jnp.zeros((sensors, LANES), f32)
            for q in range(quads):
                total += dot(map_ref[g, q, :sensors, :], sources[q]) + dot(map_ref[g, q, sensors:, :], turned[q])
            if stage > 0:
                outs[e][core] = total.astype(bf16)
            else:
                outs[0][g] = total.astype(bf16)


def last_kernel(e, n_pred, place_ref, noise_ref, *refs):
    obs, held, refs = refs[:STREAMS], refs[STREAMS:2 * STREAMS], refs[2 * STREAMS:]
    preds, (keep_ref, give_ref) = refs[:STREAMS * n_pred], refs[STREAMS * n_pred:]
    for out, core in ((give_ref, 1 - place_ref[2]), (keep_ref, place_ref[2])):
        g = CORES * (place_ref[0] ^ e) + core
        parts = []
        for s in range(STREAMS):
            now = held[s][g]
            predicted = sum(p[core].astype(f32) for p in preds[s * n_pred:(s + 1) * n_pred])
            parts.append(now + relax_step * (obs[s][g].astype(f32) - predicted - noise_ref[g] * now))
        out[:, :LANES] = jnp.concatenate([p[:, :HALF] for p in parts], 1).astype(bf16)
        out[:, LANES:] = jnp.concatenate([p[:, HALF:] for p in parts], 1).astype(bf16)


def send_kernel(place_ref, keep_ref, got_ref, out_ref):
    out_ref[place_ref[2]] = keep_ref[...]
    out_ref[1 - place_ref[2]] = got_ref[...]


def post_kernel(pairs, place_ref, scale_ref, map_ref, prior_ref, *refs):
    keeps, gives, refs = refs[:pairs], refs[pairs:2 * pairs], refs[2 * pairs + 1:]
    outs, (sides_ref, held_ref) = refs[:-2], refs[-2:]
    for e in range(pairs):
        first = CORES * (place_ref[0] ^ e)
        sides_ref[first + place_ref[2]] = sides(keeps[e][...])
        sides_ref[first + 1 - place_ref[2]] = sides(gives[e][...])
    for q, v in enumerate(source(map_ref, sides_ref, prior_ref, scale_ref[0])):
        held_ref[q] = v
    for d, out in enumerate(outs):
        out[...] = held_ref[place_ref[1] ^ d]


def end_kernel(chips, quads, place_ref, *refs):
    duals, posts, (dual_ref, post_ref) = refs[:chips], refs[chips:chips + quads], refs[chips + quads:]
    pair, quad = place_ref[0], place_ref[1]
    cells = post_ref.shape[1] // 2
    for chip in range(chips):
        e, d = divmod(chip, quads)
        for core in range(CORES):
            freq = (CORES * (pair ^ e) + core) * quads + (quad ^ d)
            dual_ref[freq, 0] = duals[chip][core, :, :LANES].astype(f32)
            dual_ref[freq, 1] = duals[chip][core, :, LANES:].astype(f32)
    for d in range(quads):
        post_ref[quad ^ d, pl.ds(0, cells, stride=2), :] = posts[d][:, :LANES].astype(f32)
        post_ref[quad ^ d, pl.ds(1, cells, stride=2), :] = posts[d][:, LANES:].astype(f32)


def on_device(forward_map, observed, noise_var, prior_rows, prior_scale):
    frequencies, halves, sensors, cells = forward_map.shape
    groups, quads, sides = (lax.axis_size(a) for a in ("sensor", "quad", "side"))
    width = prior_rows.shape[1]
    pairs = groups // CORES
    me, quad = lax.axis_index("sensor"), lax.axis_index("quad")
    place = jnp.stack([me // CORES, quad, me % CORES]).astype(jnp.int32)
    scale = lax.dynamic_slice_in_dim(prior_scale, me * quads + quad, 1, 0)
    both = ("sensor", "quad")

    held = lax.all_to_all(
        forward_map.reshape(frequencies, halves * sensors, cells), both, split_axis=0, concat_axis=0, tiled=True
    ).reshape(groups, quads, halves * sensors, cells)

    data = call(
        functools.partial(data_kernel, groups, quads),
        [SMEM, ANY, VMEM],
        [shape((sensors + 16, STREAMS * LANES), bf16)] * groups,
        [pltpu.VMEM((groups, halves, sensors, LANES), f32), pltpu.SemaphoreType.DMA((groups,))],
        moved=groups * sensors * LANES * 12,
    )(place, observed, noise_var.reshape(1, sensors))
    data = [data[0]] + [swap(data[d], "sensor", d) for d in range(1, groups)]
    diagonal = lax.dynamic_slice_in_dim(prior_rows, quad % 2 * cells, cells, 1)
    came = [swap(diagonal if d % 2 else prior_rows, "quad", d) for d in range(1, quads)]
    prior, noise, *streams = call(
        functools.partial(gather_kernel, groups, quads),
        [SMEM] + [VMEM] * (quads + groups),
        [shape((quads, cells, width), bf16), shape((groups, sensors, LANES), f32)]
        + [shape((groups, sensors, LANES), bf16)] * STREAMS,
        moved=8 * 2**20,
    )(place, prior_rows, *came, *data)

    def over_sides(partial):
        if sides == 2:
            return [partial, swap(partial, "side", 1)]
        return [lax.psum(partial, "side")]

    wide, narrow = shape((groups, sensors, LANES), f32), shape((groups, sensors, LANES), bf16)
    couple, full = shape((CORES, sensors, LANES), bf16), shape((sensors, 2 * LANES), bf16)

    def step(stage, obs, preds):
        operands = [place, scale, held, prior, obs, noise] + preds
        return call(
            functools.partial(step_kernel, stage, len(preds)),
            [SMEM, SMEM] + [VMEM] * (len(operands) - 2),
            [wide] + [couple] * pairs if stage > 0 else [narrow],
            [pltpu.VMEM((groups, LANES, halves * sensors), bf16)],
            flops=2**31,
            moved=8 * 2**20,
        )(*operands)

    first = [over_sides(step(0, streams[s], [])[0]) for s in range(STREAMS)]
    multiplier, partials = [], []
    for s in range(STREAMS):
        out, *parts = step(1, streams[s], first[s])
        multiplier.append(out)
        partials.append(parts)
    keeps, gives, duals = [None] * pairs, [None] * pairs, {}
    for e in reversed(range(pairs)):
        preds = [over_sides(partials[s][e]) for s in range(STREAMS)]
        count = len(preds[0])
        keeps[e], gives[e] = call(
            functools.partial(last_kernel, e, count),
            [SMEM] + [VMEM] * (1 + STREAMS * (2 + count)),
            [full, full],
            moved=2 * 2**20,
        )(place, noise, *streams, *multiplier, *[p for pair in preds for p in pair])
        message = call(
            send_kernel,
            [SMEM, VMEM, VMEM],
            [shape((CORES, sensors, 2 * LANES), bf16)],
            moved=2**20,
        )(place, keeps[e], swap(gives[e], "sensor", 1))[0]
        for d in reversed(range(quads)):
            away = e * quads + d
            duals[away] = swap(message, both, CORES * e * quads + d) if away else message
    post = call(
        functools.partial(post_kernel, pairs),
        [SMEM, SMEM] + [VMEM] * (2 + 2 * pairs) + [ANY],
        [shape((cells, 2 * LANES), bf16)] * quads,
        [pltpu.VMEM((groups, 2 * LANES, halves * sensors), bf16), pltpu.VMEM((quads, cells, 2 * LANES), bf16)],
        flops=2**31,
        moved=8 * 2**20,
    )(place, scale, held, prior, *keeps, *gives, duals[(pairs - 1) * quads])
    post = [post[0]] + [swap(post[d], "quad", d) for d in range(1, quads)]
    dual, posterior = call(
        functools.partial(end_kernel, pairs * quads, quads),
        [SMEM] + [VMEM] * (pairs * quads + quads),
        [shape((frequencies, halves, sensors, LANES), f32), shape((quads, cells * 2, LANES), f32)],
        moved=8 * 2**20,
    )(place, *[duals[i] for i in range(pairs * quads)], *post)
    return dual, posterior.reshape(quads, cells, 2, LANES)


def solution(mesh):
    groups, space = mesh.devices.shape

    def run(forward_map, observed, noise_var, prior_rows, prior_scale):
        quads = forward_map.shape[0] // groups
        split = Mesh(mesh.devices.reshape(groups, space // quads, quads), ("sensor", "side", "quad"))
        return jax.shard_map(
            on_device,
            mesh=split,
            in_specs=(
                P(None, None, "sensor", ("side", "quad")),
                P(None, None, "sensor", None),
                P("sensor"),
                P(("side", "quad"), None),
                P(),
            ),
            out_specs=(P(None, None, "sensor", None), P("sensor", ("side", "quad"), None, None)),
            check_vma=False,
        )(forward_map, observed, noise_var, prior_rows, prior_scale)

    return run
```

time: 182 us -> 167 us (0.918)
  waiting for transfers between devices: 97.9 us -> 91 us
  Pallas kernels: 40.9 us -> 35.3 us
    ppermute x29 -> x24, waiting for transfers between devices: 97.9 us -> 91 us  [swap(): return lax.ppermute(x, axes, [(i, i ^ distance) for i in range(count)])]
    pallas_call x9 -> x10, Pallas kernels: 38.9 us -> 33.2 us  [the longest x4 22.4 us: step(): call(functools.partial(step_kernel, stage, len(preds)), [SMEM, SMEM] + [V...]
    unnamed x12 -> x8, local copies, waits for them, and re-layouts: 3.85 us -> 2.2 us
    ppermute x29 -> x24, starting transfers between devices: 31 us -> 30.3 us  [swap(): return lax.ppermute(x, axes, [(i, i ^ distance) for i in range(count)])]
  transfers between devices with their start and end apart: 30 -> 25, of which waited for: 16 -> 11; matrix products, arithmetic and copies ran while one was open for 0% -> 0% of each run, Pallas kernels for 17% -> 15%
where the time goes in v5:
time: 167 us
  waiting for transfers between devices  91 us (54%)
  starting transfers between devices  36.8 us (22%)
  Pallas kernels  35.3 us (21%)
  local copies, waits for them, and re-layouts  2.8 us (2%)
    ppermute x24, waiting for transfers between devices, swap(): return lax.ppermute(x, axes, [(i, i ^ distance) for i in range(count)])  91 us
    ppermute x24, starting transfers between devices, swap(): return lax.ppermute(x, axes, [(i, i ^ distance) for i in range(count)])  30.3 us
    pallas_call x4, Pallas kernels, step(): call(functools.partial(step_kernel, stage, len(preds)), [SMEM, SMEM] + [V...  22.4 us
    all_to_all x1, starting transfers between devices, on_device(): lax.all_to_all(forward_map.reshape(frequencies, halves * sensors, cells),...  6.48 us
    pallas_call x1, Pallas kernels, on_device(): call(functools.partial(post_kernel, pairs), [SMEM, SMEM] + [VMEM] * (2 +...  4.88 us
  transfers between devices with their start and end apart: 25, of which 11 were waited for; matrix products, arithmetic and copies ran while one was open for 0% of the time, Pallas kernels for 15%

profile of v5, /device:TPU:0, one launch (start us, length us, event | category | flops | bytes accessed | tf_op | source)
XLA Modules:
  0.0 166.8 jit_solution(9623142059555720206)
XLA Ops:
  0.6 6.5 %all-to-all-start = ((bf16[16,512,256]{2,1,0:T(8,128)(2,1)}), bf16[16,512,256]{2,1,0:T(8,128)(2,1)}, u32[]{:S(2)}, u32[]{:S(2)}) async-start(bf16[16,512,256]{2,1,0:T(8,128)(2,1)} %bitcast.8), calls=%async_computation | async-start | bytes 8388608 | tf_op jit(solution)/shard_map/all_to_all | solution.py:203
  7.2 2.8 %collective-permute-start.2 = (bf16[256,256]{1,0:T(8,128)(2,1)S(1)}, bf16[256,256]{1,0:T(8,128)(2,1)S(1)}, u32[]{:S(2)}, u32[]{:S(2)}) collective-permute-start(bf16[256,256]{1,0:T(8,128)(2,1)S(1)} %constant_dynamic-slice_fusion), channel_id=1, source_target_pairs={{0,3},{1,2},{2,1},{3,0},{4,7},{5,6},{6,5},{7,4},{8,11},{9,10},{10,... | collective-permute-start | bytes 393224 | tf_op jit(solution)/shard_map/ppermute | solution.py:41
  10.7 2.2 %copy-done = f32[16,2,256,128]{3,2,1,0:T(8,128)S(1)} copy-done((f32[16,2,256,128]{3,2,1,0:T(8,128)S(1)}, f32[16,2,256,128]{3,2,1,0:T(8,128)}, u32[]{:S(2)}) %copy-start) | copy-done | bytes 4194328
  12.9 1.1 shard_map.68
  14.1 1.5 collective-permute-start.4
  15.9 50.4 %collective-permute-done.2.refs_2_ = bf16[256,256]{1,0:T(8,128)(2,1)S(1)} collective-permute-done((bf16[256,256]{1,0:T(8,128)(2,1)S(1)}, bf16[256,256]{1,0:T(8,128)(2,1)S(1)}, u32[]{:S(2)}, u32[]{:S(2)}) %collective-permute-start.2) | collective-permute-done | bytes 131104 | tf_op jit(solution)/shard_map/ppermute | solution.py:41
  67.5 3.8 %collective-permute-done.refs_0_ = bf16[256,256]{1,0:T(8,128)(2,1)S(1)} collective-permute-done((bf16[256,256]{1,0:T(8,128)(2,1)S(1)}, bf16[256,256]{1,0:T(8,128)(2,1)S(1)}, u32[]{:S(2)}, u32[]{:S(2)}) %collective-permute-start) | collective-permute-done | bytes 131104 | tf_op jit(solution)/shard_map/ppermute | solution.py:41
  72.3 5.6 %shard_map.72.refs_0_ = bf16[4,256,128]{2,1,0:T(8,128)(2,1)S(1)} custom-call(s32[3]{0:T(128)S(1)} %pad_add_fusion.place_ref, f32[1]{0:T(128)} %dynamic_slice.7.scale_ref, bf16[4,4,512,256]{3,2,1,0:T(8,128)(2,1)} %bitcast.5.map_ref, bf16[4,256,512]{2,1,0:T(8,128)(2,1)S(1)} %get-tuple-element.33.prior_ref, ...), custom_call_target="tpu_custom_call" | custom-call | flops 2147483648 | bytes 8388608 | tf_op jit(solution)/shard_map/pallas_call | solution.py:235
  77.9 2.7 %collective-permute-start.7 = (bf16[4,256,128]{2,1,0:T(8,128)(2,1)S(1)}, bf16[4,256,128]{2,1,0:T(8,128)(2,1)S(1)}, u32[]{:S(2)}, u32[]{:S(2)}) collective-permute-start(bf16[4,256,128]{2,1,0:T(8,128)(2,1)S(1)} %shard_map.72.refs_0_), channel_id=1, source_target_pairs={{0,4},{4,0},{1,5},{5,1},{2,6},{6,2},{3,7},{7,3},{8,12},{12,8},{9,1... | collective-permute-start | bytes 786440 | tf_op jit(solution)/shard_map/ppermute | solution.py:41
  80.5 5.6 %shard_map.70.refs_0_ = bf16[4,256,128]{2,1,0:T(8,128)(2,1)S(1)} custom-call(s32[3]{0:T(128)S(1)} %pad_add_fusion.place_ref, f32[1]{0:T(128)} %dynamic_slice.7.scale_ref, bf16[4,4,512,256]{3,2,1,0:T(8,128)(2,1)} %bitcast.5.map_ref, bf16[4,256,512]{2,1,0:T(8,128)(2,1)S(1)} %get-tuple-element.33.prior_ref, ...), custom_call_target="tpu_custom_call" | custom-call | flops 2147483648 | bytes 8388608 | tf_op jit(solution)/shard_map/pallas_call | solution.py:235
  86.5 10.3 %collective-permute-done.7.refs_1_ = bf16[4,256,128]{2,1,0:T(8,128)(2,1)S(1)} collective-permute-done((bf16[4,256,128]{2,1,0:T(8,128)(2,1)S(1)}, bf16[4,256,128]{2,1,0:T(8,128)(2,1)S(1)}, u32[]{:S(2)}, u32[]{:S(2)}) %collective-permute-start.7) | collective-permute-done | bytes 262176 | tf_op jit(solution)/shard_map/ppermute | solution.py:41
  96.9 5.6 %shard_map.73 = (f32[4,256,128]{2,1,0:T(8,128)S(1)}, bf16[2,256,128]{2,1,0:T(8,128)(2,1)S(1)}, bf16[2,256,128]{2,1,0:T(8,128)(2,1)S(1)}) custom-call(s32[3]{0:T(128)S(1)} %pad_add_fusion.place_ref, f32[1]{0:T(128)} %dynamic_slice.7.scale_ref, bf16[4,4,512,256]{3,2,1,0:T(8,128)(2,1)} %bitcast.5.map_ref, bf16[4,256,512]{2,1,0:T(8,128)(2,1)S(1)} %get-tuple-element.33.prior_ref, ...), custom_call_target="tpu_custom_call" | custom-call | flops 2147483648 | bytes 8388608 | tf_op jit(solution)/shard_map/pallas_call | solution.py:235
  102.6 5.6 %shard_map.71 = (f32[4,256,128]{2,1,0:T(8,128)S(1)}, bf16[2,256,128]{2,1,0:T(8,128)(2,1)S(1)}, bf16[2,256,128]{2,1,0:T(8,128)(2,1)S(1)}) custom-call(s32[3]{0:T(128)S(1)} %pad_add_fusion.place_ref, f32[1]{0:T(128)} %dynamic_slice.7.scale_ref, bf16[4,4,512,256]{3,2,1,0:T(8,128)(2,1)} %bitcast.5.map_ref, bf16[4,256,512]{2,1,0:T(8,128)(2,1)S(1)} %get-tuple-element.33.prior_ref, ...), custom_call_target="tpu_custom_call" | custom-call | flops 2147483648 | bytes 8388608 | tf_op jit(solution)/shard_map/pallas_call | solution.py:235
  108.2 3.0 %collective-permute-start.14 = (bf16[2,256,128]{2,1,0:T(8,128)(2,1)S(1)}, bf16[2,256,128]{2,1,0:T(8,128)(2,1)S(1)}, u32[]{:S(2)}, u32[]{:S(2)}) collective-permute-start(bf16[2,256,128]{2,1,0:T(8,128)(2,1)S(1)} %get-tuple-element.40.refs_4_), channel_id=1, source_target_pairs={{0,4},{4,0},{1,5},{5,1},{2,6},{6,2},{3,7},{7,3},{8,12},{12,8},{9,1... | collective-permute-start | bytes 393224 | tf_op jit(solution)/shard_map/ppermute | solution.py:41
  111.2 4.6 %collective-permute-done.14.refs_5_ = bf16[2,256,128]{2,1,0:T(8,128)(2,1)S(1)} collective-permute-done((bf16[2,256,128]{2,1,0:T(8,128)(2,1)S(1)}, bf16[2,256,128]{2,1,0:T(8,128)(2,1)S(1)}, u32[]{:S(2)}, u32[]{:S(2)}) %collective-permute-start.14) | collective-permute-done | bytes 131104 | tf_op jit(solution)/shard_map/ppermute | solution.py:41
  116.6 1.4 collective-permute-start.9
  118.0 1.6 collective-permute-start.8
  120.2 3.7 %collective-permute-start.20 = (bf16[2,256,256]{2,1,0:T(8,128)(2,1)S(1)}, bf16[2,256,256]{2,1,0:T(8,128)(2,1)S(1)}, u32[]{:S(2)}, u32[]{:S(2)}) collective-permute-start(bf16[2,256,256]{2,1,0:T(8,128)(2,1)S(1)} %shard_map.77), channel_id=1, source_target_pairs={{0,19},{1,18},{2,17},{3,16},{8,27},{9,26},{10,25},{11,24},{16,3},{... | collective-permute-start | bytes 786440 | tf_op jit(solution)/shard_map/ppermute | solution.py:41
  124.9 4.6 %collective-permute-done.9.refs_7_ = bf16[2,256,128]{2,1,0:T(8,128)(2,1)S(1)} collective-permute-done((bf16[2,256,128]{2,1,0:T(8,128)(2,1)S(1)}, bf16[2,256,128]{2,1,0:T(8,128)(2,1)S(1)}, u32[]{:S(2)}, u32[]{:S(2)}) %collective-permute-start.9) | collective-permute-done | bytes 131104 | tf_op jit(solution)/shard_map/ppermute | solution.py:41
  129.6 2.4 %collective-permute-done.8.refs_5_ = bf16[2,256,128]{2,1,0:T(8,128)(2,1)S(1)} collective-permute-done((bf16[2,256,128]{2,1,0:T(8,128)(2,1)S(1)}, bf16[2,256,128]{2,1,0:T(8,128)(2,1)S(1)}, u32[]{:S(2)}, u32[]{:S(2)}) %collective-permute-start.8) | collective-permute-done | bytes 131104 | tf_op jit(solution)/shard_map/ppermute | solution.py:41
  132.9 2.1 %collective-permute-start.18 = (bf16[2,256,256]{2,1,0:T(8,128)(2,1)S(1)}, bf16[2,256,256]{2,1,0:T(8,128)(2,1)S(1)}, u32[]{:S(2)}, u32[]{:S(2)}) collective-permute-start(bf16[2,256,256]{2,1,0:T(8,128)(2,1)S(1)} %shard_map.77), channel_id=1, source_target_pairs={{0,17},{1,16},{2,19},{3,18},{8,25},{9,24},{10,27},{11,26},{16,1},{... | collective-permute-start | bytes 786440 | tf_op jit(solution)/shard_map/ppermute | solution.py:41
  135.6 2.3 %collective-permute-start.13 = (bf16[2,256,256]{2,1,0:T(8,128)(2,1)S(1)}, bf16[2,256,256]{2,1,0:T(8,128)(2,1)S(1)}, u32[]{:S(2)}, u32[]{:S(2)}) collective-permute-start(bf16[2,256,256]{2,1,0:T(8,128)(2,1)S(1)} %shard_map.75.refs_0_), channel_id=1, source_target_pairs={{0,3},{1,2},{2,1},{3,0},{8,11},{9,10},{10,9},{11,8},{16,19},{17,18... | collective-permute-start | bytes 786440 | tf_op jit(solution)/shard_map/ppermute | solution.py:41
  138.1 1.4 collective-permute-start.11
  139.6 4.9 %shard_map.78 = (bf16[256,256]{1,0:T(8,128)(2,1)S(1)}, bf16[256,256]{1,0:T(8,128)(2,1)S(1)}, bf16[256,256]{1,0:T(8,128)(2,1)S(1)}, bf16[256,256]{1,0:T(8,128)(2,1)S(1)}) custom-call(s32[3]{0:T(128)S(1)} %pad_add_fusion.place_ref, f32[1]{0:T(128)} %dynamic_slice.7.scale_ref, bf16[4,4,512,256]{3,2,1,0:T(8,128)(2,1)} %bitcast.5.map_ref, ...), custom_call_target="tpu_custom_call" | custom-call | flops 2147483648 | bytes 8388608 | tf_op jit(solution)/shard_map/pallas_call | solution.py:269
  145.1 7.4 %collective-permute-done.18.refs_5_ = bf16[2,256,256]{2,1,0:T(8,128)(2,1)S(1)} collective-permute-done((bf16[2,256,256]{2,1,0:T(8,128)(2,1)S(1)}, bf16[2,256,256]{2,1,0:T(8,128)(2,1)S(1)}, u32[]{:S(2)}, u32[]{:S(2)}) %collective-permute-start.18) | collective-permute-done | bytes 262176 | tf_op jit(solution)/shard_map/ppermute | solution.py:41
  152.5 1.6 collective-permute-start.22
  154.1 2.0 %collective-permute-start.23 = (bf16[256,256]{1,0:T(8,128)(2,1)S(1)}, bf16[256,256]{1,0:T(8,128)(2,1)S(1)}, u32[]{:S(2)}, u32[]{:S(2)}) collective-permute-start(bf16[256,256]{1,0:T(8,128)(2,1)S(1)} %get-tuple-element.47), channel_id=1, source_target_pairs={{0,3},{1,2},{2,1},{3,0},{4,7},{5,6},{6,5},{7,4},{8,11},{9,10},{10,... | collective-permute-start | bytes 393224 | tf_op jit(solution)/shard_map/ppermute | solution.py:41
  156.1 1.5 collective-permute-done.12.refs_2_
  157.7 1.3 collective-permute-done.21.refs_9_
  159.0 1.5 collective-permute-done.22.refs_10_
  160.5 3.1 %collective-permute-done.23.refs_11_ = bf16[256,256]{1,0:T(8,128)(2,1)S(1)} collective-permute-done((bf16[256,256]{1,0:T(8,128)(2,1)S(1)}, bf16[256,256]{1,0:T(8,128)(2,1)S(1)}, u32[]{:S(2)}, u32[]{:S(2)}) %collective-permute-start.23) | collective-permute-done | bytes 131104 | tf_op jit(solution)/shard_map/ppermute | solution.py:41
  163.6 3.2 %shard_map.79 = (f32[16,2,256,128]{3,2,1,0:T(8,128)}, f32[4,512,128]{2,1,0:T(8,128)}) custom-call(s32[3]{0:T(128)S(1)} %pad_add_fusion.place_ref, bf16[2,256,256]{2,1,0:T(8,128)(2,1)S(1)} %shard_map.75.refs_0_, bf16[2,256,256]{2,1,0:T(8,128)(2,1)S(1)} %collective-permute-done.11.refs_1_, bf16[2,256,256]{2,1,0:T(8,128)(2,1)S(1)} %collective-permute-done.12.refs_2_, ...), custom_call_target="tpu_custom_call" | custom-call | bytes 8388608 | tf_op jit(solution)/shard_map/pallas_call | solution.py:278
  (41 shorter events, 8.4 us)
Async XLA Ops:
  0.6 6.5 %copy-start.1 = (bf16[256,512]{1,0:T(8,128)(2,1)S(1)}, bf16[256,512]{1,0:T(8,128)(2,1)}, u32[]{:S(2)}) copy-start(bf16[256,512]{1,0:T(8,128)(2,1)} %own_ref.1) | copy-start | bytes 786436
  0.6 10.0 %copy-start.2 = (f32[256]{0:T(256)S(1)}, f32[256]{0:T(256)}, u32[]{:S(2)}) copy-start(f32[256]{0:T(256)} %param.7) | copy-start | bytes 3076
  0.6 71.6 %all-to-all-start = ((bf16[16,512,256]{2,1,0:T(8,128)(2,1)}), bf16[16,512,256]{2,1,0:T(8,128)(2,1)}, u32[]{:S(2)}, u32[]{:S(2)}) async-start(bf16[16,512,256]{2,1,0:T(8,128)(2,1)} %bitcast.8), calls=%async_computation | async-start | bytes 8388608 | tf_op jit(solution)/shard_map/all_to_all | solution.py:203
  7.1 59.8 %copy-start.3 = (f32[16]{0:T(128)S(1)}, f32[16]{0:T(128)}, u32[]{:S(2)}) copy-start(f32[16]{0:T(128)} %param.9) | copy-start | bytes 196
  7.2 59.1 %collective-permute-start.2 = (bf16[256,256]{1,0:T(8,128)(2,1)S(1)}, bf16[256,256]{1,0:T(8,128)(2,1)S(1)}, u32[]{:S(2)}, u32[]{:S(2)}) collective-permute-start(bf16[256,256]{1,0:T(8,128)(2,1)S(1)} %constant_dynamic-slice_fusion), channel_id=1, source_target_pairs={{0,3},{1,2},{2,1},{3,0},{4,7},{5,6},{6,5},{7,4},{8,11},{9,10},{10,... | collective-permute-start | bytes 393224 | tf_op jit(solution)/shard_map/ppermute | solution.py:41
  10.0 61.3 %collective-permute-start.1 = (bf16[256,512]{1,0:T(8,128)(2,1)S(1)}, bf16[256,512]{1,0:T(8,128)(2,1)S(1)}, u32[]{:S(2)}, u32[]{:S(2)}) collective-permute-start(bf16[256,512]{1,0:T(8,128)(2,1)S(1)} %copy-done.1), channel_id=1, source_target_pairs={{0,2},{1,3},{2,0},{3,1},{4,6},{5,7},{6,4},{7,5},{8,10},{9,11},{10,... | collective-permute-start | bytes 786440 | tf_op jit(solution)/shard_map/ppermute | solution.py:41
  10.7 2.2 %copy-start = (f32[16,2,256,128]{3,2,1,0:T(8,128)S(1)}, f32[16,2,256,128]{3,2,1,0:T(8,128)}, u32[]{:S(2)}) copy-start(f32[16,2,256,128]{3,2,1,0:T(8,128)} %obs_ref.1) | copy-start | bytes 12582916
  14.0 57.3 %collective-permute-start.3 = (bf16[272,256]{1,0:T(8,128)(2,1)S(1)}, bf16[272,256]{1,0:T(8,128)(2,1)S(1)}, u32[]{:S(2)}, u32[]{:S(2)}) collective-permute-start(bf16[272,256]{1,0:T(8,128)(2,1)S(1)} %get-tuple-element.27), channel_id=1, source_target_pairs={{0,8},{8,0},{16,24},{24,16},{1,9},{9,1},{17,25},{25,17},{2,10},{10... | collective-permute-start | bytes 417800 | tf_op jit(solution)/shard_map/ppermute | solution.py:41
  14.1 57.2 %collective-permute-start.4 = (bf16[272,256]{1,0:T(8,128)(2,1)S(1)}, bf16[272,256]{1,0:T(8,128)(2,1)S(1)}, u32[]{:S(2)}, u32[]{:S(2)}) collective-permute-start(bf16[272,256]{1,0:T(8,128)(2,1)S(1)} %get-tuple-element.28), channel_id=1, source_target_pairs={{0,16},{8,24},{16,0},{24,8},{1,17},{9,25},{17,1},{25,9},{2,18},{10... | collective-permute-start | bytes 417800 | tf_op jit(solution)/shard_map/ppermute | solution.py:41
  15.6 55.7 %collective-permute-start.5 = (bf16[272,256]{1,0:T(8,128)(2,1)S(1)}, bf16[272,256]{1,0:T(8,128)(2,1)S(1)}, u32[]{:S(2)}, u32[]{:S(2)}) collective-permute-start(bf16[272,256]{1,0:T(8,128)(2,1)S(1)} %get-tuple-element.29), channel_id=1, source_target_pairs={{0,24},{8,16},{16,8},{24,0},{1,25},{9,17},{17,9},{25,1},{2,26},{10... | collective-permute-start | bytes 417800 | tf_op jit(solution)/shard_map/ppermute | solution.py:41
  66.3 5.0 %collective-permute-start = (bf16[256,256]{1,0:T(8,128)(2,1)S(1)}, bf16[256,256]{1,0:T(8,128)(2,1)S(1)}, u32[]{:S(2)}, u32[]{:S(2)}) collective-permute-start(bf16[256,256]{1,0:T(8,128)(2,1)S(1)} %constant_dynamic-slice_fusion), channel_id=1, source_target_pairs={{0,1},{1,0},{2,3},{3,2},{4,5},{5,4},{6,7},{7,6},{8,9},{9,8},{10,11... | collective-permute-start | bytes 393224 | tf_op jit(solution)/shard_map/ppermute | solution.py:41
  77.9 19.0 %collective-permute-start.7 = (bf16[4,256,128]{2,1,0:T(8,128)(2,1)S(1)}, bf16[4,256,128]{2,1,0:T(8,128)(2,1)S(1)}, u32[]{:S(2)}, u32[]{:S(2)}) collective-permute-start(bf16[4,256,128]{2,1,0:T(8,128)(2,1)S(1)} %shard_map.72.refs_0_), channel_id=1, source_target_pairs={{0,4},{4,0},{1,5},{5,1},{2,6},{6,2},{3,7},{7,3},{8,12},{12,8},{9,1... | collective-permute-start | bytes 786440 | tf_op jit(solution)/shard_map/ppermute | solution.py:41
  86.1 16.4 %collective-permute-start.6 = (bf16[4,256,128]{2,1,0:T(8,128)(2,1)S(1)}, bf16[4,256,128]{2,1,0:T(8,128)(2,1)S(1)}, u32[]{:S(2)}, u32[]{:S(2)}) collective-permute-start(bf16[4,256,128]{2,1,0:T(8,128)(2,1)S(1)} %shard_map.70.refs_0_), channel_id=1, source_target_pairs={{0,4},{4,0},{1,5},{5,1},{2,6},{6,2},{3,7},{7,3},{8,12},{12,8},{9,1... | collective-permute-start | bytes 786440 | tf_op jit(solution)/shard_map/ppermute | solution.py:41
  102.5 8.7 %collective-permute-start.15 = (bf16[2,256,128]{2,1,0:T(8,128)(2,1)S(1)}, bf16[2,256,128]{2,1,0:T(8,128)(2,1)S(1)}, u32[]{:S(2)}, u32[]{:S(2)}) collective-permute-start(bf16[2,256,128]{2,1,0:T(8,128)(2,1)S(1)} %get-tuple-element.41.refs_6_), channel_id=1, source_target_pairs={{0,4},{4,0},{1,5},{5,1},{2,6},{6,2},{3,7},{7,3},{8,12},{12,8},{9,1... | collective-permute-start | bytes 393224 | tf_op jit(solution)/shard_map/ppermute | solution.py:41
  108.2 7.5 %collective-permute-start.14 = (bf16[2,256,128]{2,1,0:T(8,128)(2,1)S(1)}, bf16[2,256,128]{2,1,0:T(8,128)(2,1)S(1)}, u32[]{:S(2)}, u32[]{:S(2)}) collective-permute-start(bf16[2,256,128]{2,1,0:T(8,128)(2,1)S(1)} %get-tuple-element.40.refs_4_), channel_id=1, source_target_pairs={{0,4},{4,0},{1,5},{5,1},{2,6},{6,2},{3,7},{7,3},{8,12},{12,8},{9,1... | collective-permute-start | bytes 393224 | tf_op jit(solution)/shard_map/ppermute | solution.py:41
  116.5 3.1 %collective-permute-start.16 = (bf16[256,256]{1,0:T(8,128)(2,1)S(1)}, bf16[256,256]{1,0:T(8,128)(2,1)S(1)}, u32[]{:S(2)}, u32[]{:S(2)}) collective-permute-start(bf16[256,256]{1,0:T(8,128)(2,1)S(1)} %get-tuple-element.43.refs_3_), channel_id=1, source_target_pairs={{0,8},{8,0},{16,24},{24,16},{1,9},{9,1},{17,25},{25,17},{2,10},{10... | collective-permute-start | bytes 393224 | tf_op jit(solution)/shard_map/ppermute | solution.py:41
  116.6 13.0 %collective-permute-start.9 = (bf16[2,256,128]{2,1,0:T(8,128)(2,1)S(1)}, bf16[2,256,128]{2,1,0:T(8,128)(2,1)S(1)}, u32[]{:S(2)}, u32[]{:S(2)}) collective-permute-start(bf16[2,256,128]{2,1,0:T(8,128)(2,1)S(1)} %get-tuple-element.37.refs_6_), channel_id=1, source_target_pairs={{0,4},{4,0},{1,5},{5,1},{2,6},{6,2},{3,7},{7,3},{8,12},{12,8},{9,1... | collective-permute-start | bytes 393224 | tf_op jit(solution)/shard_map/ppermute | solution.py:41
  118.0 14.0 %collective-permute-start.8 = (bf16[2,256,128]{2,1,0:T(8,128)(2,1)S(1)}, bf16[2,256,128]{2,1,0:T(8,128)(2,1)S(1)}, u32[]{:S(2)}, u32[]{:S(2)}) collective-permute-start(bf16[2,256,128]{2,1,0:T(8,128)(2,1)S(1)} %get-tuple-element.36.refs_4_), channel_id=1, source_target_pairs={{0,4},{4,0},{1,5},{5,1},{2,6},{6,2},{3,7},{7,3},{8,12},{12,8},{9,1... | collective-permute-start | bytes 393224 | tf_op jit(solution)/shard_map/ppermute | solution.py:41
  120.2 17.7 %collective-permute-start.20 = (bf16[2,256,256]{2,1,0:T(8,128)(2,1)S(1)}, bf16[2,256,256]{2,1,0:T(8,128)(2,1)S(1)}, u32[]{:S(2)}, u32[]{:S(2)}) collective-permute-start(bf16[2,256,256]{2,1,0:T(8,128)(2,1)S(1)} %shard_map.77), channel_id=1, source_target_pairs={{0,19},{1,18},{2,17},{3,16},{8,27},{9,26},{10,25},{11,24},{16,3},{... | collective-permute-start | bytes 786440 | tf_op jit(solution)/shard_map/ppermute | solution.py:41
  123.9 14.2 %collective-permute-start.17 = (bf16[2,256,256]{2,1,0:T(8,128)(2,1)S(1)}, bf16[2,256,256]{2,1,0:T(8,128)(2,1)S(1)}, u32[]{:S(2)}, u32[]{:S(2)}) collective-permute-start(bf16[2,256,256]{2,1,0:T(8,128)(2,1)S(1)} %shard_map.77), channel_id=1, source_target_pairs={{0,16},{1,17},{2,18},{3,19},{8,24},{9,25},{10,26},{11,27},{16,0},{... | collective-permute-start | bytes 786440 | tf_op jit(solution)/shard_map/ppermute | solution.py:41
  132.7 2.3 %collective-permute-start.10 = (bf16[256,256]{1,0:T(8,128)(2,1)S(1)}, bf16[256,256]{1,0:T(8,128)(2,1)S(1)}, u32[]{:S(2)}, u32[]{:S(2)}) collective-permute-start(bf16[256,256]{1,0:T(8,128)(2,1)S(1)} %get-tuple-element.39.refs_2_), channel_id=1, source_target_pairs={{0,8},{8,0},{16,24},{24,16},{1,9},{9,1},{17,25},{25,17},{2,10},{10... | collective-permute-start | bytes 393224 | tf_op jit(solution)/shard_map/ppermute | solution.py:41
  132.8 11.6 %collective-permute-start.19 = (bf16[2,256,256]{2,1,0:T(8,128)(2,1)S(1)}, bf16[2,256,256]{2,1,0:T(8,128)(2,1)S(1)}, u32[]{:S(2)}, u32[]{:S(2)}) collective-permute-start(bf16[2,256,256]{2,1,0:T(8,128)(2,1)S(1)} %shard_map.77), channel_id=1, source_target_pairs={{0,18},{1,19},{2,16},{3,17},{8,26},{9,27},{10,24},{11,25},{16,2},{... | collective-permute-start | bytes 786440 | tf_op jit(solution)/shard_map/ppermute | solution.py:41
  132.9 19.6 %collective-permute-start.18 = (bf16[2,256,256]{2,1,0:T(8,128)(2,1)S(1)}, bf16[2,256,256]{2,1,0:T(8,128)(2,1)S(1)}, u32[]{:S(2)}, u32[]{:S(2)}) collective-permute-start(bf16[2,256,256]{2,1,0:T(8,128)(2,1)S(1)} %shard_map.77), channel_id=1, source_target_pairs={{0,17},{1,16},{2,19},{3,18},{8,25},{9,24},{10,27},{11,26},{16,1},{... | collective-permute-start | bytes 786440 | tf_op jit(solution)/shard_map/ppermute | solution.py:41
  135.6 18.5 %collective-permute-start.13 = (bf16[2,256,256]{2,1,0:T(8,128)(2,1)S(1)}, bf16[2,256,256]{2,1,0:T(8,128)(2,1)S(1)}, u32[]{:S(2)}, u32[]{:S(2)}) collective-permute-start(bf16[2,256,256]{2,1,0:T(8,128)(2,1)S(1)} %shard_map.75.refs_0_), channel_id=1, source_target_pairs={{0,3},{1,2},{2,1},{3,0},{8,11},{9,10},{10,9},{11,8},{16,19},{17,18... | collective-permute-start | bytes 786440 | tf_op jit(solution)/shard_map/ppermute | solution.py:41
  137.9 19.8 %collective-permute-start.12 = (bf16[2,256,256]{2,1,0:T(8,128)(2,1)S(1)}, bf16[2,256,256]{2,1,0:T(8,128)(2,1)S(1)}, u32[]{:S(2)}, u32[]{:S(2)}) collective-permute-start(bf16[2,256,256]{2,1,0:T(8,128)(2,1)S(1)} %shard_map.75.refs_0_), channel_id=1, source_target_pairs={{0,2},{1,3},{2,0},{3,1},{8,10},{9,11},{10,8},{11,9},{16,18},{17,19... | collective-permute-start | bytes 786440 | tf_op jit(solution)/shard_map/ppermute | solution.py:41
  138.1 19.6 %collective-permute-start.11 = (bf16[2,256,256]{2,1,0:T(8,128)(2,1)S(1)}, bf16[2,256,256]{2,1,0:T(8,128)(2,1)S(1)}, u32[]{:S(2)}, u32[]{:S(2)}) collective-permute-start(bf16[2,256,256]{2,1,0:T(8,128)(2,1)S(1)} %shard_map.75.refs_0_), channel_id=1, source_target_pairs={{0,1},{1,0},{2,3},{3,2},{8,9},{9,8},{10,11},{11,10},{16,17},{17,16... | collective-permute-start | bytes 786440 | tf_op jit(solution)/shard_map/ppermute | solution.py:41
  144.5 14.5 %collective-permute-start.21 = (bf16[256,256]{1,0:T(8,128)(2,1)S(1)}, bf16[256,256]{1,0:T(8,128)(2,1)S(1)}, u32[]{:S(2)}, u32[]{:S(2)}) collective-permute-start(bf16[256,256]{1,0:T(8,128)(2,1)S(1)} %get-tuple-element.45), channel_id=1, source_target_pairs={{0,1},{1,0},{2,3},{3,2},{4,5},{5,4},{6,7},{7,6},{8,9},{9,8},{10,11... | collective-permute-start | bytes 393224 | tf_op jit(solution)/shard_map/ppermute | solution.py:41
  152.5 8.0 %collective-permute-start.22 = (bf16[256,256]{1,0:T(8,128)(2,1)S(1)}, bf16[256,256]{1,0:T(8,128)(2,1)S(1)}, u32[]{:S(2)}, u32[]{:S(2)}) collective-permute-start(bf16[256,256]{1,0:T(8,128)(2,1)S(1)} %get-tuple-element.46), channel_id=1, source_target_pairs={{0,2},{1,3},{2,0},{3,1},{4,6},{5,7},{6,4},{7,5},{8,10},{9,11},{10,... | collective-permute-start | bytes 393224 | tf_op jit(solution)/shard_map/ppermute | solution.py:41
  154.1 9.5 %collective-permute-start.23 = (bf16[256,256]{1,0:T(8,128)(2,1)S(1)}, bf16[256,256]{1,0:T(8,128)(2,1)S(1)}, u32[]{:S(2)}, u32[]{:S(2)}) collective-permute-start(bf16[256,256]{1,0:T(8,128)(2,1)S(1)} %get-tuple-element.47), channel_id=1, source_target_pairs={{0,3},{1,2},{2,1},{3,0},{4,7},{5,6},{6,5},{7,4},{8,11},{9,10},{10,... | collective-permute-start | bytes 393224 | tf_op jit(solution)/shard_map/ppermute | solution.py:41

commit v6 on v5

--- a/solution.py
+++ b/solution.py
@@ -24,11 +24,11 @@
     return jax.ShapeDtypeStruct(dims, dtype)
 
 
-def call(kernel, in_specs, out_shape, scratch=(), flops=0, moved=0):
+def call(kernel, in_specs, out_shape, scratch=(), out_specs=None, flops=0, moved=0):
     return pl.pallas_call(
         kernel,
         in_specs=in_specs,
-        out_specs=[VMEM] * len(out_shape),
+        out_specs=out_specs or [VMEM] * len(out_shape),
         out_shape=out_shape,
         scratch_shapes=list(scratch),
         cost_estimate=pl.CostEstimate(flops=flops, bytes_accessed=moved, transcendentals=0),
@@ -68,6 +68,12 @@
             part = slice(s * HALF, (s + 1) * HALF)
             outs[d][:sensors, s * LANES:(s + 1) * LANES] = jnp.concatenate([re[:, part], im[:, part]], 1).astype(bf16)
         outs[d][sensors:, :] = tail
+
+
+def prior_kernel(place_ref, own_ref, after_ref, full_ref, diagonal_ref):
+    cells = own_ref.shape[0]
+    full_ref[...] = own_ref[...]
+    diagonal_ref[...] = own_ref[:, pl.ds(pl.multiple_of((place_ref[1] & 1) * cells, cells), cells)]
 
 
 def gather_kernel(groups, quads, place_ref, own_ref, *refs):
@@ -92,7 +98,7 @@
         noise_ref[me ^ d] = jnp.broadcast_to(noise, (sensors, LANES))
 
 
-def source(map_ref, sides_ref, prior_ref, scale):
+def source(map_ref, sides_ref, prior_ref, scale, ready=None):
     groups, quads, _, cells = map_ref.shape
     per_block = prior_ref.shape[2] // cells
     out = []
@@ -102,6 +108,8 @@
         for q in members:
             u = jnp.zeros((sides_ref.shape[1], cells), f32)
             for g in range(groups):
+                if ready is not None:
+                    ready(g, q)
                 u += dot(sides_ref[g], map_ref[g, q])
             parts.append(u.astype(bf16))
         ub = jnp.concatenate(parts, 1)
@@ -114,9 +122,18 @@
     return jnp.concatenate([z, jnp.concatenate([z[:, half:], -z[:, :half]], 1)], 0).T
 
 
-def step_kernel(stage, n_pred, place_ref, scale_ref, map_ref, prior_ref, obs_ref, noise_ref, *refs):
+def step_kernel(stage, load, n_pred, place_ref, scale_ref, map_ref, prior_ref, obs_ref, noise_ref, *refs):
     groups, quads, double, _ = map_ref.shape
     sensors = double // 2
+    ready = None
+    if load:
+        copy_ref, sems, refs = refs[1], refs[3], refs[:1] + refs[2:3]
+        copies = {}
+        for q in range(quads):
+            for g in range(groups):
+                copies[g, q] = pltpu.make_async_copy(map_ref.at[g, q], copy_ref.at[g, q], sems.at[g, q])
+                copies[g, q].start()
+        map_ref, ready = copy_ref, lambda g, q: copies[g, q].wait()
     preds, refs = refs[:n_pred], refs[n_pred:]
     if stage > 0:
         next_ref, refs = refs[0], refs[1:]
@@ -129,7 +146,7 @@
             now = now + relax_step * (obs - predicted - noise_ref[g] * now)
             next_ref[g] = now
         sides_ref[g] = sides(now.astype(bf16))
-    sources = source(map_ref, sides_ref, prior_ref, scale_ref[0])
+    sources = source(map_ref, sides_ref, prior_ref, scale_ref[0], ready)
     turned = [jnp.concatenate([-v[:, HALF:], v[:, :HALF]], 1) for v in sources]
     for e in reversed(range(groups // CORES)):
         for core in range(CORES):
@@ -157,13 +174,17 @@
         out[:, LANES:] = jnp.concatenate([p[:, HALF:] for p in parts], 1).astype(bf16)
 
 
-def send_kernel(place_ref, keep_ref, got_ref, out_ref):
-    out_ref[place_ref[2]] = keep_ref[...]
-    out_ref[1 - place_ref[2]] = got_ref[...]
+def send_kernel(place_ref, keep_ref, got_ref, *refs):
+    posts, outs = refs[:len(refs) // 2], refs[len(refs) // 2:]
+    for i, out in enumerate(outs):
+        out[place_ref[2]] = keep_ref[...]
+        out[1 - place_ref[2]] = got_ref[...]
+        if posts:
+            out[CORES] = posts[i][...]
 
 
 def post_kernel(pairs, place_ref, scale_ref, map_ref, prior_ref, *refs):
-    keeps, gives, refs = refs[:pairs], refs[pairs:2 * pairs], refs[2 * pairs + 1:]
+    keeps, gives, refs = refs[:pairs], refs[pairs:2 * pairs], refs[2 * pairs:]
     outs, (sides_ref, held_ref) = refs[:-2], refs[-2:]
     for e in range(pairs):
         first = CORES * (place_ref[0] ^ e)
@@ -176,18 +197,25 @@
 
 
 def end_kernel(chips, quads, place_ref, *refs):
-    duals, posts, (dual_ref, post_ref) = refs[:chips], refs[chips:chips + quads], refs[chips + quads:]
+    came, (dual_out, post_out, dual_ref, post_ref, sems) = refs[:chips], refs[chips:]
     pair, quad = place_ref[0], place_ref[1]
     cells = post_ref.shape[1] // 2
-    for chip in range(chips):
+    sends = []
+    for chip in reversed(range(chips)):
         e, d = divmod(chip, quads)
         for core in range(CORES):
             freq = (CORES * (pair ^ e) + core) * quads + (quad ^ d)
-            dual_ref[freq, 0] = duals[chip][core, :, :LANES].astype(f32)
-            dual_ref[freq, 1] = duals[chip][core, :, LANES:].astype(f32)
-    for d in range(quads):
-        post_ref[quad ^ d, pl.ds(0, cells, stride=2), :] = posts[d][:, :LANES].astype(f32)
-        post_ref[quad ^ d, pl.ds(1, cells, stride=2), :] = posts[d][:, LANES:].astype(f32)
+            for part in range(2):
+                dual_ref[chip, core, part] = came[chip][core, :, part * LANES:(part + 1) * LANES].astype(f32)
+            sends.append(pltpu.make_async_copy(dual_ref.at[chip, core], dual_out.at[freq], sems.at[chip, core]))
+            sends[-1].start()
+        if e == 0:
+            post_ref[d, pl.ds(0, cells, stride=2), :] = came[chip][CORES, :, :LANES].astype(f32)
+            post_ref[d, pl.ds(1, cells, stride=2), :] = came[chip][CORES, :, LANES:].astype(f32)
+            sends.append(pltpu.make_async_copy(post_ref.at[d], post_out.at[quad ^ d], sems.at[chip, CORES]))
+            sends[-1].start()
+    for copy in sends:
+        copy.wait()
 
 
 def on_device(forward_map, observed, noise_var, prior_rows, prior_scale):
@@ -212,8 +240,12 @@
         moved=groups * sensors * LANES * 12,
     )(place, observed, noise_var.reshape(1, sensors))
     data = [data[0]] + [swap(data[d], "sensor", d) for d in range(1, groups)]
-    diagonal = lax.dynamic_slice_in_dim(prior_rows, quad % 2 * cells, cells, 1)
-    came = [swap(diagonal if d % 2 else prior_rows, "quad", d) for d in range(1, quads)]
+    rows, diagonal = call(
+        prior_kernel,
+        [SMEM, VMEM, ANY],
+        [shape((cells, width), bf16), shape((cells, cells), bf16)],
+    )(place, prior_rows, data[1])
+    came = [swap(diagonal if d % 2 else rows, "quad", d) for d in range(1, quads)]
     prior, noise, *streams = call(
         functools.partial(gather_kernel, groups, quads),
         [SMEM] + [VMEM] * (quads + groups),
@@ -230,21 +262,28 @@
     wide, narrow = shape((groups, sensors, LANES), f32), shape((groups, sensors, LANES), bf16)
     couple, full = shape((CORES, sensors, LANES), bf16), shape((sensors, 2 * LANES), bf16)
 
-    def step(stage, obs, preds):
-        operands = [place, scale, held, prior, obs, noise] + preds
+    def step(stage, obs, preds, where, load=False):
+        operands = [place, scale, where, prior, obs, noise] + preds
+        out = [wide] + [couple] * pairs if stage > 0 else [narrow]
+        scratch = [pltpu.VMEM((groups, LANES, halves * sensors), bf16)]
+        if load:
+            out.append(shape(held.shape, bf16))
+            scratch.append(pltpu.SemaphoreType.DMA((groups, quads)))
         return call(
-            functools.partial(step_kernel, stage, len(preds)),
-            [SMEM, SMEM] + [VMEM] * (len(operands) - 2),
-            [wide] + [couple] * pairs if stage > 0 else [narrow],
-            [pltpu.VMEM((groups, LANES, halves * sensors), bf16)],
+            functools.partial(step_kernel, stage, load, len(preds)),
+            [SMEM, SMEM, ANY if load else VMEM] + [VMEM] * (len(operands) - 3),
+            out,
+            scratch,
             flops=2**31,
             moved=8 * 2**20,
         )(*operands)
 
-    first = [over_sides(step(0, streams[s], [])[0]) for s in range(STREAMS)]
+    partial, near = step(0, streams[0], [], held, True)
+    first = [over_sides(partial)]
+    first += [over_sides(step(0, streams[s], [], near)[0]) for s in range(1, STREAMS)]
     multiplier, partials = [], []
     for s in range(STREAMS):
-        out, *parts = step(1, streams[s], first[s])
+        out, *parts = step(1, streams[s], first[s], near)
         multiplier.append(out)
         partials.append(parts)
     keeps, gives, duals = [None] * pairs, [None] * pairs, {}
@@ -257,30 +296,38 @@
             [full, full],
             moved=2 * 2**20,
         )(place, noise, *streams, *multiplier, *[p for pair in preds for p in pair])
-        message = call(
+        got = swap(gives[e], "sensor", 1)
+        posts = []
+        if e == 0:
+            posts = call(
+                functools.partial(post_kernel, pairs),
+                [SMEM, SMEM] + [VMEM] * (2 + 2 * pairs),
+                [shape((cells, 2 * LANES), bf16)] * quads,
+                [pltpu.VMEM((groups, 2 * LANES, halves * sensors), bf16), pltpu.VMEM((quads, cells, 2 * LANES), bf16)],
+                flops=2**31,
+                moved=8 * 2**20,
+            )(place, scale, near, prior, *keeps, *gives)
+        messages = call(
             send_kernel,
-            [SMEM, VMEM, VMEM],
-            [shape((CORES, sensors, 2 * LANES), bf16)],
+            [SMEM] + [VMEM] * (2 + len(posts)),
+            [shape((CORES + (e == 0), sensors, 2 * LANES), bf16)] * (len(posts) or 1),
             moved=2**20,
-        )(place, keeps[e], swap(gives[e], "sensor", 1))[0]
+        )(place, keeps[e], got, *posts)
         for d in reversed(range(quads)):
-            away = e * quads + d
-            duals[away] = swap(message, both, CORES * e * quads + d) if away else message
-    post = call(
-        functools.partial(post_kernel, pairs),
-        [SMEM, SMEM] + [VMEM] * (2 + 2 * pairs) + [ANY],
-        [shape((cells, 2 * LANES), bf16)] * quads,
-        [pltpu.VMEM((groups, 2 * LANES, halves * sensors), bf16), pltpu.VMEM((quads, cells, 2 * LANES), bf16)],
-        flops=2**31,
-        moved=8 * 2**20,
-    )(place, scale, held, prior, *keeps, *gives, duals[(pairs - 1) * quads])
-    post = [post[0]] + [swap(post[d], "quad", d) for d in range(1, quads)]
+            message = messages[d] if e == 0 else messages[0]
+            duals[e * quads + d] = swap(message, both, CORES * e * quads + d) if e + d else message
     dual, posterior = call(
         functools.partial(end_kernel, pairs * quads, quads),
-        [SMEM] + [VMEM] * (pairs * quads + quads),
+        [SMEM] + [VMEM] * (pairs * quads),
         [shape((frequencies, halves, sensors, LANES), f32), shape((quads, cells * 2, LANES), f32)],
+        [
+            pltpu.VMEM((pairs * quads, CORES, halves, sensors, LANES), f32),
+            pltpu.VMEM((quads, cells * 2, LANES), f32),
+            pltpu.SemaphoreType.DMA((pairs * quads, CORES + 1)),
+        ],
+        [ANY, ANY],
         moved=8 * 2**20,
-    )(place, *[duals[i] for i in range(pairs * quads)], *post)
+    )(place, *[duals[i] for i in range(pairs * quads)])
     return dual, posterior.reshape(quads, cells, 2, LANES)
 
 

time: 167 us -> 166 us (level)
  waiting for transfers between devices: 91 us -> 103 us
  starting transfers between devices: 36.8 us -> 30 us
  Pallas kernels: 35.3 us -> 29.6 us
    ppermute x24 -> x21, waiting for transfers between devices: 91 us -> 103 us  [swap(): return lax.ppermute(x, axes, [(i, i ^ distance) for i in range(count)])]
    ppermute x24 -> x21, starting transfers between devices: 30.3 us -> 23.5 us  [swap(): return lax.ppermute(x, axes, [(i, i ^ distance) for i in range(count)])]
    pallas_call x6 -> x7, Pallas kernels: 23.6 us -> 19.7 us  [the longest x4 17.9 us: step(): call(functools.partial(step_kernel, stage, load, len(preds)), [SMEM, SMEM...]
  transfers between devices with their start and end apart: 25 -> 22, of which waited for: 11 -> 13; matrix products, arithmetic and copies ran while one was open for 0% -> 0% of each run, Pallas kernels for 15% -> 10%
where the time goes in v6:
time: 166 us
  waiting for transfers between devices  103 us (62%)
  starting transfers between devices  30 us (18%)
  Pallas kernels  29.6 us (18%)
  local copies, waits for them, and re-layouts  2.79 us (2%)
    ppermute x21, waiting for transfers between devices, swap(): return lax.ppermute(x, axes, [(i, i ^ distance) for i in range(count)])  103 us
    ppermute x21, starting transfers between devices, swap(): return lax.ppermute(x, axes, [(i, i ^ distance) for i in range(count)])  23.5 us
    pallas_call x4, Pallas kernels, step(): call(functools.partial(step_kernel, stage, load, len(preds)), [SMEM, SMEM...  17.9 us
    all_to_all x1, starting transfers between devices, on_device(): lax.all_to_all(forward_map.reshape(frequencies, halves * sensors, cells),...  6.48 us
  transfers between devices with their start and end apart: 22, of which 13 were waited for; matrix products, arithmetic and copies ran while one was open for 0% of the time, Pallas kernels for 10%

profile of v6, /device:TPU:0, one launch (start us, length us, event | category | flops | bytes accessed | tf_op | source)
XLA Modules:
  0.0 166.0 jit_solution(15441333104169021300)
XLA Ops:
  0.6 6.5 %all-to-all-start = ((bf16[16,512,256]{2,1,0:T(8,128)(2,1)}), bf16[16,512,256]{2,1,0:T(8,128)(2,1)}, u32[]{:S(2)}, u32[]{:S(2)}) async-start(bf16[16,512,256]{2,1,0:T(8,128)(2,1)} %bitcast.8), calls=%async_computation | async-start | bytes 8388608 | tf_op jit(solution)/shard_map/all_to_all | solution.py:231
  7.3 2.2 %copy-done = f32[16,2,256,128]{3,2,1,0:T(8,128)S(1)} copy-done((f32[16,2,256,128]{3,2,1,0:T(8,128)S(1)}, f32[16,2,256,128]{3,2,1,0:T(8,128)}, u32[]{:S(2)}) %copy-start) | copy-done | bytes 4194328
  9.4 1.1 shard_map.68
  12.6 1.9 %collective-permute-start.2 = (bf16[256,512]{1,0:T(8,128)(2,1)S(1)}, bf16[256,512]{1,0:T(8,128)(2,1)S(1)}, u32[]{:S(2)}, u32[]{:S(2)}) collective-permute-start(bf16[256,512]{1,0:T(8,128)(2,1)S(1)} %get-tuple-element.36), channel_id=1, source_target_pairs={{0,2},{1,3},{2,0},{3,1},{4,6},{5,7},{6,4},{7,5},{8,10},{9,11},{10,... | collective-permute-start | bytes 786440 | tf_op jit(solution)/shard_map/ppermute | solution.py:41
  14.5 1.5 collective-permute-start.4
  16.0 1.5 collective-permute-start.3
  18.6 47.7 %collective-permute-done.4.refs_5_ = bf16[272,256]{1,0:T(8,128)(2,1)S(1)} collective-permute-done((bf16[272,256]{1,0:T(8,128)(2,1)S(1)}, bf16[272,256]{1,0:T(8,128)(2,1)S(1)}, u32[]{:S(2)}, u32[]{:S(2)}) %collective-permute-start.4) | collective-permute-done | bytes 139296 | tf_op jit(solution)/shard_map/ppermute | solution.py:41
  66.3 2.0 %collective-permute-done.5.refs_6_ = bf16[272,256]{1,0:T(8,128)(2,1)S(1)} collective-permute-done((bf16[272,256]{1,0:T(8,128)(2,1)S(1)}, bf16[272,256]{1,0:T(8,128)(2,1)S(1)}, u32[]{:S(2)}, u32[]{:S(2)}) %collective-permute-start.5) | collective-permute-done | bytes 139296 | tf_op jit(solution)/shard_map/ppermute | solution.py:41
  68.3 1.4 collective-permute-done.3.refs_2_
  70.8 6.0 %shard_map.71 = (bf16[4,256,128]{2,1,0:T(8,128)(2,1)S(1)}, bf16[4,4,512,256]{3,2,1,0:T(8,128)(2,1)S(1)}) custom-call(s32[3]{0:T(128)S(1)} %pad_add_fusion.place_ref, f32[1]{0:T(128)} %dynamic_slice.3.scale_ref, bf16[4,4,512,256]{3,2,1,0:T(8,128)(2,1)} %bitcast.5.map_ref, bf16[4,256,512]{2,1,0:T(8,128)(2,1)S(1)} %get-tuple-element.43.prior_ref, ...), custom_call_target="tpu_custom_call" | custom-call | flops 2147483648 | bytes 8388608 | tf_op jit(solution)/shard_map/pallas_call | solution.py:272
  76.8 3.9 %shard_map.73.refs_0_ = bf16[4,256,128]{2,1,0:T(8,128)(2,1)S(1)} custom-call(s32[3]{0:T(128)S(1)} %pad_add_fusion.place_ref, f32[1]{0:T(128)} %dynamic_slice.3.scale_ref, bf16[4,4,512,256]{3,2,1,0:T(8,128)(2,1)S(1)} %get-tuple-element.44.map_ref, bf16[4,256,512]{2,1,0:T(8,128)(2,1)S(1)} %get-tuple-element.43.prior_ref, ...), custom_call_target="tpu_custom_call" | custom-call | flops 2147483648 | bytes 8388608 | tf_op jit(solution)/shard_map/pallas_call | solution.py:272
  80.7 2.7 %collective-permute-start.7 = (bf16[4,256,128]{2,1,0:T(8,128)(2,1)S(1)}, bf16[4,256,128]{2,1,0:T(8,128)(2,1)S(1)}, u32[]{:S(2)}, u32[]{:S(2)}) collective-permute-start(bf16[4,256,128]{2,1,0:T(8,128)(2,1)S(1)} %shard_map.73.refs_0_), channel_id=1, source_target_pairs={{0,4},{4,0},{1,5},{5,1},{2,6},{6,2},{3,7},{7,3},{8,12},{12,8},{9,1... | collective-permute-start | bytes 786440 | tf_op jit(solution)/shard_map/ppermute | solution.py:41
  83.7 15.2 %collective-permute-done.7.refs_1_ = bf16[4,256,128]{2,1,0:T(8,128)(2,1)S(1)} collective-permute-done((bf16[4,256,128]{2,1,0:T(8,128)(2,1)S(1)}, bf16[4,256,128]{2,1,0:T(8,128)(2,1)S(1)}, u32[]{:S(2)}, u32[]{:S(2)}) %collective-permute-start.7) | collective-permute-done | bytes 262176 | tf_op jit(solution)/shard_map/ppermute | solution.py:41
  99.0 4.0 %shard_map.74 = (f32[4,256,128]{2,1,0:T(8,128)S(1)}, bf16[2,256,128]{2,1,0:T(8,128)(2,1)S(1)}, bf16[2,256,128]{2,1,0:T(8,128)(2,1)S(1)}) custom-call(s32[3]{0:T(128)S(1)} %pad_add_fusion.place_ref, f32[1]{0:T(128)} %dynamic_slice.3.scale_ref, bf16[4,4,512,256]{3,2,1,0:T(8,128)(2,1)S(1)} %get-tuple-element.44.map_ref, ...), custom_call_target="tpu_custom_call" | custom-call | flops 2147483648 | bytes 8388608 | tf_op jit(solution)/shard_map/pallas_call | solution.py:272
  103.0 1.5 collective-permute-done.6.refs_1_
  104.5 4.0 %shard_map.72 = (f32[4,256,128]{2,1,0:T(8,128)S(1)}, bf16[2,256,128]{2,1,0:T(8,128)(2,1)S(1)}, bf16[2,256,128]{2,1,0:T(8,128)(2,1)S(1)}) custom-call(s32[3]{0:T(128)S(1)} %pad_add_fusion.place_ref, f32[1]{0:T(128)} %dynamic_slice.3.scale_ref, bf16[4,4,512,256]{3,2,1,0:T(8,128)(2,1)S(1)} %get-tuple-element.44.map_ref, ...), custom_call_target="tpu_custom_call" | custom-call | flops 2147483648 | bytes 8388608 | tf_op jit(solution)/shard_map/pallas_call | solution.py:272
  108.4 1.5 collective-permute-start.11
  109.9 1.5 collective-permute-start.9
  111.4 1.4 collective-permute-start.8
  112.9 9.9 %collective-permute-done.11.refs_5_ = bf16[2,256,128]{2,1,0:T(8,128)(2,1)S(1)} collective-permute-done((bf16[2,256,128]{2,1,0:T(8,128)(2,1)S(1)}, bf16[2,256,128]{2,1,0:T(8,128)(2,1)S(1)}, u32[]{:S(2)}, u32[]{:S(2)}) %collective-permute-start.11) | collective-permute-done | bytes 131104 | tf_op jit(solution)/shard_map/ppermute | solution.py:41
  123.7 1.9 %collective-permute-done.9.refs_7_ = bf16[2,256,128]{2,1,0:T(8,128)(2,1)S(1)} collective-permute-done((bf16[2,256,128]{2,1,0:T(8,128)(2,1)S(1)}, bf16[2,256,128]{2,1,0:T(8,128)(2,1)S(1)}, u32[]{:S(2)}, u32[]{:S(2)}) %collective-permute-start.9) | collective-permute-done | bytes 131104 | tf_op jit(solution)/shard_map/ppermute | solution.py:41
  125.6 2.7 %collective-permute-done.8.refs_5_ = bf16[2,256,128]{2,1,0:T(8,128)(2,1)S(1)} collective-permute-done((bf16[2,256,128]{2,1,0:T(8,128)(2,1)S(1)}, bf16[2,256,128]{2,1,0:T(8,128)(2,1)S(1)}, u32[]{:S(2)}, u32[]{:S(2)}) %collective-permute-start.8) | collective-permute-done | bytes 131104 | tf_op jit(solution)/shard_map/ppermute | solution.py:41
  130.2 3.4 %collective-permute-start.19 = (bf16[2,256,256]{2,1,0:T(8,128)(2,1)S(1)}, bf16[2,256,256]{2,1,0:T(8,128)(2,1)S(1)}, u32[]{:S(2)}, u32[]{:S(2)}) collective-permute-start(bf16[2,256,256]{2,1,0:T(8,128)(2,1)S(1)} %shard_map.79), channel_id=1, source_target_pairs={{0,18},{1,19},{2,16},{3,17},{8,26},{9,27},{10,24},{11,25},{16,2},{... | collective-permute-start | bytes 786440 | tf_op jit(solution)/shard_map/ppermute | solution.py:41
  133.6 3.2 %shard_map.77 = (bf16[256,256]{1,0:T(8,128)(2,1)S(1)}, bf16[256,256]{1,0:T(8,128)(2,1)S(1)}, bf16[256,256]{1,0:T(8,128)(2,1)S(1)}, bf16[256,256]{1,0:T(8,128)(2,1)S(1)}) custom-call(s32[3]{0:T(128)S(1)} %pad_add_fusion.place_ref, f32[1]{0:T(128)} %dynamic_slice.3.scale_ref, bf16[4,4,512,256]{3,2,1,0:T(8,128)(2,1)S(1)} %get-tuple-element.44.map_ref, ...), custom_call_target="tpu_custom_call" | custom-call | flops 2147483648 | bytes 8388608 | tf_op jit(solution)/shard_map/pallas_call | solution.py:302
  138.2 2.9 %collective-permute-start.15 = (bf16[3,256,256]{2,1,0:T(8,128)(2,1)S(1)}, bf16[3,256,256]{2,1,0:T(8,128)(2,1)S(1)}, u32[]{:S(2)}, u32[]{:S(2)}) collective-permute-start(bf16[3,256,256]{2,1,0:T(8,128)(2,1)S(1)} %get-tuple-element.63), channel_id=1, source_target_pairs={{0,3},{1,2},{2,1},{3,0},{8,11},{9,10},{10,9},{11,8},{16,19},{17,18... | collective-permute-start | bytes 1179656 | tf_op jit(solution)/shard_map/ppermute | solution.py:41
  141.1 1.6 collective-permute-start.18
  142.7 3.7 %collective-permute-done.19.refs_6_ = bf16[2,256,256]{2,1,0:T(8,128)(2,1)S(1)} collective-permute-done((bf16[2,256,256]{2,1,0:T(8,128)(2,1)S(1)}, bf16[2,256,256]{2,1,0:T(8,128)(2,1)S(1)}, u32[]{:S(2)}, u32[]{:S(2)}) %collective-permute-start.19) | collective-permute-done | bytes 262176 | tf_op jit(solution)/shard_map/ppermute | solution.py:41
  146.3 1.1 collective-permute-start.17
  147.4 4.3 %collective-permute-done.18.refs_5_ = bf16[2,256,256]{2,1,0:T(8,128)(2,1)S(1)} collective-permute-done((bf16[2,256,256]{2,1,0:T(8,128)(2,1)S(1)}, bf16[2,256,256]{2,1,0:T(8,128)(2,1)S(1)}, u32[]{:S(2)}, u32[]{:S(2)}) %collective-permute-start.18) | collective-permute-done | bytes 262176 | tf_op jit(solution)/shard_map/ppermute | solution.py:41
  151.7 5.5 %collective-permute-done.17.refs_4_ = bf16[2,256,256]{2,1,0:T(8,128)(2,1)S(1)} collective-permute-done((bf16[2,256,256]{2,1,0:T(8,128)(2,1)S(1)}, bf16[2,256,256]{2,1,0:T(8,128)(2,1)S(1)}, u32[]{:S(2)}, u32[]{:S(2)}) %collective-permute-start.17) | collective-permute-done | bytes 262176 | tf_op jit(solution)/shard_map/ppermute | solution.py:41
  157.2 5.7 %collective-permute-done.13.refs_1_ = bf16[3,256,256]{2,1,0:T(8,128)(2,1)S(1)} collective-permute-done((bf16[3,256,256]{2,1,0:T(8,128)(2,1)S(1)}, bf16[3,256,256]{2,1,0:T(8,128)(2,1)S(1)}, u32[]{:S(2)}, u32[]{:S(2)}) %collective-permute-start.13) | collective-permute-done | bytes 393248 | tf_op jit(solution)/shard_map/ppermute | solution.py:41
  162.9 3.1 %shard_map.80 = (f32[16,2,256,128]{3,2,1,0:T(8,128)}, f32[4,512,128]{2,1,0:T(8,128)}) custom-call(s32[3]{0:T(128)S(1)} %pad_add_fusion.place_ref, bf16[3,256,256]{2,1,0:T(8,128)(2,1)S(1)} %get-tuple-element.60.refs_0_, bf16[3,256,256]{2,1,0:T(8,128)(2,1)S(1)} %collective-permute-done.13.refs_1_, bf16[3,256,256]{2,1,0:T(8,128)(2,1)S(1)} %collective-permute-done.14.refs_2_, ...), custom_call_target="tpu_custom_call" | custom-call | bytes 8388608 | tf_op jit(solution)/shard_map/pallas_call | solution.py:319
  (35 shorter events, 8.7 us)
Async XLA Ops:
  0.6 6.6 %copy-start.2 = (f32[256]{0:T(256)S(1)}, f32[256]{0:T(256)}, u32[]{:S(2)}) copy-start(f32[256]{0:T(256)} %param.7) | copy-start | bytes 3076
  0.6 11.3 %copy-start.1 = (bf16[256,512]{1,0:T(8,128)(2,1)S(1)}, bf16[256,512]{1,0:T(8,128)(2,1)}, u32[]{:S(2)}) copy-start(bf16[256,512]{1,0:T(8,128)(2,1)} %own_ref.3) | copy-start | bytes 786436
  0.6 70.1 %all-to-all-start = ((bf16[16,512,256]{2,1,0:T(8,128)(2,1)}), bf16[16,512,256]{2,1,0:T(8,128)(2,1)}, u32[]{:S(2)}, u32[]{:S(2)}) async-start(bf16[16,512,256]{2,1,0:T(8,128)(2,1)} %bitcast.8), calls=%async_computation | async-start | bytes 8388608 | tf_op jit(solution)/shard_map/all_to_all | solution.py:231
  7.1 10.9 %copy-start.3 = (f32[16]{0:T(128)S(1)}, f32[16]{0:T(128)}, u32[]{:S(2)}) copy-start(f32[16]{0:T(128)} %param.9) | copy-start | bytes 196
  7.3 2.2 %copy-start = (f32[16,2,256,128]{3,2,1,0:T(8,128)S(1)}, f32[16,2,256,128]{3,2,1,0:T(8,128)}, u32[]{:S(2)}) copy-start(f32[16,2,256,128]{3,2,1,0:T(8,128)} %obs_ref.1) | copy-start | bytes 12582916
  10.6 1.4 collective-permute-start
  12.6 57.2 %collective-permute-start.2 = (bf16[256,512]{1,0:T(8,128)(2,1)S(1)}, bf16[256,512]{1,0:T(8,128)(2,1)S(1)}, u32[]{:S(2)}, u32[]{:S(2)}) collective-permute-start(bf16[256,512]{1,0:T(8,128)(2,1)S(1)} %get-tuple-element.36), channel_id=1, source_target_pairs={{0,2},{1,3},{2,0},{3,1},{4,6},{5,7},{6,4},{7,5},{8,10},{9,11},{10,... | collective-permute-start | bytes 786440 | tf_op jit(solution)/shard_map/ppermute | solution.py:41
  14.5 51.8 %collective-permute-start.4 = (bf16[272,256]{1,0:T(8,128)(2,1)S(1)}, bf16[272,256]{1,0:T(8,128)(2,1)S(1)}, u32[]{:S(2)}, u32[]{:S(2)}) collective-permute-start(bf16[272,256]{1,0:T(8,128)(2,1)S(1)} %get-tuple-element.38), channel_id=1, source_target_pairs={{0,16},{8,24},{16,0},{24,8},{1,17},{9,25},{17,1},{25,9},{2,18},{10... | collective-permute-start | bytes 417800 | tf_op jit(solution)/shard_map/ppermute | solution.py:41
  16.0 52.4 %collective-permute-start.5 = (bf16[272,256]{1,0:T(8,128)(2,1)S(1)}, bf16[272,256]{1,0:T(8,128)(2,1)S(1)}, u32[]{:S(2)}, u32[]{:S(2)}) collective-permute-start(bf16[272,256]{1,0:T(8,128)(2,1)S(1)} %get-tuple-element.39), channel_id=1, source_target_pairs={{0,24},{8,16},{16,8},{24,0},{1,25},{9,17},{17,9},{25,1},{2,26},{10... | collective-permute-start | bytes 417800 | tf_op jit(solution)/shard_map/ppermute | solution.py:41
  16.0 53.8 %collective-permute-start.3 = (bf16[256,256]{1,0:T(8,128)(2,1)S(1)}, bf16[256,256]{1,0:T(8,128)(2,1)S(1)}, u32[]{:S(2)}, u32[]{:S(2)}) collective-permute-start(bf16[256,256]{1,0:T(8,128)(2,1)S(1)} %get-tuple-element.35), channel_id=1, source_target_pairs={{0,3},{1,2},{2,1},{3,0},{4,7},{5,6},{6,5},{7,4},{8,11},{9,10},{10,... | collective-permute-start | bytes 393224 | tf_op jit(solution)/shard_map/ppermute | solution.py:41
  17.4 52.4 %collective-permute-start.1 = (bf16[256,256]{1,0:T(8,128)(2,1)S(1)}, bf16[256,256]{1,0:T(8,128)(2,1)S(1)}, u32[]{:S(2)}, u32[]{:S(2)}) collective-permute-start(bf16[256,256]{1,0:T(8,128)(2,1)S(1)} %get-tuple-element.35), channel_id=1, source_target_pairs={{0,1},{1,0},{2,3},{3,2},{4,5},{5,4},{6,7},{7,6},{8,9},{9,8},{10,11... | collective-permute-start | bytes 393224 | tf_op jit(solution)/shard_map/ppermute | solution.py:41
  80.7 18.2 %collective-permute-start.7 = (bf16[4,256,128]{2,1,0:T(8,128)(2,1)S(1)}, bf16[4,256,128]{2,1,0:T(8,128)(2,1)S(1)}, u32[]{:S(2)}, u32[]{:S(2)}) collective-permute-start(bf16[4,256,128]{2,1,0:T(8,128)(2,1)S(1)} %shard_map.73.refs_0_), channel_id=1, source_target_pairs={{0,4},{4,0},{1,5},{5,1},{2,6},{6,2},{3,7},{7,3},{8,12},{12,8},{9,1... | collective-permute-start | bytes 786440 | tf_op jit(solution)/shard_map/ppermute | solution.py:41
  83.4 21.1 %collective-permute-start.6 = (bf16[4,256,128]{2,1,0:T(8,128)(2,1)S(1)}, bf16[4,256,128]{2,1,0:T(8,128)(2,1)S(1)}, u32[]{:S(2)}, u32[]{:S(2)}) collective-permute-start(bf16[4,256,128]{2,1,0:T(8,128)(2,1)S(1)} %get-tuple-element.45.refs_0_), channel_id=1, source_target_pairs={{0,4},{4,0},{1,5},{5,1},{2,6},{6,2},{3,7},{7,3},{8,12},{12,8},{9,1... | collective-permute-start | bytes 786440 | tf_op jit(solution)/shard_map/ppermute | solution.py:41
  102.9 9.9 %collective-permute-start.12 = (bf16[2,256,128]{2,1,0:T(8,128)(2,1)S(1)}, bf16[2,256,128]{2,1,0:T(8,128)(2,1)S(1)}, u32[]{:S(2)}, u32[]{:S(2)}) collective-permute-start(bf16[2,256,128]{2,1,0:T(8,128)(2,1)S(1)} %get-tuple-element.53.refs_6_), channel_id=1, source_target_pairs={{0,4},{4,0},{1,5},{5,1},{2,6},{6,2},{3,7},{7,3},{8,12},{12,8},{9,1... | collective-permute-start | bytes 393224 | tf_op jit(solution)/shard_map/ppermute | solution.py:41
  108.4 14.4 %collective-permute-start.11 = (bf16[2,256,128]{2,1,0:T(8,128)(2,1)S(1)}, bf16[2,256,128]{2,1,0:T(8,128)(2,1)S(1)}, u32[]{:S(2)}, u32[]{:S(2)}) collective-permute-start(bf16[2,256,128]{2,1,0:T(8,128)(2,1)S(1)} %get-tuple-element.52.refs_4_), channel_id=1, source_target_pairs={{0,4},{4,0},{1,5},{5,1},{2,6},{6,2},{3,7},{7,3},{8,12},{12,8},{9,1... | collective-permute-start | bytes 393224 | tf_op jit(solution)/shard_map/ppermute | solution.py:41
  109.9 15.7 %collective-permute-start.9 = (bf16[2,256,128]{2,1,0:T(8,128)(2,1)S(1)}, bf16[2,256,128]{2,1,0:T(8,128)(2,1)S(1)}, u32[]{:S(2)}, u32[]{:S(2)}) collective-permute-start(bf16[2,256,128]{2,1,0:T(8,128)(2,1)S(1)} %get-tuple-element.49.refs_6_), channel_id=1, source_target_pairs={{0,4},{4,0},{1,5},{5,1},{2,6},{6,2},{3,7},{7,3},{8,12},{12,8},{9,1... | collective-permute-start | bytes 393224 | tf_op jit(solution)/shard_map/ppermute | solution.py:41
  111.4 16.9 %collective-permute-start.8 = (bf16[2,256,128]{2,1,0:T(8,128)(2,1)S(1)}, bf16[2,256,128]{2,1,0:T(8,128)(2,1)S(1)}, u32[]{:S(2)}, u32[]{:S(2)}) collective-permute-start(bf16[2,256,128]{2,1,0:T(8,128)(2,1)S(1)} %get-tuple-element.48.refs_4_), channel_id=1, source_target_pairs={{0,4},{4,0},{1,5},{5,1},{2,6},{6,2},{3,7},{7,3},{8,12},{12,8},{9,1... | collective-permute-start | bytes 393224 | tf_op jit(solution)/shard_map/ppermute | solution.py:41
  123.6 5.6 %collective-permute-start.16 = (bf16[256,256]{1,0:T(8,128)(2,1)S(1)}, bf16[256,256]{1,0:T(8,128)(2,1)S(1)}, u32[]{:S(2)}, u32[]{:S(2)}) collective-permute-start(bf16[256,256]{1,0:T(8,128)(2,1)S(1)} %get-tuple-element.55.refs_3_), channel_id=1, source_target_pairs={{0,8},{8,0},{16,24},{24,16},{1,9},{9,1},{17,25},{25,17},{2,10},{10... | collective-permute-start | bytes 393224 | tf_op jit(solution)/shard_map/ppermute | solution.py:41
  129.1 7.7 %collective-permute-start.10 = (bf16[256,256]{1,0:T(8,128)(2,1)S(1)}, bf16[256,256]{1,0:T(8,128)(2,1)S(1)}, u32[]{:S(2)}, u32[]{:S(2)}) collective-permute-start(bf16[256,256]{1,0:T(8,128)(2,1)S(1)} %get-tuple-element.51.refs_2_), channel_id=1, source_target_pairs={{0,8},{8,0},{16,24},{24,16},{1,9},{9,1},{17,25},{25,17},{2,10},{10... | collective-permute-start | bytes 393224 | tf_op jit(solution)/shard_map/ppermute | solution.py:41
  129.8 11.3 %collective-permute-start.20 = (bf16[2,256,256]{2,1,0:T(8,128)(2,1)S(1)}, bf16[2,256,256]{2,1,0:T(8,128)(2,1)S(1)}, u32[]{:S(2)}, u32[]{:S(2)}) collective-permute-start(bf16[2,256,256]{2,1,0:T(8,128)(2,1)S(1)} %shard_map.79), channel_id=1, source_target_pairs={{0,19},{1,18},{2,17},{3,16},{8,27},{9,26},{10,25},{11,24},{16,3},{... | collective-permute-start | bytes 786440 | tf_op jit(solution)/shard_map/ppermute | solution.py:41
  130.2 16.1 %collective-permute-start.19 = (bf16[2,256,256]{2,1,0:T(8,128)(2,1)S(1)}, bf16[2,256,256]{2,1,0:T(8,128)(2,1)S(1)}, u32[]{:S(2)}, u32[]{:S(2)}) collective-permute-start(bf16[2,256,256]{2,1,0:T(8,128)(2,1)S(1)} %shard_map.79), channel_id=1, source_target_pairs={{0,18},{1,19},{2,16},{3,17},{8,26},{9,27},{10,24},{11,25},{16,2},{... | collective-permute-start | bytes 786440 | tf_op jit(solution)/shard_map/ppermute | solution.py:41
  137.5 25.4 %collective-permute-start.13 = (bf16[3,256,256]{2,1,0:T(8,128)(2,1)S(1)}, bf16[3,256,256]{2,1,0:T(8,128)(2,1)S(1)}, u32[]{:S(2)}, u32[]{:S(2)}) collective-permute-start(bf16[3,256,256]{2,1,0:T(8,128)(2,1)S(1)} %get-tuple-element.61), channel_id=1, source_target_pairs={{0,1},{1,0},{2,3},{3,2},{8,9},{9,8},{10,11},{11,10},{16,17},{17,16... | collective-permute-start | bytes 1179656 | tf_op jit(solution)/shard_map/ppermute | solution.py:41
  138.2 24.7 %collective-permute-start.14 = (bf16[3,256,256]{2,1,0:T(8,128)(2,1)S(1)}, bf16[3,256,256]{2,1,0:T(8,128)(2,1)S(1)}, u32[]{:S(2)}, u32[]{:S(2)}) collective-permute-start(bf16[3,256,256]{2,1,0:T(8,128)(2,1)S(1)} %get-tuple-element.62), channel_id=1, source_target_pairs={{0,2},{1,3},{2,0},{3,1},{8,10},{9,11},{10,8},{11,9},{16,18},{17,19... | collective-permute-start | bytes 1179656 | tf_op jit(solution)/shard_map/ppermute | solution.py:41
  138.2 24.7 %collective-permute-start.15 = (bf16[3,256,256]{2,1,0:T(8,128)(2,1)S(1)}, bf16[3,256,256]{2,1,0:T(8,128)(2,1)S(1)}, u32[]{:S(2)}, u32[]{:S(2)}) collective-permute-start(bf16[3,256,256]{2,1,0:T(8,128)(2,1)S(1)} %get-tuple-element.63), channel_id=1, source_target_pairs={{0,3},{1,2},{2,1},{3,0},{8,11},{9,10},{10,9},{11,8},{16,19},{17,18... | collective-permute-start | bytes 1179656 | tf_op jit(solution)/shard_map/ppermute | solution.py:41
  141.1 10.6 %collective-permute-start.18 = (bf16[2,256,256]{2,1,0:T(8,128)(2,1)S(1)}, bf16[2,256,256]{2,1,0:T(8,128)(2,1)S(1)}, u32[]{:S(2)}, u32[]{:S(2)}) collective-permute-start(bf16[2,256,256]{2,1,0:T(8,128)(2,1)S(1)} %shard_map.79), channel_id=1, source_target_pairs={{0,17},{1,16},{2,19},{3,18},{8,25},{9,24},{10,27},{11,26},{16,1},{... | collective-permute-start | bytes 786440 | tf_op jit(solution)/shard_map/ppermute | solution.py:41
  146.3 10.8 %collective-permute-start.17 = (bf16[2,256,256]{2,1,0:T(8,128)(2,1)S(1)}, bf16[2,256,256]{2,1,0:T(8,128)(2,1)S(1)}, u32[]{:S(2)}, u32[]{:S(2)}) collective-permute-start(bf16[2,256,256]{2,1,0:T(8,128)(2,1)S(1)} %shard_map.79), channel_id=1, source_target_pairs={{0,16},{1,17},{2,18},{3,19},{8,24},{9,25},{10,26},{11,27},{16,0},{... | collective-permute-start | bytes 786440 | tf_op jit(solution)/shard_map/ppermute | solution.py:41

commit v7 on v3

v7 whole, which is shorter than its diff:
```python
import functools

import jax
import jax.numpy as jnp
from jax import lax
from jax.experimental import pallas as pl
from jax.experimental.pallas import tpu as pltpu
from jax.sharding import Mesh, PartitionSpec as P

ITERS = 2
relax_step = 0.25
CORES = 2
LANES = 128
HALF = LANES // CORES
VMEM_LIMIT = 12 * 2**20
WHOLE_VMEM = 56 * 2**20
VMEM = pl.BlockSpec(memory_space=pltpu.VMEM)
SMEM = pl.BlockSpec(memory_space=pltpu.SMEM)
ANY = pl.BlockSpec(memory_space=pl.ANY)
bf16, f32 = jnp.bfloat16, jnp.float32


def shape(dims, dtype):
    return jax.ShapeDtypeStruct(dims, dtype)


def call(kernel, in_specs, out_shape, scratch=(), out_specs=None, flops=0, moved=0, limit=VMEM_LIMIT):
    return pl.pallas_call(
        kernel,
        in_specs=in_specs,
        out_specs=out_specs or [VMEM] * len(out_shape),
        out_shape=out_shape,
        scratch_shapes=list(scratch),
        cost_estimate=pl.CostEstimate(flops=flops, bytes_accessed=moved, transcendentals=0),
        compiler_params=pltpu.CompilerParams(vmem_limit_bytes=limit),
    )


def dot(a, b):
    return jnp.dot(a, b, preferred_element_type=f32)


def dot_nt(a, b):
    return lax.dot_general(a, b, (((1,), (1,)), ((), ())), preferred_element_type=f32)


class Plan:
    def __init__(self, groups, quads, sensors, cells, width):
        self.groups, self.quads, self.sensors, self.cells, self.width = groups, quads, sensors, cells, width
        self.pairs = groups // CORES
        self.chips = self.pairs * quads
        self.per_block = width // cells
        self.map_rows = 2 * sensors
        self.share = cells // CORES

    def extra(self, d):
        e, dq = divmod(d, self.quads)
        if dq == 0:
            return CORES * self.sensors + 16
        return self.share * self.per_block if e == 0 else 0

    def rows(self, d):
        return CORES * self.map_rows + self.extra(d)

    def order(self):
        far, order = self.chips - 1, []
        for d in sorted(range(1, far), key=lambda d: -bin(d).count("1")):
            for x in (d, far - d):
                if x not in order:
                    order.append(x)
        return order[:2] + [far] + order[2:]


def pack_kernel(plan, distances, place_ref, map_ref, obs_ref, prior_ref, noise_ref, *refs):
    refs = refs[-len(distances) - 3:]
    outs, (held, lines, sems) = dict(zip(distances, refs)), refs[len(distances):]
    pair, quad, core = place_ref[0], place_ref[1], place_ref[2]
    at = CORES * plan.map_rows
    data = [d for d in distances if d % plan.quads == 0]
    loads = {}
    for d in data:
        for j in range(CORES):
            freq = (CORES * (pair ^ (d // plan.quads)) + j) * plan.quads + quad
            loads[d, j] = pltpu.make_async_copy(obs_ref.at[freq], held.at[d // plan.quads, j], sems.at[d, j])
            loads[d, j].start()
    copies = []
    for d in distances:
        e, dq = divmod(d, plan.quads)
        for j in range(CORES):
            freq = (CORES * (pair ^ e) + j) * plan.quads + (quad ^ dq)
            to = outs[d].at[pl.ds(j * plan.map_rows, plan.map_rows)]
            copies.append(pltpu.make_async_copy(map_ref.at[freq], to, sems.at[d, CORES + j]))
            copies[-1].start()
    priors = [d for d in distances if 0 < d < plan.quads]
    if priors:
        half = prior_ref[pl.ds(pl.multiple_of(core * plan.share, plan.share), plan.share), :]
        for k in range(plan.per_block):
            lines[0, k * plan.share:(k + 1) * plan.share, :] = half[:, k * plan.cells:(k + 1) * plan.cells]
        size = plan.share * plan.per_block
        for d in priors:
            to = outs[d].at[pl.ds(at, size)]
            copies.append(pltpu.make_async_copy(lines.at[0, pl.ds(0, size)], to, sems.at[d, 2 * CORES]))
            copies[-1].start()
    if data:
        noise = noise_ref[...]
        high = noise.astype(bf16)
        low = (noise - high.astype(f32)).astype(bf16)
        wide = (8, plan.sensors)
        tail = jnp.concatenate([jnp.broadcast_to(high, wide), jnp.broadcast_to(low, wide)], 0)
    for d in data:
        e = d // plan.quads
        for j in range(CORES):
            loads[d, j].wait()
            re, im = held[e, j, 0], held[e, j, 1]
            for s in range(CORES):
                part = slice(s * HALF, (s + 1) * HALF)
                lines[1 + e, j * plan.sensors:(j + 1) * plan.sensors, s * LANES:(s + 1) * LANES] = (
                    jnp.concatenate([re[:, part], im[:, part]], 1).astype(bf16)
                )
        size = plan.extra(d)
        lines[1 + e, size - 16:size, :] = tail
        to = outs[d].at[pl.ds(at, size)]
        copies.append(pltpu.make_async_copy(lines.at[1 + e, pl.ds(0, size)], to, sems.at[d, 2 * CORES]))
        copies[-1].start()
    for copy in copies:
        copy.wait()


def gather_kernel(plan, place_ref, own_ref, *refs):
    mine, theirs = refs[:plan.chips], refs[plan.chips:2 * plan.chips]
    prior_ref, noise_ref, *streams = refs[2 * plan.chips:]
    quad, core = place_ref[1], place_ref[2]
    at = CORES * plan.map_rows
    share, cells, sensors = plan.share, plan.cells, plan.sensors
    for k in range(plan.per_block):
        column = k ^ (quad & (plan.per_block - 1))
        to = slice(k * cells, (k + 1) * cells)
        prior_ref[0, :, to] = own_ref[:, pl.ds(pl.multiple_of(column * cells, cells), cells)]
        for dq in range(1, plan.quads):
            span = pl.ds(pl.multiple_of(at + column * share, share), share)
            for part, ref in ((core, mine[dq]), (1 - core, theirs[dq])):
                prior_ref[dq, pl.ds(pl.multiple_of(part * share, share), share), to] = ref[span, :]
    row = lax.broadcasted_iota(jnp.int32, (sensors, sensors), 0)
    col = lax.broadcasted_iota(jnp.int32, (sensors, sensors), 1)
    lanes = pl.ds(pl.multiple_of(core * LANES, LANES), LANES)
    for e in range(plan.pairs):
        for s, refs_s in enumerate((mine, theirs)):
            ref, r = refs_s[e * plan.quads], CORES * e + s
            for j in range(CORES):
                streams[j][r] = ref[at + j * sensors:at + (j + 1) * sensors, lanes]
            both = ref[at + CORES * sensors:, :].astype(f32)
            noise_row = both[0:1, :] + both[8:9, :]
            noise = jnp.sum(jnp.where(row == col, noise_row, 0.0), 1, keepdims=True)
            noise_ref[r] = jnp.broadcast_to(noise, (sensors, LANES))


def sides(z):
    return jnp.concatenate([z, jnp.concatenate([z[:, HALF:], -z[:, :HALF]], 1)], 0).T


def source(plan, chunk, sides_ref, prior_ref, scale):
    out = []
    for block in range(plan.quads // plan.per_block):
        quads = range(block * plan.per_block, (block + 1) * plan.per_block)
        parts = []
        for dq in quads:
            u = jnp.zeros((LANES, plan.cells), f32)
            for r in range(plan.groups):
                u += dot(sides_ref[r], chunk(r, dq)[...])
            parts.append(u.astype(bf16))
        ub = jnp.concatenate(parts, 1)
        out += [(dot_nt(prior_ref[dq], ub) * scale).astype(bf16) for dq in quads]
    return out


def chunks(plan, refs, start):
    rows = pl.ds(start, plan.map_rows)
    return lambda r, dq: refs[(r % CORES) * plan.chips + r // CORES * plan.quads + dq].at[rows]


def step_kernel(plan, stage, start, n_pred, scale_ref, prior_ref, obs_ref, noise_ref, *refs):
    chunk, refs = chunks(plan, refs, start), refs[2 * plan.chips:]
    preds, refs = refs[:n_pred], refs[n_pred:]
    if stage > 0:
        next_ref, refs = refs[0], refs[1:]
    outs, sides_ref = refs[:-1], refs[-1]
    for r in range(plan.groups):
        obs = obs_ref[r].astype(f32)
        now = relax_step * obs
        if stage > 0:
            predicted = sum(p[r].astype(f32) for p in preds)
            now = now + relax_step * (obs - predicted - noise_ref[r] * now)
            next_ref[r] = now
        sides_ref[r] = sides(now.astype(bf16))
    sources = source(plan, chunk, sides_ref, prior_ref, scale_ref[0])
    turned = [jnp.concatenate([-v[:, HALF:], v[:, :HALF]], 1) for v in sources]
    for r in reversed(range(plan.groups)):
        total = jnp.zeros((plan.sensors, LANES), f32)
        for dq in range(plan.quads):
            block = chunk(r, dq)
            total += dot(block[:plan.sensors, :], sources[dq]) + dot(block[plan.sensors:, :], turned[dq])
        if len(outs) == 1:
            outs[0][r] = total.astype(bf16)
        else:
            outs[r // CORES][r % CORES] = total.astype(bf16)


def last_kernel(plan, e, n_pred, noise_ref, *refs):
    obs, held, refs = refs[:CORES], refs[CORES:2 * CORES], refs[2 * CORES:]
    preds, (keep_ref, give_ref) = refs[:CORES * n_pred], refs[CORES * n_pred:]
    for j in range(CORES):
        for s, out in ((1, give_ref), (0, keep_ref)):
            r = CORES * e + s
            now = held[j][r]
            predicted = sum(p[s].astype(f32) for p in preds[j * n_pred:(j + 1) * n_pred])
            now = now + relax_step * (obs[j][r].astype(f32) - predicted - noise_ref[r] * now)
            out[j] = now.astype(bf16)


def merge(flag, mine, theirs):
    low, high = jnp.where(flag, theirs, mine), jnp.where(flag, mine, theirs)
    re = jnp.concatenate([low[:, :HALF], high[:, :HALF]], 1)
    im = jnp.concatenate([low[:, HALF:], high[:, HALF:]], 1)
    return re, im


def send_kernel(quads, place_ref, keep_ref, got_ref, *refs):
    posts, outs = refs[:-quads], refs[-quads:]
    flag = place_ref[2] == 1
    for d, out in enumerate(outs):
        pieces = [(keep_ref[j], got_ref[j]) for j in range(CORES)]
        if posts:
            pieces.append((posts[0][d], posts[1][d]))
        for i, (mine, theirs) in enumerate(pieces):
            re, im = merge(flag, mine.astype(f32), theirs.astype(f32))
            out[i, :, :LANES] = re.astype(bf16)
            out[i, :, LANES:] = im.astype(bf16)


def post_kernel(plan, place_ref, scale_ref, prior_ref, *refs):
    maps, refs = refs[:2 * plan.chips], refs[2 * plan.chips:]
    keeps, gives, refs = refs[:plan.pairs], refs[plan.pairs:2 * plan.pairs], refs[2 * plan.pairs:]
    mine_ref, give_ref, sides_ref, held_ref = refs
    core = place_ref[2]
    for j in range(CORES):
        chunk = chunks(plan, maps, j * plan.map_rows)
        for r in range(plan.groups):
            sides_ref[r] = sides((gives if r % CORES else keeps)[r // CORES][j])
        for dq, v in enumerate(source(plan, chunk, sides_ref, prior_ref, scale_ref[j])):
            held_ref[j, dq] = v
    mine_ref[...] = held_ref[core]
    give_ref[...] = held_ref[1 - core]


def end_kernel(chips, quads, place_ref, *refs):
    came, (dual_out, post_out, dual_ref, post_ref, sems) = refs[:chips], refs[chips:]
    pair, quad = place_ref[0], place_ref[1]
    cells = post_ref.shape[1] // 2
    sends = []
    for chip in reversed(range(chips)):
        e, d = divmod(chip, quads)
        for j in range(CORES):
            freq = (CORES * (pair ^ e) + j) * quads + (quad ^ d)
            for part in range(2):
                dual_ref[chip, j, part] = came[chip][j, :, part * LANES:(part + 1) * LANES].astype(f32)
            sends.append(pltpu.make_async_copy(dual_ref.at[chip, j], dual_out.at[freq], sems.at[chip, j]))
            sends[-1].start()
        if e == 0:
            post_ref[d, pl.ds(0, cells, stride=2), :] = came[chip][CORES, :, :LANES].astype(f32)
            post_ref[d, pl.ds(1, cells, stride=2), :] = came[chip][CORES, :, LANES:].astype(f32)
            sends.append(pltpu.make_async_copy(post_ref.at[d], post_out.at[quad ^ d], sems.at[chip, CORES]))
            sends[-1].start()
    for copy in sends:
        copy.wait()


def on_device(forward_map, observed, noise_var, prior_rows, prior_scale):
    frequencies, halves, sensors, cells = forward_map.shape
    groups, quads, count = (lax.axis_size(a) for a in ("sensor", "quad", "side"))
    plan = Plan(groups, quads, sensors, cells, prior_rows.shape[1])
    pairs = plan.pairs
    me, quad = lax.axis_index("sensor"), lax.axis_index("quad")
    pair, core = me // CORES, me % CORES
    place = jnp.stack([pair, quad, core]).astype(jnp.int32)
    scales = jnp.stack([prior_scale[(CORES * pair + j) * quads + quad] for j in range(CORES)])
    both = ("sensor", "quad")

    def swap(x, axes, distance):
        return lax.ppermute(x, axes, [(i, i ^ distance) for i in range(lax.axis_size(axes))])

    def to_chip(x, d):
        e, dq = divmod(d, quads)
        return swap(x, both, CORES * e * quads + dq)

    def to_sibling(x):
        return swap(x, "sensor", 1)

    flat = forward_map.reshape(frequencies, halves * sensors, cells)
    line = max(plan.extra(d) for d in range(plan.chips))
    order, mine = plan.order(), [None] * plan.chips
    for distances, after in (([0] + order[:5], None), (order[5:], order[0])):
        messages = call(
            functools.partial(pack_kernel, plan, distances),
            [SMEM, ANY, ANY, VMEM, VMEM] + [ANY] * (after is not None),
            [shape((plan.rows(d), cells), bf16) for d in distances],
            [
                pltpu.VMEM((plan.pairs, CORES, halves, sensors, LANES), f32),
                pltpu.VMEM((1 + plan.pairs, line, cells), bf16),
                pltpu.SemaphoreType.DMA((plan.chips, 2 * CORES + 1)),
            ],
            [ANY] * len(distances),
            moved=2**20,
            limit=WHOLE_VMEM,
        )(place, flat, observed, prior_rows, noise_var.reshape(1, sensors), *([] if after is None else [mine[after]]))
        for d, message in zip(distances, messages):
            mine[d] = to_chip(message, d) if d else message
    maps = mine + [to_sibling(x) for x in mine]

    prior, noise, *streams = call(
        functools.partial(gather_kernel, plan),
        [SMEM] + [VMEM] * (1 + 2 * plan.chips),
        [shape((quads, cells, plan.width), bf16), shape((groups, sensors, LANES), f32)]
        + [shape((groups, sensors, LANES), bf16)] * CORES,
        moved=4 * 2**20,
    )(place, prior_rows, *maps)

    def over_sides(partial):
        if count == 2:
            return [partial, swap(partial, "side", 1)]
        return [lax.psum(partial, "side")]

    wide, narrow = shape((groups, sensors, LANES), f32), shape((groups, sensors, LANES), bf16)
    couple = shape((CORES, sensors, LANES), bf16)
    sides_scratch = pltpu.VMEM((groups, LANES, halves * sensors), bf16)

    def step(stage, j, preds):
        operands = [scales[j:j + 1], prior, streams[j], noise] + maps + preds
        return call(
            functools.partial(step_kernel, plan, stage, j * plan.map_rows, len(preds)),
            [SMEM] + [VMEM] * (len(operands) - 1),
            [narrow] if stage == 0 else [wide] + [couple] * plan.pairs,
            [sides_scratch],
            flops=2**31,
            moved=8 * 2**20,
        )(*operands)

    first = [over_sides(step(0, j, [])[0]) for j in range(CORES)]
    multiplier, partials = [], []
    for j in range(CORES):
        held, *parts = step(1, j, first[j])
        multiplier.append(held)
        partials.append(parts)
    keeps, gives = [None] * plan.pairs, [None] * plan.pairs
    duals = [None] * plan.chips
    for e in reversed(range(plan.pairs)):
        preds = [over_sides(partials[j][e]) for j in range(CORES)]
        preds = preds[0] + preds[1]
        keeps[e], gives[e] = call(
            functools.partial(last_kernel, plan, e, len(preds) // CORES),
            [VMEM] * (1 + 2 * CORES + len(preds)),
            [couple, couple],
            moved=2 * 2**20,
        )(noise, *streams, *multiplier, *preds)
        got, posts = to_sibling(gives[e]), []
        if e == 0:
            cut = shape((quads, cells, LANES), bf16)
            own, other = call(
                functools.partial(post_kernel, plan),
                [SMEM, SMEM] + [VMEM] * (1 + len(maps) + 2 * pairs),
                [cut, cut],
                [sides_scratch, pltpu.VMEM((CORES, quads, cells, LANES), bf16)],
                flops=2**31,
                moved=8 * 2**20,
            )(place, scales, prior, *maps, *keeps, *gives)
            posts = [own, to_sibling(other)]
        kinds = quads if e == 0 else 1
        messages = call(
            functools.partial(send_kernel, kinds),
            [SMEM] + [VMEM] * (2 + len(posts)),
            [shape((CORES + (e == 0), sensors, 2 * LANES), bf16)] * kinds,
            moved=2**20,
        )(place, keeps[e], got, *posts)
        for dq in reversed(range(quads)):
            d = e * quads + dq
            message = messages[dq] if e == 0 else messages[0]
            duals[d] = to_chip(message, d) if d else message
    dual, posterior = call(
        functools.partial(end_kernel, plan.chips, quads),
        [SMEM] + [VMEM] * plan.chips,
        [shape((frequencies, halves, sensors, LANES), f32), shape((quads, cells * 2, LANES), f32)],
        [
            pltpu.VMEM((plan.chips, CORES, halves, sensors, LANES), f32),
            pltpu.VMEM((quads, cells * 2, LANES), f32),
            pltpu.SemaphoreType.DMA((plan.chips, CORES + 1)),
        ],
        [ANY, ANY],
        moved=8 * 2**20,
    )(place, *duals)
    return dual, posterior.reshape(quads, cells, 2, LANES)


def solution(mesh):
    groups, space = mesh.devices.shape

    def run(forward_map, observed, noise_var, prior_rows, prior_scale):
        quads = forward_map.shape[0] // groups
        split = Mesh(mesh.devices.reshape(groups, space // quads, quads), ("sensor", "side", "quad"))
        return jax.shard_map(
            on_device,
            mesh=split,
            in_specs=(
                P(None, None, "sensor", ("side", "quad")),
                P(None, None, "sensor", None),
                P("sensor"),
                P(("side", "quad"), None),
                P(),
            ),
            out_specs=(P(None, None, "sensor", None), P("sensor", ("side", "quad"), None, None)),
            check_vma=False,
        )(forward_map, observed, noise_var, prior_rows, prior_scale)

    return run
```

time: 195 us -> 288 us (1.48)
  Pallas kernels: 38.7 us -> 168 us
  waiting for transfers between devices: 105 us -> 73.5 us
  local copies, waits for them, and re-layouts: 14 us -> 9.92 us
  starting transfers between devices: 36 us -> 33 us
    pallas_call x9 -> x10, Pallas kernels: 35.7 us -> 165 us  [the longest x2 132 us: on_device(): call(functools.partial(pack_kernel, plan, distances), [SMEM, ANY, ANY, VM...]
    ppermute x30 -> x31, waiting for transfers between devices: 96.3 us -> 73.5 us  [swap(): lax.ppermute(x, axes, [(i, i ^ distance) for i in range(lax.axis_size(axe...]
    ppermute x4 -> x0, waiting for transfers between devices: 8.76 us -> none  [on_device(): lax.ppermute(posts[i], both, post_route(groups, quads, *divmod(i, half)))]
    unnamed x34 -> x36, local copies, waits for them, and re-layouts: 13.4 us -> 9.27 us
    ppermute x30 -> x31, starting transfers between devices: 33.2 us -> 33 us  [swap(): lax.ppermute(x, axes, [(i, i ^ distance) for i in range(lax.axis_size(axe...]
  transfers between devices with their start and end apart: 34 -> 31, of which waited for: 13 -> 12; matrix products, arithmetic and copies ran while one was open for 0% -> 1% of each run, Pallas kernels for 13% -> 20%
where the time goes in v7:
time: 288 us; the launch traced here: 287 us
  Pallas kernels  168 us (58%)
  waiting for transfers between devices  73.5 us (26%)
  starting transfers between devices  33 us (11%)
  local copies, waits for them, and re-layouts  9.92 us (3%)
    pallas_call x2, Pallas kernels, on_device(): call(functools.partial(pack_kernel, plan, distances), [SMEM, ANY, ANY, VM...  132 us
    ppermute x31, waiting for transfers between devices, swap(): lax.ppermute(x, axes, [(i, i ^ distance) for i in range(lax.axis_size(axe...  73.5 us
    ppermute x31, starting transfers between devices, swap(): lax.ppermute(x, axes, [(i, i ^ distance) for i in range(lax.axis_size(axe...  33 us
    pallas_call x4, Pallas kernels, step(): call(functools.partial(step_kernel, plan, stage, j * plan.map_rows, len(p...  22.6 us
    unnamed x36, local copies, waits for them, and re-layouts  9.27 us
  transfers between devices with their start and end apart: 31, of which 12 were waited for; matrix products, arithmetic and copies ran while one was open for 1% of the time, Pallas kernels for 20%

profile of v7, /device:TPU:0, one launch (start us, length us, event | category | flops | bytes accessed | tf_op | source)
XLA Modules:
  0.0 287.0 jit_solution(8029503727452021975)
XLA Ops:
  1.3 97.7 %shard_map.68 = (bf16[1552,256]{1,0:T(8,128)(2,1)}, bf16[1280,256]{1,0:T(8,128)(2,1)}, bf16[1552,256]{1,0:T(8,128)(2,1)}, bf16[1024,256]{1,0:T(8,128)(2,1)}, bf1...) custom-call(s32[3]{0:T(128)} %pad_add_fusion.place_ref, bf16[16,512,256]{2,1,0:T(8,128)(2,1)} %bitcast.6, ...), custom_call_target="tpu_custom_call" | custom-call | bytes 1048576 | tf_op jit(solution)/shard_map/pallas_call | solution.py:302
  99.0 4.0 %collective-permute-start = (bf16[1280,256]{1,0:T(8,128)(2,1)}, bf16[1280,256]{1,0:T(8,128)(2,1)S(1)}, u32[]{:S(2)}, u32[]{:S(2)}) collective-permute-start(bf16[1280,256]{1,0:T(8,128)(2,1)} %get-tuple-element.33), channel_id=1, source_target_pairs={{0,3},{1,2},{2,1},{3,0},{8,11},{9,10},{10,9},{11,8},{16,19},{17,18... | collective-permute-start | bytes 1966088 | tf_op jit(solution)/shard_map/ppermute | solution.py:289
  103.0 1.5 collective-permute-start.3
  105.1 3.8 %collective-permute-start.6 = (bf16[1024,256]{1,0:T(8,128)(2,1)}, bf16[1024,256]{1,0:T(8,128)(2,1)S(1)}, u32[]{:S(2)}, u32[]{:S(2)}) collective-permute-start(bf16[1024,256]{1,0:T(8,128)(2,1)} %get-tuple-element.39), channel_id=1, source_target_pairs={{0,19},{1,18},{2,17},{3,16},{8,27},{9,26},{10,25},{11,24},{16,3},{... | collective-permute-start | bytes 1572872 | tf_op jit(solution)/shard_map/ppermute | solution.py:289
  108.9 9.9 %collective-permute-done.refs_0_.refs_3_ = bf16[1280,256]{1,0:T(8,128)(2,1)S(1)} collective-permute-done((bf16[1280,256]{1,0:T(8,128)(2,1)}, bf16[1280,256]{1,0:T(8,128)(2,1)S(1)}, u32[]{:S(2)}, u32[]{:S(2)}) %collective-permute-start) | collective-permute-done | bytes 655392 | tf_op jit(solution)/shard_map/ppermute | solution.py:289
  119.7 34.2 %shard_map.69 = (bf16[1024,256]{1,0:T(8,128)(2,1)}, bf16[1280,256]{1,0:T(8,128)(2,1)}) custom-call(s32[3]{0:T(128)} %pad_add_fusion.place_ref, bf16[16,512,256]{2,1,0:T(8,128)(2,1)} %bitcast.7, f32[16,2,256,128]{3,2,1,0:T(8,128)} %obs_ref.3, bf16[256,512]{1,0:T(8,128)(2,1)} %own_ref.1, f32[1,256]{1,0:T(1,128)} %bitcast.9, bf16[1280,256]{1,0:T(8,128)(2,1)} %copy-done), custom_call_target="tpu_custom_call" | custom-call | bytes 1048576 | tf_op jit(solution)/shard_map/pallas_call | solution.py:302
  153.9 2.0 collective-permute-start.1
  158.0 2.5 collective-permute-start.5
  162.6 8.1 %collective-permute-done.1.refs_1_ = bf16[1280,256]{1,0:T(8,128)(2,1)S(1)} collective-permute-done((bf16[1280,256]{1,0:T(8,128)(2,1)}, bf16[1280,256]{1,0:T(8,128)(2,1)S(1)}, u32[]{:S(2)}, u32[]{:S(2)}) %collective-permute-start.1) | collective-permute-done | bytes 655392 | tf_op jit(solution)/shard_map/ppermute | solution.py:289
  170.7 2.3 collective-permute-done.5.refs_6_
  173.7 1.6 collective-permute-done.13.refs_14_
  180.6 2.7 shard_map.70
  183.3 5.7 %shard_map.71.refs_16_ = bf16[4,256,128]{2,1,0:T(8,128)(2,1)S(1)} custom-call(f32[1]{0:T(128)} %get-tuple-element.63.scale_ref, bf16[4,256,512]{2,1,0:T(8,128)(2,1)S(1)} %get-tuple-element.43.prior_ref, bf16[4,256,128]{2,1,0:T(8,128)(2,1)S(1)} %get-tuple-element.41.obs_ref.refs_0_, f32[4,256,128]{2,1,0:T(8,128)S(1)} %get-tuple-element.40.noise_ref, ...), custom_call_target="tpu_custom_call" | custom-call | flops 2147483648 | bytes 8388608 | tf_op jit(solution)/shard_map/pallas_call | solution.py:338
  189.0 2.6 collective-permute-start.15
  191.6 5.6 %shard_map.73.refs_16_ = bf16[4,256,128]{2,1,0:T(8,128)(2,1)S(1)} custom-call(f32[1]{0:T(128)} %get-tuple-element.62.scale_ref, bf16[4,256,512]{2,1,0:T(8,128)(2,1)S(1)} %get-tuple-element.43.prior_ref, bf16[4,256,128]{2,1,0:T(8,128)(2,1)S(1)} %get-tuple-element.42.obs_ref.refs_1_, f32[4,256,128]{2,1,0:T(8,128)S(1)} %get-tuple-element.40.noise_ref, ...), custom_call_target="tpu_custom_call" | custom-call | flops 2147483648 | bytes 8388608 | tf_op jit(solution)/shard_map/pallas_call | solution.py:338
  197.7 12.7 %collective-permute-done.15.refs_17_ = bf16[4,256,128]{2,1,0:T(8,128)(2,1)S(1)} collective-permute-done((bf16[4,256,128]{2,1,0:T(8,128)(2,1)S(1)}, bf16[4,256,128]{2,1,0:T(8,128)(2,1)S(1)}, u32[]{:S(2)}, u32[]{:S(2)}) %collective-permute-start.15) | collective-permute-done | bytes 262176 | tf_op jit(solution)/shard_map/ppermute | solution.py:289
  210.4 5.7 %shard_map.72 = (f32[4,256,128]{2,1,0:T(8,128)S(1)}, bf16[2,256,128]{2,1,0:T(8,128)(2,1)S(1)}, bf16[2,256,128]{2,1,0:T(8,128)(2,1)S(1)}) custom-call(f32[1]{0:T(128)} %get-tuple-element.63.scale_ref, bf16[4,256,512]{2,1,0:T(8,128)(2,1)S(1)} %get-tuple-element.43.prior_ref, bf16[4,256,128]{2,1,0:T(8,128)(2,1)S(1)} %get-tuple-element.41.obs_ref.refs_0_, ...), custom_call_target="tpu_custom_call" | custom-call | flops 2147483648 | bytes 8388608 | tf_op jit(solution)/shard_map/pallas_call | solution.py:338
  216.2 5.6 %shard_map.74 = (f32[4,256,128]{2,1,0:T(8,128)S(1)}, bf16[2,256,128]{2,1,0:T(8,128)(2,1)S(1)}, bf16[2,256,128]{2,1,0:T(8,128)(2,1)S(1)}) custom-call(f32[1]{0:T(128)} %get-tuple-element.62.scale_ref, bf16[4,256,512]{2,1,0:T(8,128)(2,1)S(1)} %get-tuple-element.43.prior_ref, bf16[4,256,128]{2,1,0:T(8,128)(2,1)S(1)} %get-tuple-element.42.obs_ref.refs_1_, ...), custom_call_target="tpu_custom_call" | custom-call | flops 2147483648 | bytes 8388608 | tf_op jit(solution)/shard_map/pallas_call | solution.py:338
  221.8 3.0 %collective-permute-start.21 = (bf16[2,256,128]{2,1,0:T(8,128)(2,1)S(1)}, bf16[2,256,128]{2,1,0:T(8,128)(2,1)S(1)}, u32[]{:S(2)}, u32[]{:S(2)}) collective-permute-start(bf16[2,256,128]{2,1,0:T(8,128)(2,1)S(1)} %get-tuple-element.51.refs_6_), channel_id=1, source_target_pairs={{0,4},{4,0},{1,5},{5,1},{2,6},{6,2},{3,7},{7,3},{8,12},{12,8},{9,1... | collective-permute-start | bytes 393224 | tf_op jit(solution)/shard_map/ppermute | solution.py:289
  224.8 2.8 collective-permute-start.18
  229.0 8.6 %collective-permute-done.21.refs_7_ = bf16[2,256,128]{2,1,0:T(8,128)(2,1)S(1)} collective-permute-done((bf16[2,256,128]{2,1,0:T(8,128)(2,1)S(1)}, bf16[2,256,128]{2,1,0:T(8,128)(2,1)S(1)}, u32[]{:S(2)}, u32[]{:S(2)}) %collective-permute-start.21) | collective-permute-done | bytes 131104 | tf_op jit(solution)/shard_map/ppermute | solution.py:289
  238.0 2.2 collective-permute-done.17.refs_5_
  240.2 1.4 collective-permute-done.18.refs_7_
  241.7 5.0 %shard_map.77 = (bf16[4,256,128]{2,1,0:T(8,128)(2,1)S(1)}, bf16[4,256,128]{2,1,0:T(8,128)(2,1)S(1)}) custom-call(s32[3]{0:T(128)S(1)} %copy-done.16, f32[2]{0:T(128)S(1)} %pad_maximum_fusion.scale_ref, bf16[4,256,512]{2,1,0:T(8,128)(2,1)S(1)} %get-tuple-element.43.prior_ref, bf16[1552,256]{1,0:T(8,128)(2,1)S(1)} %copy-done.3, ...), custom_call_target="tpu_custom_call" | custom-call | flops 2147483648 | bytes 8388608 | tf_op jit(solution)/shard_map/pallas_call | solution.py:367
  248.0 1.6 collective-permute-start.27
  251.4 1.5 collective-permute-start.23
  252.9 2.0 collective-permute-start.25
  254.9 2.3 collective-permute-done.27.refs_4_
  258.0 4.4 %collective-permute-done.28.refs_5_ = bf16[2,256,256]{2,1,0:T(8,128)(2,1)S(1)} collective-permute-done((bf16[2,256,256]{2,1,0:T(8,128)(2,1)S(1)}, bf16[2,256,256]{2,1,0:T(8,128)(2,1)S(1)}, u32[]{:S(2)}, u32[]{:S(2)}) %collective-permute-start.28) | collective-permute-done | bytes 262176 | tf_op jit(solution)/shard_map/ppermute | solution.py:289
  263.7 16.2 %collective-permute-done.29.refs_6_ = bf16[2,256,256]{2,1,0:T(8,128)(2,1)S(1)} collective-permute-done((bf16[2,256,256]{2,1,0:T(8,128)(2,1)S(1)}, bf16[2,256,256]{2,1,0:T(8,128)(2,1)S(1)}, u32[]{:S(2)}, u32[]{:S(2)}) %collective-permute-start.29) | collective-permute-done | bytes 262176 | tf_op jit(solution)/shard_map/ppermute | solution.py:289
  280.0 3.8 %collective-permute-done.30.refs_7_ = bf16[2,256,256]{2,1,0:T(8,128)(2,1)S(1)} collective-permute-done((bf16[2,256,256]{2,1,0:T(8,128)(2,1)S(1)}, bf16[2,256,256]{2,1,0:T(8,128)(2,1)S(1)}, u32[]{:S(2)}, u32[]{:S(2)}) %collective-permute-start.30) | collective-permute-done | bytes 262176 | tf_op jit(solution)/shard_map/ppermute | solution.py:289
  283.8 3.1 %shard_map.80 = (f32[16,2,256,128]{3,2,1,0:T(8,128)}, f32[4,512,128]{2,1,0:T(8,128)}) custom-call(s32[3]{0:T(128)S(1)} %copy-done.16, bf16[3,256,256]{2,1,0:T(8,128)(2,1)S(1)} %get-tuple-element.56.refs_0_, bf16[3,256,256]{2,1,0:T(8,128)(2,1)S(1)} %collective-permute-done.23.refs_1_, bf16[3,256,256]{2,1,0:T(8,128)(2,1)S(1)} %collective-permute-done.24.refs_2_, ...), custom_call_target="tpu_custom_call" | custom-call | bytes 8388608 | tf_op jit(solution)/shard_map/pallas_call | solution.py:387
  (82 shorter events, 19.9 us)
Async XLA Ops:
  99.0 19.8 %collective-permute-start = (bf16[1280,256]{1,0:T(8,128)(2,1)}, bf16[1280,256]{1,0:T(8,128)(2,1)S(1)}, u32[]{:S(2)}, u32[]{:S(2)}) collective-permute-start(bf16[1280,256]{1,0:T(8,128)(2,1)} %get-tuple-element.33), channel_id=1, source_target_pairs={{0,3},{1,2},{2,1},{3,0},{8,11},{9,10},{10,9},{11,8},{16,19},{17,18... | collective-permute-start | bytes 1966088 | tf_op jit(solution)/shard_map/ppermute | solution.py:289
  103.0 55.0 %collective-permute-start.3 = (bf16[1552,256]{1,0:T(8,128)(2,1)}, bf16[1552,256]{1,0:T(8,128)(2,1)S(1)}, u32[]{:S(2)}, u32[]{:S(2)}) collective-permute-start(bf16[1552,256]{1,0:T(8,128)(2,1)} %get-tuple-element.36), channel_id=1, source_target_pairs={{0,16},{1,17},{2,18},{3,19},{8,24},{9,25},{10,26},{11,27},{16,0},{... | collective-permute-start | bytes 2383880 | tf_op jit(solution)/shard_map/ppermute | solution.py:289
  104.5 52.2 %collective-permute-start.2 = (bf16[1280,256]{1,0:T(8,128)(2,1)}, bf16[1280,256]{1,0:T(8,128)(2,1)}, u32[]{:S(2)}, u32[]{:S(2)}) collective-permute-start(bf16[1280,256]{1,0:T(8,128)(2,1)} %get-tuple-element.35), channel_id=1, source_target_pairs={{0,2},{1,3},{2,0},{3,1},{8,10},{9,11},{10,8},{11,9},{16,18},{17,19... | collective-permute-start | bytes 1966088 | tf_op jit(solution)/shard_map/ppermute | solution.py:289
  105.0 48.9 %collective-permute-start.4 = (bf16[1024,256]{1,0:T(8,128)(2,1)}, bf16[1024,256]{1,0:T(8,128)(2,1)S(1)}, u32[]{:S(2)}, u32[]{:S(2)}) collective-permute-start(bf16[1024,256]{1,0:T(8,128)(2,1)} %get-tuple-element.37), channel_id=1, source_target_pairs={{0,17},{1,16},{2,19},{3,18},{8,25},{9,24},{10,27},{11,26},{16,1},{... | collective-permute-start | bytes 1572872 | tf_op jit(solution)/shard_map/ppermute | solution.py:289
  105.1 50.7 %collective-permute-start.6 = (bf16[1024,256]{1,0:T(8,128)(2,1)}, bf16[1024,256]{1,0:T(8,128)(2,1)S(1)}, u32[]{:S(2)}, u32[]{:S(2)}) collective-permute-start(bf16[1024,256]{1,0:T(8,128)(2,1)} %get-tuple-element.39), channel_id=1, source_target_pairs={{0,19},{1,18},{2,17},{3,16},{8,27},{9,26},{10,25},{11,24},{16,3},{... | collective-permute-start | bytes 1572872 | tf_op jit(solution)/shard_map/ppermute | solution.py:289
  118.8 56.5 %copy-start.16 = (s32[3]{0:T(128)S(1)}, s32[3]{0:T(128)}, u32[]{:S(2)}) copy-start(s32[3]{0:T(128)} %pad_add_fusion.place_ref) | copy-start | bytes 40
  118.8 41.7 %collective-permute-start.7 = (bf16[1552,256]{1,0:T(8,128)(2,1)}, bf16[1552,256]{1,0:T(8,128)(2,1)S(1)}, u32[]{:S(2)}, u32[]{:S(2)}) collective-permute-start(bf16[1552,256]{1,0:T(8,128)(2,1)} %get-tuple-element.32.refs_0_), channel_id=1, source_target_pairs={{0,8},{8,0},{16,24},{24,16},{1,9},{9,1},{17,25},{25,17},{2,10},{10... | collective-permute-start | bytes 2383880 | tf_op jit(solution)/shard_map/ppermute | solution.py:289
  153.9 16.9 %collective-permute-start.1 = (bf16[1280,256]{1,0:T(8,128)(2,1)}, bf16[1280,256]{1,0:T(8,128)(2,1)S(1)}, u32[]{:S(2)}, u32[]{:S(2)}) collective-permute-start(bf16[1280,256]{1,0:T(8,128)(2,1)} %get-tuple-element.34), channel_id=1, source_target_pairs={{0,1},{1,0},{2,3},{3,2},{8,9},{9,8},{10,11},{11,10},{16,17},{17,16... | collective-permute-start | bytes 1966088 | tf_op jit(solution)/shard_map/ppermute | solution.py:289
  155.9 4.6 %collective-permute-start.12 = (bf16[1024,256]{1,0:T(8,128)(2,1)S(1)}, bf16[1024,256]{1,0:T(8,128)(2,1)S(1)}, u32[]{:S(2)}, u32[]{:S(2)}) collective-permute-start(bf16[1024,256]{1,0:T(8,128)(2,1)S(1)} %collective-permute-done.4.refs_5_), channel_id=1, source_target_pairs={{0,8},{8,0},{16,24},{24,16},{1,9},{9,1},{17,25},{25,17},{2,10},{10... | collective-permute-start | bytes 1572872 | tf_op jit(solution)/shard_map/ppermute | solution.py:289
  156.7 5.1 %collective-permute-start.14 = (bf16[1024,256]{1,0:T(8,128)(2,1)S(1)}, bf16[1024,256]{1,0:T(8,128)(2,1)S(1)}, u32[]{:S(2)}, u32[]{:S(2)}) collective-permute-start(bf16[1024,256]{1,0:T(8,128)(2,1)S(1)} %collective-permute-done.6.refs_7_), channel_id=1, source_target_pairs={{0,8},{8,0},{16,24},{24,16},{1,9},{9,1},{17,25},{25,17},{2,10},{10... | collective-permute-start | bytes 1572872 | tf_op jit(solution)/shard_map/ppermute | solution.py:289
  158.0 15.0 %collective-permute-start.5 = (bf16[1024,256]{1,0:T(8,128)(2,1)}, bf16[1024,256]{1,0:T(8,128)(2,1)}, u32[]{:S(2)}, u32[]{:S(2)}) collective-permute-start(bf16[1024,256]{1,0:T(8,128)(2,1)} %get-tuple-element.38), channel_id=1, source_target_pairs={{0,18},{1,19},{2,16},{3,17},{8,26},{9,27},{10,24},{11,25},{16,2},{... | collective-permute-start | bytes 1572872 | tf_op jit(solution)/shard_map/ppermute | solution.py:289
  160.5 13.2 %collective-permute-start.11 = (bf16[1552,256]{1,0:T(8,128)(2,1)S(1)}, bf16[1552,256]{1,0:T(8,128)(2,1)}, u32[]{:S(2)}, u32[]{:S(2)}) collective-permute-start(bf16[1552,256]{1,0:T(8,128)(2,1)S(1)} %collective-permute-done.3.refs_4_), channel_id=1, source_target_pairs={{0,8},{8,0},{16,24},{24,16},{1,9},{9,1},{17,25},{25,17},{2,10},{10... | collective-permute-start | bytes 2383880 | tf_op jit(solution)/shard_map/ppermute | solution.py:289
  161.3 12.4 %collective-permute-start.9 = (bf16[1280,256]{1,0:T(8,128)(2,1)}, bf16[1280,256]{1,0:T(8,128)(2,1)}, u32[]{:S(2)}, u32[]{:S(2)}) collective-permute-start(bf16[1280,256]{1,0:T(8,128)(2,1)} %collective-permute-done.2.refs_2_), channel_id=1, source_target_pairs={{0,8},{8,0},{16,24},{24,16},{1,9},{9,1},{17,25},{25,17},{2,10},{10... | collective-permute-start | bytes 1966088 | tf_op jit(solution)/shard_map/ppermute | solution.py:289
  162.6 11.1 %collective-permute-start.10 = (bf16[1280,256]{1,0:T(8,128)(2,1)}, bf16[1280,256]{1,0:T(8,128)(2,1)}, u32[]{:S(2)}, u32[]{:S(2)}) collective-permute-start(bf16[1280,256]{1,0:T(8,128)(2,1)} %copy-done), channel_id=1, source_target_pairs={{0,8},{8,0},{16,24},{24,16},{1,9},{9,1},{17,25},{25,17},{2,10},{10... | collective-permute-start | bytes 1966088 | tf_op jit(solution)/shard_map/ppermute | solution.py:289
  170.7 4.6 %collective-permute-start.8 = (bf16[1280,256]{1,0:T(8,128)(2,1)S(1)}, bf16[1280,256]{1,0:T(8,128)(2,1)}, u32[]{:S(2)}, u32[]{:S(2)}) collective-permute-start(bf16[1280,256]{1,0:T(8,128)(2,1)S(1)} %collective-permute-done.1.refs_1_), channel_id=1, source_target_pairs={{0,8},{8,0},{16,24},{24,16},{1,9},{9,1},{17,25},{25,17},{2,10},{10... | collective-permute-start | bytes 1966088 | tf_op jit(solution)/shard_map/ppermute | solution.py:289
  173.1 2.3 collective-permute-start.13
  189.0 21.4 %collective-permute-start.15 = (bf16[4,256,128]{2,1,0:T(8,128)(2,1)S(1)}, bf16[4,256,128]{2,1,0:T(8,128)(2,1)S(1)}, u32[]{:S(2)}, u32[]{:S(2)}) collective-permute-start(bf16[4,256,128]{2,1,0:T(8,128)(2,1)S(1)} %shard_map.71.refs_16_), channel_id=1, source_target_pairs={{0,4},{4,0},{1,5},{5,1},{2,6},{6,2},{3,7},{7,3},{8,12},{12,8},{9,1... | collective-permute-start | bytes 786440 | tf_op jit(solution)/shard_map/ppermute | solution.py:289
  197.3 18.9 %collective-permute-start.16 = (bf16[4,256,128]{2,1,0:T(8,128)(2,1)S(1)}, bf16[4,256,128]{2,1,0:T(8,128)(2,1)S(1)}, u32[]{:S(2)}, u32[]{:S(2)}) collective-permute-start(bf16[4,256,128]{2,1,0:T(8,128)(2,1)S(1)} %shard_map.73.refs_16_), channel_id=1, source_target_pairs={{0,4},{4,0},{1,5},{5,1},{2,6},{6,2},{3,7},{7,3},{8,12},{12,8},{9,1... | collective-permute-start | bytes 786440 | tf_op jit(solution)/shard_map/ppermute | solution.py:289
  216.1 12.9 %collective-permute-start.20 = (bf16[2,256,128]{2,1,0:T(8,128)(2,1)S(1)}, bf16[2,256,128]{2,1,0:T(8,128)(2,1)S(1)}, u32[]{:S(2)}, u32[]{:S(2)}) collective-permute-start(bf16[2,256,128]{2,1,0:T(8,128)(2,1)S(1)} %get-tuple-element.50.refs_4_), channel_id=1, source_target_pairs={{0,4},{4,0},{1,5},{5,1},{2,6},{6,2},{3,7},{7,3},{8,12},{12,8},{9,1... | collective-permute-start | bytes 393224 | tf_op jit(solution)/shard_map/ppermute | solution.py:289
  221.8 15.8 %collective-permute-start.21 = (bf16[2,256,128]{2,1,0:T(8,128)(2,1)S(1)}, bf16[2,256,128]{2,1,0:T(8,128)(2,1)S(1)}, u32[]{:S(2)}, u32[]{:S(2)}) collective-permute-start(bf16[2,256,128]{2,1,0:T(8,128)(2,1)S(1)} %get-tuple-element.51.refs_6_), channel_id=1, source_target_pairs={{0,4},{4,0},{1,5},{5,1},{2,6},{6,2},{3,7},{7,3},{8,12},{12,8},{9,1... | collective-permute-start | bytes 393224 | tf_op jit(solution)/shard_map/ppermute | solution.py:289
  224.7 15.4 %collective-permute-start.17 = (bf16[2,256,128]{2,1,0:T(8,128)(2,1)S(1)}, bf16[2,256,128]{2,1,0:T(8,128)(2,1)S(1)}, u32[]{:S(2)}, u32[]{:S(2)}) collective-permute-start(bf16[2,256,128]{2,1,0:T(8,128)(2,1)S(1)} %get-tuple-element.46.refs_4_), channel_id=1, source_target_pairs={{0,4},{4,0},{1,5},{5,1},{2,6},{6,2},{3,7},{7,3},{8,12},{12,8},{9,1... | collective-permute-start | bytes 393224 | tf_op jit(solution)/shard_map/ppermute | solution.py:289
  224.8 16.8 %collective-permute-start.18 = (bf16[2,256,128]{2,1,0:T(8,128)(2,1)S(1)}, bf16[2,256,128]{2,1,0:T(8,128)(2,1)S(1)}, u32[]{:S(2)}, u32[]{:S(2)}) collective-permute-start(bf16[2,256,128]{2,1,0:T(8,128)(2,1)S(1)} %get-tuple-element.47.refs_6_), channel_id=1, source_target_pairs={{0,4},{4,0},{1,5},{5,1},{2,6},{6,2},{3,7},{7,3},{8,12},{12,8},{9,1... | collective-permute-start | bytes 393224 | tf_op jit(solution)/shard_map/ppermute | solution.py:289
  237.7 9.6 %collective-permute-start.26 = (bf16[2,256,128]{2,1,0:T(8,128)(2,1)S(1)}, bf16[2,256,128]{2,1,0:T(8,128)(2,1)S(1)}, u32[]{:S(2)}, u32[]{:S(2)}) collective-permute-start(bf16[2,256,128]{2,1,0:T(8,128)(2,1)S(1)} %get-tuple-element.53.refs_19_), channel_id=1, source_target_pairs={{0,8},{8,0},{16,24},{24,16},{1,9},{9,1},{17,25},{25,17},{2,10},{10... | collective-permute-start | bytes 393224 | tf_op jit(solution)/shard_map/ppermute | solution.py:289
  246.8 3.4 %collective-permute-start.22 = (bf16[4,256,128]{2,1,0:T(8,128)(2,1)S(1)}, bf16[4,256,128]{2,1,0:T(8,128)(2,1)S(1)}, u32[]{:S(2)}, u32[]{:S(2)}) collective-permute-start(bf16[4,256,128]{2,1,0:T(8,128)(2,1)S(1)} %get-tuple-element.55), channel_id=1, source_target_pairs={{0,8},{8,0},{16,24},{24,16},{1,9},{9,1},{17,25},{25,17},{2,10},{10... | collective-permute-start | bytes 786440 | tf_op jit(solution)/shard_map/ppermute | solution.py:289
  246.8 3.3 %collective-permute-start.19 = (bf16[2,256,128]{2,1,0:T(8,128)(2,1)S(1)}, bf16[2,256,128]{2,1,0:T(8,128)(2,1)S(1)}, u32[]{:S(2)}, u32[]{:S(2)}) collective-permute-start(bf16[2,256,128]{2,1,0:T(8,128)(2,1)S(1)} %get-tuple-element.49.refs_18_), channel_id=1, source_target_pairs={{0,8},{8,0},{16,24},{24,16},{1,9},{9,1},{17,25},{25,17},{2,10},{10... | collective-permute-start | bytes 393224 | tf_op jit(solution)/shard_map/ppermute | solution.py:289
  248.0 9.2 %collective-permute-start.27 = (bf16[2,256,256]{2,1,0:T(8,128)(2,1)S(1)}, bf16[2,256,256]{2,1,0:T(8,128)(2,1)S(1)}, u32[]{:S(2)}, u32[]{:S(2)}) collective-permute-start(bf16[2,256,256]{2,1,0:T(8,128)(2,1)S(1)} %shard_map.79), channel_id=1, source_target_pairs={{0,16},{1,17},{2,18},{3,19},{8,24},{9,25},{10,26},{11,27},{16,0},{... | collective-permute-start | bytes 786440 | tf_op jit(solution)/shard_map/ppermute | solution.py:289
  249.6 12.8 %collective-permute-start.28 = (bf16[2,256,256]{2,1,0:T(8,128)(2,1)S(1)}, bf16[2,256,256]{2,1,0:T(8,128)(2,1)S(1)}, u32[]{:S(2)}, u32[]{:S(2)}) collective-permute-start(bf16[2,256,256]{2,1,0:T(8,128)(2,1)S(1)} %shard_map.79), channel_id=1, source_target_pairs={{0,17},{1,16},{2,19},{3,18},{8,25},{9,24},{10,27},{11,26},{16,1},{... | collective-permute-start | bytes 786440 | tf_op jit(solution)/shard_map/ppermute | solution.py:289
  251.4 32.4 %collective-permute-start.23 = (bf16[3,256,256]{2,1,0:T(8,128)(2,1)S(1)}, bf16[3,256,256]{2,1,0:T(8,128)(2,1)S(1)}, u32[]{:S(2)}, u32[]{:S(2)}) collective-permute-start(bf16[3,256,256]{2,1,0:T(8,128)(2,1)S(1)} %get-tuple-element.57), channel_id=1, source_target_pairs={{0,1},{1,0},{2,3},{3,2},{8,9},{9,8},{10,11},{11,10},{16,17},{17,16... | collective-permute-start | bytes 1179656 | tf_op jit(solution)/shard_map/ppermute | solution.py:289
  252.9 30.8 %collective-permute-start.24 = (bf16[3,256,256]{2,1,0:T(8,128)(2,1)S(1)}, bf16[3,256,256]{2,1,0:T(8,128)(2,1)S(1)}, u32[]{:S(2)}, u32[]{:S(2)}) collective-permute-start(bf16[3,256,256]{2,1,0:T(8,128)(2,1)S(1)} %get-tuple-element.58), channel_id=1, source_target_pairs={{0,2},{1,3},{2,0},{3,1},{8,10},{9,11},{10,8},{11,9},{16,18},{17,19... | collective-permute-start | bytes 1179656 | tf_op jit(solution)/shard_map/ppermute | solution.py:289
  252.9 30.8 %collective-permute-start.25 = (bf16[3,256,256]{2,1,0:T(8,128)(2,1)S(1)}, bf16[3,256,256]{2,1,0:T(8,128)(2,1)S(1)}, u32[]{:S(2)}, u32[]{:S(2)}) collective-permute-start(bf16[3,256,256]{2,1,0:T(8,128)(2,1)S(1)} %get-tuple-element.59), channel_id=1, source_target_pairs={{0,3},{1,2},{2,1},{3,0},{8,11},{9,10},{10,9},{11,8},{16,19},{17,18... | collective-permute-start | bytes 1179656 | tf_op jit(solution)/shard_map/ppermute | solution.py:289
  257.2 22.7 %collective-permute-start.29 = (bf16[2,256,256]{2,1,0:T(8,128)(2,1)S(1)}, bf16[2,256,256]{2,1,0:T(8,128)(2,1)S(1)}, u32[]{:S(2)}, u32[]{:S(2)}) collective-permute-start(bf16[2,256,256]{2,1,0:T(8,128)(2,1)S(1)} %shard_map.79), channel_id=1, source_target_pairs={{0,18},{1,19},{2,16},{3,17},{8,26},{9,27},{10,24},{11,25},{16,2},{... | collective-permute-start | bytes 786440 | tf_op jit(solution)/shard_map/ppermute | solution.py:289
  262.4 21.3 %collective-permute-start.30 = (bf16[2,256,256]{2,1,0:T(8,128)(2,1)S(1)}, bf16[2,256,256]{2,1,0:T(8,128)(2,1)S(1)}, u32[]{:S(2)}, u32[]{:S(2)}) collective-permute-start(bf16[2,256,256]{2,1,0:T(8,128)(2,1)S(1)} %shard_map.79), channel_id=1, source_target_pairs={{0,19},{1,18},{2,17},{3,16},{8,27},{9,26},{10,25},{11,24},{16,3},{... | collective-permute-start | bytes 786440 | tf_op jit(solution)/shard_map/ppermute | solution.py:289
  (17 other events, 203.4 us)

commit v8 on v6

--- a/solution.py
+++ b/solution.py
@@ -24,9 +24,10 @@
     return jax.ShapeDtypeStruct(dims, dtype)
 
 
-def call(kernel, in_specs, out_shape, scratch=(), out_specs=None, flops=0, moved=0):
+def call(kernel, in_specs, out_shape, scratch=(), out_specs=None, flops=0, moved=0, aliases=None):
     return pl.pallas_call(
         kernel,
+        input_output_aliases=aliases or {},
         in_specs=in_specs,
         out_specs=out_specs or [VMEM] * len(out_shape),
         out_shape=out_shape,
@@ -98,7 +99,7 @@
         noise_ref[me ^ d] = jnp.broadcast_to(noise, (sensors, LANES))
 
 
-def source(map_ref, sides_ref, prior_ref, scale, ready=None):
+def source(map_ref, sides_ref, prior_ref, scale):
     groups, quads, _, cells = map_ref.shape
     per_block = prior_ref.shape[2] // cells
     out = []
@@ -108,8 +109,6 @@
         for q in members:
             u = jnp.zeros((sides_ref.shape[1], cells), f32)
             for g in range(groups):
-                if ready is not None:
-                    ready(g, q)
                 u += dot(sides_ref[g], map_ref[g, q])
             parts.append(u.astype(bf16))
         ub = jnp.concatenate(parts, 1)
@@ -122,18 +121,15 @@
     return jnp.concatenate([z, jnp.concatenate([z[:, half:], -z[:, :half]], 1)], 0).T
 
 
-def step_kernel(stage, load, n_pred, place_ref, scale_ref, map_ref, prior_ref, obs_ref, noise_ref, *refs):
+def bring_kernel(map_ref, out_ref, sem):
+    copy = pltpu.make_async_copy(map_ref, out_ref, sem)
+    copy.start()
+    copy.wait()
+
+
+def step_kernel(stage, n_pred, place_ref, scale_ref, map_ref, prior_ref, obs_ref, noise_ref, *refs):
     groups, quads, double, _ = map_ref.shape
     sensors = double // 2
-    ready = None
-    if load:
-        copy_ref, sems, refs = refs[1], refs[3], refs[:1] + refs[2:3]
-        copies = {}
-        for q in range(quads):
-            for g in range(groups):
-                copies[g, q] = pltpu.make_async_copy(map_ref.at[g, q], copy_ref.at[g, q], sems.at[g, q])
-                copies[g, q].start()
-        map_ref, ready = copy_ref, lambda g, q: copies[g, q].wait()
     preds, refs = refs[:n_pred], refs[n_pred:]
     if stage > 0:
         next_ref, refs = refs[0], refs[1:]
@@ -146,7 +142,7 @@
             now = now + relax_step * (obs - predicted - noise_ref[g] * now)
             next_ref[g] = now
         sides_ref[g] = sides(now.astype(bf16))
-    sources = source(map_ref, sides_ref, prior_ref, scale_ref[0], ready)
+    sources = source(map_ref, sides_ref, prior_ref, scale_ref[0])
     turned = [jnp.concatenate([-v[:, HALF:], v[:, :HALF]], 1) for v in sources]
     for e in reversed(range(groups // CORES)):
         for core in range(CORES):
@@ -184,7 +180,7 @@
 
 
 def post_kernel(pairs, place_ref, scale_ref, map_ref, prior_ref, *refs):
-    keeps, gives, refs = refs[:pairs], refs[pairs:2 * pairs], refs[2 * pairs:]
+    keeps, gives, refs = refs[:pairs], refs[pairs:2 * pairs], refs[2 * pairs + 1:]
     outs, (sides_ref, held_ref) = refs[:-2], refs[-2:]
     for e in range(pairs):
         first = CORES * (place_ref[0] ^ e)
@@ -196,23 +192,24 @@
         out[...] = held_ref[place_ref[1] ^ d]
 
 
-def end_kernel(chips, quads, place_ref, *refs):
-    came, (dual_out, post_out, dual_ref, post_ref, sems) = refs[:chips], refs[chips:]
+def end_kernel(e, quads, follows, place_ref, *refs):
+    came, refs = refs[:quads], refs[quads + follows:]
+    dual_out, dual_ref, sems, *post = refs if e else refs[:1] + refs[2:4] + refs[1:2] + refs[4:]
     pair, quad = place_ref[0], place_ref[1]
-    cells = post_ref.shape[1] // 2
     sends = []
-    for chip in reversed(range(chips)):
-        e, d = divmod(chip, quads)
+    for d in reversed(range(quads)):
         for core in range(CORES):
             freq = (CORES * (pair ^ e) + core) * quads + (quad ^ d)
             for part in range(2):
-                dual_ref[chip, core, part] = came[chip][core, :, part * LANES:(part + 1) * LANES].astype(f32)
-            sends.append(pltpu.make_async_copy(dual_ref.at[chip, core], dual_out.at[freq], sems.at[chip, core]))
+                dual_ref[d, core, part] = came[d][core, :, part * LANES:(part + 1) * LANES].astype(f32)
+            sends.append(pltpu.make_async_copy(dual_ref.at[d, core], dual_out.at[freq], sems.at[d, core]))
             sends[-1].start()
         if e == 0:
-            post_ref[d, pl.ds(0, cells, stride=2), :] = came[chip][CORES, :, :LANES].astype(f32)
-            post_ref[d, pl.ds(1, cells, stride=2), :] = came[chip][CORES, :, LANES:].astype(f32)
-            sends.append(pltpu.make_async_copy(post_ref.at[d], post_out.at[quad ^ d], sems.at[chip, CORES]))
+            post_out, post_ref = post
+            cells = post_ref.shape[1] // 2
+            post_ref[d, pl.ds(0, cells, stride=2), :] = came[d][CORES, :, :LANES].astype(f32)
+            post_ref[d, pl.ds(1, cells, stride=2), :] = came[d][CORES, :, LANES:].astype(f32)
+            sends.append(pltpu.make_async_copy(post_ref.at[d], post_out.at[quad ^ d], sems.at[d, CORES]))
             sends[-1].start()
     for copy in sends:
         copy.wait()
@@ -262,28 +259,23 @@
     wide, narrow = shape((groups, sensors, LANES), f32), shape((groups, sensors, LANES), bf16)
     couple, full = shape((CORES, sensors, LANES), bf16), shape((sensors, 2 * LANES), bf16)
 
-    def step(stage, obs, preds, where, load=False):
-        operands = [place, scale, where, prior, obs, noise] + preds
-        out = [wide] + [couple] * pairs if stage > 0 else [narrow]
-        scratch = [pltpu.VMEM((groups, LANES, halves * sensors), bf16)]
-        if load:
-            out.append(shape(held.shape, bf16))
-            scratch.append(pltpu.SemaphoreType.DMA((groups, quads)))
+    near = call(bring_kernel, [ANY], [shape(held.shape, bf16)], [pltpu.SemaphoreType.DMA], moved=8 * 2**20)(held)[0]
+
+    def step(stage, obs, preds):
+        operands = [place, scale, near, prior, obs, noise] + preds
         return call(
-            functools.partial(step_kernel, stage, load, len(preds)),
-            [SMEM, SMEM, ANY if load else VMEM] + [VMEM] * (len(operands) - 3),
-            out,
-            scratch,
+            functools.partial(step_kernel, stage, len(preds)),
+            [SMEM, SMEM] + [VMEM] * (len(operands) - 2),
+            [wide] + [couple] * pairs if stage > 0 else [narrow],
+            [pltpu.VMEM((groups, LANES, halves * sensors), bf16)],
             flops=2**31,
             moved=8 * 2**20,
         )(*operands)
 
-    partial, near = step(0, streams[0], [], held, True)
-    first = [over_sides(partial)]
-    first += [over_sides(step(0, streams[s], [], near)[0]) for s in range(1, STREAMS)]
+    first = [over_sides(step(0, streams[s], [])[0]) for s in range(STREAMS)]
     multiplier, partials = [], []
     for s in range(STREAMS):
-        out, *parts = step(1, streams[s], first[s], near)
+        out, *parts = step(1, streams[s], first[s])
         multiplier.append(out)
         partials.append(parts)
     keeps, gives, duals = [None] * pairs, [None] * pairs, {}
@@ -301,12 +293,12 @@
         if e == 0:
             posts = call(
                 functools.partial(post_kernel, pairs),
-                [SMEM, SMEM] + [VMEM] * (2 + 2 * pairs),
+                [SMEM, SMEM] + [VMEM] * (2 + 2 * pairs) + [ANY],
                 [shape((cells, 2 * LANES), bf16)] * quads,
                 [pltpu.VMEM((groups, 2 * LANES, halves * sensors), bf16), pltpu.VMEM((quads, cells, 2 * LANES), bf16)],
                 flops=2**31,
                 moved=8 * 2**20,
-            )(place, scale, near, prior, *keeps, *gives)
+            )(place, scale, near, prior, *keeps, *gives, duals[(pairs - 1) * quads])
         messages = call(
             send_kernel,
             [SMEM] + [VMEM] * (2 + len(posts)),
@@ -316,19 +308,27 @@
         for d in reversed(range(quads)):
             message = messages[d] if e == 0 else messages[0]
             duals[e * quads + d] = swap(message, both, CORES * e * quads + d) if e + d else message
-    dual, posterior = call(
-        functools.partial(end_kernel, pairs * quads, quads),
-        [SMEM] + [VMEM] * (pairs * quads),
-        [shape((frequencies, halves, sensors, LANES), f32), shape((quads, cells * 2, LANES), f32)],
-        [
-            pltpu.VMEM((pairs * quads, CORES, halves, sensors, LANES), f32),
-            pltpu.VMEM((quads, cells * 2, LANES), f32),
-            pltpu.SemaphoreType.DMA((pairs * quads, CORES + 1)),
-        ],
-        [ANY, ANY],
-        moved=8 * 2**20,
-    )(place, *[duals[i] for i in range(pairs * quads)])
-    return dual, posterior.reshape(quads, cells, 2, LANES)
+    dual = None
+    for e in reversed(range(pairs)):
+        operands = [place] + [duals[e * quads + d] for d in range(quads)] + ([] if dual is None else [dual])
+        out = [shape((frequencies, halves, sensors, LANES), f32)]
+        scratch = [
+            pltpu.VMEM((quads, CORES, halves, sensors, LANES), f32),
+            pltpu.SemaphoreType.DMA((quads, CORES + 1)),
+        ]
+        if e == 0:
+            out.append(shape((quads, cells * 2, LANES), f32))
+            scratch.append(pltpu.VMEM((quads, cells * 2, LANES), f32))
+        dual, *posterior = call(
+            functools.partial(end_kernel, e, quads, dual is not None),
+            [SMEM] + [VMEM] * quads + [ANY] * (dual is not None),
+            out,
+            scratch,
+            [ANY] * len(out),
+            moved=4 * 2**20,
+            aliases=None if dual is None else {quads + 1: 0},
+        )(*operands)
+    return dual, posterior[0].reshape(quads, cells, 2, LANES)
 
 
 def solution(mesh):

time: 166 us -> 171 us (1.030)
  waiting for transfers between devices: 103 us -> 106 us
    ppermute x21, waiting for transfers between devices: 103 us -> 106 us  [swap(): return lax.ppermute(x, axes, [(i, i ^ distance) for i in range(count)])]
    pallas_call x5 -> x7, Pallas kernels: 21 us -> 22.3 us  [the longest x4 15.8 us: step(): call(functools.partial(step_kernel, stage, len(preds)), [SMEM, SMEM] + [V...]
  transfers between devices with their start and end apart: 22 -> 22, of which waited for: 13 -> 12; matrix products, arithmetic and copies ran while one was open for 0% -> 0% of each run, Pallas kernels for 10% -> 12%
where the time goes in v8:
time: 171 us
  waiting for transfers between devices  106 us (62%)
  Pallas kernels  30.9 us (18%)
  starting transfers between devices  30.1 us (18%)
  local copies, waits for them, and re-layouts  2.79 us (2%)
    ppermute x21, waiting for transfers between devices, swap(): return lax.ppermute(x, axes, [(i, i ^ distance) for i in range(count)])  106 us
    ppermute x21, starting transfers between devices, swap(): return lax.ppermute(x, axes, [(i, i ^ distance) for i in range(count)])  23.6 us
    pallas_call x4, Pallas kernels, step(): call(functools.partial(step_kernel, stage, len(preds)), [SMEM, SMEM] + [V...  15.8 us
    all_to_all x1, starting transfers between devices, on_device(): lax.all_to_all(forward_map.reshape(frequencies, halves * sensors, cells),...  6.48 us
    pallas_call x2, Pallas kernels, on_device(): call(functools.partial(end_kernel, e, quads, dual is not None), [SMEM] +...  4.28 us
  transfers between devices with their start and end apart: 22, of which 12 were waited for; matrix products, arithmetic and copies ran while one was open for 0% of the time, Pallas kernels for 12%

profile of v8, /device:TPU:0, one launch (start us, length us, event | category | flops | bytes accessed | tf_op | source)
XLA Modules:
  0.0 170.5 jit_solution(14631304313353962498)
XLA Ops:
  0.6 6.5 %all-to-all-start = ((bf16[16,512,256]{2,1,0:T(8,128)(2,1)}), bf16[16,512,256]{2,1,0:T(8,128)(2,1)}, u32[]{:S(2)}, u32[]{:S(2)}) async-start(bf16[16,512,256]{2,1,0:T(8,128)(2,1)} %bitcast.8), calls=%async_computation | async-start | bytes 8388608 | tf_op jit(solution)/shard_map/all_to_all | solution.py:228
  7.3 2.2 %copy-done = f32[16,2,256,128]{3,2,1,0:T(8,128)S(1)} copy-done((f32[16,2,256,128]{3,2,1,0:T(8,128)S(1)}, f32[16,2,256,128]{3,2,1,0:T(8,128)}, u32[]{:S(2)}) %copy-start) | copy-done | bytes 4194328
  9.4 1.1 shard_map.68
  12.6 1.9 %collective-permute-start.2 = (bf16[256,512]{1,0:T(8,128)(2,1)S(1)}, bf16[256,512]{1,0:T(8,128)(2,1)S(1)}, u32[]{:S(2)}, u32[]{:S(2)}) collective-permute-start(bf16[256,512]{1,0:T(8,128)(2,1)S(1)} %get-tuple-element.34), channel_id=1, source_target_pairs={{0,2},{1,3},{2,0},{3,1},{4,6},{5,7},{6,4},{7,5},{8,10},{9,11},{10,... | collective-permute-start | bytes 786440 | tf_op jit(solution)/shard_map/ppermute | solution.py:42
  14.5 1.5 collective-permute-start.4
  16.0 1.5 collective-permute-start.3
  18.6 47.7 %collective-permute-done.4.refs_5_ = bf16[272,256]{1,0:T(8,128)(2,1)S(1)} collective-permute-done((bf16[272,256]{1,0:T(8,128)(2,1)S(1)}, bf16[272,256]{1,0:T(8,128)(2,1)S(1)}, u32[]{:S(2)}, u32[]{:S(2)}) %collective-permute-start.4) | collective-permute-done | bytes 139296 | tf_op jit(solution)/shard_map/ppermute | solution.py:42
  66.3 2.0 %collective-permute-done.5.refs_6_ = bf16[272,256]{1,0:T(8,128)(2,1)S(1)} collective-permute-done((bf16[272,256]{1,0:T(8,128)(2,1)S(1)}, bf16[272,256]{1,0:T(8,128)(2,1)S(1)}, u32[]{:S(2)}, u32[]{:S(2)}) %collective-permute-start.5) | collective-permute-done | bytes 139296 | tf_op jit(solution)/shard_map/ppermute | solution.py:42
  68.3 1.4 collective-permute-done.3.refs_2_
  70.8 2.2 %shard_map.71.map_ref = bf16[4,4,512,256]{3,2,1,0:T(8,128)(2,1)S(1)} custom-call(bf16[4,4,512,256]{3,2,1,0:T(8,128)(2,1)} %bitcast.5.map_ref), custom_call_target="tpu_custom_call" | custom-call | bytes 8388608 | tf_op jit(solution)/shard_map/pallas_call | solution.py:262
  73.0 3.9 %shard_map.74.refs_0_ = bf16[4,256,128]{2,1,0:T(8,128)(2,1)S(1)} custom-call(s32[3]{0:T(128)S(1)} %pad_add_fusion.place_ref, f32[1]{0:T(128)} %dynamic_slice.3.scale_ref, bf16[4,4,512,256]{3,2,1,0:T(8,128)(2,1)S(1)} %shard_map.71.map_ref, bf16[4,256,512]{2,1,0:T(8,128)(2,1)S(1)} %get-tuple-element.41.prior_ref, ...), custom_call_target="tpu_custom_call" | custom-call | flops 2147483648 | bytes 8388608 | tf_op jit(solution)/shard_map/pallas_call | solution.py:266
  76.9 2.7 %collective-permute-start.7 = (bf16[4,256,128]{2,1,0:T(8,128)(2,1)S(1)}, bf16[4,256,128]{2,1,0:T(8,128)(2,1)S(1)}, u32[]{:S(2)}, u32[]{:S(2)}) collective-permute-start(bf16[4,256,128]{2,1,0:T(8,128)(2,1)S(1)} %shard_map.74.refs_0_), channel_id=1, source_target_pairs={{0,4},{4,0},{1,5},{5,1},{2,6},{6,2},{3,7},{7,3},{8,12},{12,8},{9,1... | collective-permute-start | bytes 786440 | tf_op jit(solution)/shard_map/ppermute | solution.py:42
  79.6 3.9 %shard_map.72.refs_0_ = bf16[4,256,128]{2,1,0:T(8,128)(2,1)S(1)} custom-call(s32[3]{0:T(128)S(1)} %pad_add_fusion.place_ref, f32[1]{0:T(128)} %dynamic_slice.3.scale_ref, bf16[4,4,512,256]{3,2,1,0:T(8,128)(2,1)S(1)} %shard_map.71.map_ref, bf16[4,256,512]{2,1,0:T(8,128)(2,1)S(1)} %get-tuple-element.41.prior_ref, ...), custom_call_target="tpu_custom_call" | custom-call | flops 2147483648 | bytes 8388608 | tf_op jit(solution)/shard_map/pallas_call | solution.py:266
  83.9 11.2 %collective-permute-done.7.refs_1_ = bf16[4,256,128]{2,1,0:T(8,128)(2,1)S(1)} collective-permute-done((bf16[4,256,128]{2,1,0:T(8,128)(2,1)S(1)}, bf16[4,256,128]{2,1,0:T(8,128)(2,1)S(1)}, u32[]{:S(2)}, u32[]{:S(2)}) %collective-permute-start.7) | collective-permute-done | bytes 262176 | tf_op jit(solution)/shard_map/ppermute | solution.py:42
  95.1 4.0 %shard_map.75 = (f32[4,256,128]{2,1,0:T(8,128)S(1)}, bf16[2,256,128]{2,1,0:T(8,128)(2,1)S(1)}, bf16[2,256,128]{2,1,0:T(8,128)(2,1)S(1)}) custom-call(s32[3]{0:T(128)S(1)} %pad_add_fusion.place_ref, f32[1]{0:T(128)} %dynamic_slice.3.scale_ref, bf16[4,4,512,256]{3,2,1,0:T(8,128)(2,1)S(1)} %shard_map.71.map_ref, ...), custom_call_target="tpu_custom_call" | custom-call | flops 2147483648 | bytes 8388608 | tf_op jit(solution)/shard_map/pallas_call | solution.py:266
  99.2 1.5 collective-permute-done.6.refs_1_
  100.7 4.0 %shard_map.73 = (f32[4,256,128]{2,1,0:T(8,128)S(1)}, bf16[2,256,128]{2,1,0:T(8,128)(2,1)S(1)}, bf16[2,256,128]{2,1,0:T(8,128)(2,1)S(1)}) custom-call(s32[3]{0:T(128)S(1)} %pad_add_fusion.place_ref, f32[1]{0:T(128)} %dynamic_slice.3.scale_ref, bf16[4,4,512,256]{3,2,1,0:T(8,128)(2,1)S(1)} %shard_map.71.map_ref, ...), custom_call_target="tpu_custom_call" | custom-call | flops 2147483648 | bytes 8388608 | tf_op jit(solution)/shard_map/pallas_call | solution.py:266
  104.6 1.5 collective-permute-start.11
  106.8 6.4 %collective-permute-done.11.refs_5_ = bf16[2,256,128]{2,1,0:T(8,128)(2,1)S(1)} collective-permute-done((bf16[2,256,128]{2,1,0:T(8,128)(2,1)S(1)}, bf16[2,256,128]{2,1,0:T(8,128)(2,1)S(1)}, u32[]{:S(2)}, u32[]{:S(2)}) %collective-permute-start.11) | collective-permute-done | bytes 131104 | tf_op jit(solution)/shard_map/ppermute | solution.py:42
  114.1 1.3 collective-permute-done.13.got_ref
  116.0 1.1 collective-permute-start.14
  117.1 2.9 %collective-permute-start.8 = (bf16[2,256,128]{2,1,0:T(8,128)(2,1)S(1)}, bf16[2,256,128]{2,1,0:T(8,128)(2,1)S(1)}, u32[]{:S(2)}, u32[]{:S(2)}) collective-permute-start(bf16[2,256,128]{2,1,0:T(8,128)(2,1)S(1)} %get-tuple-element.44.refs_4_), channel_id=1, source_target_pairs={{0,4},{4,0},{1,5},{5,1},{2,6},{6,2},{3,7},{7,3},{8,12},{12,8},{9,1... | collective-permute-start | bytes 393224 | tf_op jit(solution)/shard_map/ppermute | solution.py:42
  120.1 8.7 %collective-permute-done.9.refs_7_ = bf16[2,256,128]{2,1,0:T(8,128)(2,1)S(1)} collective-permute-done((bf16[2,256,128]{2,1,0:T(8,128)(2,1)S(1)}, bf16[2,256,128]{2,1,0:T(8,128)(2,1)S(1)}, u32[]{:S(2)}, u32[]{:S(2)}) %collective-permute-start.9) | collective-permute-done | bytes 131104 | tf_op jit(solution)/shard_map/ppermute | solution.py:42
  128.8 2.7 %collective-permute-done.8.refs_5_ = bf16[2,256,128]{2,1,0:T(8,128)(2,1)S(1)} collective-permute-done((bf16[2,256,128]{2,1,0:T(8,128)(2,1)S(1)}, bf16[2,256,128]{2,1,0:T(8,128)(2,1)S(1)}, u32[]{:S(2)}, u32[]{:S(2)}) %collective-permute-start.8) | collective-permute-done | bytes 131104 | tf_op jit(solution)/shard_map/ppermute | solution.py:42
  132.4 3.2 %shard_map.79 = (bf16[256,256]{1,0:T(8,128)(2,1)S(1)}, bf16[256,256]{1,0:T(8,128)(2,1)S(1)}, bf16[256,256]{1,0:T(8,128)(2,1)S(1)}, bf16[256,256]{1,0:T(8,128)(2,1)S(1)}) custom-call(s32[3]{0:T(128)S(1)} %pad_add_fusion.place_ref, f32[1]{0:T(128)} %dynamic_slice.3.scale_ref, bf16[4,4,512,256]{3,2,1,0:T(8,128)(2,1)S(1)} %shard_map.71.map_ref, ...), custom_call_target="tpu_custom_call" | custom-call | flops 2147483648 | bytes 8388608 | tf_op jit(solution)/shard_map/pallas_call | solution.py:294
  136.4 1.5 collective-permute-start.15
  137.9 2.5 %collective-permute-start.16 = (bf16[3,256,256]{2,1,0:T(8,128)(2,1)S(1)}, bf16[3,256,256]{2,1,0:T(8,128)(2,1)S(1)}, u32[]{:S(2)}, u32[]{:S(2)}) collective-permute-start(bf16[3,256,256]{2,1,0:T(8,128)(2,1)S(1)} %get-tuple-element.58), channel_id=1, source_target_pairs={{0,2},{1,3},{2,0},{3,1},{8,10},{9,11},{10,8},{11,9},{16,18},{17,19... | collective-permute-start | bytes 1179656 | tf_op jit(solution)/shard_map/ppermute | solution.py:42
  141.2 2.5 %collective-permute-start.19 = (bf16[2,256,256]{2,1,0:T(8,128)(2,1)S(1)}, bf16[2,256,256]{2,1,0:T(8,128)(2,1)S(1)}, u32[]{:S(2)}, u32[]{:S(2)}) collective-permute-start(bf16[2,256,256]{2,1,0:T(8,128)(2,1)S(1)} %shard_map.78), channel_id=1, source_target_pairs={{0,18},{1,19},{2,16},{3,17},{8,26},{9,27},{10,24},{11,25},{16,2},{... | collective-permute-start | bytes 786440 | tf_op jit(solution)/shard_map/ppermute | solution.py:42
  143.7 1.5 collective-permute-start.18
  145.2 20.9 %collective-permute-done.19.refs_2_ = bf16[2,256,256]{2,1,0:T(8,128)(2,1)S(1)} collective-permute-done((bf16[2,256,256]{2,1,0:T(8,128)(2,1)S(1)}, bf16[2,256,256]{2,1,0:T(8,128)(2,1)S(1)}, u32[]{:S(2)}, u32[]{:S(2)}) %collective-permute-start.19) | collective-permute-done | bytes 262176 | tf_op jit(solution)/shard_map/ppermute | solution.py:42
  166.2 2.0 %shard_map.81.refs_4_ = f32[16,2,256,128]{3,2,1,0:T(8,128)} custom-call(s32[3]{0:T(128)S(1)} %pad_add_fusion.place_ref, bf16[2,256,256]{2,1,0:T(8,128)(2,1)S(1)} %collective-permute-done.14.refs_4_.refs_0_, bf16[2,256,256]{2,1,0:T(8,128)(2,1)S(1)} %collective-permute-done.18.refs_1_, bf16[2,256,256]{2,1,0:T(8,128)(2,1)S(1)} %collective-permute-done.19.refs_2_, ...), custom_call_target="tpu_custom_call" | custom-call | bytes 4194304 | tf_op jit(solution)/shard_map/pallas_call | solution.py:322
  168.2 2.3 %shard_map.82 = (f32[16,2,256,128]{3,2,1,0:T(8,128)}, f32[4,512,128]{2,1,0:T(8,128)}) custom-call(s32[3]{0:T(128)S(1)} %pad_add_fusion.place_ref, bf16[3,256,256]{2,1,0:T(8,128)(2,1)S(1)} %get-tuple-element.56.refs_0_, bf16[3,256,256]{2,1,0:T(8,128)(2,1)S(1)} %collective-permute-done.15.refs_1_, ...), custom_call_target="tpu_custom_call", output_to_operand_aliasing={{0}: (5, {})} | custom-call | bytes 4194304 | tf_op jit(solution)/shard_map/pallas_call | solution.py:322
  (37 shorter events, 9.3 us)
Async XLA Ops:
  0.6 6.6 %copy-start.2 = (f32[256]{0:T(256)S(1)}, f32[256]{0:T(256)}, u32[]{:S(2)}) copy-start(f32[256]{0:T(256)} %param.7) | copy-start | bytes 3076
  0.6 11.3 %copy-start.1 = (bf16[256,512]{1,0:T(8,128)(2,1)S(1)}, bf16[256,512]{1,0:T(8,128)(2,1)}, u32[]{:S(2)}) copy-start(bf16[256,512]{1,0:T(8,128)(2,1)} %own_ref.3) | copy-start | bytes 786436
  0.6 70.1 %all-to-all-start = ((bf16[16,512,256]{2,1,0:T(8,128)(2,1)}), bf16[16,512,256]{2,1,0:T(8,128)(2,1)}, u32[]{:S(2)}, u32[]{:S(2)}) async-start(bf16[16,512,256]{2,1,0:T(8,128)(2,1)} %bitcast.8), calls=%async_computation | async-start | bytes 8388608 | tf_op jit(solution)/shard_map/all_to_all | solution.py:228
  7.1 10.9 %copy-start.3 = (f32[16]{0:T(128)S(1)}, f32[16]{0:T(128)}, u32[]{:S(2)}) copy-start(f32[16]{0:T(128)} %param.9) | copy-start | bytes 196
  7.3 2.2 %copy-start = (f32[16,2,256,128]{3,2,1,0:T(8,128)S(1)}, f32[16,2,256,128]{3,2,1,0:T(8,128)}, u32[]{:S(2)}) copy-start(f32[16,2,256,128]{3,2,1,0:T(8,128)} %obs_ref.1) | copy-start | bytes 12582916
  10.6 1.4 collective-permute-start
  12.6 57.2 %collective-permute-start.2 = (bf16[256,512]{1,0:T(8,128)(2,1)S(1)}, bf16[256,512]{1,0:T(8,128)(2,1)S(1)}, u32[]{:S(2)}, u32[]{:S(2)}) collective-permute-start(bf16[256,512]{1,0:T(8,128)(2,1)S(1)} %get-tuple-element.34), channel_id=1, source_target_pairs={{0,2},{1,3},{2,0},{3,1},{4,6},{5,7},{6,4},{7,5},{8,10},{9,11},{10,... | collective-permute-start | bytes 786440 | tf_op jit(solution)/shard_map/ppermute | solution.py:42
  14.5 51.8 %collective-permute-start.4 = (bf16[272,256]{1,0:T(8,128)(2,1)S(1)}, bf16[272,256]{1,0:T(8,128)(2,1)S(1)}, u32[]{:S(2)}, u32[]{:S(2)}) collective-permute-start(bf16[272,256]{1,0:T(8,128)(2,1)S(1)} %get-tuple-element.36), channel_id=1, source_target_pairs={{0,16},{8,24},{16,0},{24,8},{1,17},{9,25},{17,1},{25,9},{2,18},{10... | collective-permute-start | bytes 417800 | tf_op jit(solution)/shard_map/ppermute | solution.py:42
  16.0 52.4 %collective-permute-start.5 = (bf16[272,256]{1,0:T(8,128)(2,1)S(1)}, bf16[272,256]{1,0:T(8,128)(2,1)S(1)}, u32[]{:S(2)}, u32[]{:S(2)}) collective-permute-start(bf16[272,256]{1,0:T(8,128)(2,1)S(1)} %get-tuple-element.37), channel_id=1, source_target_pairs={{0,24},{8,16},{16,8},{24,0},{1,25},{9,17},{17,9},{25,1},{2,26},{10... | collective-permute-start | bytes 417800 | tf_op jit(solution)/shard_map/ppermute | solution.py:42
  16.0 53.8 %collective-permute-start.3 = (bf16[256,256]{1,0:T(8,128)(2,1)S(1)}, bf16[256,256]{1,0:T(8,128)(2,1)S(1)}, u32[]{:S(2)}, u32[]{:S(2)}) collective-permute-start(bf16[256,256]{1,0:T(8,128)(2,1)S(1)} %get-tuple-element.33), channel_id=1, source_target_pairs={{0,3},{1,2},{2,1},{3,0},{4,7},{5,6},{6,5},{7,4},{8,11},{9,10},{10,... | collective-permute-start | bytes 393224 | tf_op jit(solution)/shard_map/ppermute | solution.py:42
  17.4 52.4 %collective-permute-start.1 = (bf16[256,256]{1,0:T(8,128)(2,1)S(1)}, bf16[256,256]{1,0:T(8,128)(2,1)S(1)}, u32[]{:S(2)}, u32[]{:S(2)}) collective-permute-start(bf16[256,256]{1,0:T(8,128)(2,1)S(1)} %get-tuple-element.33), channel_id=1, source_target_pairs={{0,1},{1,0},{2,3},{3,2},{4,5},{5,4},{6,7},{7,6},{8,9},{9,8},{10,11... | collective-permute-start | bytes 393224 | tf_op jit(solution)/shard_map/ppermute | solution.py:42
  76.9 18.2 %collective-permute-start.7 = (bf16[4,256,128]{2,1,0:T(8,128)(2,1)S(1)}, bf16[4,256,128]{2,1,0:T(8,128)(2,1)S(1)}, u32[]{:S(2)}, u32[]{:S(2)}) collective-permute-start(bf16[4,256,128]{2,1,0:T(8,128)(2,1)S(1)} %shard_map.74.refs_0_), channel_id=1, source_target_pairs={{0,4},{4,0},{1,5},{5,1},{2,6},{6,2},{3,7},{7,3},{8,12},{12,8},{9,1... | collective-permute-start | bytes 786440 | tf_op jit(solution)/shard_map/ppermute | solution.py:42
  83.5 17.1 %collective-permute-start.6 = (bf16[4,256,128]{2,1,0:T(8,128)(2,1)S(1)}, bf16[4,256,128]{2,1,0:T(8,128)(2,1)S(1)}, u32[]{:S(2)}, u32[]{:S(2)}) collective-permute-start(bf16[4,256,128]{2,1,0:T(8,128)(2,1)S(1)} %shard_map.72.refs_0_), channel_id=1, source_target_pairs={{0,4},{4,0},{1,5},{5,1},{2,6},{6,2},{3,7},{7,3},{8,12},{12,8},{9,1... | collective-permute-start | bytes 786440 | tf_op jit(solution)/shard_map/ppermute | solution.py:42
  99.1 7.8 %collective-permute-start.12 = (bf16[2,256,128]{2,1,0:T(8,128)(2,1)S(1)}, bf16[2,256,128]{2,1,0:T(8,128)(2,1)S(1)}, u32[]{:S(2)}, u32[]{:S(2)}) collective-permute-start(bf16[2,256,128]{2,1,0:T(8,128)(2,1)S(1)} %get-tuple-element.49.refs_6_), channel_id=1, source_target_pairs={{0,4},{4,0},{1,5},{5,1},{2,6},{6,2},{3,7},{7,3},{8,12},{12,8},{9,1... | collective-permute-start | bytes 393224 | tf_op jit(solution)/shard_map/ppermute | solution.py:42
  104.6 8.6 %collective-permute-start.11 = (bf16[2,256,128]{2,1,0:T(8,128)(2,1)S(1)}, bf16[2,256,128]{2,1,0:T(8,128)(2,1)S(1)}, u32[]{:S(2)}, u32[]{:S(2)}) collective-permute-start(bf16[2,256,128]{2,1,0:T(8,128)(2,1)S(1)} %get-tuple-element.48.refs_4_), channel_id=1, source_target_pairs={{0,4},{4,0},{1,5},{5,1},{2,6},{6,2},{3,7},{7,3},{8,12},{12,8},{9,1... | collective-permute-start | bytes 393224 | tf_op jit(solution)/shard_map/ppermute | solution.py:42
  114.0 1.4 collective-permute-start.13
  116.0 16.4 %collective-permute-start.14 = (bf16[2,256,256]{2,1,0:T(8,128)(2,1)S(1)}, bf16[2,256,256]{2,1,0:T(8,128)(2,1)S(1)}, u32[]{:S(2)}, u32[]{:S(2)}) collective-permute-start(bf16[2,256,256]{2,1,0:T(8,128)(2,1)S(1)} %shard_map.78), channel_id=1, source_target_pairs={{0,16},{1,17},{2,18},{3,19},{8,24},{9,25},{10,26},{11,27},{16,0},{... | collective-permute-start | bytes 786440 | tf_op jit(solution)/shard_map/ppermute | solution.py:42
  117.1 11.6 %collective-permute-start.9 = (bf16[2,256,128]{2,1,0:T(8,128)(2,1)S(1)}, bf16[2,256,128]{2,1,0:T(8,128)(2,1)S(1)}, u32[]{:S(2)}, u32[]{:S(2)}) collective-permute-start(bf16[2,256,128]{2,1,0:T(8,128)(2,1)S(1)} %get-tuple-element.45.refs_6_), channel_id=1, source_target_pairs={{0,4},{4,0},{1,5},{5,1},{2,6},{6,2},{3,7},{7,3},{8,12},{12,8},{9,1... | collective-permute-start | bytes 393224 | tf_op jit(solution)/shard_map/ppermute | solution.py:42
  117.1 14.4 %collective-permute-start.8 = (bf16[2,256,128]{2,1,0:T(8,128)(2,1)S(1)}, bf16[2,256,128]{2,1,0:T(8,128)(2,1)S(1)}, u32[]{:S(2)}, u32[]{:S(2)}) collective-permute-start(bf16[2,256,128]{2,1,0:T(8,128)(2,1)S(1)} %get-tuple-element.44.refs_4_), channel_id=1, source_target_pairs={{0,4},{4,0},{1,5},{5,1},{2,6},{6,2},{3,7},{7,3},{8,12},{12,8},{9,1... | collective-permute-start | bytes 393224 | tf_op jit(solution)/shard_map/ppermute | solution.py:42
  132.3 3.4 %collective-permute-start.10 = (bf16[256,256]{1,0:T(8,128)(2,1)S(1)}, bf16[256,256]{1,0:T(8,128)(2,1)S(1)}, u32[]{:S(2)}, u32[]{:S(2)}) collective-permute-start(bf16[256,256]{1,0:T(8,128)(2,1)S(1)} %get-tuple-element.47.refs_2_), channel_id=1, source_target_pairs={{0,8},{8,0},{16,24},{24,16},{1,9},{9,1},{17,25},{25,17},{2,10},{10... | collective-permute-start | bytes 393224 | tf_op jit(solution)/shard_map/ppermute | solution.py:42
  132.4 11.4 %collective-permute-start.20 = (bf16[2,256,256]{2,1,0:T(8,128)(2,1)S(1)}, bf16[2,256,256]{2,1,0:T(8,128)(2,1)S(1)}, u32[]{:S(2)}, u32[]{:S(2)}) collective-permute-start(bf16[2,256,256]{2,1,0:T(8,128)(2,1)S(1)} %shard_map.78), channel_id=1, source_target_pairs={{0,19},{1,18},{2,17},{3,16},{8,27},{9,26},{10,25},{11,24},{16,3},{... | collective-permute-start | bytes 786440 | tf_op jit(solution)/shard_map/ppermute | solution.py:42
  136.4 31.8 %collective-permute-start.15 = (bf16[3,256,256]{2,1,0:T(8,128)(2,1)S(1)}, bf16[3,256,256]{2,1,0:T(8,128)(2,1)S(1)}, u32[]{:S(2)}, u32[]{:S(2)}) collective-permute-start(bf16[3,256,256]{2,1,0:T(8,128)(2,1)S(1)} %get-tuple-element.57), channel_id=1, source_target_pairs={{0,1},{1,0},{2,3},{3,2},{8,9},{9,8},{10,11},{11,10},{16,17},{17,16... | collective-permute-start | bytes 1179656 | tf_op jit(solution)/shard_map/ppermute | solution.py:42
  137.9 30.3 %collective-permute-start.16 = (bf16[3,256,256]{2,1,0:T(8,128)(2,1)S(1)}, bf16[3,256,256]{2,1,0:T(8,128)(2,1)S(1)}, u32[]{:S(2)}, u32[]{:S(2)}) collective-permute-start(bf16[3,256,256]{2,1,0:T(8,128)(2,1)S(1)} %get-tuple-element.58), channel_id=1, source_target_pairs={{0,2},{1,3},{2,0},{3,1},{8,10},{9,11},{10,8},{11,9},{16,18},{17,19... | collective-permute-start | bytes 1179656 | tf_op jit(solution)/shard_map/ppermute | solution.py:42
  140.3 27.8 %collective-permute-start.17 = (bf16[3,256,256]{2,1,0:T(8,128)(2,1)S(1)}, bf16[3,256,256]{2,1,0:T(8,128)(2,1)S(1)}, u32[]{:S(2)}, u32[]{:S(2)}) collective-permute-start(bf16[3,256,256]{2,1,0:T(8,128)(2,1)S(1)} %get-tuple-element.59), channel_id=1, source_target_pairs={{0,3},{1,2},{2,1},{3,0},{8,11},{9,10},{10,9},{11,8},{16,19},{17,18... | collective-permute-start | bytes 1179656 | tf_op jit(solution)/shard_map/ppermute | solution.py:42
  141.2 25.0 %collective-permute-start.19 = (bf16[2,256,256]{2,1,0:T(8,128)(2,1)S(1)}, bf16[2,256,256]{2,1,0:T(8,128)(2,1)S(1)}, u32[]{:S(2)}, u32[]{:S(2)}) collective-permute-start(bf16[2,256,256]{2,1,0:T(8,128)(2,1)S(1)} %shard_map.78), channel_id=1, source_target_pairs={{0,18},{1,19},{2,16},{3,17},{8,26},{9,27},{10,24},{11,25},{16,2},{... | collective-permute-start | bytes 786440 | tf_op jit(solution)/shard_map/ppermute | solution.py:42
  143.7 22.5 %collective-permute-start.18 = (bf16[2,256,256]{2,1,0:T(8,128)(2,1)S(1)}, bf16[2,256,256]{2,1,0:T(8,128)(2,1)S(1)}, u32[]{:S(2)}, u32[]{:S(2)}) collective-permute-start(bf16[2,256,256]{2,1,0:T(8,128)(2,1)S(1)} %shard_map.78), channel_id=1, source_target_pairs={{0,17},{1,16},{2,19},{3,18},{8,25},{9,24},{10,27},{11,26},{16,1},{... | collective-permute-start | bytes 786440 | tf_op jit(solution)/shard_map/ppermute | solution.py:42

commit v9 on v5

--- a/solution.py
+++ b/solution.py
@@ -24,11 +24,12 @@
     return jax.ShapeDtypeStruct(dims, dtype)
 
 
-def call(kernel, in_specs, out_shape, scratch=(), flops=0, moved=0):
+def call(kernel, in_specs, out_shape, scratch=(), out_specs=None, flops=0, moved=0, aliases=None):
     return pl.pallas_call(
         kernel,
+        input_output_aliases=aliases or {},
         in_specs=in_specs,
-        out_specs=[VMEM] * len(out_shape),
+        out_specs=out_specs or [VMEM] * len(out_shape),
         out_shape=out_shape,
         scratch_shapes=list(scratch),
         cost_estimate=pl.CostEstimate(flops=flops, bytes_accessed=moved, transcendentals=0),
@@ -68,6 +69,12 @@
             part = slice(s * HALF, (s + 1) * HALF)
             outs[d][:sensors, s * LANES:(s + 1) * LANES] = jnp.concatenate([re[:, part], im[:, part]], 1).astype(bf16)
         outs[d][sensors:, :] = tail
+
+
+def prior_kernel(place_ref, own_ref, after_ref, full_ref, diagonal_ref):
+    cells = own_ref.shape[0]
+    full_ref[...] = own_ref[...]
+    diagonal_ref[...] = own_ref[:, pl.ds(pl.multiple_of((place_ref[1] & 1) * cells, cells), cells)]
 
 
 def gather_kernel(groups, quads, place_ref, own_ref, *refs):
@@ -114,13 +121,19 @@
     return jnp.concatenate([z, jnp.concatenate([z[:, half:], -z[:, :half]], 1)], 0).T
 
 
-def step_kernel(stage, n_pred, place_ref, scale_ref, map_ref, prior_ref, obs_ref, noise_ref, *refs):
+def bring_kernel(map_ref, out_ref, sem):
+    copy = pltpu.make_async_copy(map_ref, out_ref, sem)
+    copy.start()
+    copy.wait()
+
+
+def step_kernel(stage, n_pred, scale_ref, map_ref, prior_ref, obs_ref, noise_ref, *refs):
     groups, quads, double, _ = map_ref.shape
     sensors = double // 2
     preds, refs = refs[:n_pred], refs[n_pred:]
     if stage > 0:
         next_ref, refs = refs[0], refs[1:]
-    outs, sides_ref = refs[:-1], refs[-1]
+    out_ref, sides_ref = refs
     for g in range(groups):
         obs = obs_ref[g].astype(f32)
         now = relax_step * obs
@@ -131,70 +144,65 @@
         sides_ref[g] = sides(now.astype(bf16))
     sources = source(map_ref, sides_ref, prior_ref, scale_ref[0])
     turned = [jnp.concatenate([-v[:, HALF:], v[:, :HALF]], 1) for v in sources]
-    for e in reversed(range(groups // CORES)):
-        for core in range(CORES):
-            g = CORES * (place_ref[0] ^ e) + core if stage > 0 else CORES * e + core
-            total = jnp.zeros((sensors, LANES), f32)
-            for q in range(quads):
-                total += dot(map_ref[g, q, :sensors, :], sources[q]) + dot(map_ref[g, q, sensors:, :], turned[q])
-            if stage > 0:
-                outs[e][core] = total.astype(bf16)
-            else:
-                outs[0][g] = total.astype(bf16)
-
-
-def last_kernel(e, n_pred, place_ref, noise_ref, *refs):
-    obs, held, refs = refs[:STREAMS], refs[STREAMS:2 * STREAMS], refs[2 * STREAMS:]
-    preds, (keep_ref, give_ref) = refs[:STREAMS * n_pred], refs[STREAMS * n_pred:]
-    for out, core in ((give_ref, 1 - place_ref[2]), (keep_ref, place_ref[2])):
-        g = CORES * (place_ref[0] ^ e) + core
-        parts = []
-        for s in range(STREAMS):
-            now = held[s][g]
-            predicted = sum(p[core].astype(f32) for p in preds[s * n_pred:(s + 1) * n_pred])
-            parts.append(now + relax_step * (obs[s][g].astype(f32) - predicted - noise_ref[g] * now))
-        out[:, :LANES] = jnp.concatenate([p[:, :HALF] for p in parts], 1).astype(bf16)
-        out[:, LANES:] = jnp.concatenate([p[:, HALF:] for p in parts], 1).astype(bf16)
-
-
-def send_kernel(place_ref, keep_ref, got_ref, out_ref):
-    out_ref[place_ref[2]] = keep_ref[...]
-    out_ref[1 - place_ref[2]] = got_ref[...]
-
-
-def post_kernel(pairs, place_ref, scale_ref, map_ref, prior_ref, *refs):
-    keeps, gives, refs = refs[:pairs], refs[pairs:2 * pairs], refs[2 * pairs + 1:]
+    for g in range(groups):
+        total = jnp.zeros((sensors, LANES), f32)
+        for q in range(quads):
+            total += dot(map_ref[g, q, :sensors, :], sources[q]) + dot(map_ref[g, q, sensors:, :], turned[q])
+        out_ref[g] = total.astype(bf16)
+
+
+def last_kernel(n_pred, noise_ref, obs_ref, held_ref, *refs):
+    preds, (final_ref, out_ref) = refs[:n_pred], refs[n_pred:]
+    for g in range(final_ref.shape[0]):
+        now = held_ref[g]
+        predicted = sum(p[g].astype(f32) for p in preds)
+        now = now + relax_step * (obs_ref[g].astype(f32) - predicted - noise_ref[g] * now)
+        now = now.astype(bf16)
+        final_ref[g] = now
+        for q in range(out_ref.shape[1]):
+            out_ref[g, q] = now
+
+
+def join(streams):
+    return jnp.concatenate([x[:, :HALF] for x in streams] + [x[:, HALF:] for x in streams], 1)
+
+
+def post_kernel(place_ref, scale_ref, map_ref, prior_ref, *refs):
+    finals, refs = refs[:STREAMS], refs[STREAMS:]
     outs, (sides_ref, held_ref) = refs[:-2], refs[-2:]
-    for e in range(pairs):
-        first = CORES * (place_ref[0] ^ e)
-        sides_ref[first + place_ref[2]] = sides(keeps[e][...])
-        sides_ref[first + 1 - place_ref[2]] = sides(gives[e][...])
+    for g in range(map_ref.shape[0]):
+        sides_ref[g] = sides(join([x[g] for x in finals]))
     for q, v in enumerate(source(map_ref, sides_ref, prior_ref, scale_ref[0])):
         held_ref[q] = v
     for d, out in enumerate(outs):
         out[...] = held_ref[place_ref[1] ^ d]
 
 
-def end_kernel(chips, quads, place_ref, *refs):
-    duals, posts, (dual_ref, post_ref) = refs[:chips], refs[chips:chips + quads], refs[chips + quads:]
-    pair, quad = place_ref[0], place_ref[1]
+def end_kernel(quads, place_ref, *refs):
+    came, posts, refs = refs[:STREAMS], refs[STREAMS:STREAMS + quads], refs[STREAMS + quads:]
+    dual_out, post_out, dual_ref, post_ref, sems = refs
+    quad = place_ref[1]
     cells = post_ref.shape[1] // 2
-    for chip in range(chips):
-        e, d = divmod(chip, quads)
-        for core in range(CORES):
-            freq = (CORES * (pair ^ e) + core) * quads + (quad ^ d)
-            dual_ref[freq, 0] = duals[chip][core, :, :LANES].astype(f32)
-            dual_ref[freq, 1] = duals[chip][core, :, LANES:].astype(f32)
+    sends = []
     for d in range(quads):
-        post_ref[quad ^ d, pl.ds(0, cells, stride=2), :] = posts[d][:, :LANES].astype(f32)
-        post_ref[quad ^ d, pl.ds(1, cells, stride=2), :] = posts[d][:, LANES:].astype(f32)
+        post_ref[d, pl.ds(0, cells, stride=2), :] = posts[d][:, :LANES].astype(f32)
+        post_ref[d, pl.ds(1, cells, stride=2), :] = posts[d][:, LANES:].astype(f32)
+        sends.append(pltpu.make_async_copy(post_ref.at[d], post_out.at[quad ^ d], sems.at[d]))
+        sends[-1].start()
+    for freq in range(dual_ref.shape[0]):
+        both = join([x[freq].astype(f32) for x in came])
+        dual_ref[freq, 0] = both[:, :LANES]
+        dual_ref[freq, 1] = both[:, LANES:]
+        sends.append(pltpu.make_async_copy(dual_ref.at[freq], dual_out.at[freq], sems.at[quads + freq]))
+        sends[-1].start()
+    for copy in sends:
+        copy.wait()
 
 
 def on_device(forward_map, observed, noise_var, prior_rows, prior_scale):
     frequencies, halves, sensors, cells = forward_map.shape
     groups, quads, sides = (lax.axis_size(a) for a in ("sensor", "quad", "side"))
     width = prior_rows.shape[1]
-    pairs = groups // CORES
     me, quad = lax.axis_index("sensor"), lax.axis_index("quad")
     place = jnp.stack([me // CORES, quad, me % CORES]).astype(jnp.int32)
     scale = lax.dynamic_slice_in_dim(prior_scale, me * quads + quad, 1, 0)
@@ -212,8 +220,12 @@
         moved=groups * sensors * LANES * 12,
     )(place, observed, noise_var.reshape(1, sensors))
     data = [data[0]] + [swap(data[d], "sensor", d) for d in range(1, groups)]
-    diagonal = lax.dynamic_slice_in_dim(prior_rows, quad % 2 * cells, cells, 1)
-    came = [swap(diagonal if d % 2 else prior_rows, "quad", d) for d in range(1, quads)]
+    rows, diagonal = call(
+        prior_kernel,
+        [SMEM, VMEM, ANY],
+        [shape((cells, width), bf16), shape((cells, cells), bf16)],
+    )(place, prior_rows, data[1])
+    came = [swap(diagonal if d % 2 else rows, "quad", d) for d in range(1, quads)]
     prior, noise, *streams = call(
         functools.partial(gather_kernel, groups, quads),
         [SMEM] + [VMEM] * (quads + groups),
@@ -228,59 +240,55 @@
         return [lax.psum(partial, "side")]
 
     wide, narrow = shape((groups, sensors, LANES), f32), shape((groups, sensors, LANES), bf16)
-    couple, full = shape((CORES, sensors, LANES), bf16), shape((sensors, 2 * LANES), bf16)
+
+    near = call(bring_kernel, [ANY], [shape(held.shape, bf16)], [pltpu.SemaphoreType.DMA], moved=8 * 2**20)(held)[0]
 
     def step(stage, obs, preds):
-        operands = [place, scale, held, prior, obs, noise] + preds
+        operands = [scale, near, prior, obs, noise] + preds
         return call(
             functools.partial(step_kernel, stage, len(preds)),
-            [SMEM, SMEM] + [VMEM] * (len(operands) - 2),
-            [wide] + [couple] * pairs if stage > 0 else [narrow],
+            [SMEM] + [VMEM] * (len(operands) - 1),
+            [wide, narrow] if stage > 0 else [narrow],
             [pltpu.VMEM((groups, LANES, halves * sensors), bf16)],
             flops=2**31,
             moved=8 * 2**20,
         )(*operands)
 
     first = [over_sides(step(0, streams[s], [])[0]) for s in range(STREAMS)]
-    multiplier, partials = [], []
+    finals, duals = [], []
     for s in range(STREAMS):
-        out, *parts = step(1, streams[s], first[s])
-        multiplier.append(out)
-        partials.append(parts)
-    keeps, gives, duals = [None] * pairs, [None] * pairs, {}
-    for e in reversed(range(pairs)):
-        preds = [over_sides(partials[s][e]) for s in range(STREAMS)]
-        count = len(preds[0])
-        keeps[e], gives[e] = call(
-            functools.partial(last_kernel, e, count),
-            [SMEM] + [VMEM] * (1 + STREAMS * (2 + count)),
-            [full, full],
+        held_s, partial = step(1, streams[s], first[s])
+        preds = over_sides(partial)
+        final, out = call(
+            functools.partial(last_kernel, len(preds)),
+            [VMEM] * (3 + len(preds)),
+            [narrow, shape((groups, quads, sensors, LANES), bf16)],
             moved=2 * 2**20,
-        )(place, noise, *streams, *multiplier, *[p for pair in preds for p in pair])
-        message = call(
-            send_kernel,
-            [SMEM, VMEM, VMEM],
-            [shape((CORES, sensors, 2 * LANES), bf16)],
-            moved=2**20,
-        )(place, keeps[e], swap(gives[e], "sensor", 1))[0]
-        for d in reversed(range(quads)):
-            away = e * quads + d
-            duals[away] = swap(message, both, CORES * e * quads + d) if away else message
-    post = call(
-        functools.partial(post_kernel, pairs),
-        [SMEM, SMEM] + [VMEM] * (2 + 2 * pairs) + [ANY],
+        )(noise, streams[s], held_s, *preds)
+        finals.append(final)
+        out = out.reshape(frequencies, sensors, LANES)
+        duals.append(lax.all_to_all(out, both, split_axis=0, concat_axis=0, tiled=True))
+    posts = call(
+        post_kernel,
+        [SMEM, SMEM] + [VMEM] * (2 + STREAMS),
         [shape((cells, 2 * LANES), bf16)] * quads,
         [pltpu.VMEM((groups, 2 * LANES, halves * sensors), bf16), pltpu.VMEM((quads, cells, 2 * LANES), bf16)],
         flops=2**31,
         moved=8 * 2**20,
-    )(place, scale, held, prior, *keeps, *gives, duals[(pairs - 1) * quads])
-    post = [post[0]] + [swap(post[d], "quad", d) for d in range(1, quads)]
+    )(place, scale, near, prior, *finals)
+    posts = [posts[0]] + [swap(posts[d], "quad", d) for d in range(1, quads)]
     dual, posterior = call(
-        functools.partial(end_kernel, pairs * quads, quads),
-        [SMEM] + [VMEM] * (pairs * quads + quads),
+        functools.partial(end_kernel, quads),
+        [SMEM] + [VMEM] * (STREAMS + quads),
         [shape((frequencies, halves, sensors, LANES), f32), shape((quads, cells * 2, LANES), f32)],
+        [
+            pltpu.VMEM((frequencies, halves, sensors, LANES), f32),
+            pltpu.VMEM((quads, cells * 2, LANES), f32),
+            pltpu.SemaphoreType.DMA((quads + frequencies,)),
+        ],
+        [ANY, ANY],
         moved=8 * 2**20,
-    )(place, *[duals[i] for i in range(pairs * quads)], *post)
+    )(place, *duals, *posts)
     return dual, posterior.reshape(quads, cells, 2, LANES)
 
 

time: 167 us -> 181 us (1.084)
  waiting for transfers between devices: 91 us -> 113 us
  starting transfers between devices: 36.8 us -> 28.3 us
  Pallas kernels: 35.3 us -> 27.1 us
  local copies, waits for them, and re-layouts: 2.8 us -> 10.8 us
    ppermute x24 -> x13, waiting for transfers between devices: 91 us -> 113 us  [swap(): return lax.ppermute(x, axes, [(i, i ^ distance) for i in range(count)])]
    ppermute x24 -> x13, starting transfers between devices: 30.3 us -> 14.4 us  [swap(): return lax.ppermute(x, axes, [(i, i ^ distance) for i in range(count)])]
    pallas_call x10, Pallas kernels: 33.2 us -> 25 us  [the longest x4 13.7 us: step(): call(functools.partial(step_kernel, stage, len(preds)), [SMEM] + [VMEM] *...]
    unnamed x8 -> x22, local copies, waits for them, and re-layouts: 2.2 us -> 10.2 us
    all_to_all x0 -> x2, starting transfers between devices: none -> 7.4 us  [on_device(): lax.all_to_all(out, both, split_axis=0, concat_axis=0, tiled=True)]
  transfers between devices with their start and end apart: 25 -> 16, of which waited for: 11 -> 9; matrix products, arithmetic and copies ran while one was open for 0% -> 0% of each run, Pallas kernels for 15% -> 8%
where the time goes in v9:
time: 181 us; the launch traced here: 180 us
  waiting for transfers between devices  113 us (62%)
  starting transfers between devices  28.3 us (16%)
  Pallas kernels  27.1 us (15%)
  local copies, waits for them, and re-layouts  10.8 us (6%)
    ppermute x13, waiting for transfers between devices, swap(): return lax.ppermute(x, axes, [(i, i ^ distance) for i in range(count)])  113 us
    ppermute x13, starting transfers between devices, swap(): return lax.ppermute(x, axes, [(i, i ^ distance) for i in range(count)])  14.4 us
    pallas_call x4, Pallas kernels, step(): call(functools.partial(step_kernel, stage, len(preds)), [SMEM] + [VMEM] *...  13.7 us
    unnamed x22, local copies, waits for them, and re-layouts  10.2 us
    all_to_all x2, starting transfers between devices, on_device(): lax.all_to_all(out, both, split_axis=0, concat_axis=0, tiled=True)  7.4 us
    all_to_all x1, starting transfers between devices, on_device(): lax.all_to_all(forward_map.reshape(frequencies, halves * sensors, cells),...  6.48 us
  transfers between devices with their start and end apart: 16, of which 9 were waited for; matrix products, arithmetic and copies ran while one was open for 0% of the time, Pallas kernels for 8%

profile of v9, /device:TPU:0, one launch (start us, length us, event | category | flops | bytes accessed | tf_op | source)
XLA Modules:
  0.0 180.0 jit_solution(5979083271751042856)
XLA Ops:
  0.6 6.5 %all-to-all-start = ((bf16[16,512,256]{2,1,0:T(8,128)(2,1)}), bf16[16,512,256]{2,1,0:T(8,128)(2,1)}, u32[]{:S(2)}, u32[]{:S(2)}) async-start(bf16[16,512,256]{2,1,0:T(8,128)(2,1)} %bitcast.10), calls=%async_computation | async-start | bytes 8388608 | tf_op jit(solution)/shard_map/all_to_all | solution.py:211
  7.3 2.2 %copy-done = f32[16,2,256,128]{3,2,1,0:T(8,128)S(1)} copy-done((f32[16,2,256,128]{3,2,1,0:T(8,128)S(1)}, f32[16,2,256,128]{3,2,1,0:T(8,128)}, u32[]{:S(2)}) %copy-start) | copy-done | bytes 4194328
  12.6 1.9 %collective-permute-start.2 = (bf16[256,512]{1,0:T(8,128)(2,1)S(1)}, bf16[256,512]{1,0:T(8,128)(2,1)S(1)}, u32[]{:S(2)}, u32[]{:S(2)}) collective-permute-start(bf16[256,512]{1,0:T(8,128)(2,1)S(1)} %get-tuple-element.28), channel_id=1, source_target_pairs={{0,2},{1,3},{2,0},{3,1},{4,6},{5,7},{6,4},{7,5},{8,10},{9,11},{10,... | collective-permute-start | bytes 786440 | tf_op jit(solution)/shard_map/ppermute | solution.py:42
  14.5 1.5 collective-permute-start.4
  16.0 1.5 collective-permute-start.3
  18.6 47.7 %collective-permute-done.4.refs_5_ = bf16[272,256]{1,0:T(8,128)(2,1)S(1)} collective-permute-done((bf16[272,256]{1,0:T(8,128)(2,1)S(1)}, bf16[272,256]{1,0:T(8,128)(2,1)S(1)}, u32[]{:S(2)}, u32[]{:S(2)}) %collective-permute-start.4) | collective-permute-done | bytes 139296 | tf_op jit(solution)/shard_map/ppermute | solution.py:42
  66.3 2.0 %collective-permute-done.5.refs_6_ = bf16[272,256]{1,0:T(8,128)(2,1)S(1)} collective-permute-done((bf16[272,256]{1,0:T(8,128)(2,1)S(1)}, bf16[272,256]{1,0:T(8,128)(2,1)S(1)}, u32[]{:S(2)}, u32[]{:S(2)}) %collective-permute-start.5) | collective-permute-done | bytes 139296 | tf_op jit(solution)/shard_map/ppermute | solution.py:42
  68.3 1.4 collective-permute-done.3.refs_2_
  71.7 2.3 %shard_map.71.map_ref = bf16[4,4,512,256]{3,2,1,0:T(8,128)(2,1)S(1)} custom-call(bf16[4,4,512,256]{3,2,1,0:T(8,128)(2,1)} %bitcast.5.map_ref), custom_call_target="tpu_custom_call" | custom-call | bytes 8388608 | tf_op jit(solution)/shard_map/pallas_call | solution.py:244
  74.2 3.4 %shard_map.75.refs_0_ = bf16[4,256,128]{2,1,0:T(8,128)(2,1)S(1)} custom-call(f32[1]{0:T(128)} %dynamic_slice.3.scale_ref, bf16[4,4,512,256]{3,2,1,0:T(8,128)(2,1)S(1)} %shard_map.71.map_ref, bf16[4,256,512]{2,1,0:T(8,128)(2,1)S(1)} %copy-done.7, bf16[4,256,128]{2,1,0:T(8,128)(2,1)S(1)} %get-tuple-element.38.obs_ref, ...), custom_call_target="tpu_custom_call" | custom-call | flops 2147483648 | bytes 8388608 | tf_op jit(solution)/shard_map/pallas_call | solution.py:248
  77.7 2.7 %collective-permute-start.8 = (bf16[4,256,128]{2,1,0:T(8,128)(2,1)S(1)}, bf16[4,256,128]{2,1,0:T(8,128)(2,1)S(1)}, u32[]{:S(2)}, u32[]{:S(2)}) collective-permute-start(bf16[4,256,128]{2,1,0:T(8,128)(2,1)S(1)} %shard_map.75.refs_0_), channel_id=1, source_target_pairs={{0,4},{4,0},{1,5},{5,1},{2,6},{6,2},{3,7},{7,3},{8,12},{12,8},{9,1... | collective-permute-start | bytes 786440 | tf_op jit(solution)/shard_map/ppermute | solution.py:42
  80.3 9.8 %collective-permute-done.8.refs_1_ = bf16[4,256,128]{2,1,0:T(8,128)(2,1)S(1)} collective-permute-done((bf16[4,256,128]{2,1,0:T(8,128)(2,1)S(1)}, bf16[4,256,128]{2,1,0:T(8,128)(2,1)S(1)}, u32[]{:S(2)}, u32[]{:S(2)}) %collective-permute-start.8) | collective-permute-done | bytes 262176 | tf_op jit(solution)/shard_map/ppermute | solution.py:42
  90.2 3.4 %shard_map.76 = (f32[4,256,128]{2,1,0:T(8,128)S(1)}, bf16[4,256,128]{2,1,0:T(8,128)(2,1)S(1)}) custom-call(f32[1]{0:T(128)} %dynamic_slice.3.scale_ref, bf16[4,4,512,256]{3,2,1,0:T(8,128)(2,1)S(1)} %shard_map.71.map_ref, bf16[4,256,512]{2,1,0:T(8,128)(2,1)S(1)} %copy-done.7, bf16[4,256,128]{2,1,0:T(8,128)(2,1)S(1)} %get-tuple-element.38.obs_ref, ...), custom_call_target="tpu_custom_call" | custom-call | flops 2147483648 | bytes 8388608 | tf_op jit(solution)/shard_map/pallas_call | solution.py:248
  93.7 13.4 %collective-permute-done.9.refs_1_ = bf16[4,256,128]{2,1,0:T(8,128)(2,1)S(1)} collective-permute-done((bf16[4,256,128]{2,1,0:T(8,128)(2,1)S(1)}, bf16[4,256,128]{2,1,0:T(8,128)(2,1)S(1)}, u32[]{:S(2)}, u32[]{:S(2)}) %collective-permute-start.9) | collective-permute-done | bytes 262176 | tf_op jit(solution)/shard_map/ppermute | solution.py:42
  107.1 1.1 shard_map.77
  108.2 3.7 %all-to-all-start.2 = ((bf16[16,256,128]{2,1,0:T(8,128)(2,1)}), bf16[16,256,128]{2,1,0:T(8,128)(2,1)S(1)}, u32[]{:S(2)}, u32[]{:S(2)}) async-start(bf16[16,256,128]{2,1,0:T(8,128)(2,1)} %bitcast.7), calls=%async_computation.2 | async-start | bytes 2097152 | tf_op jit(solution)/shard_map/all_to_all | solution.py:270
  111.9 2.2 %copy-done.2 = bf16[4,4,512,256]{3,2,1,0:T(8,128)(2,1)S(1)} copy-done((bf16[4,4,512,256]{3,2,1,0:T(8,128)(2,1)S(1)}, bf16[4,4,512,256]{3,2,1,0:T(8,128)(2,1)}, u32[]{:S(2)}) %copy-start.2) | copy-done | bytes 4194328
  114.1 1.2 copy-done.8
  115.3 3.4 %shard_map.72.refs_0_ = bf16[4,256,128]{2,1,0:T(8,128)(2,1)S(1)} custom-call(f32[1]{0:T(128)} %dynamic_slice.3.scale_ref, bf16[4,4,512,256]{3,2,1,0:T(8,128)(2,1)S(1)} %copy-done.2, bf16[4,256,512]{2,1,0:T(8,128)(2,1)S(1)} %copy-done.8, bf16[4,256,128]{2,1,0:T(8,128)(2,1)S(1)} %get-tuple-element.33.obs_ref, f32[4,256,128]{2,1,0:T(8,128)S(1)} %get-tuple-element.32.noise_ref), custom_call_target="tpu_custom_call" | custom-call | flops 2147483648 | bytes 8388608 | tf_op jit(solution)/shard_map/pallas_call | solution.py:248
  118.7 2.2 %collective-permute-start.6 = (bf16[4,256,128]{2,1,0:T(8,128)(2,1)S(1)}, bf16[4,256,128]{2,1,0:T(8,128)(2,1)S(1)}, u32[]{:S(2)}, u32[]{:S(2)}) collective-permute-start(bf16[4,256,128]{2,1,0:T(8,128)(2,1)S(1)} %shard_map.72.refs_0_), channel_id=1, source_target_pairs={{0,4},{4,0},{1,5},{5,1},{2,6},{6,2},{3,7},{7,3},{8,12},{12,8},{9,1... | collective-permute-start | bytes 786440 | tf_op jit(solution)/shard_map/ppermute | solution.py:42
  120.9 12.9 %collective-permute-done.6.refs_1_ = bf16[4,256,128]{2,1,0:T(8,128)(2,1)S(1)} collective-permute-done((bf16[4,256,128]{2,1,0:T(8,128)(2,1)S(1)}, bf16[4,256,128]{2,1,0:T(8,128)(2,1)S(1)}, u32[]{:S(2)}, u32[]{:S(2)}) %collective-permute-start.6) | collective-permute-done | bytes 262176 | tf_op jit(solution)/shard_map/ppermute | solution.py:42
  133.9 3.4 %shard_map.73 = (f32[4,256,128]{2,1,0:T(8,128)S(1)}, bf16[4,256,128]{2,1,0:T(8,128)(2,1)S(1)}) custom-call(f32[1]{0:T(128)} %dynamic_slice.3.scale_ref, bf16[4,4,512,256]{3,2,1,0:T(8,128)(2,1)S(1)} %copy-done.2, bf16[4,256,512]{2,1,0:T(8,128)(2,1)S(1)} %copy-done.8, bf16[4,256,128]{2,1,0:T(8,128)(2,1)S(1)} %get-tuple-element.33.obs_ref, ...), custom_call_target="tpu_custom_call" | custom-call | flops 2147483648 | bytes 8388608 | tf_op jit(solution)/shard_map/pallas_call | solution.py:248
  137.4 12.0 %collective-permute-done.7.refs_1_ = bf16[4,256,128]{2,1,0:T(8,128)(2,1)S(1)} collective-permute-done((bf16[4,256,128]{2,1,0:T(8,128)(2,1)S(1)}, bf16[4,256,128]{2,1,0:T(8,128)(2,1)S(1)}, u32[]{:S(2)}, u32[]{:S(2)}) %collective-permute-start.7) | collective-permute-done | bytes 262176 | tf_op jit(solution)/shard_map/ppermute | solution.py:42
  149.3 1.1 shard_map.74
  150.5 3.7 %all-to-all-start.1 = ((bf16[16,256,128]{2,1,0:T(8,128)(2,1)}), bf16[16,256,128]{2,1,0:T(8,128)(2,1)S(1)}, u32[]{:S(2)}, u32[]{:S(2)}) async-start(bf16[16,256,128]{2,1,0:T(8,128)(2,1)} %bitcast.6), calls=%async_computation.1 | async-start | bytes 2097152 | tf_op jit(solution)/shard_map/all_to_all | solution.py:270
  154.2 2.2 %copy-done.3 = bf16[4,4,512,256]{3,2,1,0:T(8,128)(2,1)S(1)} copy-done((bf16[4,4,512,256]{3,2,1,0:T(8,128)(2,1)S(1)}, bf16[4,4,512,256]{3,2,1,0:T(8,128)(2,1)}, u32[]{:S(2)}) %copy-start.3) | copy-done | bytes 4194328
  156.4 1.2 copy-done.9
  157.6 3.1 %shard_map.78 = (bf16[256,256]{1,0:T(8,128)(2,1)S(1)}, bf16[256,256]{1,0:T(8,128)(2,1)S(1)}, bf16[256,256]{1,0:T(8,128)(2,1)S(1)}, bf16[256,256]{1,0:T(8,128)(2,1)S(1)}) custom-call(s32[3]{0:T(128)S(1)} %pad_add_fusion.place_ref, f32[1]{0:T(128)} %dynamic_slice.3.scale_ref, bf16[4,4,512,256]{3,2,1,0:T(8,128)(2,1)S(1)} %copy-done.3, ...), custom_call_target="tpu_custom_call" | custom-call | flops 2147483648 | bytes 8388608 | tf_op jit(solution)/shard_map/pallas_call | solution.py:271
  160.7 2.0 %collective-permute-start.10 = (bf16[256,256]{1,0:T(8,128)(2,1)S(1)}, bf16[256,256]{1,0:T(8,128)(2,1)S(1)}, u32[]{:S(2)}, u32[]{:S(2)}) collective-permute-start(bf16[256,256]{1,0:T(8,128)(2,1)S(1)} %get-tuple-element.45), channel_id=1, source_target_pairs={{0,1},{1,0},{2,3},{3,2},{4,5},{5,4},{6,7},{7,6},{8,9},{9,8},{10,11... | collective-permute-start | bytes 393224 | tf_op jit(solution)/shard_map/ppermute | solution.py:42
  162.7 1.4 collective-permute-start.11
  164.3 12.6 %collective-permute-done.10.refs_3_ = bf16[256,256]{1,0:T(8,128)(2,1)S(1)} collective-permute-done((bf16[256,256]{1,0:T(8,128)(2,1)S(1)}, bf16[256,256]{1,0:T(8,128)(2,1)S(1)}, u32[]{:S(2)}, u32[]{:S(2)}) %collective-permute-start.10) | collective-permute-done | bytes 131104 | tf_op jit(solution)/shard_map/ppermute | solution.py:42
  176.9 3.1 %shard_map.79 = (f32[16,2,256,128]{3,2,1,0:T(8,128)}, f32[4,512,128]{2,1,0:T(8,128)}) custom-call(s32[3]{0:T(128)S(1)} %pad_add_fusion.place_ref, bf16[16,256,128]{2,1,0:T(8,128)(2,1)S(1)} %all-to-all-done.1.refs_0_, bf16[16,256,128]{2,1,0:T(8,128)(2,1)S(1)} %all-to-all-done.2.refs_1_, bf16[256,256]{1,0:T(8,128)(2,1)S(1)} %get-tuple-element.44.refs_2_, ...), custom_call_target="tpu_custom_call" | custom-call | bytes 8388608 | tf_op jit(solution)/shard_map/pallas_call | solution.py:280
  (36 shorter events, 6.8 us)
Async XLA Ops:
  0.6 6.6 %copy-start.5 = (f32[256]{0:T(256)S(1)}, f32[256]{0:T(256)}, u32[]{:S(2)}) copy-start(f32[256]{0:T(256)} %param.7) | copy-start | bytes 3076
  0.6 11.3 %copy-start.4 = (bf16[256,512]{1,0:T(8,128)(2,1)S(1)}, bf16[256,512]{1,0:T(8,128)(2,1)}, u32[]{:S(2)}) copy-start(bf16[256,512]{1,0:T(8,128)(2,1)} %own_ref.3) | copy-start | bytes 786436
  0.6 71.1 %all-to-all-start = ((bf16[16,512,256]{2,1,0:T(8,128)(2,1)}), bf16[16,512,256]{2,1,0:T(8,128)(2,1)}, u32[]{:S(2)}, u32[]{:S(2)}) async-start(bf16[16,512,256]{2,1,0:T(8,128)(2,1)} %bitcast.10), calls=%async_computation | async-start | bytes 8388608 | tf_op jit(solution)/shard_map/all_to_all | solution.py:211
  7.1 10.9 %copy-start.10 = (f32[16]{0:T(128)S(1)}, f32[16]{0:T(128)}, u32[]{:S(2)}) copy-start(f32[16]{0:T(128)} %param.9) | copy-start | bytes 196
  7.3 2.2 %copy-start = (f32[16,2,256,128]{3,2,1,0:T(8,128)S(1)}, f32[16,2,256,128]{3,2,1,0:T(8,128)}, u32[]{:S(2)}) copy-start(f32[16,2,256,128]{3,2,1,0:T(8,128)} %obs_ref.1) | copy-start | bytes 12582916
  10.6 1.4 collective-permute-start
  12.6 57.2 %collective-permute-start.2 = (bf16[256,512]{1,0:T(8,128)(2,1)S(1)}, bf16[256,512]{1,0:T(8,128)(2,1)S(1)}, u32[]{:S(2)}, u32[]{:S(2)}) collective-permute-start(bf16[256,512]{1,0:T(8,128)(2,1)S(1)} %get-tuple-element.28), channel_id=1, source_target_pairs={{0,2},{1,3},{2,0},{3,1},{4,6},{5,7},{6,4},{7,5},{8,10},{9,11},{10,... | collective-permute-start | bytes 786440 | tf_op jit(solution)/shard_map/ppermute | solution.py:42
  14.5 51.8 %collective-permute-start.4 = (bf16[272,256]{1,0:T(8,128)(2,1)S(1)}, bf16[272,256]{1,0:T(8,128)(2,1)S(1)}, u32[]{:S(2)}, u32[]{:S(2)}) collective-permute-start(bf16[272,256]{1,0:T(8,128)(2,1)S(1)} %get-tuple-element.30), channel_id=1, source_target_pairs={{0,16},{8,24},{16,0},{24,8},{1,17},{9,25},{17,1},{25,9},{2,18},{10... | collective-permute-start | bytes 417800 | tf_op jit(solution)/shard_map/ppermute | solution.py:42
  16.0 52.4 %collective-permute-start.5 = (bf16[272,256]{1,0:T(8,128)(2,1)S(1)}, bf16[272,256]{1,0:T(8,128)(2,1)S(1)}, u32[]{:S(2)}, u32[]{:S(2)}) collective-permute-start(bf16[272,256]{1,0:T(8,128)(2,1)S(1)} %get-tuple-element.31), channel_id=1, source_target_pairs={{0,24},{8,16},{16,8},{24,0},{1,25},{9,17},{17,9},{25,1},{2,26},{10... | collective-permute-start | bytes 417800 | tf_op jit(solution)/shard_map/ppermute | solution.py:42
  16.0 53.8 %collective-permute-start.3 = (bf16[256,256]{1,0:T(8,128)(2,1)S(1)}, bf16[256,256]{1,0:T(8,128)(2,1)S(1)}, u32[]{:S(2)}, u32[]{:S(2)}) collective-permute-start(bf16[256,256]{1,0:T(8,128)(2,1)S(1)} %get-tuple-element.27), channel_id=1, source_target_pairs={{0,3},{1,2},{2,1},{3,0},{4,7},{5,6},{6,5},{7,4},{8,11},{9,10},{10,... | collective-permute-start | bytes 393224 | tf_op jit(solution)/shard_map/ppermute | solution.py:42
  17.4 52.4 %collective-permute-start.1 = (bf16[256,256]{1,0:T(8,128)(2,1)S(1)}, bf16[256,256]{1,0:T(8,128)(2,1)S(1)}, u32[]{:S(2)}, u32[]{:S(2)}) collective-permute-start(bf16[256,256]{1,0:T(8,128)(2,1)S(1)} %get-tuple-element.27), channel_id=1, source_target_pairs={{0,1},{1,0},{2,3},{3,2},{4,5},{5,4},{6,7},{7,6},{8,9},{9,8},{10,11... | collective-permute-start | bytes 393224 | tf_op jit(solution)/shard_map/ppermute | solution.py:42
  70.8 1.0 copy-start.6
  71.7 2.5 %copy-start.7 = (bf16[4,256,512]{2,1,0:T(8,128)(2,1)S(1)}, bf16[4,256,512]{2,1,0:T(8,128)(2,1)}, u32[]{:S(2)}) copy-start(bf16[4,256,512]{2,1,0:T(8,128)(2,1)} %copy-done.6) | copy-start | bytes 3145732
  74.0 19.5 %copy-start.1 = (bf16[4,4,512,256]{3,2,1,0:T(8,128)(2,1)}, bf16[4,4,512,256]{3,2,1,0:T(8,128)(2,1)S(1)}, u32[]{:S(2)}) copy-start(bf16[4,4,512,256]{3,2,1,0:T(8,128)(2,1)S(1)} %shard_map.71.map_ref) | copy-start | bytes 12582916
  77.7 12.5 %collective-permute-start.8 = (bf16[4,256,128]{2,1,0:T(8,128)(2,1)S(1)}, bf16[4,256,128]{2,1,0:T(8,128)(2,1)S(1)}, u32[]{:S(2)}, u32[]{:S(2)}) collective-permute-start(bf16[4,256,128]{2,1,0:T(8,128)(2,1)S(1)} %shard_map.75.refs_0_), channel_id=1, source_target_pairs={{0,4},{4,0},{1,5},{5,1},{2,6},{6,2},{3,7},{7,3},{8,12},{12,8},{9,1... | collective-permute-start | bytes 786440 | tf_op jit(solution)/shard_map/ppermute | solution.py:42
  93.6 13.5 %collective-permute-start.9 = (bf16[4,256,128]{2,1,0:T(8,128)(2,1)S(1)}, bf16[4,256,128]{2,1,0:T(8,128)(2,1)S(1)}, u32[]{:S(2)}, u32[]{:S(2)}) collective-permute-start(bf16[4,256,128]{2,1,0:T(8,128)(2,1)S(1)} %get-tuple-element.40.refs_0_), channel_id=1, source_target_pairs={{0,4},{4,0},{1,5},{5,1},{2,6},{6,2},{3,7},{7,3},{8,12},{12,8},{9,1... | collective-permute-start | bytes 786440 | tf_op jit(solution)/shard_map/ppermute | solution.py:42
  108.2 42.2 %all-to-all-start.2 = ((bf16[16,256,128]{2,1,0:T(8,128)(2,1)}), bf16[16,256,128]{2,1,0:T(8,128)(2,1)S(1)}, u32[]{:S(2)}, u32[]{:S(2)}) async-start(bf16[16,256,128]{2,1,0:T(8,128)(2,1)} %bitcast.7), calls=%async_computation.2 | async-start | bytes 2097152 | tf_op jit(solution)/shard_map/all_to_all | solution.py:270
  111.9 2.2 %copy-start.2 = (bf16[4,4,512,256]{3,2,1,0:T(8,128)(2,1)S(1)}, bf16[4,4,512,256]{3,2,1,0:T(8,128)(2,1)}, u32[]{:S(2)}) copy-start(bf16[4,4,512,256]{3,2,1,0:T(8,128)(2,1)} %copy-done.1) | copy-start | bytes 12582916
  114.1 1.2 copy-start.8
  118.7 15.1 %collective-permute-start.6 = (bf16[4,256,128]{2,1,0:T(8,128)(2,1)S(1)}, bf16[4,256,128]{2,1,0:T(8,128)(2,1)S(1)}, u32[]{:S(2)}, u32[]{:S(2)}) collective-permute-start(bf16[4,256,128]{2,1,0:T(8,128)(2,1)S(1)} %shard_map.72.refs_0_), channel_id=1, source_target_pairs={{0,4},{4,0},{1,5},{5,1},{2,6},{6,2},{3,7},{7,3},{8,12},{12,8},{9,1... | collective-permute-start | bytes 786440 | tf_op jit(solution)/shard_map/ppermute | solution.py:42
  137.3 12.0 %collective-permute-start.7 = (bf16[4,256,128]{2,1,0:T(8,128)(2,1)S(1)}, bf16[4,256,128]{2,1,0:T(8,128)(2,1)S(1)}, u32[]{:S(2)}, u32[]{:S(2)}) collective-permute-start(bf16[4,256,128]{2,1,0:T(8,128)(2,1)S(1)} %get-tuple-element.36.refs_0_), channel_id=1, source_target_pairs={{0,4},{4,0},{1,5},{5,1},{2,6},{6,2},{3,7},{7,3},{8,12},{12,8},{9,1... | collective-permute-start | bytes 786440 | tf_op jit(solution)/shard_map/ppermute | solution.py:42
  150.5 26.4 %all-to-all-start.1 = ((bf16[16,256,128]{2,1,0:T(8,128)(2,1)}), bf16[16,256,128]{2,1,0:T(8,128)(2,1)S(1)}, u32[]{:S(2)}, u32[]{:S(2)}) async-start(bf16[16,256,128]{2,1,0:T(8,128)(2,1)} %bitcast.6), calls=%async_computation.1 | async-start | bytes 2097152 | tf_op jit(solution)/shard_map/all_to_all | solution.py:270
  154.2 2.2 %copy-start.3 = (bf16[4,4,512,256]{3,2,1,0:T(8,128)(2,1)S(1)}, bf16[4,4,512,256]{3,2,1,0:T(8,128)(2,1)}, u32[]{:S(2)}) copy-start(bf16[4,4,512,256]{3,2,1,0:T(8,128)(2,1)} %copy-done.1) | copy-start | bytes 12582916
  156.4 1.2 copy-start.9
  160.7 16.1 %collective-permute-start.10 = (bf16[256,256]{1,0:T(8,128)(2,1)S(1)}, bf16[256,256]{1,0:T(8,128)(2,1)S(1)}, u32[]{:S(2)}, u32[]{:S(2)}) collective-permute-start(bf16[256,256]{1,0:T(8,128)(2,1)S(1)} %get-tuple-element.45), channel_id=1, source_target_pairs={{0,1},{1,0},{2,3},{3,2},{4,5},{5,4},{6,7},{7,6},{8,9},{9,8},{10,11... | collective-permute-start | bytes 393224 | tf_op jit(solution)/shard_map/ppermute | solution.py:42
  162.7 14.1 %collective-permute-start.11 = (bf16[256,256]{1,0:T(8,128)(2,1)S(1)}, bf16[256,256]{1,0:T(8,128)(2,1)S(1)}, u32[]{:S(2)}, u32[]{:S(2)}) collective-permute-start(bf16[256,256]{1,0:T(8,128)(2,1)S(1)} %get-tuple-element.46), channel_id=1, source_target_pairs={{0,2},{1,3},{2,0},{3,1},{4,6},{5,7},{6,4},{7,5},{8,10},{9,11},{10,... | collective-permute-start | bytes 393224 | tf_op jit(solution)/shard_map/ppermute | solution.py:42
  164.2 12.7 %collective-permute-start.12 = (bf16[256,256]{1,0:T(8,128)(2,1)S(1)}, bf16[256,256]{1,0:T(8,128)(2,1)S(1)}, u32[]{:S(2)}, u32[]{:S(2)}) collective-permute-start(bf16[256,256]{1,0:T(8,128)(2,1)S(1)} %get-tuple-element.47), channel_id=1, source_target_pairs={{0,3},{1,2},{2,1},{3,0},{4,7},{5,6},{6,5},{7,4},{8,11},{9,10},{10,... | collective-permute-start | bytes 393224 | tf_op jit(solution)/shard_map/ppermute | solution.py:42

commit v10 on v9

v10 whole, which is shorter than its diff:
```python
import functools

import jax
import jax.numpy as jnp
from jax import lax
from jax.experimental import pallas as pl
from jax.experimental.pallas import tpu as pltpu
from jax.sharding import Mesh, PartitionSpec as P

ITERS = 2
relax_step = 0.25
CORES = 2
LANES = 128
HALF = LANES // 2
VMEM_LIMIT = 16 * 2**20
VMEM = pl.BlockSpec(memory_space=pltpu.VMEM)
SMEM = pl.BlockSpec(memory_space=pltpu.SMEM)
ANY = pl.BlockSpec(memory_space=pl.ANY)
bf16, f32 = jnp.bfloat16, jnp.float32


def shape(dims, dtype):
    return jax.ShapeDtypeStruct(dims, dtype)


def call(kernel, in_specs, out_shape, scratch=(), out_specs=None, flops=0, moved=0, aliases=None):
    return pl.pallas_call(
        kernel,
        input_output_aliases=aliases or {},
        in_specs=in_specs,
        out_specs=out_specs or [VMEM] * len(out_shape),
        out_shape=out_shape,
        scratch_shapes=list(scratch),
        cost_estimate=pl.CostEstimate(flops=flops, bytes_accessed=moved, transcendentals=0),
        compiler_params=pltpu.CompilerParams(vmem_limit_bytes=VMEM_LIMIT),
    )


def dot(a, b):
    return jnp.dot(a, b, preferred_element_type=f32)


def dot_nt(a, b):
    return lax.dot_general(a, b, (((1,), (1,)), ((), ())), preferred_element_type=f32)


def data_kernel(groups, quads, place_ref, obs_ref, noise_ref, *refs):
    outs, (held, sems) = refs[:groups], refs[groups:]
    sensors = obs_ref.shape[2]
    loads = []
    for e in range(groups // CORES):
        for j in range(CORES):
            freq = (CORES * (place_ref[0] ^ e) + j) * quads + place_ref[1]
            loads.append(pltpu.make_async_copy(obs_ref.at[freq], held.at[e, j], sems.at[e, j]))
            loads[-1].start()
    noise = noise_ref[...]
    high = noise.astype(bf16)
    low = (noise - high.astype(f32)).astype(bf16)
    tail = jnp.concatenate([jnp.broadcast_to(high, (8, sensors)), jnp.broadcast_to(low, (8, sensors))], 0)
    for load in loads:
        load.wait()
    for d in range(groups):
        e, s = divmod(d, CORES)
        second = (place_ref[2] ^ s) == 1
        for j in range(CORES):
            re, im = held[e, j, 0], held[e, j, 1]
            low_half = jnp.concatenate([re[:, :HALF], im[:, :HALF]], 1)
            high_half = jnp.concatenate([re[:, HALF:], im[:, HALF:]], 1)
            outs[d][:sensors, j * LANES:(j + 1) * LANES] = jnp.where(second, high_half, low_half).astype(bf16)
        outs[d][sensors:, :] = tail


def cut_kernel(place_ref, map_ref, after_ref, out_ref):
    out_ref[...] = map_ref[...]


def prior_kernel(place_ref, own_ref, after_ref, full_ref, diagonal_ref):
    cells = own_ref.shape[0]
    full_ref[...] = own_ref[...]
    diagonal_ref[...] = own_ref[:, pl.ds(pl.multiple_of((place_ref[1] & 1) * cells, cells), cells)]


def gather_kernel(groups, quads, place_ref, own_ref, *refs):
    came, data = refs[:quads - 1], refs[quads - 1:quads - 1 + groups]
    prior_ref, noise_ref, *streams = refs[quads - 1 + groups:]
    quad = place_ref[1]
    sensors, cells = streams[0].shape[1], own_ref.shape[0]
    on, off = (pl.ds(pl.multiple_of(p * cells, cells), cells) for p in (quad & 1, 1 - (quad & 1)))
    for d in range(0, quads, 2):
        rows = own_ref if d == 0 else came[d - 1]
        prior_ref[quad ^ d] = rows[...]
        prior_ref[quad ^ d ^ 1, :, on] = rows[:, off].T
        prior_ref[quad ^ d ^ 1, :, off] = came[d][...]
    row = lax.broadcasted_iota(jnp.int32, (sensors, sensors), 0)
    col = lax.broadcasted_iota(jnp.int32, (sensors, sensors), 1)
    for d in range(groups):
        at = CORES * (place_ref[0] ^ (d // CORES)) + d % CORES
        for s in range(CORES):
            streams[s][at] = data[d][:sensors, s * LANES:(s + 1) * LANES]
        both = data[d][sensors:, :].astype(f32)
        noise_row = both[0:1, :] + both[8:9, :]
        noise = jnp.sum(jnp.where(row == col, noise_row, 0.0), 1, keepdims=True)
        noise_ref[at] = jnp.broadcast_to(noise, (sensors, LANES))


def chunk(maps, r, q):
    return maps[r % CORES][r // CORES, q]


def source(maps, sides_ref, prior_ref, scale):
    pairs, quads, _, cells = maps[0].shape
    per_block = prior_ref.shape[2] // cells
    out = []
    for block in range(quads // per_block):
        members = range(block * per_block, (block + 1) * per_block)
        parts = []
        for q in members:
            u = jnp.zeros((LANES, cells), f32)
            for r in range(pairs * CORES):
                u += dot(sides_ref[r], chunk(maps, r, q))
            parts.append(u.astype(bf16))
        ub = jnp.concatenate(parts, 1)
        out += [(dot_nt(prior_ref[q], ub) * scale).astype(bf16) for q in members]
    return out


def sides(z):
    half = z.shape[1] // 2
    return jnp.concatenate([z, jnp.concatenate([z[:, half:], -z[:, :half]], 1)], 0).T


def bring_kernel(map_ref, out_ref, sem):
    copy = pltpu.make_async_copy(map_ref, out_ref, sem)
    copy.start()
    copy.wait()


def step_kernel(stage, n_pred, scale_ref, mine_ref, theirs_ref, prior_ref, obs_ref, noise_ref, *refs):
    maps = (mine_ref, theirs_ref)
    pairs, quads, double, _ = mine_ref.shape
    sensors = double // 2
    preds, refs = refs[:n_pred], refs[n_pred:]
    if stage > 0:
        next_ref, refs = refs[0], refs[1:]
    out_ref, sides_ref = refs
    for r in range(pairs * CORES):
        obs = obs_ref[r].astype(f32)
        now = relax_step * obs
        if stage > 0:
            predicted = sum(p[r].astype(f32) for p in preds)
            now = now + relax_step * (obs - predicted - noise_ref[r] * now)
            next_ref[r] = now
        sides_ref[r] = sides(now.astype(bf16))
    sources = source(maps, sides_ref, prior_ref, scale_ref[0])
    turned = [jnp.concatenate([-v[:, HALF:], v[:, :HALF]], 1) for v in sources]
    for r in range(pairs * CORES):
        total = jnp.zeros((sensors, LANES), f32)
        for q in range(quads):
            rows = chunk(maps, r, q)
            total += dot(rows[:sensors], sources[q]) + dot(rows[sensors:], turned[q])
        out_ref[r] = total.astype(bf16)


def last_kernel(n_pred, place_ref, noise_ref, obs_ref, held_ref, *refs):
    preds, (final_ref, out_ref) = refs[:n_pred], refs[n_pred:]
    for r in range(final_ref.shape[0]):
        now = held_ref[r]
        predicted = sum(p[r].astype(f32) for p in preds)
        now = now + relax_step * (obs_ref[r].astype(f32) - predicted - noise_ref[r] * now)
        now = now.astype(bf16)
        final_ref[r] = now
        for q in range(out_ref.shape[1]):
            out_ref[r // CORES * CORES + (place_ref[2] ^ (r % CORES)), q] = now


def join(streams):
    return jnp.concatenate([x[:, :HALF] for x in streams] + [x[:, HALF:] for x in streams], 1)


def post_kernel(scale_ref, mine_ref, theirs_ref, prior_ref, final_ref, out_ref, sides_ref):
    for r in range(final_ref.shape[0]):
        sides_ref[r] = sides(final_ref[r])
    for q, v in enumerate(source((mine_ref, theirs_ref), sides_ref, prior_ref, scale_ref[0])):
        out_ref[q] = v


def part_kernel(place_ref, first_ref, second_ref, mine_ref, give_ref):
    flag = place_ref[2] == 1
    first, second = first_ref[...].astype(f32), second_ref[...].astype(f32)
    mine_ref[...] = jnp.where(flag, second, first).astype(bf16)
    give_ref[...] = jnp.where(flag, first, second).astype(bf16)


def merge_kernel(place_ref, mine_ref, got_ref, *outs):
    flag = place_ref[2] == 1
    for d, out in enumerate(outs):
        mine, got = mine_ref[place_ref[1] ^ d].astype(f32), got_ref[place_ref[1] ^ d].astype(f32)
        out[...] = join([jnp.where(flag, got, mine), jnp.where(flag, mine, got)]).astype(bf16)


def end_kernel(pairs, quads, place_ref, *refs):
    came, posts, refs = refs[:CORES], refs[CORES:CORES + quads], refs[CORES + quads:]
    dual_out, post_out, dual_ref, post_ref, sems = refs
    quad = place_ref[1]
    cells = post_ref.shape[1] // 2
    sends = []
    for d in range(quads):
        post_ref[d, pl.ds(0, cells, stride=2), :] = posts[d][:, :LANES].astype(f32)
        post_ref[d, pl.ds(1, cells, stride=2), :] = posts[d][:, LANES:].astype(f32)
        sends.append(pltpu.make_async_copy(post_ref.at[d], post_out.at[quad ^ d], sems.at[d]))
        sends[-1].start()
    for j in range(CORES):
        for pair in range(pairs):
            for q in range(quads):
                freq = (CORES * pair + j) * quads + q
                both = join([came[j][pair, core, q].astype(f32) for core in range(CORES)])
                dual_ref[freq, 0] = both[:, :LANES]
                dual_ref[freq, 1] = both[:, LANES:]
                sends.append(pltpu.make_async_copy(dual_ref.at[freq], dual_out.at[freq], sems.at[quads + freq]))
                sends[-1].start()
    for copy in sends:
        copy.wait()


def on_device(forward_map, observed, noise_var, prior_rows, prior_scale):
    frequencies, halves, sensors, cells = forward_map.shape
    pairs, quads, count = (lax.axis_size(a) for a in ("pair", "quad", "side"))
    groups, width = pairs * CORES, prior_rows.shape[1]
    pair, core, quad = (lax.axis_index(a) for a in ("pair", "core", "quad"))
    place = jnp.stack([pair, quad, core]).astype(jnp.int32)

    def swap(x, axes, distance):
        return lax.ppermute(x, axes, [(i, i ^ distance) for i in range(lax.axis_size(axes))])

    def to_chips(x):
        return lax.all_to_all(x, ("pair", "quad"), split_axis=0, concat_axis=0, tiled=True)

    whole = forward_map.reshape(pairs, CORES, quads, halves * sensors, cells)
    arrived = [to_chips(whole[:, 0].reshape(pairs * quads, halves * sensors, cells))]

    data = call(
        functools.partial(data_kernel, groups, quads),
        [SMEM, ANY, VMEM],
        [shape((sensors + 16, CORES * LANES), bf16)] * groups,
        [pltpu.VMEM((pairs, CORES, halves, sensors, LANES), f32), pltpu.SemaphoreType.DMA((pairs, CORES))],
        moved=groups * sensors * LANES * 12,
    )(place, observed, noise_var.reshape(1, sensors))
    data = [data[0]] + [swap(data[d], ("pair", "core"), d) for d in range(1, groups)]
    rows, diagonal = call(
        prior_kernel,
        [SMEM, VMEM, ANY],
        [shape((cells, width), bf16), shape((cells, cells), bf16)],
    )(place, prior_rows, data[1])
    came = [swap(diagonal if d % 2 else rows, "quad", d) for d in range(1, quads)]
    prior, noise, *streams = call(
        functools.partial(gather_kernel, groups, quads),
        [SMEM] + [VMEM] * (quads + groups),
        [shape((quads, cells, width), bf16), shape((groups, sensors, LANES), f32)]
        + [shape((groups, sensors, LANES), bf16)] * CORES,
        moved=8 * 2**20,
    )(place, prior_rows, *came, *data)

    for j in range(1, CORES):
        cut = pl.pallas_call(
            cut_kernel,
            grid_spec=pltpu.PrefetchScalarGridSpec(
                num_scalar_prefetch=1,
                grid=(pairs, quads),
                in_specs=[
                    pl.BlockSpec((1, 1, 1, halves * sensors, cells), lambda p, q, place: (p, j, q, 0, 0)),
                    ANY,
                ],
                out_specs=pl.BlockSpec((1, 1, 1, halves * sensors, cells), lambda p, q, place: (p, 0, q, 0, 0)),
            ),
            out_shape=shape((pairs, 1, quads, halves * sensors, cells), bf16),
        )(place, whole, data[1])
        arrived.append(to_chips(cut.reshape(pairs * quads, halves * sensors, cells)))

    def over_sides(partial):
        if count == 2:
            return [partial, swap(partial, "side", 1)]
        return [lax.psum(partial, "side")]

    wide, narrow = shape((groups, sensors, LANES), f32), shape((groups, sensors, LANES), bf16)
    sides_scratch = pltpu.VMEM((groups, LANES, halves * sensors), bf16)
    duals, posts = [], []
    for j in range(CORES):
        scale = prior_scale[(CORES * pair + j) * quads + quad].reshape(1)
        mine = arrived[j].reshape(pairs, quads, halves * sensors, cells)
        mine = call(bring_kernel, [ANY], [shape(mine.shape, bf16)], [pltpu.SemaphoreType.DMA], moved=4 * 2**20)(mine)[0]
        maps = [mine, swap(mine, "core", 1)]

        def step(stage, preds):
            operands = [scale, *maps, prior, streams[j], noise] + preds
            return call(
                functools.partial(step_kernel, stage, len(preds)),
                [SMEM] + [VMEM] * (len(operands) - 1),
                [wide, narrow] if stage > 0 else [narrow],
                [sides_scratch],
                flops=2**31,
                moved=8 * 2**20,
            )(*operands)

        preds = over_sides(step(0, [])[0])
        held, partial = step(1, preds)
        preds = over_sides(partial)
        final, out = call(
            functools.partial(last_kernel, len(preds)),
            [SMEM] + [VMEM] * (3 + len(preds)),
            [narrow, shape((groups, quads, sensors, LANES), bf16)],
            moved=2 * 2**20,
        )(place, noise, streams[j], held, *preds)
        out = out.reshape(frequencies, sensors, LANES)
        out = lax.all_to_all(out, ("pair", "core", "quad"), split_axis=0, concat_axis=0, tiled=True)
        duals.append(out.reshape(pairs, CORES, quads, sensors, LANES))
        posts.append(
            call(
                post_kernel,
                [SMEM] + [VMEM] * 4,
                [shape((quads, cells, LANES), bf16)],
                [sides_scratch],
                flops=2**30,
                moved=8 * 2**20,
            )(scale, *maps, prior, final)[0]
        )
    piece = shape((quads, cells, LANES), bf16)
    mine, give = call(part_kernel, [SMEM, VMEM, VMEM], [piece, piece], moved=2**20)(place, *posts)
    posts = call(
        merge_kernel,
        [SMEM, VMEM, VMEM],
        [shape((cells, 2 * LANES), bf16)] * quads,
        moved=2**20,
    )(place, mine, swap(give, "core", 1))
    posts = [posts[0]] + [swap(posts[d], "quad", d) for d in range(1, quads)]
    dual, posterior = call(
        functools.partial(end_kernel, pairs, quads),
        [SMEM] + [VMEM] * (CORES + quads),
        [shape((frequencies, halves, sensors, LANES), f32), shape((quads, cells * 2, LANES), f32)],
        [
            pltpu.VMEM((frequencies, halves, sensors, LANES), f32),
            pltpu.VMEM((quads, cells * 2, LANES), f32),
            pltpu.SemaphoreType.DMA((quads + frequencies,)),
        ],
        [ANY, ANY],
        moved=8 * 2**20,
    )(place, *duals, *posts)
    return dual, posterior.reshape(quads, cells, 2, LANES)


def solution(mesh):
    groups, space = mesh.devices.shape

    def run(forward_map, observed, noise_var, prior_rows, prior_scale):
        quads = forward_map.shape[0] // groups
        split = Mesh(
            mesh.devices.reshape(groups // CORES, CORES, space // quads, quads), ("pair", "core", "side", "quad")
        )
        return jax.shard_map(
            on_device,
            mesh=split,
            in_specs=(
                P(None, None, ("pair", "core"), ("side", "quad")),
                P(None, None, ("pair", "core"), None),
                P(("pair", "core")),
                P(("side", "quad"), None),
                P(),
            ),
            out_specs=(P(None, None, ("pair", "core"), None), P(("pair", "core"), ("side", "quad"), None, None)),
            check_vma=False,
        )(forward_map, observed, noise_var, prior_rows, prior_scale)

    return run
```

time: 181 us -> 207 us (1.14)
  Pallas kernels: 27.1 us -> 49.3 us
  waiting for transfers between devices: 113 us -> 103 us
  local copies, waits for them, and re-layouts: 10.8 us -> 20.4 us
  starting transfers between devices: 28.3 us -> 32.1 us
    ppermute x13 -> x16, waiting for transfers between devices: 113 us -> 85 us  [swap(): lax.ppermute(x, axes, [(i, i ^ distance) for i in range(lax.axis_size(axe...]
    all_to_all x3 -> x4, waiting for transfers between devices: 0.01 us -> 17.6 us  [the longest x2 17.6 us: to_chips(): lax.all_to_all(x, ('pair', 'quad'), split_axis=0, concat_axis=0, tiled=True)]
    pallas_call x5 -> x10, Pallas kernels: 10.7 us -> 24.3 us  [the longest x2 8.2 us: on_device(): call(post_kernel, [SMEM] + [VMEM] * 4, [shape((quads, cells, LANES), bf16...]
    pallas_call x4, Pallas kernels: 13.7 us -> 21.1 us  [step(): call(functools.partial(step_kernel, stage, len(preds)), [SMEM] + [VMEM] *...]
    unnamed x22 -> x54, local copies, waits for them, and re-layouts: 10.2 us -> 16.7 us
    all_to_all x3 -> x4, starting transfers between devices: 13.9 us -> 18.9 us  [the longest x2 10.7 us: to_chips(): lax.all_to_all(x, ('pair', 'quad'), split_axis=0, concat_axis=0, tiled=True)]
    slice x0 -> x1, local copies, waits for them, and re-layouts: none -> 3.05 us  [on_device(): whole[:, 0].reshape(pairs * quads, halves * sensors, cells)]
    ppermute x13 -> x16, starting transfers between devices: 14.4 us -> 13.2 us  [swap(): lax.ppermute(x, axes, [(i, i ^ distance) for i in range(lax.axis_size(axe...]
  transfers between devices with their start and end apart: 16 -> 20, of which waited for: 9 -> 10; matrix products, arithmetic and copies ran while one was open for 0% -> 0% of each run, Pallas kernels for 8% -> 22%
where the time goes in v10:
time: 207 us; the launch traced here: 205 us
  waiting for transfers between devices  103 us (50%)
  Pallas kernels  49.3 us (24%)
  starting transfers between devices  32.1 us (16%)
  local copies, waits for them, and re-layouts  20.4 us (10%)
    ppermute x16, waiting for transfers between devices, swap(): lax.ppermute(x, axes, [(i, i ^ distance) for i in range(lax.axis_size(axe...  85 us
    pallas_call x4, Pallas kernels, step(): call(functools.partial(step_kernel, stage, len(preds)), [SMEM] + [VMEM] *...  21.1 us
    all_to_all x2, waiting for transfers between devices, to_chips(): lax.all_to_all(x, ('pair', 'quad'), split_axis=0, concat_axis=0, tiled=True)  17.6 us
    unnamed x54, local copies, waits for them, and re-layouts  16.7 us
    ppermute x16, starting transfers between devices, swap(): lax.ppermute(x, axes, [(i, i ^ distance) for i in range(lax.axis_size(axe...  13.2 us
    all_to_all x2, starting transfers between devices, to_chips(): lax.all_to_all(x, ('pair', 'quad'), split_axis=0, concat_axis=0, tiled=True)  10.7 us
    pallas_call x2, Pallas kernels, on_device(): call(post_kernel, [SMEM] + [VMEM] * 4, [shape((quads, cells, LANES), bf16...  8.2 us
    all_to_all x2, starting transfers between devices, on_device(): lax.all_to_all(out, ('pair', 'core', 'quad'), split_axis=0, concat_axis=0...  8.19 us
  transfers between devices with their start and end apart: 20, of which 10 were waited for; matrix products, arithmetic and copies ran while one was open for 0% of the time, Pallas kernels for 22%

profile of v10, /device:TPU:0, one launch (start us, length us, event | category | flops | bytes accessed | tf_op | source)
XLA Modules:
  0.0 205.5 jit_solution(11247696696465639979)
XLA Ops:
  0.6 3.0 %slice.4 = bf16[2,1,4,512,256]{4,3,2,1,0:T(8,128)(2,1)} slice(bf16[2,2,4,512,256]{4,3,2,1,0:T(8,128)(2,1)} %bitcast.19), slice={[0:2], [0:1], [0:4], [0:512], [0:256]} | slice | bytes 4194304 | tf_op jit(solution)/shard_map/slice | solution.py:239
  3.7 6.3 %all-to-all-start = ((bf16[8,512,256]{2,1,0:T(8,128)(2,1)}), bf16[8,512,256]{2,1,0:T(8,128)(2,1)S(1)}, u32[]{:S(2)}, u32[]{:S(2)}) async-start(bf16[8,512,256]{2,1,0:T(8,128)(2,1)} %bitcast.22), calls=%async_computation | async-start | bytes 4194304 | tf_op jit(solution)/shard_map/all_to_all | solution.py:236
  10.1 2.2 %copy-done.2 = f32[16,2,256,128]{3,2,1,0:T(8,128)S(1)} copy-done((f32[16,2,256,128]{3,2,1,0:T(8,128)S(1)}, f32[16,2,256,128]{3,2,1,0:T(8,128)}, u32[]{:S(2)}) %copy-start.2) | copy-done | bytes 4194328
  12.3 1.7 shard_map.68
  14.1 1.3 collective-permute-done.after_ref.refs_4_
  16.1 6.3 %shard_map.75 = bf16[2,1,4,512,256]{4,3,2,1,0:T(8,128)(2,1)} custom-call(s32[3]{0:T(128)} %copy-done.23, bf16[2,2,4,512,256]{4,3,2,1,0:T(8,128)(2,1)} %bitcast.20, bf16[272,256]{1,0:T(8,128)(2,1)} %copy-done.9), custom_call_target="tpu_custom_call" | custom-call | tf_op jit(solution)/shard_map/pallas_call | solution.py:264
  22.4 17.6 %all-to-all-done = bf16[8,512,256]{2,1,0:T(8,128)(2,1)S(1)} async-done(((bf16[8,512,256]{2,1,0:T(8,128)(2,1)}), bf16[8,512,256]{2,1,0:T(8,128)(2,1)S(1)}, u32[]{:S(2)}, u32[]{:S(2)}) %all-to-all-start) | async-done | bytes 2097184 | tf_op jit(solution)/shard_map/all_to_all | solution.py:236
  41.3 4.4 %all-to-all-start.2 = ((bf16[8,512,256]{2,1,0:T(8,128)(2,1)}), bf16[8,512,256]{2,1,0:T(8,128)(2,1)}, u32[]{:S(2)}, u32[]{:S(2)}) async-start(bf16[8,512,256]{2,1,0:T(8,128)(2,1)} %bitcast.21), calls=%async_computation.2 | async-start | bytes 4194304 | tf_op jit(solution)/shard_map/all_to_all | solution.py:236
  45.7 1.6 copy-done.1
  47.5 2.0 collective-permute-start.4
  50.9 1.7 collective-permute-start.2
  52.6 1.5 collective-permute-start.1
  54.1 25.1 %collective-permute-done.4.refs_5_ = bf16[272,256]{1,0:T(8,128)(2,1)S(1)} collective-permute-done((bf16[272,256]{1,0:T(8,128)(2,1)}, bf16[272,256]{1,0:T(8,128)(2,1)S(1)}, u32[]{:S(2)}, u32[]{:S(2)}) %collective-permute-start.4) | collective-permute-done | bytes 139296 | tf_op jit(solution)/shard_map/ppermute | solution.py:233
  79.1 2.9 %shard_map.76.mine_ref = bf16[2,4,512,256]{3,2,1,0:T(8,128)(2,1)} custom-call(bf16[2,4,512,256]{3,2,1,0:T(8,128)(2,1)} %bitcast.10.map_ref), custom_call_target="tpu_custom_call" | custom-call | bytes 4194304 | tf_op jit(solution)/shard_map/pallas_call | solution.py:290
  83.5 1.7 collective-permute-done.3.refs_2_
  89.3 4.9 %shard_map.72.refs_0_ = bf16[4,256,128]{2,1,0:T(8,128)(2,1)S(1)} custom-call(f32[1]{0:T(128)} %get-tuple-element.55.scale_ref, bf16[2,4,512,256]{3,2,1,0:T(8,128)(2,1)S(1)} %shard_map.71.mine_ref, bf16[2,4,512,256]{3,2,1,0:T(8,128)(2,1)} %collective-permute-done.6.theirs_ref, bf16[4,256,512]{2,1,0:T(8,128)(2,1)S(1)} %get-tuple-element.36.prior_ref, ...), custom_call_target="tpu_custom_call" | custom-call | flops 2147483648 | bytes 8388608 | tf_op jit(solution)/shard_map/pallas_call | solution.py:295
  94.2 2.6 %collective-permute-start.7 = (bf16[4,256,128]{2,1,0:T(8,128)(2,1)S(1)}, bf16[4,256,128]{2,1,0:T(8,128)(2,1)S(1)}, u32[]{:S(2)}, u32[]{:S(2)}) collective-permute-start(bf16[4,256,128]{2,1,0:T(8,128)(2,1)S(1)} %shard_map.72.refs_0_), channel_id=1, source_target_pairs={{0,4},{4,0},{1,5},{5,1},{2,6},{6,2},{3,7},{7,3},{8,12},{12,8},{9,1... | collective-permute-start | bytes 786440 | tf_op jit(solution)/shard_map/ppermute | solution.py:233
  96.9 8.8 %collective-permute-done.7.refs_1_ = bf16[4,256,128]{2,1,0:T(8,128)(2,1)S(1)} collective-permute-done((bf16[4,256,128]{2,1,0:T(8,128)(2,1)S(1)}, bf16[4,256,128]{2,1,0:T(8,128)(2,1)S(1)}, u32[]{:S(2)}, u32[]{:S(2)}) %collective-permute-start.7) | collective-permute-done | bytes 262176 | tf_op jit(solution)/shard_map/ppermute | solution.py:233
  105.7 4.9 %shard_map.73 = (f32[4,256,128]{2,1,0:T(8,128)S(1)}, bf16[4,256,128]{2,1,0:T(8,128)(2,1)S(1)}) custom-call(f32[1]{0:T(128)} %get-tuple-element.55.scale_ref, bf16[2,4,512,256]{3,2,1,0:T(8,128)(2,1)S(1)} %shard_map.71.mine_ref, bf16[2,4,512,256]{3,2,1,0:T(8,128)(2,1)} %collective-permute-done.6.theirs_ref, ...), custom_call_target="tpu_custom_call" | custom-call | flops 2147483648 | bytes 8388608 | tf_op jit(solution)/shard_map/pallas_call | solution.py:295
  110.7 12.8 %collective-permute-done.8.refs_1_ = bf16[4,256,128]{2,1,0:T(8,128)(2,1)S(1)} collective-permute-done((bf16[4,256,128]{2,1,0:T(8,128)(2,1)S(1)}, bf16[4,256,128]{2,1,0:T(8,128)(2,1)S(1)}, u32[]{:S(2)}, u32[]{:S(2)}) %collective-permute-start.8) | collective-permute-done | bytes 262176 | tf_op jit(solution)/shard_map/ppermute | solution.py:233
  125.2 3.8 %all-to-all-start.1 = ((bf16[16,256,128]{2,1,0:T(8,128)(2,1)}), bf16[16,256,128]{2,1,0:T(8,128)(2,1)S(1)}, u32[]{:S(2)}, u32[]{:S(2)}) async-start(bf16[16,256,128]{2,1,0:T(8,128)(2,1)} %bitcast.17), calls=%async_computation.1 | async-start | bytes 2097152 | tf_op jit(solution)/shard_map/all_to_all | solution.py:314
  132.3 5.6 %shard_map.77.refs_0_ = bf16[4,256,128]{2,1,0:T(8,128)(2,1)S(1)} custom-call(f32[1]{0:T(128)} %get-tuple-element.54.scale_ref, bf16[2,4,512,256]{3,2,1,0:T(8,128)(2,1)} %shard_map.76.mine_ref, bf16[2,4,512,256]{3,2,1,0:T(8,128)(2,1)} %collective-permute-done.9.theirs_ref, bf16[4,256,512]{2,1,0:T(8,128)(2,1)S(1)} %copy-done.4, ...), custom_call_target="tpu_custom_call" | custom-call | flops 2147483648 | bytes 8388608 | tf_op jit(solution)/shard_map/pallas_call | solution.py:295
  139.0 14.0 %collective-permute-done.10.refs_1_ = bf16[4,256,128]{2,1,0:T(8,128)(2,1)S(1)} collective-permute-done((bf16[4,256,128]{2,1,0:T(8,128)(2,1)S(1)}, bf16[4,256,128]{2,1,0:T(8,128)(2,1)S(1)}, u32[]{:S(2)}, u32[]{:S(2)}) %collective-permute-start.10) | collective-permute-done | bytes 262176 | tf_op jit(solution)/shard_map/ppermute | solution.py:233
  153.0 5.6 %shard_map.78 = (f32[4,256,128]{2,1,0:T(8,128)S(1)}, bf16[4,256,128]{2,1,0:T(8,128)(2,1)S(1)}) custom-call(f32[1]{0:T(128)} %get-tuple-element.54.scale_ref, bf16[2,4,512,256]{3,2,1,0:T(8,128)(2,1)} %shard_map.76.mine_ref, bf16[2,4,512,256]{3,2,1,0:T(8,128)(2,1)} %collective-permute-done.9.theirs_ref, bf16[4,256,512]{2,1,0:T(8,128)(2,1)S(1)} %copy-done.4, ...), custom_call_target="tpu_custom_call" | custom-call | flops 2147483648 | bytes 8388608 | tf_op jit(solution)/shard_map/pallas_call | solution.py:295
  158.7 13.5 %collective-permute-done.11.refs_1_ = bf16[4,256,128]{2,1,0:T(8,128)(2,1)S(1)} collective-permute-done((bf16[4,256,128]{2,1,0:T(8,128)(2,1)S(1)}, bf16[4,256,128]{2,1,0:T(8,128)(2,1)S(1)}, u32[]{:S(2)}, u32[]{:S(2)}) %collective-permute-start.11) | collective-permute-done | bytes 262176 | tf_op jit(solution)/shard_map/ppermute | solution.py:233
  174.7 4.3 %all-to-all-start.3 = ((bf16[16,256,128]{2,1,0:T(8,128)(2,1)}), bf16[16,256,128]{2,1,0:T(8,128)(2,1)}, u32[]{:S(2)}, u32[]{:S(2)}) async-start(bf16[16,256,128]{2,1,0:T(8,128)(2,1)} %bitcast.16), calls=%async_computation.3 | async-start | bytes 2097152 | tf_op jit(solution)/shard_map/all_to_all | solution.py:314
  180.3 3.8 %shard_map.80.first_ref = bf16[4,256,128]{2,1,0:T(8,128)(2,1)S(1)} custom-call(f32[1]{0:T(128)} %get-tuple-element.55.scale_ref, bf16[2,4,512,256]{3,2,1,0:T(8,128)(2,1)S(1)} %shard_map.71.mine_ref, bf16[2,4,512,256]{3,2,1,0:T(8,128)(2,1)} %collective-permute-done.6.theirs_ref, bf16[4,256,512]{2,1,0:T(8,128)(2,1)S(1)} %copy-done.5, ...), custom_call_target="tpu_custom_call" | custom-call | flops 1073741824 | bytes 8388608 | tf_op jit(solution)/shard_map/pallas_call | solution.py:317
  184.1 4.4 %shard_map.81.second_ref = bf16[4,256,128]{2,1,0:T(8,128)(2,1)S(1)} custom-call(f32[1]{0:T(128)} %get-tuple-element.54.scale_ref, bf16[2,4,512,256]{3,2,1,0:T(8,128)(2,1)} %shard_map.76.mine_ref, bf16[2,4,512,256]{3,2,1,0:T(8,128)(2,1)} %collective-permute-done.9.theirs_ref, bf16[4,256,512]{2,1,0:T(8,128)(2,1)S(1)} %copy-done.5, ...), custom_call_target="tpu_custom_call" | custom-call | flops 1073741824 | bytes 8388608 | tf_op jit(solution)/shard_map/pallas_call | solution.py:317
  191.6 1.8 collective-permute-start.13
  193.4 1.5 collective-permute-start.14
  195.1 6.4 %collective-permute-done.13.refs_3_ = bf16[256,256]{1,0:T(8,128)(2,1)S(1)} collective-permute-done((bf16[256,256]{1,0:T(8,128)(2,1)S(1)}, bf16[256,256]{1,0:T(8,128)(2,1)S(1)}, u32[]{:S(2)}, u32[]{:S(2)}) %collective-permute-start.13) | collective-permute-done | bytes 131104 | tf_op jit(solution)/shard_map/ppermute | solution.py:233
  201.5 3.8 %shard_map.84 = (f32[16,2,256,128]{3,2,1,0:T(8,128)}, f32[4,512,128]{2,1,0:T(8,128)}) custom-call(s32[3]{0:T(128)S(1)} %copy-done.24, bf16[2,2,4,256,128]{4,3,2,1,0:T(8,128)(2,1)S(1)} %bitcast.15, bf16[2,2,4,256,128]{4,3,2,1,0:T(8,128)(2,1)} %bitcast.12.refs_1_, bf16[256,256]{1,0:T(8,128)(2,1)S(1)} %get-tuple-element.48.refs_2_, ...), custom_call_target="tpu_custom_call" | custom-call | bytes 8388608 | tf_op jit(solution)/shard_map/pallas_call | solution.py:335
  (82 shorter events, 22.4 us)
Async XLA Ops:
  3.7 6.4 %copy-start.25 = (f32[256]{0:T(256)S(1)}, f32[256]{0:T(256)}, u32[]{:S(2)}) copy-start(f32[256]{0:T(256)} %param.7) | copy-start | bytes 3076
  3.7 36.3 %all-to-all-start = ((bf16[8,512,256]{2,1,0:T(8,128)(2,1)}), bf16[8,512,256]{2,1,0:T(8,128)(2,1)S(1)}, u32[]{:S(2)}, u32[]{:S(2)}) async-start(bf16[8,512,256]{2,1,0:T(8,128)(2,1)} %bitcast.22), calls=%async_computation | async-start | bytes 4194304 | tf_op jit(solution)/shard_map/all_to_all | solution.py:236
  10.1 3.9 %copy-start.23 = (s32[3]{0:T(128)}, s32[3]{0:T(128)S(1)}, u32[]{:S(2)}) copy-start(s32[3]{0:T(128)S(1)} %pad_add_fusion.place_ref) | copy-start | bytes 40
  10.1 2.2 %copy-start.2 = (f32[16,2,256,128]{3,2,1,0:T(8,128)S(1)}, f32[16,2,256,128]{3,2,1,0:T(8,128)}, u32[]{:S(2)}) copy-start(f32[16,2,256,128]{3,2,1,0:T(8,128)} %obs_ref.1) | copy-start | bytes 12582916
  14.0 1.4 collective-permute-start
  41.3 37.8 %all-to-all-start.2 = ((bf16[8,512,256]{2,1,0:T(8,128)(2,1)}), bf16[8,512,256]{2,1,0:T(8,128)(2,1)}, u32[]{:S(2)}, u32[]{:S(2)}) async-start(bf16[8,512,256]{2,1,0:T(8,128)(2,1)} %bitcast.21), calls=%async_computation.2 | async-start | bytes 4194304 | tf_op jit(solution)/shard_map/all_to_all | solution.py:236
  47.3 2.3 %copy-start.10 = (bf16[272,256]{1,0:T(8,128)(2,1)S(1)}, bf16[272,256]{1,0:T(8,128)(2,1)}, u32[]{:S(2)}) copy-start(bf16[272,256]{1,0:T(8,128)(2,1)} %copy-done.9) | copy-start | bytes 417796
  47.3 2.3 %copy-start.11 = (bf16[256,512]{1,0:T(8,128)(2,1)S(1)}, bf16[256,512]{1,0:T(8,128)(2,1)}, u32[]{:S(2)}) copy-start(bf16[256,512]{1,0:T(8,128)(2,1)} %own_ref.3) | copy-start | bytes 786436
  47.3 2.3 %copy-start.24 = (s32[3]{0:T(128)S(1)}, s32[3]{0:T(128)}, u32[]{:S(2)}) copy-start(s32[3]{0:T(128)} %copy-done.23) | copy-start | bytes 40
  47.4 41.9 %collective-permute-start.6 = (bf16[2,4,512,256]{3,2,1,0:T(8,128)(2,1)S(1)}, bf16[2,4,512,256]{3,2,1,0:T(8,128)(2,1)}, u32[]{:S(2)}, u32[]{:S(2)}) collective-permute-start(bf16[2,4,512,256]{3,2,1,0:T(8,128)(2,1)S(1)} %shard_map.71.mine_ref), channel_id=1, source_target_pairs={{0,8},{8,0},{1,9},{9,1},{2,10},{10,2},{3,11},{11,3},{4,12},{12,4},... | collective-permute-start | bytes 6291464 | tf_op jit(solution)/shard_map/ppermute | solution.py:233
  47.5 31.6 %collective-permute-start.4 = (bf16[272,256]{1,0:T(8,128)(2,1)}, bf16[272,256]{1,0:T(8,128)(2,1)S(1)}, u32[]{:S(2)}, u32[]{:S(2)}) collective-permute-start(bf16[272,256]{1,0:T(8,128)(2,1)} %get-tuple-element.32), channel_id=1, source_target_pairs={{0,16},{8,24},{16,0},{24,8},{1,17},{9,25},{17,1},{25,9},{2,18},{10... | collective-permute-start | bytes 417800 | tf_op jit(solution)/shard_map/ppermute | solution.py:233
  49.5 32.6 %collective-permute-start.5 = (bf16[272,256]{1,0:T(8,128)(2,1)}, bf16[272,256]{1,0:T(8,128)(2,1)S(1)}, u32[]{:S(2)}, u32[]{:S(2)}) collective-permute-start(bf16[272,256]{1,0:T(8,128)(2,1)} %get-tuple-element.33), channel_id=1, source_target_pairs={{0,24},{8,16},{16,8},{24,0},{1,25},{9,17},{17,9},{25,1},{2,26},{10... | collective-permute-start | bytes 417800 | tf_op jit(solution)/shard_map/ppermute | solution.py:233
  50.9 35.0 %collective-permute-start.2 = (bf16[256,512]{1,0:T(8,128)(2,1)}, bf16[256,512]{1,0:T(8,128)(2,1)S(1)}, u32[]{:S(2)}, u32[]{:S(2)}) collective-permute-start(bf16[256,512]{1,0:T(8,128)(2,1)} %get-tuple-element.30), channel_id=1, source_target_pairs={{0,2},{1,3},{2,0},{3,1},{4,6},{5,7},{6,4},{7,5},{8,10},{9,11},{10,... | collective-permute-start | bytes 786440 | tf_op jit(solution)/shard_map/ppermute | solution.py:233
  52.6 30.3 %collective-permute-start.1 = (bf16[256,256]{1,0:T(8,128)(2,1)}, bf16[256,256]{1,0:T(8,128)(2,1)S(1)}, u32[]{:S(2)}, u32[]{:S(2)}) collective-permute-start(bf16[256,256]{1,0:T(8,128)(2,1)} %get-tuple-element.29), channel_id=1, source_target_pairs={{0,1},{1,0},{2,3},{3,2},{4,5},{5,4},{6,7},{7,6},{8,9},{9,8},{10,11... | collective-permute-start | bytes 393224 | tf_op jit(solution)/shard_map/ppermute | solution.py:233
  79.1 6.1 %collective-permute-start.3 = (bf16[256,256]{1,0:T(8,128)(2,1)}, bf16[256,256]{1,0:T(8,128)(2,1)S(1)}, u32[]{:S(2)}, u32[]{:S(2)}) collective-permute-start(bf16[256,256]{1,0:T(8,128)(2,1)} %get-tuple-element.29), channel_id=1, source_target_pairs={{0,3},{1,2},{2,1},{3,0},{4,7},{5,6},{6,5},{7,4},{8,11},{9,10},{10,... | collective-permute-start | bytes 393224 | tf_op jit(solution)/shard_map/ppermute | solution.py:233
  79.1 3.0 %copy-start.26 = (f32[16]{0:T(128)S(1)}, f32[16]{0:T(128)}, u32[]{:S(2)}) copy-start(f32[16]{0:T(128)} %param.9) | copy-start | bytes 196
  82.1 47.0 %collective-permute-start.9 = (bf16[2,4,512,256]{3,2,1,0:T(8,128)(2,1)}, bf16[2,4,512,256]{3,2,1,0:T(8,128)(2,1)}, u32[]{:S(2)}, u32[]{:S(2)}) collective-permute-start(bf16[2,4,512,256]{3,2,1,0:T(8,128)(2,1)} %shard_map.76.mine_ref), channel_id=1, source_target_pairs={{0,8},{8,0},{1,9},{9,1},{2,10},{10,2},{3,11},{11,3},{4,12},{12,4},... | collective-permute-start | bytes 6291464 | tf_op jit(solution)/shard_map/ppermute | solution.py:233
  89.3 16.4 %copy-start.3 = (bf16[4,256,512]{2,1,0:T(8,128)(2,1)}, bf16[4,256,512]{2,1,0:T(8,128)(2,1)S(1)}, u32[]{:S(2)}) copy-start(bf16[4,256,512]{2,1,0:T(8,128)(2,1)S(1)} %get-tuple-element.36.prior_ref) | copy-start | bytes 3145732
  89.3 34.2 %copy-start.6 = (f32[4,256,128]{2,1,0:T(8,128)}, f32[4,256,128]{2,1,0:T(8,128)S(1)}, u32[]{:S(2)}) copy-start(f32[4,256,128]{2,1,0:T(8,128)S(1)} %get-tuple-element.34.noise_ref) | copy-start | bytes 1572868
  94.2 11.5 %collective-permute-start.7 = (bf16[4,256,128]{2,1,0:T(8,128)(2,1)S(1)}, bf16[4,256,128]{2,1,0:T(8,128)(2,1)S(1)}, u32[]{:S(2)}, u32[]{:S(2)}) collective-permute-start(bf16[4,256,128]{2,1,0:T(8,128)(2,1)S(1)} %shard_map.72.refs_0_), channel_id=1, source_target_pairs={{0,4},{4,0},{1,5},{5,1},{2,6},{6,2},{3,7},{7,3},{8,12},{12,8},{9,1... | collective-permute-start | bytes 786440 | tf_op jit(solution)/shard_map/ppermute | solution.py:233
  110.6 12.9 %collective-permute-start.8 = (bf16[4,256,128]{2,1,0:T(8,128)(2,1)S(1)}, bf16[4,256,128]{2,1,0:T(8,128)(2,1)S(1)}, u32[]{:S(2)}, u32[]{:S(2)}) collective-permute-start(bf16[4,256,128]{2,1,0:T(8,128)(2,1)S(1)} %get-tuple-element.38.refs_0_), channel_id=1, source_target_pairs={{0,4},{4,0},{1,5},{5,1},{2,6},{6,2},{3,7},{7,3},{8,12},{12,8},{9,1... | collective-permute-start | bytes 786440 | tf_op jit(solution)/shard_map/ppermute | solution.py:233
  125.2 49.5 %all-to-all-start.1 = ((bf16[16,256,128]{2,1,0:T(8,128)(2,1)}), bf16[16,256,128]{2,1,0:T(8,128)(2,1)S(1)}, u32[]{:S(2)}, u32[]{:S(2)}) async-start(bf16[16,256,128]{2,1,0:T(8,128)(2,1)} %bitcast.17), calls=%async_computation.1 | async-start | bytes 2097152 | tf_op jit(solution)/shard_map/all_to_all | solution.py:314
  132.3 20.7 %copy-start.18 = (bf16[4,256,128]{2,1,0:T(8,128)(2,1)S(1)}, bf16[4,256,128]{2,1,0:T(8,128)(2,1)}, u32[]{:S(2)}) copy-start(bf16[4,256,128]{2,1,0:T(8,128)(2,1)} %copy-done.16) | copy-start | bytes 786436
  137.9 34.3 %copy-start.8 = (f32[4,256,128]{2,1,0:T(8,128)S(1)}, f32[4,256,128]{2,1,0:T(8,128)}, u32[]{:S(2)}) copy-start(f32[4,256,128]{2,1,0:T(8,128)} %copy-done.6) | copy-start | bytes 1572868
  137.9 15.1 %collective-permute-start.10 = (bf16[4,256,128]{2,1,0:T(8,128)(2,1)S(1)}, bf16[4,256,128]{2,1,0:T(8,128)(2,1)S(1)}, u32[]{:S(2)}, u32[]{:S(2)}) collective-permute-start(bf16[4,256,128]{2,1,0:T(8,128)(2,1)S(1)} %shard_map.77.refs_0_), channel_id=1, source_target_pairs={{0,4},{4,0},{1,5},{5,1},{2,6},{6,2},{3,7},{7,3},{8,12},{12,8},{9,1... | collective-permute-start | bytes 786440 | tf_op jit(solution)/shard_map/ppermute | solution.py:233
  158.6 13.6 %collective-permute-start.11 = (bf16[4,256,128]{2,1,0:T(8,128)(2,1)S(1)}, bf16[4,256,128]{2,1,0:T(8,128)(2,1)S(1)}, u32[]{:S(2)}, u32[]{:S(2)}) collective-permute-start(bf16[4,256,128]{2,1,0:T(8,128)(2,1)S(1)} %get-tuple-element.42.refs_0_), channel_id=1, source_target_pairs={{0,4},{4,0},{1,5},{5,1},{2,6},{6,2},{3,7},{7,3},{8,12},{12,8},{9,1... | collective-permute-start | bytes 786440 | tf_op jit(solution)/shard_map/ppermute | solution.py:233
  174.7 26.9 %all-to-all-start.3 = ((bf16[16,256,128]{2,1,0:T(8,128)(2,1)}), bf16[16,256,128]{2,1,0:T(8,128)(2,1)}, u32[]{:S(2)}, u32[]{:S(2)}) async-start(bf16[16,256,128]{2,1,0:T(8,128)(2,1)} %bitcast.16), calls=%async_computation.3 | async-start | bytes 2097152 | tf_op jit(solution)/shard_map/all_to_all | solution.py:314
  180.3 3.8 %copy-start.15 = (bf16[4,256,128]{2,1,0:T(8,128)(2,1)S(1)}, bf16[4,256,128]{2,1,0:T(8,128)(2,1)}, u32[]{:S(2)}) copy-start(bf16[4,256,128]{2,1,0:T(8,128)(2,1)} %copy-done.14) | copy-start | bytes 786436
  189.2 1.6 collective-permute-start.12
  191.6 10.0 %collective-permute-start.13 = (bf16[256,256]{1,0:T(8,128)(2,1)S(1)}, bf16[256,256]{1,0:T(8,128)(2,1)S(1)}, u32[]{:S(2)}, u32[]{:S(2)}) collective-permute-start(bf16[256,256]{1,0:T(8,128)(2,1)S(1)} %get-tuple-element.49), channel_id=1, source_target_pairs={{0,1},{1,0},{2,3},{3,2},{4,5},{5,4},{6,7},{7,6},{8,9},{9,8},{10,11... | collective-permute-start | bytes 393224 | tf_op jit(solution)/shard_map/ppermute | solution.py:233
  193.4 8.2 %collective-permute-start.14 = (bf16[256,256]{1,0:T(8,128)(2,1)S(1)}, bf16[256,256]{1,0:T(8,128)(2,1)S(1)}, u32[]{:S(2)}, u32[]{:S(2)}) collective-permute-start(bf16[256,256]{1,0:T(8,128)(2,1)S(1)} %get-tuple-element.50), channel_id=1, source_target_pairs={{0,2},{1,3},{2,0},{3,1},{4,6},{5,7},{6,4},{7,5},{8,10},{9,11},{10,... | collective-permute-start | bytes 393224 | tf_op jit(solution)/shard_map/ppermute | solution.py:233
  194.8 6.7 %collective-permute-start.15 = (bf16[256,256]{1,0:T(8,128)(2,1)S(1)}, bf16[256,256]{1,0:T(8,128)(2,1)S(1)}, u32[]{:S(2)}, u32[]{:S(2)}) collective-permute-start(bf16[256,256]{1,0:T(8,128)(2,1)S(1)} %get-tuple-element.51), channel_id=1, source_target_pairs={{0,3},{1,2},{2,1},{3,0},{4,7},{5,6},{6,5},{7,4},{8,11},{9,10},{10,... | collective-permute-start | bytes 393224 | tf_op jit(solution)/shard_map/ppermute | solution.py:233
  (15 other events, 14.5 us)

commit v11 on v9

--- a/solution.py
+++ b/solution.py
@@ -79,7 +79,7 @@
 
 def gather_kernel(groups, quads, place_ref, own_ref, *refs):
     came, data = refs[:quads - 1], refs[quads - 1:quads - 1 + groups]
-    prior_ref, noise_ref, *streams = refs[quads - 1 + groups:]
+    prior_ref, noise_ref, *streams = refs[quads + groups:]
     me, quad = place_ref[0] * CORES + place_ref[2], place_ref[1]
     sensors, cells = streams[0].shape[1], own_ref.shape[0]
     on, off = (pl.ds(pl.multiple_of(p * cells, cells), cells) for p in (quad & 1, 1 - (quad & 1)))
@@ -127,10 +127,10 @@
     copy.wait()
 
 
-def step_kernel(stage, n_pred, scale_ref, map_ref, prior_ref, obs_ref, noise_ref, *refs):
+def step_kernel(stage, n_pred, n_after, scale_ref, map_ref, prior_ref, obs_ref, noise_ref, *refs):
     groups, quads, double, _ = map_ref.shape
     sensors = double // 2
-    preds, refs = refs[:n_pred], refs[n_pred:]
+    preds, refs = refs[:n_pred], refs[n_pred + n_after:]
     if stage > 0:
         next_ref, refs = refs[0], refs[1:]
     out_ref, sides_ref = refs
@@ -151,50 +151,63 @@
         out_ref[g] = total.astype(bf16)
 
 
-def last_kernel(n_pred, noise_ref, obs_ref, held_ref, *refs):
-    preds, (final_ref, out_ref) = refs[:n_pred], refs[n_pred:]
-    for g in range(final_ref.shape[0]):
-        now = held_ref[g]
-        predicted = sum(p[g].astype(f32) for p in preds)
-        now = now + relax_step * (obs_ref[g].astype(f32) - predicted - noise_ref[g] * now)
-        now = now.astype(bf16)
-        final_ref[g] = now
-        for q in range(out_ref.shape[1]):
-            out_ref[g, q] = now
+def last_kernel(n_pred, place_ref, noise_ref, *refs):
+    obs, held, refs = refs[:STREAMS], refs[STREAMS:2 * STREAMS], refs[2 * STREAMS:]
+    preds, (keep_ref, give_ref) = refs[:STREAMS * n_pred], refs[STREAMS * n_pred:]
+    for e in range(keep_ref.shape[0]):
+        for out, core in ((give_ref, 1 - place_ref[2]), (keep_ref, place_ref[2])):
+            g = CORES * (place_ref[0] ^ e) + core
+            parts = []
+            for s in range(STREAMS):
+                now = held[s][g]
+                predicted = sum(p[g].astype(f32) for p in preds[s * n_pred:(s + 1) * n_pred])
+                parts.append(now + relax_step * (obs[s][g].astype(f32) - predicted - noise_ref[g] * now))
+            out[e] = join(parts).astype(bf16)
 
 
 def join(streams):
     return jnp.concatenate([x[:, :HALF] for x in streams] + [x[:, HALF:] for x in streams], 1)
 
 
-def post_kernel(place_ref, scale_ref, map_ref, prior_ref, *refs):
-    finals, refs = refs[:STREAMS], refs[STREAMS:]
+def send_kernel(e, place_ref, keep_ref, got_ref, *refs):
+    posts, outs = refs[:len(refs) // 2], refs[len(refs) // 2:]
+    for i, out in enumerate(outs):
+        out[place_ref[2]] = keep_ref[e]
+        out[1 - place_ref[2]] = got_ref[e]
+        if posts:
+            out[CORES] = posts[i][...]
+
+
+def post_kernel(place_ref, scale_ref, map_ref, prior_ref, keep_ref, give_ref, *refs):
     outs, (sides_ref, held_ref) = refs[:-2], refs[-2:]
-    for g in range(map_ref.shape[0]):
-        sides_ref[g] = sides(join([x[g] for x in finals]))
+    for e in range(keep_ref.shape[0]):
+        first = CORES * (place_ref[0] ^ e)
+        sides_ref[first + place_ref[2]] = sides(keep_ref[e])
+        sides_ref[first + 1 - place_ref[2]] = sides(give_ref[e])
     for q, v in enumerate(source(map_ref, sides_ref, prior_ref, scale_ref[0])):
         held_ref[q] = v
     for d, out in enumerate(outs):
         out[...] = held_ref[place_ref[1] ^ d]
 
 
-def end_kernel(quads, place_ref, *refs):
-    came, posts, refs = refs[:STREAMS], refs[STREAMS:STREAMS + quads], refs[STREAMS + quads:]
-    dual_out, post_out, dual_ref, post_ref, sems = refs
-    quad = place_ref[1]
+def end_kernel(chips, quads, place_ref, *refs):
+    came, (dual_out, post_out, dual_ref, post_ref, sems) = refs[:chips], refs[chips:]
+    pair, quad = place_ref[0], place_ref[1]
     cells = post_ref.shape[1] // 2
     sends = []
-    for d in range(quads):
-        post_ref[d, pl.ds(0, cells, stride=2), :] = posts[d][:, :LANES].astype(f32)
-        post_ref[d, pl.ds(1, cells, stride=2), :] = posts[d][:, LANES:].astype(f32)
-        sends.append(pltpu.make_async_copy(post_ref.at[d], post_out.at[quad ^ d], sems.at[d]))
-        sends[-1].start()
-    for freq in range(dual_ref.shape[0]):
-        both = join([x[freq].astype(f32) for x in came])
-        dual_ref[freq, 0] = both[:, :LANES]
-        dual_ref[freq, 1] = both[:, LANES:]
-        sends.append(pltpu.make_async_copy(dual_ref.at[freq], dual_out.at[freq], sems.at[quads + freq]))
-        sends[-1].start()
+    for chip in reversed(range(chips)):
+        e, d = divmod(chip, quads)
+        for core in range(CORES):
+            freq = (CORES * (pair ^ e) + core) * quads + (quad ^ d)
+            for part in range(2):
+                dual_ref[chip, core, part] = came[chip][core, :, part * LANES:(part + 1) * LANES].astype(f32)
+            sends.append(pltpu.make_async_copy(dual_ref.at[chip, core], dual_out.at[freq], sems.at[chip, core]))
+            sends[-1].start()
+        if e == 0:
+            post_ref[d, pl.ds(0, cells, stride=2), :] = came[chip][CORES, :, :LANES].astype(f32)
+            post_ref[d, pl.ds(1, cells, stride=2), :] = came[chip][CORES, :, LANES:].astype(f32)
+            sends.append(pltpu.make_async_copy(post_ref.at[d], post_out.at[quad ^ d], sems.at[chip, CORES]))
+            sends[-1].start()
     for copy in sends:
         copy.wait()
 
@@ -226,13 +239,15 @@
         [shape((cells, width), bf16), shape((cells, cells), bf16)],
     )(place, prior_rows, data[1])
     came = [swap(diagonal if d % 2 else rows, "quad", d) for d in range(1, quads)]
+    near = call(bring_kernel, [ANY], [shape(held.shape, bf16)], [pltpu.SemaphoreType.DMA], moved=8 * 2**20)(held)[0]
+
     prior, noise, *streams = call(
         functools.partial(gather_kernel, groups, quads),
-        [SMEM] + [VMEM] * (quads + groups),
+        [SMEM] + [VMEM] * (quads + groups) + [ANY],
         [shape((quads, cells, width), bf16), shape((groups, sensors, LANES), f32)]
         + [shape((groups, sensors, LANES), bf16)] * STREAMS,
         moved=8 * 2**20,
-    )(place, prior_rows, *came, *data)
+    )(place, prior_rows, *came, *data, near)
 
     def over_sides(partial):
         if sides == 2:
@@ -241,54 +256,62 @@
 
     wide, narrow = shape((groups, sensors, LANES), f32), shape((groups, sensors, LANES), bf16)
 
-    near = call(bring_kernel, [ANY], [shape(held.shape, bf16)], [pltpu.SemaphoreType.DMA], moved=8 * 2**20)(held)[0]
-
-    def step(stage, obs, preds):
+    def step(stage, obs, preds, after=()):
         operands = [scale, near, prior, obs, noise] + preds
         return call(
-            functools.partial(step_kernel, stage, len(preds)),
-            [SMEM] + [VMEM] * (len(operands) - 1),
+            functools.partial(step_kernel, stage, len(preds), len(after)),
+            [SMEM] + [VMEM] * (len(operands) - 1) + [ANY] * len(after),
             [wide, narrow] if stage > 0 else [narrow],
             [pltpu.VMEM((groups, LANES, halves * sensors), bf16)],
             flops=2**31,
             moved=8 * 2**20,
-        )(*operands)
-
-    first = [over_sides(step(0, streams[s], [])[0]) for s in range(STREAMS)]
-    finals, duals = [], []
-    for s in range(STREAMS):
-        held_s, partial = step(1, streams[s], first[s])
-        preds = over_sides(partial)
-        final, out = call(
-            functools.partial(last_kernel, len(preds)),
-            [VMEM] * (3 + len(preds)),
-            [narrow, shape((groups, quads, sensors, LANES), bf16)],
-            moved=2 * 2**20,
-        )(noise, streams[s], held_s, *preds)
-        finals.append(final)
-        out = out.reshape(frequencies, sensors, LANES)
-        duals.append(lax.all_to_all(out, both, split_axis=0, concat_axis=0, tiled=True))
+        )(*operands, *after)
+
+    partials = [step(0, streams[s], [])[0] for s in range(STREAMS)]
+    preds = [over_sides(x) for x in partials]
+    steps = [step(1, streams[s], preds[s], partials[s + 1:]) for s in range(STREAMS)]
+    preds = [over_sides(x) for _, x in steps]
+    pairs, count = groups // CORES, len(preds[0])
+    part = shape((pairs, sensors, 2 * LANES), bf16)
+    keep, give = call(
+        functools.partial(last_kernel, count),
+        [SMEM] + [VMEM] * (1 + STREAMS * (2 + count)),
+        [part, part],
+        moved=2 * 2**20,
+    )(place, noise, *streams, *[held for held, _ in steps], *[p for both_sides in preds for p in both_sides])
+    got = swap(give, "sensor", 1)
     posts = call(
         post_kernel,
-        [SMEM, SMEM] + [VMEM] * (2 + STREAMS),
+        [SMEM, SMEM] + [VMEM] * 4,
         [shape((cells, 2 * LANES), bf16)] * quads,
         [pltpu.VMEM((groups, 2 * LANES, halves * sensors), bf16), pltpu.VMEM((quads, cells, 2 * LANES), bf16)],
         flops=2**31,
         moved=8 * 2**20,
-    )(place, scale, near, prior, *finals)
-    posts = [posts[0]] + [swap(posts[d], "quad", d) for d in range(1, quads)]
+    )(place, scale, near, prior, keep, give)
+    duals = {}
+    for e in reversed(range(pairs)):
+        extra = list(posts) if e == 0 else []
+        messages = call(
+            functools.partial(send_kernel, e),
+            [SMEM] + [VMEM] * (2 + len(extra)),
+            [shape((CORES + (e == 0), sensors, 2 * LANES), bf16)] * (len(extra) or 1),
+            moved=2**20,
+        )(place, keep, got, *extra)
+        for d in reversed(range(quads)):
+            message = messages[d] if e == 0 else messages[0]
+            duals[e * quads + d] = swap(message, both, CORES * e * quads + d) if e + d else message
     dual, posterior = call(
-        functools.partial(end_kernel, quads),
-        [SMEM] + [VMEM] * (STREAMS + quads),
+        functools.partial(end_kernel, pairs * quads, quads),
+        [SMEM] + [VMEM] * (pairs * quads),
         [shape((frequencies, halves, sensors, LANES), f32), shape((quads, cells * 2, LANES), f32)],
         [
-            pltpu.VMEM((frequencies, halves, sensors, LANES), f32),
+            pltpu.VMEM((pairs * quads, CORES, halves, sensors, LANES), f32),
             pltpu.VMEM((quads, cells * 2, LANES), f32),
-            pltpu.SemaphoreType.DMA((quads + frequencies,)),
+            pltpu.SemaphoreType.DMA((pairs * quads, CORES + 1)),
         ],
         [ANY, ANY],
         moved=8 * 2**20,
-    )(place, *duals, *posts)
+    )(place, *[duals[i] for i in range(pairs * quads)])
     return dual, posterior.reshape(quads, cells, 2, LANES)
 
 

time: 181 us -> 160 us (0.88)
  waiting for transfers between devices: 113 us -> 102 us
  local copies, waits for them, and re-layouts: 10.8 us -> 2.79 us
    ppermute x13 -> x18, waiting for transfers between devices: 113 us -> 59.3 us  [swap(): return lax.ppermute(x, axes, [(i, i ^ distance) for i in range(count)])]
    all_to_all x1, waiting for transfers between devices: 0.01 us -> 43.1 us  [on_device(): lax.all_to_all(forward_map.reshape(frequencies, halves * sensors, cells),...]
    unnamed x22 -> x8, local copies, waits for them, and re-layouts: 10.2 us -> 2.2 us
    all_to_all x2 -> x0, starting transfers between devices: 7.4 us -> none  [on_device(): lax.all_to_all(out, both, split_axis=0, concat_axis=0, tiled=True)]
    ppermute x13 -> x18, starting transfers between devices: 14.4 us -> 20.1 us  [swap(): return lax.ppermute(x, axes, [(i, i ^ distance) for i in range(count)])]
    pallas_call x8 -> x9, Pallas kernels: 22.1 us -> 22.3 us  [the longest x4 13.7 us: step(): call(functools.partial(step_kernel, stage, len(preds), len(after)), [SMEM...]
  transfers between devices with their start and end apart: 16 -> 19, of which waited for: 9 -> 14; matrix products, arithmetic and copies ran while one was open for 0% -> 0% of each run, Pallas kernels for 8% -> 11%
where the time goes in v11:
time: 160 us
  waiting for transfers between devices  102 us (64%)
  Pallas kernels  27.1 us (17%)
  starting transfers between devices  26.6 us (17%)
  local copies, waits for them, and re-layouts  2.79 us (2%)
    ppermute x18, waiting for transfers between devices, swap(): return lax.ppermute(x, axes, [(i, i ^ distance) for i in range(count)])  59.3 us
    all_to_all x1, waiting for transfers between devices, on_device(): lax.all_to_all(forward_map.reshape(frequencies, halves * sensors, cells),...  43.1 us
    ppermute x18, starting transfers between devices, swap(): return lax.ppermute(x, axes, [(i, i ^ distance) for i in range(count)])  20.1 us
    pallas_call x4, Pallas kernels, step(): call(functools.partial(step_kernel, stage, len(preds), len(after)), [SMEM...  13.7 us
    all_to_all x1, starting transfers between devices, on_device(): lax.all_to_all(forward_map.reshape(frequencies, halves * sensors, cells),...  6.48 us
    pallas_call x1, Pallas kernels, on_device(): call(post_kernel, [SMEM, SMEM] + [VMEM] * 4, [shape((cells, 2 * LANES), b...  3.24 us
  transfers between devices with their start and end apart: 19, of which 14 were waited for; matrix products, arithmetic and copies ran while one was open for 0% of the time, Pallas kernels for 11%

profile of v11, /device:TPU:0, one launch (start us, length us, event | category | flops | bytes accessed | tf_op | source)
XLA Modules:
  0.0 159.7 jit_solution(6847572793071777836)
XLA Ops:
  0.6 6.5 %all-to-all-start = ((bf16[16,512,256]{2,1,0:T(8,128)(2,1)}), bf16[16,512,256]{2,1,0:T(8,128)(2,1)}, u32[]{:S(2)}, u32[]{:S(2)}) async-start(bf16[16,512,256]{2,1,0:T(8,128)(2,1)} %bitcast.8), calls=%async_computation | async-start | bytes 8388608 | tf_op jit(solution)/shard_map/all_to_all | solution.py:224
  7.3 2.2 %copy-done = f32[16,2,256,128]{3,2,1,0:T(8,128)S(1)} copy-done((f32[16,2,256,128]{3,2,1,0:T(8,128)S(1)}, f32[16,2,256,128]{3,2,1,0:T(8,128)}, u32[]{:S(2)}) %copy-start) | copy-done | bytes 4194328
  9.4 1.1 shard_map.68
  12.6 1.9 %collective-permute-start.2 = (bf16[256,512]{1,0:T(8,128)(2,1)S(1)}, bf16[256,512]{1,0:T(8,128)(2,1)S(1)}, u32[]{:S(2)}, u32[]{:S(2)}) collective-permute-start(bf16[256,512]{1,0:T(8,128)(2,1)S(1)} %get-tuple-element.30), channel_id=1, source_target_pairs={{0,2},{1,3},{2,0},{3,1},{4,6},{5,7},{6,4},{7,5},{8,10},{9,11},{10,... | collective-permute-start | bytes 786440 | tf_op jit(solution)/shard_map/ppermute | solution.py:42
  14.5 1.5 collective-permute-start.4
  16.0 1.5 collective-permute-start.3
  18.6 43.1 %all-to-all-done = bf16[16,512,256]{2,1,0:T(8,128)(2,1)} async-done(((bf16[16,512,256]{2,1,0:T(8,128)(2,1)}), bf16[16,512,256]{2,1,0:T(8,128)(2,1)}, u32[]{:S(2)}, u32[]{:S(2)}) %all-to-all-start) | async-done | bytes 4194336 | tf_op jit(solution)/shard_map/all_to_all | solution.py:224
  61.7 2.2 %shard_map.70.refs_7_.map_ref = bf16[4,4,512,256]{3,2,1,0:T(8,128)(2,1)S(1)} custom-call(bf16[4,4,512,256]{3,2,1,0:T(8,128)(2,1)} %bitcast.5.map_ref), custom_call_target="tpu_custom_call" | custom-call | bytes 8388608 | tf_op jit(solution)/shard_map/pallas_call | solution.py:242
  63.9 2.4 %collective-permute-done.4.refs_5_ = bf16[272,256]{1,0:T(8,128)(2,1)S(1)} collective-permute-done((bf16[272,256]{1,0:T(8,128)(2,1)S(1)}, bf16[272,256]{1,0:T(8,128)(2,1)S(1)}, u32[]{:S(2)}, u32[]{:S(2)}) %collective-permute-start.4) | collective-permute-done | bytes 139296 | tf_op jit(solution)/shard_map/ppermute | solution.py:42
  66.3 2.0 %collective-permute-done.5.refs_6_ = bf16[272,256]{1,0:T(8,128)(2,1)S(1)} collective-permute-done((bf16[272,256]{1,0:T(8,128)(2,1)S(1)}, bf16[272,256]{1,0:T(8,128)(2,1)S(1)}, u32[]{:S(2)}, u32[]{:S(2)}) %collective-permute-start.5) | collective-permute-done | bytes 139296 | tf_op jit(solution)/shard_map/ppermute | solution.py:42
  68.3 1.4 collective-permute-done.3.refs_2_
  70.8 3.4 %shard_map.72.refs_0_ = bf16[4,256,128]{2,1,0:T(8,128)(2,1)S(1)} custom-call(f32[1]{0:T(128)} %dynamic_slice.3.scale_ref, bf16[4,4,512,256]{3,2,1,0:T(8,128)(2,1)S(1)} %shard_map.70.refs_7_.map_ref, bf16[4,256,512]{2,1,0:T(8,128)(2,1)S(1)} %get-tuple-element.37.prior_ref, bf16[4,256,128]{2,1,0:T(8,128)(2,1)S(1)} %get-tuple-element.35.obs_ref.refs_0_, ...), custom_call_target="tpu_custom_call" | custom-call | flops 2147483648 | bytes 8388608 | tf_op jit(solution)/shard_map/pallas_call | solution.py:261
  74.2 2.6 %collective-permute-start.6 = (bf16[4,256,128]{2,1,0:T(8,128)(2,1)S(1)}, bf16[4,256,128]{2,1,0:T(8,128)(2,1)S(1)}, u32[]{:S(2)}, u32[]{:S(2)}) collective-permute-start(bf16[4,256,128]{2,1,0:T(8,128)(2,1)S(1)} %shard_map.72.refs_0_), channel_id=1, source_target_pairs={{0,4},{4,0},{1,5},{5,1},{2,6},{6,2},{3,7},{7,3},{8,12},{12,8},{9,1... | collective-permute-start | bytes 786440 | tf_op jit(solution)/shard_map/ppermute | solution.py:42
  76.8 3.4 %shard_map.73.refs_2_.refs_0_ = bf16[4,256,128]{2,1,0:T(8,128)(2,1)S(1)} custom-call(f32[1]{0:T(128)} %dynamic_slice.3.scale_ref, bf16[4,4,512,256]{3,2,1,0:T(8,128)(2,1)S(1)} %shard_map.70.refs_7_.map_ref, bf16[4,256,512]{2,1,0:T(8,128)(2,1)S(1)} %get-tuple-element.37.prior_ref, bf16[4,256,128]{2,1,0:T(8,128)(2,1)S(1)} %get-tuple-element.36.obs_ref.refs_1_, ...), custom_call_target="tpu_custom_call" | custom-call | flops 2147483648 | bytes 8388608 | tf_op jit(solution)/shard_map/pallas_call | solution.py:261
  80.7 11.7 %collective-permute-done.6.refs_1_ = bf16[4,256,128]{2,1,0:T(8,128)(2,1)S(1)} collective-permute-done((bf16[4,256,128]{2,1,0:T(8,128)(2,1)S(1)}, bf16[4,256,128]{2,1,0:T(8,128)(2,1)S(1)}, u32[]{:S(2)}, u32[]{:S(2)}) %collective-permute-start.6) | collective-permute-done | bytes 262176 | tf_op jit(solution)/shard_map/ppermute | solution.py:42
  92.4 3.4 %shard_map.74 = (f32[4,256,128]{2,1,0:T(8,128)S(1)}, bf16[4,256,128]{2,1,0:T(8,128)(2,1)S(1)}) custom-call(f32[1]{0:T(128)} %dynamic_slice.3.scale_ref, bf16[4,4,512,256]{3,2,1,0:T(8,128)(2,1)S(1)} %shard_map.70.refs_7_.map_ref, bf16[4,256,512]{2,1,0:T(8,128)(2,1)S(1)} %get-tuple-element.37.prior_ref, ...), custom_call_target="tpu_custom_call" | custom-call | flops 2147483648 | bytes 8388608 | tf_op jit(solution)/shard_map/pallas_call | solution.py:261
  95.9 2.0 %collective-permute-done.7.refs_1_ = bf16[4,256,128]{2,1,0:T(8,128)(2,1)S(1)} collective-permute-done((bf16[4,256,128]{2,1,0:T(8,128)(2,1)S(1)}, bf16[4,256,128]{2,1,0:T(8,128)(2,1)S(1)}, u32[]{:S(2)}, u32[]{:S(2)}) %collective-permute-start.7) | collective-permute-done | bytes 262176 | tf_op jit(solution)/shard_map/ppermute | solution.py:42
  97.9 3.4 %shard_map.75 = (f32[4,256,128]{2,1,0:T(8,128)S(1)}, bf16[4,256,128]{2,1,0:T(8,128)(2,1)S(1)}) custom-call(f32[1]{0:T(128)} %dynamic_slice.3.scale_ref, bf16[4,4,512,256]{3,2,1,0:T(8,128)(2,1)S(1)} %shard_map.70.refs_7_.map_ref, bf16[4,256,512]{2,1,0:T(8,128)(2,1)S(1)} %get-tuple-element.37.prior_ref, ...), custom_call_target="tpu_custom_call" | custom-call | flops 2147483648 | bytes 8388608 | tf_op jit(solution)/shard_map/pallas_call | solution.py:261
  102.3 12.6 %collective-permute-done.8.refs_5_ = bf16[4,256,128]{2,1,0:T(8,128)(2,1)S(1)} collective-permute-done((bf16[4,256,128]{2,1,0:T(8,128)(2,1)S(1)}, bf16[4,256,128]{2,1,0:T(8,128)(2,1)S(1)}, u32[]{:S(2)}, u32[]{:S(2)}) %collective-permute-start.8) | collective-permute-done | bytes 262176 | tf_op jit(solution)/shard_map/ppermute | solution.py:42
  114.9 5.5 %collective-permute-done.9.refs_7_ = bf16[4,256,128]{2,1,0:T(8,128)(2,1)S(1)} collective-permute-done((bf16[4,256,128]{2,1,0:T(8,128)(2,1)S(1)}, bf16[4,256,128]{2,1,0:T(8,128)(2,1)S(1)}, u32[]{:S(2)}, u32[]{:S(2)}) %collective-permute-start.9) | collective-permute-done | bytes 262176 | tf_op jit(solution)/shard_map/ppermute | solution.py:42
  121.6 1.5 collective-permute-done.10.got_ref
  123.6 1.1 collective-permute-start.17
  124.8 2.7 %collective-permute-start.16 = (bf16[2,256,256]{2,1,0:T(8,128)(2,1)S(1)}, bf16[2,256,256]{2,1,0:T(8,128)(2,1)S(1)}, u32[]{:S(2)}, u32[]{:S(2)}) collective-permute-start(bf16[2,256,256]{2,1,0:T(8,128)(2,1)S(1)} %shard_map.79), channel_id=1, source_target_pairs={{0,18},{1,19},{2,16},{3,17},{8,26},{9,27},{10,24},{11,25},{16,2},{... | collective-permute-start | bytes 786440 | tf_op jit(solution)/shard_map/ppermute | solution.py:42
  127.5 3.2 %shard_map.77 = (bf16[256,256]{1,0:T(8,128)(2,1)S(1)}, bf16[256,256]{1,0:T(8,128)(2,1)S(1)}, bf16[256,256]{1,0:T(8,128)(2,1)S(1)}, bf16[256,256]{1,0:T(8,128)(2,1)S(1)}) custom-call(s32[3]{0:T(128)S(1)} %pad_add_fusion.place_ref, f32[1]{0:T(128)} %dynamic_slice.3.scale_ref, bf16[4,4,512,256]{3,2,1,0:T(8,128)(2,1)S(1)} %shard_map.70.refs_7_.map_ref, ...), custom_call_target="tpu_custom_call" | custom-call | flops 2147483648 | bytes 8388608 | tf_op jit(solution)/shard_map/pallas_call | solution.py:283
  132.1 2.9 %collective-permute-start.13 = (bf16[3,256,256]{2,1,0:T(8,128)(2,1)S(1)}, bf16[3,256,256]{2,1,0:T(8,128)(2,1)S(1)}, u32[]{:S(2)}, u32[]{:S(2)}) collective-permute-start(bf16[3,256,256]{2,1,0:T(8,128)(2,1)S(1)} %get-tuple-element.51), channel_id=1, source_target_pairs={{0,3},{1,2},{2,1},{3,0},{8,11},{9,10},{10,9},{11,8},{16,19},{17,18... | collective-permute-start | bytes 1179656 | tf_op jit(solution)/shard_map/ppermute | solution.py:42
  135.0 1.6 %collective-permute-start.15 = (bf16[2,256,256]{2,1,0:T(8,128)(2,1)S(1)}, bf16[2,256,256]{2,1,0:T(8,128)(2,1)S(1)}, u32[]{:S(2)}, u32[]{:S(2)}) collective-permute-start(bf16[2,256,256]{2,1,0:T(8,128)(2,1)S(1)} %shard_map.79), channel_id=1, source_target_pairs={{0,17},{1,16},{2,19},{3,18},{8,25},{9,24},{10,27},{11,26},{16,1},{... | collective-permute-start | bytes 786440 | tf_op jit(solution)/shard_map/ppermute | solution.py:42
  136.6 3.7 %collective-permute-done.16.refs_6_ = bf16[2,256,256]{2,1,0:T(8,128)(2,1)S(1)} collective-permute-done((bf16[2,256,256]{2,1,0:T(8,128)(2,1)S(1)}, bf16[2,256,256]{2,1,0:T(8,128)(2,1)S(1)}, u32[]{:S(2)}, u32[]{:S(2)}) %collective-permute-start.16) | collective-permute-done | bytes 262176 | tf_op jit(solution)/shard_map/ppermute | solution.py:42
  140.3 1.1 collective-permute-start.14
  141.4 4.2 %collective-permute-done.15.refs_5_ = bf16[2,256,256]{2,1,0:T(8,128)(2,1)S(1)} collective-permute-done((bf16[2,256,256]{2,1,0:T(8,128)(2,1)S(1)}, bf16[2,256,256]{2,1,0:T(8,128)(2,1)S(1)}, u32[]{:S(2)}, u32[]{:S(2)}) %collective-permute-start.15) | collective-permute-done | bytes 262176 | tf_op jit(solution)/shard_map/ppermute | solution.py:42
  145.6 5.2 %collective-permute-done.14.refs_4_ = bf16[2,256,256]{2,1,0:T(8,128)(2,1)S(1)} collective-permute-done((bf16[2,256,256]{2,1,0:T(8,128)(2,1)S(1)}, bf16[2,256,256]{2,1,0:T(8,128)(2,1)S(1)}, u32[]{:S(2)}, u32[]{:S(2)}) %collective-permute-start.14) | collective-permute-done | bytes 262176 | tf_op jit(solution)/shard_map/ppermute | solution.py:42
  150.7 5.9 %collective-permute-done.11.refs_1_ = bf16[3,256,256]{2,1,0:T(8,128)(2,1)S(1)} collective-permute-done((bf16[3,256,256]{2,1,0:T(8,128)(2,1)S(1)}, bf16[3,256,256]{2,1,0:T(8,128)(2,1)S(1)}, u32[]{:S(2)}, u32[]{:S(2)}) %collective-permute-start.11) | collective-permute-done | bytes 393248 | tf_op jit(solution)/shard_map/ppermute | solution.py:42
  156.6 3.1 %shard_map.80 = (f32[16,2,256,128]{3,2,1,0:T(8,128)}, f32[4,512,128]{2,1,0:T(8,128)}) custom-call(s32[3]{0:T(128)S(1)} %pad_add_fusion.place_ref, bf16[3,256,256]{2,1,0:T(8,128)(2,1)S(1)} %get-tuple-element.48.refs_0_, bf16[3,256,256]{2,1,0:T(8,128)(2,1)S(1)} %collective-permute-done.11.refs_1_, bf16[3,256,256]{2,1,0:T(8,128)(2,1)S(1)} %collective-permute-done.12.refs_2_, ...), custom_call_target="tpu_custom_call" | custom-call | bytes 8388608 | tf_op jit(solution)/shard_map/pallas_call | solution.py:303
  (29 shorter events, 8.6 us)
Async XLA Ops:
  0.6 6.6 %copy-start.2 = (f32[256]{0:T(256)S(1)}, f32[256]{0:T(256)}, u32[]{:S(2)}) copy-start(f32[256]{0:T(256)} %param.7) | copy-start | bytes 3076
  0.6 11.3 %copy-start.1 = (bf16[256,512]{1,0:T(8,128)(2,1)S(1)}, bf16[256,512]{1,0:T(8,128)(2,1)}, u32[]{:S(2)}) copy-start(bf16[256,512]{1,0:T(8,128)(2,1)} %own_ref.3) | copy-start | bytes 786436
  0.6 61.0 %all-to-all-start = ((bf16[16,512,256]{2,1,0:T(8,128)(2,1)}), bf16[16,512,256]{2,1,0:T(8,128)(2,1)}, u32[]{:S(2)}, u32[]{:S(2)}) async-start(bf16[16,512,256]{2,1,0:T(8,128)(2,1)} %bitcast.8), calls=%async_computation | async-start | bytes 8388608 | tf_op jit(solution)/shard_map/all_to_all | solution.py:224
  7.1 10.9 %copy-start.3 = (f32[16]{0:T(128)S(1)}, f32[16]{0:T(128)}, u32[]{:S(2)}) copy-start(f32[16]{0:T(128)} %param.9) | copy-start | bytes 196
  7.3 2.2 %copy-start = (f32[16,2,256,128]{3,2,1,0:T(8,128)S(1)}, f32[16,2,256,128]{3,2,1,0:T(8,128)}, u32[]{:S(2)}) copy-start(f32[16,2,256,128]{3,2,1,0:T(8,128)} %obs_ref.1) | copy-start | bytes 12582916
  10.6 1.4 collective-permute-start
  12.6 57.2 %collective-permute-start.2 = (bf16[256,512]{1,0:T(8,128)(2,1)S(1)}, bf16[256,512]{1,0:T(8,128)(2,1)S(1)}, u32[]{:S(2)}, u32[]{:S(2)}) collective-permute-start(bf16[256,512]{1,0:T(8,128)(2,1)S(1)} %get-tuple-element.30), channel_id=1, source_target_pairs={{0,2},{1,3},{2,0},{3,1},{4,6},{5,7},{6,4},{7,5},{8,10},{9,11},{10,... | collective-permute-start | bytes 786440 | tf_op jit(solution)/shard_map/ppermute | solution.py:42
  14.5 51.8 %collective-permute-start.4 = (bf16[272,256]{1,0:T(8,128)(2,1)S(1)}, bf16[272,256]{1,0:T(8,128)(2,1)S(1)}, u32[]{:S(2)}, u32[]{:S(2)}) collective-permute-start(bf16[272,256]{1,0:T(8,128)(2,1)S(1)} %get-tuple-element.32), channel_id=1, source_target_pairs={{0,16},{8,24},{16,0},{24,8},{1,17},{9,25},{17,1},{25,9},{2,18},{10... | collective-permute-start | bytes 417800 | tf_op jit(solution)/shard_map/ppermute | solution.py:42
  16.0 52.4 %collective-permute-start.5 = (bf16[272,256]{1,0:T(8,128)(2,1)S(1)}, bf16[272,256]{1,0:T(8,128)(2,1)S(1)}, u32[]{:S(2)}, u32[]{:S(2)}) collective-permute-start(bf16[272,256]{1,0:T(8,128)(2,1)S(1)} %get-tuple-element.33), channel_id=1, source_target_pairs={{0,24},{8,16},{16,8},{24,0},{1,25},{9,17},{17,9},{25,1},{2,26},{10... | collective-permute-start | bytes 417800 | tf_op jit(solution)/shard_map/ppermute | solution.py:42
  16.0 53.8 %collective-permute-start.3 = (bf16[256,256]{1,0:T(8,128)(2,1)S(1)}, bf16[256,256]{1,0:T(8,128)(2,1)S(1)}, u32[]{:S(2)}, u32[]{:S(2)}) collective-permute-start(bf16[256,256]{1,0:T(8,128)(2,1)S(1)} %get-tuple-element.29), channel_id=1, source_target_pairs={{0,3},{1,2},{2,1},{3,0},{4,7},{5,6},{6,5},{7,4},{8,11},{9,10},{10,... | collective-permute-start | bytes 393224 | tf_op jit(solution)/shard_map/ppermute | solution.py:42
  17.4 52.4 %collective-permute-start.1 = (bf16[256,256]{1,0:T(8,128)(2,1)S(1)}, bf16[256,256]{1,0:T(8,128)(2,1)S(1)}, u32[]{:S(2)}, u32[]{:S(2)}) collective-permute-start(bf16[256,256]{1,0:T(8,128)(2,1)S(1)} %get-tuple-element.29), channel_id=1, source_target_pairs={{0,1},{1,0},{2,3},{3,2},{4,5},{5,4},{6,7},{7,6},{8,9},{9,8},{10,11... | collective-permute-start | bytes 393224 | tf_op jit(solution)/shard_map/ppermute | solution.py:42
  74.2 18.2 %collective-permute-start.6 = (bf16[4,256,128]{2,1,0:T(8,128)(2,1)S(1)}, bf16[4,256,128]{2,1,0:T(8,128)(2,1)S(1)}, u32[]{:S(2)}, u32[]{:S(2)}) collective-permute-start(bf16[4,256,128]{2,1,0:T(8,128)(2,1)S(1)} %shard_map.72.refs_0_), channel_id=1, source_target_pairs={{0,4},{4,0},{1,5},{5,1},{2,6},{6,2},{3,7},{7,3},{8,12},{12,8},{9,1... | collective-permute-start | bytes 786440 | tf_op jit(solution)/shard_map/ppermute | solution.py:42
  80.3 17.7 %collective-permute-start.7 = (bf16[4,256,128]{2,1,0:T(8,128)(2,1)S(1)}, bf16[4,256,128]{2,1,0:T(8,128)(2,1)S(1)}, u32[]{:S(2)}, u32[]{:S(2)}) collective-permute-start(bf16[4,256,128]{2,1,0:T(8,128)(2,1)S(1)} %shard_map.73.refs_2_.refs_0_), channel_id=1, source_target_pairs={{0,4},{4,0},{1,5},{5,1},{2,6},{6,2},{3,7},{7,3},{8,12},{12,8},{9,1... | collective-permute-start | bytes 786440 | tf_op jit(solution)/shard_map/ppermute | solution.py:42
  95.9 19.1 %collective-permute-start.8 = (bf16[4,256,128]{2,1,0:T(8,128)(2,1)S(1)}, bf16[4,256,128]{2,1,0:T(8,128)(2,1)S(1)}, u32[]{:S(2)}, u32[]{:S(2)}) collective-permute-start(bf16[4,256,128]{2,1,0:T(8,128)(2,1)S(1)} %get-tuple-element.40.refs_4_), channel_id=1, source_target_pairs={{0,4},{4,0},{1,5},{5,1},{2,6},{6,2},{3,7},{7,3},{8,12},{12,8},{9,1... | collective-permute-start | bytes 786440 | tf_op jit(solution)/shard_map/ppermute | solution.py:42
  101.4 19.1 %collective-permute-start.9 = (bf16[4,256,128]{2,1,0:T(8,128)(2,1)S(1)}, bf16[4,256,128]{2,1,0:T(8,128)(2,1)S(1)}, u32[]{:S(2)}, u32[]{:S(2)}) collective-permute-start(bf16[4,256,128]{2,1,0:T(8,128)(2,1)S(1)} %get-tuple-element.41.refs_6_), channel_id=1, source_target_pairs={{0,4},{4,0},{1,5},{5,1},{2,6},{6,2},{3,7},{7,3},{8,12},{12,8},{9,1... | collective-permute-start | bytes 786440 | tf_op jit(solution)/shard_map/ppermute | solution.py:42
  121.5 1.6 collective-permute-start.10
  123.6 11.3 %collective-permute-start.17 = (bf16[2,256,256]{2,1,0:T(8,128)(2,1)S(1)}, bf16[2,256,256]{2,1,0:T(8,128)(2,1)S(1)}, u32[]{:S(2)}, u32[]{:S(2)}) collective-permute-start(bf16[2,256,256]{2,1,0:T(8,128)(2,1)S(1)} %shard_map.79), channel_id=1, source_target_pairs={{0,19},{1,18},{2,17},{3,16},{8,27},{9,26},{10,25},{11,24},{16,3},{... | collective-permute-start | bytes 786440 | tf_op jit(solution)/shard_map/ppermute | solution.py:42
  124.8 15.5 %collective-permute-start.16 = (bf16[2,256,256]{2,1,0:T(8,128)(2,1)S(1)}, bf16[2,256,256]{2,1,0:T(8,128)(2,1)S(1)}, u32[]{:S(2)}, u32[]{:S(2)}) collective-permute-start(bf16[2,256,256]{2,1,0:T(8,128)(2,1)S(1)} %shard_map.79), channel_id=1, source_target_pairs={{0,18},{1,19},{2,16},{3,17},{8,26},{9,27},{10,24},{11,25},{16,2},{... | collective-permute-start | bytes 786440 | tf_op jit(solution)/shard_map/ppermute | solution.py:42
  131.4 25.2 %collective-permute-start.11 = (bf16[3,256,256]{2,1,0:T(8,128)(2,1)S(1)}, bf16[3,256,256]{2,1,0:T(8,128)(2,1)S(1)}, u32[]{:S(2)}, u32[]{:S(2)}) collective-permute-start(bf16[3,256,256]{2,1,0:T(8,128)(2,1)S(1)} %get-tuple-element.49), channel_id=1, source_target_pairs={{0,1},{1,0},{2,3},{3,2},{8,9},{9,8},{10,11},{11,10},{16,17},{17,16... | collective-permute-start | bytes 1179656 | tf_op jit(solution)/shard_map/ppermute | solution.py:42
  132.1 24.6 %collective-permute-start.12 = (bf16[3,256,256]{2,1,0:T(8,128)(2,1)S(1)}, bf16[3,256,256]{2,1,0:T(8,128)(2,1)S(1)}, u32[]{:S(2)}, u32[]{:S(2)}) collective-permute-start(bf16[3,256,256]{2,1,0:T(8,128)(2,1)S(1)} %get-tuple-element.50), channel_id=1, source_target_pairs={{0,2},{1,3},{2,0},{3,1},{8,10},{9,11},{10,8},{11,9},{16,18},{17,19... | collective-permute-start | bytes 1179656 | tf_op jit(solution)/shard_map/ppermute | solution.py:42
  132.1 24.6 %collective-permute-start.13 = (bf16[3,256,256]{2,1,0:T(8,128)(2,1)S(1)}, bf16[3,256,256]{2,1,0:T(8,128)(2,1)S(1)}, u32[]{:S(2)}, u32[]{:S(2)}) collective-permute-start(bf16[3,256,256]{2,1,0:T(8,128)(2,1)S(1)} %get-tuple-element.51), channel_id=1, source_target_pairs={{0,3},{1,2},{2,1},{3,0},{8,11},{9,10},{10,9},{11,8},{16,19},{17,18... | collective-permute-start | bytes 1179656 | tf_op jit(solution)/shard_map/ppermute | solution.py:42
  135.0 10.6 %collective-permute-start.15 = (bf16[2,256,256]{2,1,0:T(8,128)(2,1)S(1)}, bf16[2,256,256]{2,1,0:T(8,128)(2,1)S(1)}, u32[]{:S(2)}, u32[]{:S(2)}) collective-permute-start(bf16[2,256,256]{2,1,0:T(8,128)(2,1)S(1)} %shard_map.79), channel_id=1, source_target_pairs={{0,17},{1,16},{2,19},{3,18},{8,25},{9,24},{10,27},{11,26},{16,1},{... | collective-permute-start | bytes 786440 | tf_op jit(solution)/shard_map/ppermute | solution.py:42
  140.3 10.4 %collective-permute-start.14 = (bf16[2,256,256]{2,1,0:T(8,128)(2,1)S(1)}, bf16[2,256,256]{2,1,0:T(8,128)(2,1)S(1)}, u32[]{:S(2)}, u32[]{:S(2)}) collective-permute-start(bf16[2,256,256]{2,1,0:T(8,128)(2,1)S(1)} %shard_map.79), channel_id=1, source_target_pairs={{0,16},{1,17},{2,18},{3,19},{8,24},{9,25},{10,26},{11,27},{16,0},{... | collective-permute-start | bytes 786440 | tf_op jit(solution)/shard_map/ppermute | solution.py:42

commit v12 on v11

--- a/solution.py
+++ b/solution.py
@@ -50,12 +50,17 @@
     return lax.dot_general(a, b, (((1,), (1,)), ((), ())), preferred_element_type=f32)
 
 
-def data_kernel(groups, quads, place_ref, obs_ref, noise_ref, *refs):
+def my_place():
+    me = lax.axis_index("sensor")
+    return me // CORES, lax.axis_index("quad"), me % CORES
+
+
+def data_kernel(groups, quads, obs_ref, noise_ref, *refs):
     outs, (held, sems) = refs[:groups], refs[groups:]
     sensors = obs_ref.shape[2]
     copies = []
     for d in range(groups):
-        freq = ((place_ref[0] * CORES + place_ref[2]) ^ d) * quads + place_ref[1]
+        freq = ((my_place()[0] * CORES + my_place()[2]) ^ d) * quads + my_place()[1]
         copies.append(pltpu.make_async_copy(obs_ref.at[freq], held.at[d], sems.at[d]))
         copies[-1].start()
     noise = noise_ref[...]
@@ -71,16 +76,17 @@
         outs[d][sensors:, :] = tail
 
 
-def prior_kernel(place_ref, own_ref, after_ref, full_ref, diagonal_ref):
+def prior_kernel(scale_ref, own_ref, after_ref, full_ref, diagonal_ref, wide_ref):
     cells = own_ref.shape[0]
     full_ref[...] = own_ref[...]
-    diagonal_ref[...] = own_ref[:, pl.ds(pl.multiple_of((place_ref[1] & 1) * cells, cells), cells)]
-
-
-def gather_kernel(groups, quads, place_ref, own_ref, *refs):
+    wide_ref[...] = jnp.full(wide_ref.shape, scale_ref[0], f32)
+    diagonal_ref[...] = own_ref[:, pl.ds(pl.multiple_of((my_place()[1] & 1) * cells, cells), cells)]
+
+
+def gather_kernel(groups, quads, own_ref, *refs):
     came, data = refs[:quads - 1], refs[quads - 1:quads - 1 + groups]
     prior_ref, noise_ref, *streams = refs[quads + groups:]
-    me, quad = place_ref[0] * CORES + place_ref[2], place_ref[1]
+    me, quad = my_place()[0] * CORES + my_place()[2], my_place()[1]
     sensors, cells = streams[0].shape[1], own_ref.shape[0]
     on, off = (pl.ds(pl.multiple_of(p * cells, cells), cells) for p in (quad & 1, 1 - (quad & 1)))
     for d in range(0, quads, 2):
@@ -132,67 +138,76 @@
     sensors = double // 2
     preds, refs = refs[:n_pred], refs[n_pred + n_after:]
     if stage > 0:
-        next_ref, refs = refs[0], refs[1:]
-    out_ref, sides_ref = refs
+        outs, (sides_ref, now_ref, partial_ref) = refs[:4], refs[4:]
+    else:
+        out_ref, sides_ref = refs
     for g in range(groups):
         obs = obs_ref[g].astype(f32)
         now = relax_step * obs
         if stage > 0:
             predicted = sum(p[g].astype(f32) for p in preds)
             now = now + relax_step * (obs - predicted - noise_ref[g] * now)
-            next_ref[g] = now
+            now_ref[g] = now + relax_step * (obs - noise_ref[g] * now)
         sides_ref[g] = sides(now.astype(bf16))
-    sources = source(map_ref, sides_ref, prior_ref, scale_ref[0])
+    sources = source(map_ref, sides_ref, prior_ref, scale_ref[0:1, 0:1])
     turned = [jnp.concatenate([-v[:, HALF:], v[:, :HALF]], 1) for v in sources]
     for g in range(groups):
         total = jnp.zeros((sensors, LANES), f32)
         for q in range(quads):
             total += dot(map_ref[g, q, :sensors, :], sources[q]) + dot(map_ref[g, q, sensors:, :], turned[q])
-        out_ref[g] = total.astype(bf16)
-
-
-def last_kernel(n_pred, place_ref, noise_ref, *refs):
-    obs, held, refs = refs[:STREAMS], refs[STREAMS:2 * STREAMS], refs[2 * STREAMS:]
-    preds, (keep_ref, give_ref) = refs[:STREAMS * n_pred], refs[STREAMS * n_pred:]
-    for e in range(keep_ref.shape[0]):
-        for out, core in ((give_ref, 1 - place_ref[2]), (keep_ref, place_ref[2])):
-            g = CORES * (place_ref[0] ^ e) + core
-            parts = []
-            for s in range(STREAMS):
-                now = held[s][g]
-                predicted = sum(p[g].astype(f32) for p in preds[s * n_pred:(s + 1) * n_pred])
-                parts.append(now + relax_step * (obs[s][g].astype(f32) - predicted - noise_ref[g] * now))
-            out[e] = join(parts).astype(bf16)
+        if stage == 0:
+            out_ref[g] = total.astype(bf16)
+        else:
+            now_ref[g] -= relax_step * total
+            partial_ref[g] = total.astype(bf16)
+    if stage > 0:
+        for e in range(groups // CORES):
+            for parity, core in ((0, my_place()[2]), (1, 1 - my_place()[2])):
+                g = CORES * (my_place()[0] ^ e) + core
+                outs[parity][e] = partial_ref[g]
+                outs[2 + parity][e] = now_ref[g].astype(outs[2 + parity].dtype)
+
+
+def last_kernel(pairs, *refs):
+    mine, theirs, keeps, gots = (refs[i * STREAMS:(i + 1) * STREAMS] for i in range(4))
+    *outs, give_ref = refs[4 * STREAMS:]
+    core = my_place()[2]
+    for e in range(pairs):
+        own = join([keeps[s][e] - relax_step * mine[s][e].astype(f32) for s in range(STREAMS)])
+        other = join([gots[s][e].astype(f32) - relax_step * theirs[s][e].astype(f32) for s in range(STREAMS)])
+        outs[e][core] = own.astype(bf16)
+        outs[e][1 - core] = other.astype(bf16)
+        give_ref[e] = other.astype(bf16)
 
 
 def join(streams):
     return jnp.concatenate([x[:, :HALF] for x in streams] + [x[:, HALF:] for x in streams], 1)
 
 
-def send_kernel(e, place_ref, keep_ref, got_ref, *refs):
+def send_kernel(dual_ref, *refs):
     posts, outs = refs[:len(refs) // 2], refs[len(refs) // 2:]
-    for i, out in enumerate(outs):
-        out[place_ref[2]] = keep_ref[e]
-        out[1 - place_ref[2]] = got_ref[e]
-        if posts:
-            out[CORES] = posts[i][...]
-
-
-def post_kernel(place_ref, scale_ref, map_ref, prior_ref, keep_ref, give_ref, *refs):
+    for post, out in zip(posts, outs):
+        out[:CORES] = dual_ref[...]
+        out[CORES] = post[...]
+
+
+def post_kernel(pairs, scale_ref, map_ref, prior_ref, *refs):
+    duals, got_ref, refs = refs[:pairs], refs[pairs], refs[pairs + 1:]
     outs, (sides_ref, held_ref) = refs[:-2], refs[-2:]
-    for e in range(keep_ref.shape[0]):
-        first = CORES * (place_ref[0] ^ e)
-        sides_ref[first + place_ref[2]] = sides(keep_ref[e])
-        sides_ref[first + 1 - place_ref[2]] = sides(give_ref[e])
-    for q, v in enumerate(source(map_ref, sides_ref, prior_ref, scale_ref[0])):
+    core = my_place()[2]
+    for e in range(pairs):
+        first = CORES * (my_place()[0] ^ e)
+        sides_ref[first + core] = sides(duals[e][core])
+        sides_ref[first + 1 - core] = sides(got_ref[e])
+    for q, v in enumerate(source(map_ref, sides_ref, prior_ref, scale_ref[0:1, 0:1])):
         held_ref[q] = v
     for d, out in enumerate(outs):
-        out[...] = held_ref[place_ref[1] ^ d]
-
-
-def end_kernel(chips, quads, place_ref, *refs):
+        out[...] = held_ref[my_place()[1] ^ d]
+
+
+def end_kernel(chips, quads, *refs):
     came, (dual_out, post_out, dual_ref, post_ref, sems) = refs[:chips], refs[chips:]
-    pair, quad = place_ref[0], place_ref[1]
+    pair, quad = my_place()[0], my_place()[1]
     cells = post_ref.shape[1] // 2
     sends = []
     for chip in reversed(range(chips)):
@@ -214,10 +229,9 @@
 
 def on_device(forward_map, observed, noise_var, prior_rows, prior_scale):
     frequencies, halves, sensors, cells = forward_map.shape
-    groups, quads, sides = (lax.axis_size(a) for a in ("sensor", "quad", "side"))
+    groups, quads, count = (lax.axis_size(a) for a in ("sensor", "quad", "side"))
     width = prior_rows.shape[1]
     me, quad = lax.axis_index("sensor"), lax.axis_index("quad")
-    place = jnp.stack([me // CORES, quad, me % CORES]).astype(jnp.int32)
     scale = lax.dynamic_slice_in_dim(prior_scale, me * quads + quad, 1, 0)
     both = ("sensor", "quad")
 
@@ -227,30 +241,30 @@
 
     data = call(
         functools.partial(data_kernel, groups, quads),
-        [SMEM, ANY, VMEM],
+        [ANY, VMEM],
         [shape((sensors + 16, STREAMS * LANES), bf16)] * groups,
         [pltpu.VMEM((groups, halves, sensors, LANES), f32), pltpu.SemaphoreType.DMA((groups,))],
         moved=groups * sensors * LANES * 12,
-    )(place, observed, noise_var.reshape(1, sensors))
+    )(observed, noise_var.reshape(1, sensors))
     data = [data[0]] + [swap(data[d], "sensor", d) for d in range(1, groups)]
-    rows, diagonal = call(
+    rows, diagonal, scale = call(
         prior_kernel,
         [SMEM, VMEM, ANY],
-        [shape((cells, width), bf16), shape((cells, cells), bf16)],
-    )(place, prior_rows, data[1])
+        [shape((cells, width), bf16), shape((cells, cells), bf16), shape((8, LANES), f32)],
+    )(scale, prior_rows, data[1])
     came = [swap(diagonal if d % 2 else rows, "quad", d) for d in range(1, quads)]
     near = call(bring_kernel, [ANY], [shape(held.shape, bf16)], [pltpu.SemaphoreType.DMA], moved=8 * 2**20)(held)[0]
 
     prior, noise, *streams = call(
         functools.partial(gather_kernel, groups, quads),
-        [SMEM] + [VMEM] * (quads + groups) + [ANY],
+        [VMEM] * (quads + groups) + [ANY],
         [shape((quads, cells, width), bf16), shape((groups, sensors, LANES), f32)]
         + [shape((groups, sensors, LANES), bf16)] * STREAMS,
         moved=8 * 2**20,
-    )(place, prior_rows, *came, *data, near)
+    )(prior_rows, *came, *data, near)
 
     def over_sides(partial):
-        if sides == 2:
+        if count == 2:
             return [partial, swap(partial, "side", 1)]
         return [lax.psum(partial, "side")]
 
@@ -258,51 +272,65 @@
 
     def step(stage, obs, preds, after=()):
         operands = [scale, near, prior, obs, noise] + preds
+        scratch = [pltpu.VMEM((groups, LANES, halves * sensors), bf16)]
+        if stage > 0:
+            scratch += [pltpu.VMEM((groups, sensors, LANES), f32), pltpu.VMEM((groups, sensors, LANES), bf16)]
         return call(
             functools.partial(step_kernel, stage, len(preds), len(after)),
-            [SMEM] + [VMEM] * (len(operands) - 1) + [ANY] * len(after),
-            [wide, narrow] if stage > 0 else [narrow],
-            [pltpu.VMEM((groups, LANES, halves * sensors), bf16)],
+            [VMEM] * len(operands) + [ANY] * len(after),
+            [part, part, shape(part.shape, f32), part] if stage > 0 else [narrow],
+            scratch,
             flops=2**31,
             moved=8 * 2**20,
         )(*operands, *after)
 
+    pairs = groups // CORES
+    part = shape((pairs, sensors, LANES), bf16)
     partials = [step(0, streams[s], [])[0] for s in range(STREAMS)]
     preds = [over_sides(x) for x in partials]
     steps = [step(1, streams[s], preds[s], partials[s + 1:]) for s in range(STREAMS)]
-    preds = [over_sides(x) for _, x in steps]
-    pairs, count = groups // CORES, len(preds[0])
-    part = shape((pairs, sensors, 2 * LANES), bf16)
-    keep, give = call(
-        functools.partial(last_kernel, count),
-        [SMEM] + [VMEM] * (1 + STREAMS * (2 + count)),
-        [part, part],
+
+    def to_other_sides(x, cross):
+        if count == 2:
+            return lax.ppermute(
+                x, ("sensor", "side"), [(i, i ^ (1 + CORES * cross)) for i in range(groups * count)]
+            )
+        rest = lax.psum(x.astype(f32), "side") - x.astype(f32)
+        return (swap(rest, "sensor", 1) if cross else rest).astype(bf16)
+
+    mine = [to_other_sides(x[0], 0) for x in steps]
+    theirs = [to_other_sides(x[1], 1) for x in steps]
+    keeps, gots = [x[2] for x in steps], [swap(x[3], "sensor", 1) for x in steps]
+    message = shape((CORES, sensors, 2 * LANES), bf16)
+    *finals, give = call(
+        functools.partial(last_kernel, pairs),
+        [VMEM] * (4 * STREAMS),
+        [message] * pairs + [shape((pairs, sensors, 2 * LANES), bf16)],
         moved=2 * 2**20,
-    )(place, noise, *streams, *[held for held, _ in steps], *[p for both_sides in preds for p in both_sides])
+    )(*mine, *theirs, *keeps, *gots)
     got = swap(give, "sensor", 1)
     posts = call(
-        post_kernel,
-        [SMEM, SMEM] + [VMEM] * 4,
+        functools.partial(post_kernel, pairs),
+        [VMEM] * (4 + pairs),
         [shape((cells, 2 * LANES), bf16)] * quads,
         [pltpu.VMEM((groups, 2 * LANES, halves * sensors), bf16), pltpu.VMEM((quads, cells, 2 * LANES), bf16)],
         flops=2**31,
         moved=8 * 2**20,
-    )(place, scale, near, prior, keep, give)
+    )(scale, near, prior, *finals, got)
+    near_ones = call(
+        send_kernel,
+        [VMEM] * (1 + quads),
+        [shape((CORES + 1, sensors, 2 * LANES), bf16)] * quads,
+        moved=2**20,
+    )(finals[0], *posts)
     duals = {}
     for e in reversed(range(pairs)):
-        extra = list(posts) if e == 0 else []
-        messages = call(
-            functools.partial(send_kernel, e),
-            [SMEM] + [VMEM] * (2 + len(extra)),
-            [shape((CORES + (e == 0), sensors, 2 * LANES), bf16)] * (len(extra) or 1),
-            moved=2**20,
-        )(place, keep, got, *extra)
         for d in reversed(range(quads)):
-            message = messages[d] if e == 0 else messages[0]
-            duals[e * quads + d] = swap(message, both, CORES * e * quads + d) if e + d else message
+            out = near_ones[d] if e == 0 else finals[e]
+            duals[e * quads + d] = swap(out, both, CORES * e * quads + d) if e + d else out
     dual, posterior = call(
         functools.partial(end_kernel, pairs * quads, quads),
-        [SMEM] + [VMEM] * (pairs * quads),
+        [VMEM] * (pairs * quads),
         [shape((frequencies, halves, sensors, LANES), f32), shape((quads, cells * 2, LANES), f32)],
         [
             pltpu.VMEM((pairs * quads, CORES, halves, sensors, LANES), f32),
@@ -311,7 +339,7 @@
         ],
         [ANY, ANY],
         moved=8 * 2**20,
-    )(place, *[duals[i] for i in range(pairs * quads)])
+    )(*[duals[i] for i in range(pairs * quads)])
     return dual, posterior.reshape(quads, cells, 2, LANES)
 
 

time: 160 us -> 155 us (0.969)
  Pallas kernels: 27.1 us -> 20.1 us
  starting transfers between devices: 26.6 us -> 31.4 us
  waiting for transfers between devices: 102 us -> 99.4 us
    ppermute x18, waiting for transfers between devices: 59.3 us -> 39.8 us  [swap(): return lax.ppermute(x, axes, [(i, i ^ distance) for i in range(count)])]
    ppermute x0 -> x4, waiting for transfers between devices: none -> 15.3 us  [to_other_sides(): lax.ppermute(x, ('sensor', 'side'), [(i, i ^ 1 + CORES * cross) for i in...]
    pallas_call x11 -> x10, Pallas kernels: 24.3 us -> 17.2 us  [the longest x4 11.3 us: step(): call(functools.partial(step_kernel, stage, len(preds), len(after)), [VMEM...]
    ppermute x0 -> x4, starting transfers between devices: none -> 4.47 us  [to_other_sides(): lax.ppermute(x, ('sensor', 'side'), [(i, i ^ 1 + CORES * cross) for i in...]
  transfers between devices with their start and end apart: 19 -> 23, of which waited for: 14 -> 16; matrix products, arithmetic and copies ran while one was open for 0% -> 0% of each run, Pallas kernels for 11% -> 9%
where the time goes in v12:
time: 155 us; the launch traced here: 154 us
  waiting for transfers between devices  99.4 us (64%)
  starting transfers between devices  31.4 us (20%)
  Pallas kernels  20.1 us (13%)
  local copies, waits for them, and re-layouts  2.78 us (2%)
    all_to_all x1, waiting for transfers between devices, on_device(): lax.all_to_all(forward_map.reshape(frequencies, halves * sensors, cells),...  44.2 us
    ppermute x18, waiting for transfers between devices, swap(): return lax.ppermute(x, axes, [(i, i ^ distance) for i in range(count)])  39.8 us
    ppermute x18, starting transfers between devices, swap(): return lax.ppermute(x, axes, [(i, i ^ distance) for i in range(count)])  20.5 us
    ppermute x4, waiting for transfers between devices, to_other_sides(): lax.ppermute(x, ('sensor', 'side'), [(i, i ^ 1 + CORES * cross) for i in...  15.3 us
    pallas_call x4, Pallas kernels, step(): call(functools.partial(step_kernel, stage, len(preds), len(after)), [VMEM...  11.3 us
    all_to_all x1, starting transfers between devices, on_device(): lax.all_to_all(forward_map.reshape(frequencies, halves * sensors, cells),...  6.35 us
    ppermute x4, starting transfers between devices, to_other_sides(): lax.ppermute(x, ('sensor', 'side'), [(i, i ^ 1 + CORES * cross) for i in...  4.47 us
  transfers between devices with their start and end apart: 23, of which 16 were waited for; matrix products, arithmetic and copies ran while one was open for 0% of the time, Pallas kernels for 9%

profile of v12, /device:TPU:0, one launch (start us, length us, event | category | flops | bytes accessed | tf_op | source)
XLA Modules:
  0.0 154.4 jit_solution(8115120759068368075)
XLA Ops:
  0.6 6.4 %all-to-all-start = ((bf16[16,512,256]{2,1,0:T(8,128)(2,1)}), bf16[16,512,256]{2,1,0:T(8,128)(2,1)}, u32[]{:S(2)}, u32[]{:S(2)}) async-start(bf16[16,512,256]{2,1,0:T(8,128)(2,1)} %bitcast.5), calls=%async_computation | async-start | bytes 8388608 | tf_op jit(solution)/shard_map/all_to_all | solution.py:238
  7.0 2.2 %copy-done = f32[16,2,256,128]{3,2,1,0:T(8,128)S(1)} copy-done((f32[16,2,256,128]{3,2,1,0:T(8,128)S(1)}, f32[16,2,256,128]{3,2,1,0:T(8,128)}, u32[]{:S(2)}) %copy-start) | copy-done | bytes 4194328
  11.9 1.9 %collective-permute-start.2 = (bf16[256,512]{1,0:T(8,128)(2,1)S(1)}, bf16[256,512]{1,0:T(8,128)(2,1)S(1)}, u32[]{:S(2)}, u32[]{:S(2)}) collective-permute-start(bf16[256,512]{1,0:T(8,128)(2,1)S(1)} %get-tuple-element.37), channel_id=1, source_target_pairs={{0,2},{1,3},{2,0},{3,1},{4,6},{5,7},{6,4},{7,5},{8,10},{9,11},{10,... | collective-permute-start | bytes 786440 | tf_op jit(solution)/shard_map/ppermute | solution.py:42
  13.8 1.5 collective-permute-start.4
  15.3 1.5 collective-permute-start.3
  17.3 44.2 %all-to-all-done = bf16[16,512,256]{2,1,0:T(8,128)(2,1)} async-done(((bf16[16,512,256]{2,1,0:T(8,128)(2,1)}), bf16[16,512,256]{2,1,0:T(8,128)(2,1)}, u32[]{:S(2)}, u32[]{:S(2)}) %all-to-all-start) | async-done | bytes 4194336 | tf_op jit(solution)/shard_map/all_to_all | solution.py:238
  61.5 2.2 %shard_map.70.refs_7_.map_ref = bf16[4,4,512,256]{3,2,1,0:T(8,128)(2,1)S(1)} custom-call(bf16[4,4,512,256]{3,2,1,0:T(8,128)(2,1)} %bitcast.2.map_ref), custom_call_target="tpu_custom_call" | custom-call | bytes 8388608 | tf_op jit(solution)/shard_map/pallas_call | solution.py:256
  63.7 2.4 %collective-permute-done.4.refs_5_ = bf16[272,256]{1,0:T(8,128)(2,1)S(1)} collective-permute-done((bf16[272,256]{1,0:T(8,128)(2,1)S(1)}, bf16[272,256]{1,0:T(8,128)(2,1)S(1)}, u32[]{:S(2)}, u32[]{:S(2)}) %collective-permute-start.4) | collective-permute-done | bytes 139296 | tf_op jit(solution)/shard_map/ppermute | solution.py:42
  66.2 2.0 %collective-permute-done.5.refs_6_ = bf16[272,256]{1,0:T(8,128)(2,1)S(1)} collective-permute-done((bf16[272,256]{1,0:T(8,128)(2,1)S(1)}, bf16[272,256]{1,0:T(8,128)(2,1)S(1)}, u32[]{:S(2)}, u32[]{:S(2)}) %collective-permute-start.5) | collective-permute-done | bytes 139296 | tf_op jit(solution)/shard_map/ppermute | solution.py:42
  68.2 1.4 collective-permute-done.3.refs_2_
  70.1 2.8 %shard_map.72.refs_0_ = bf16[4,256,128]{2,1,0:T(8,128)(2,1)S(1)} custom-call(f32[8,128]{1,0:T(8,128)S(1)} %get-tuple-element.35.scale_ref, bf16[4,4,512,256]{3,2,1,0:T(8,128)(2,1)S(1)} %shard_map.70.refs_7_.map_ref, bf16[4,256,512]{2,1,0:T(8,128)(2,1)S(1)} %get-tuple-element.41.prior_ref, bf16[4,256,128]{2,1,0:T(8,128)(2,1)S(1)} %get-tuple-element.42.obs_ref, ...), custom_call_target="tpu_custom_call" | custom-call | flops 2147483648 | bytes 8388608 | tf_op jit(solution)/shard_map/pallas_call | solution.py:278
  72.8 2.7 %collective-permute-start.6 = (bf16[4,256,128]{2,1,0:T(8,128)(2,1)S(1)}, bf16[4,256,128]{2,1,0:T(8,128)(2,1)S(1)}, u32[]{:S(2)}, u32[]{:S(2)}) collective-permute-start(bf16[4,256,128]{2,1,0:T(8,128)(2,1)S(1)} %shard_map.72.refs_0_), channel_id=1, source_target_pairs={{0,4},{4,0},{1,5},{5,1},{2,6},{6,2},{3,7},{7,3},{8,12},{12,8},{9,1... | collective-permute-start | bytes 786440 | tf_op jit(solution)/shard_map/ppermute | solution.py:42
  75.5 2.8 %shard_map.73.refs_2_.refs_0_ = bf16[4,256,128]{2,1,0:T(8,128)(2,1)S(1)} custom-call(f32[8,128]{1,0:T(8,128)S(1)} %get-tuple-element.35.scale_ref, bf16[4,4,512,256]{3,2,1,0:T(8,128)(2,1)S(1)} %shard_map.70.refs_7_.map_ref, bf16[4,256,512]{2,1,0:T(8,128)(2,1)S(1)} %get-tuple-element.41.prior_ref, bf16[4,256,128]{2,1,0:T(8,128)(2,1)S(1)} %get-tuple-element.44.obs_ref, ...), custom_call_target="tpu_custom_call" | custom-call | flops 2147483648 | bytes 8388608 | tf_op jit(solution)/shard_map/pallas_call | solution.py:278
  78.7 12.4 %collective-permute-done.6.refs_1_ = bf16[4,256,128]{2,1,0:T(8,128)(2,1)S(1)} collective-permute-done((bf16[4,256,128]{2,1,0:T(8,128)(2,1)S(1)}, bf16[4,256,128]{2,1,0:T(8,128)(2,1)S(1)}, u32[]{:S(2)}, u32[]{:S(2)}) %collective-permute-start.6) | collective-permute-done | bytes 262176 | tf_op jit(solution)/shard_map/ppermute | solution.py:42
  91.1 2.9 %shard_map.74 = (bf16[2,256,128]{2,1,0:T(8,128)(2,1)S(1)}, bf16[2,256,128]{2,1,0:T(8,128)(2,1)S(1)}, f32[2,256,128]{2,1,0:T(8,128)S(1)}, bf16[2,256,128]{2,1,0:T(8,128)(2,1)S(1)}) custom-call(f32[8,128]{1,0:T(8,128)S(1)} %get-tuple-element.35.scale_ref, bf16[4,4,512,256]{3,2,1,0:T(8,128)(2,1)S(1)} %shard_map.70.refs_7_.map_ref, ...), custom_call_target="tpu_custom_call" | custom-call | flops 2147483648 | bytes 8388608 | tf_op jit(solution)/shard_map/pallas_call | solution.py:278
  94.0 2.2 %collective-permute-start.10 = (bf16[2,256,128]{2,1,0:T(8,128)(2,1)S(1)}, bf16[2,256,128]{2,1,0:T(8,128)(2,1)S(1)}, u32[]{:S(2)}, u32[]{:S(2)}) collective-permute-start(bf16[2,256,128]{2,1,0:T(8,128)(2,1)S(1)} %get-tuple-element.47), channel_id=1, source_target_pairs={{0,12},{4,8},{8,4},{12,0},{16,28},{20,24},{24,20},{28,16},{1,13},{... | collective-permute-start | bytes 393224 | tf_op jit(solution)/shard_map/ppermute | solution.py:295
  98.1 2.9 %shard_map.75 = (bf16[2,256,128]{2,1,0:T(8,128)(2,1)S(1)}, bf16[2,256,128]{2,1,0:T(8,128)(2,1)S(1)}, f32[2,256,128]{2,1,0:T(8,128)S(1)}, bf16[2,256,128]{2,1,0:T(8,128)(2,1)S(1)}) custom-call(f32[8,128]{1,0:T(8,128)S(1)} %get-tuple-element.35.scale_ref, bf16[4,4,512,256]{3,2,1,0:T(8,128)(2,1)S(1)} %shard_map.70.refs_7_.map_ref, ...), custom_call_target="tpu_custom_call" | custom-call | flops 2147483648 | bytes 8388608 | tf_op jit(solution)/shard_map/pallas_call | solution.py:278
  101.0 2.2 %collective-permute-start.11 = (bf16[2,256,128]{2,1,0:T(8,128)(2,1)S(1)}, bf16[2,256,128]{2,1,0:T(8,128)(2,1)S(1)}, u32[]{:S(2)}, u32[]{:S(2)}) collective-permute-start(bf16[2,256,128]{2,1,0:T(8,128)(2,1)S(1)} %get-tuple-element.48), channel_id=1, source_target_pairs={{0,12},{4,8},{8,4},{12,0},{16,28},{20,24},{24,20},{28,16},{1,13},{... | collective-permute-start | bytes 393224 | tf_op jit(solution)/shard_map/ppermute | solution.py:295
  103.2 3.8 %collective-permute-done.7.refs_0_ = bf16[2,256,128]{2,1,0:T(8,128)(2,1)S(1)} collective-permute-done((bf16[2,256,128]{2,1,0:T(8,128)(2,1)S(1)}, bf16[2,256,128]{2,1,0:T(8,128)(2,1)S(1)}, u32[]{:S(2)}, u32[]{:S(2)}) %collective-permute-start.7) | collective-permute-done | bytes 131104 | tf_op jit(solution)/shard_map/ppermute | solution.py:295
  106.9 1.7 %collective-permute-done.10.refs_2_ = bf16[2,256,128]{2,1,0:T(8,128)(2,1)S(1)} collective-permute-done((bf16[2,256,128]{2,1,0:T(8,128)(2,1)S(1)}, bf16[2,256,128]{2,1,0:T(8,128)(2,1)S(1)}, u32[]{:S(2)}, u32[]{:S(2)}) %collective-permute-start.10) | collective-permute-done | bytes 131104 | tf_op jit(solution)/shard_map/ppermute | solution.py:295
  108.7 8.1 %collective-permute-done.9.refs_1_ = bf16[2,256,128]{2,1,0:T(8,128)(2,1)S(1)} collective-permute-done((bf16[2,256,128]{2,1,0:T(8,128)(2,1)S(1)}, bf16[2,256,128]{2,1,0:T(8,128)(2,1)S(1)}, u32[]{:S(2)}, u32[]{:S(2)}) %collective-permute-start.9) | collective-permute-done | bytes 131104 | tf_op jit(solution)/shard_map/ppermute | solution.py:295
  116.8 1.7 %collective-permute-done.11.refs_3_ = bf16[2,256,128]{2,1,0:T(8,128)(2,1)S(1)} collective-permute-done((bf16[2,256,128]{2,1,0:T(8,128)(2,1)S(1)}, bf16[2,256,128]{2,1,0:T(8,128)(2,1)S(1)}, u32[]{:S(2)}, u32[]{:S(2)}) %collective-permute-start.11) | collective-permute-done | bytes 131104 | tf_op jit(solution)/shard_map/ppermute | solution.py:295
  119.2 1.4 collective-permute-start.21
  120.6 2.4 %collective-permute-start.20 = (bf16[2,256,256]{2,1,0:T(8,128)(2,1)S(1)}, bf16[2,256,256]{2,1,0:T(8,128)(2,1)S(1)}, u32[]{:S(2)}, u32[]{:S(2)}) collective-permute-start(bf16[2,256,256]{2,1,0:T(8,128)(2,1)S(1)} %get-tuple-element.54.refs_1_), channel_id=1, source_target_pairs={{0,18},{1,19},{2,16},{3,17},{8,26},{9,27},{10,24},{11,25},{16,2},{... | collective-permute-start | bytes 786440 | tf_op jit(solution)/shard_map/ppermute | solution.py:42
  123.0 2.1 %shard_map.77 = (bf16[256,256]{1,0:T(8,128)(2,1)S(1)}, bf16[256,256]{1,0:T(8,128)(2,1)S(1)}, bf16[256,256]{1,0:T(8,128)(2,1)S(1)}, bf16[256,256]{1,0:T(8,128)(2,1)S(1)}) custom-call(f32[8,128]{1,0:T(8,128)S(1)} %get-tuple-element.35.scale_ref, bf16[4,4,512,256]{3,2,1,0:T(8,128)(2,1)S(1)} %shard_map.70.refs_7_.map_ref, ...), custom_call_target="tpu_custom_call" | custom-call | flops 2147483648 | bytes 8388608 | tf_op jit(solution)/shard_map/pallas_call | solution.py:312
  125.9 2.9 %collective-permute-start.17 = (bf16[3,256,256]{2,1,0:T(8,128)(2,1)S(1)}, bf16[3,256,256]{2,1,0:T(8,128)(2,1)S(1)}, u32[]{:S(2)}, u32[]{:S(2)}) collective-permute-start(bf16[3,256,256]{2,1,0:T(8,128)(2,1)S(1)} %get-tuple-element.63), channel_id=1, source_target_pairs={{0,3},{1,2},{2,1},{3,0},{8,11},{9,10},{10,9},{11,8},{16,19},{17,18... | collective-permute-start | bytes 1179656 | tf_op jit(solution)/shard_map/ppermute | solution.py:42
  130.2 2.0 %collective-permute-start.19 = (bf16[2,256,256]{2,1,0:T(8,128)(2,1)S(1)}, bf16[2,256,256]{2,1,0:T(8,128)(2,1)S(1)}, u32[]{:S(2)}, u32[]{:S(2)}) collective-permute-start(bf16[2,256,256]{2,1,0:T(8,128)(2,1)S(1)} %get-tuple-element.54.refs_1_), channel_id=1, source_target_pairs={{0,17},{1,16},{2,19},{3,18},{8,25},{9,24},{10,27},{11,26},{16,1},{... | collective-permute-start | bytes 786440 | tf_op jit(solution)/shard_map/ppermute | solution.py:42
  132.1 3.8 %collective-permute-done.20.refs_6_ = bf16[2,256,256]{2,1,0:T(8,128)(2,1)S(1)} collective-permute-done((bf16[2,256,256]{2,1,0:T(8,128)(2,1)S(1)}, bf16[2,256,256]{2,1,0:T(8,128)(2,1)S(1)}, u32[]{:S(2)}, u32[]{:S(2)}) %collective-permute-start.20) | collective-permute-done | bytes 262176 | tf_op jit(solution)/shard_map/ppermute | solution.py:42
  136.9 4.0 %collective-permute-done.19.refs_5_ = bf16[2,256,256]{2,1,0:T(8,128)(2,1)S(1)} collective-permute-done((bf16[2,256,256]{2,1,0:T(8,128)(2,1)S(1)}, bf16[2,256,256]{2,1,0:T(8,128)(2,1)S(1)}, u32[]{:S(2)}, u32[]{:S(2)}) %collective-permute-start.19) | collective-permute-done | bytes 262176 | tf_op jit(solution)/shard_map/ppermute | solution.py:42
  140.9 5.5 %collective-permute-done.18.refs_4_ = bf16[2,256,256]{2,1,0:T(8,128)(2,1)S(1)} collective-permute-done((bf16[2,256,256]{2,1,0:T(8,128)(2,1)S(1)}, bf16[2,256,256]{2,1,0:T(8,128)(2,1)S(1)}, u32[]{:S(2)}, u32[]{:S(2)}) %collective-permute-start.18) | collective-permute-done | bytes 262176 | tf_op jit(solution)/shard_map/ppermute | solution.py:42
  146.3 5.5 %collective-permute-done.15.refs_1_ = bf16[3,256,256]{2,1,0:T(8,128)(2,1)S(1)} collective-permute-done((bf16[3,256,256]{2,1,0:T(8,128)(2,1)S(1)}, bf16[3,256,256]{2,1,0:T(8,128)(2,1)S(1)}, u32[]{:S(2)}, u32[]{:S(2)}) %collective-permute-start.15) | collective-permute-done | bytes 393248 | tf_op jit(solution)/shard_map/ppermute | solution.py:42
  151.8 2.5 %shard_map.79 = (f32[16,2,256,128]{3,2,1,0:T(8,128)}, f32[4,512,128]{2,1,0:T(8,128)}) custom-call(bf16[3,256,256]{2,1,0:T(8,128)(2,1)S(1)} %get-tuple-element.60.refs_0_, bf16[3,256,256]{2,1,0:T(8,128)(2,1)S(1)} %collective-permute-done.15.refs_1_, bf16[3,256,256]{2,1,0:T(8,128)(2,1)S(1)} %collective-permute-done.16.refs_2_, ...), custom_call_target="tpu_custom_call" | custom-call | bytes 8388608 | tf_op jit(solution)/shard_map/pallas_call | solution.py:331
  (35 shorter events, 9.9 us)
Async XLA Ops:
  0.6 6.4 %copy-start.2 = (f32[256]{0:T(256)S(1)}, f32[256]{0:T(256)}, u32[]{:S(2)}) copy-start(f32[256]{0:T(256)} %param.7) | copy-start | bytes 3076
  0.6 60.9 %all-to-all-start = ((bf16[16,512,256]{2,1,0:T(8,128)(2,1)}), bf16[16,512,256]{2,1,0:T(8,128)(2,1)}, u32[]{:S(2)}, u32[]{:S(2)}) async-start(bf16[16,512,256]{2,1,0:T(8,128)(2,1)} %bitcast.5), calls=%async_computation | async-start | bytes 8388608 | tf_op jit(solution)/shard_map/all_to_all | solution.py:238
  7.0 3.2 %copy-start.3 = (f32[16]{0:T(128)S(1)}, f32[16]{0:T(128)}, u32[]{:S(2)}) copy-start(f32[16]{0:T(128)} %param.9) | copy-start | bytes 196
  7.0 2.2 %copy-start = (f32[16,2,256,128]{3,2,1,0:T(8,128)S(1)}, f32[16,2,256,128]{3,2,1,0:T(8,128)}, u32[]{:S(2)}) copy-start(f32[16,2,256,128]{3,2,1,0:T(8,128)} %obs_ref.1) | copy-start | bytes 12582916
  9.2 2.0 %copy-start.1 = (bf16[256,512]{1,0:T(8,128)(2,1)S(1)}, bf16[256,512]{1,0:T(8,128)(2,1)}, u32[]{:S(2)}) copy-start(bf16[256,512]{1,0:T(8,128)(2,1)} %own_ref.3) | copy-start | bytes 786436
  9.8 1.4 collective-permute-start
  11.9 57.8 %collective-permute-start.2 = (bf16[256,512]{1,0:T(8,128)(2,1)S(1)}, bf16[256,512]{1,0:T(8,128)(2,1)S(1)}, u32[]{:S(2)}, u32[]{:S(2)}) collective-permute-start(bf16[256,512]{1,0:T(8,128)(2,1)S(1)} %get-tuple-element.37), channel_id=1, source_target_pairs={{0,2},{1,3},{2,0},{3,1},{4,6},{5,7},{6,4},{7,5},{8,10},{9,11},{10,... | collective-permute-start | bytes 786440 | tf_op jit(solution)/shard_map/ppermute | solution.py:42
  13.8 52.3 %collective-permute-start.4 = (bf16[272,256]{1,0:T(8,128)(2,1)S(1)}, bf16[272,256]{1,0:T(8,128)(2,1)S(1)}, u32[]{:S(2)}, u32[]{:S(2)}) collective-permute-start(bf16[272,256]{1,0:T(8,128)(2,1)S(1)} %get-tuple-element.39), channel_id=1, source_target_pairs={{0,16},{8,24},{16,0},{24,8},{1,17},{9,25},{17,1},{25,9},{2,18},{10... | collective-permute-start | bytes 417800 | tf_op jit(solution)/shard_map/ppermute | solution.py:42
  15.3 52.9 %collective-permute-start.5 = (bf16[272,256]{1,0:T(8,128)(2,1)S(1)}, bf16[272,256]{1,0:T(8,128)(2,1)S(1)}, u32[]{:S(2)}, u32[]{:S(2)}) collective-permute-start(bf16[272,256]{1,0:T(8,128)(2,1)S(1)} %get-tuple-element.40), channel_id=1, source_target_pairs={{0,24},{8,16},{16,8},{24,0},{1,25},{9,17},{17,9},{25,1},{2,26},{10... | collective-permute-start | bytes 417800 | tf_op jit(solution)/shard_map/ppermute | solution.py:42
  15.3 54.4 %collective-permute-start.3 = (bf16[256,256]{1,0:T(8,128)(2,1)S(1)}, bf16[256,256]{1,0:T(8,128)(2,1)S(1)}, u32[]{:S(2)}, u32[]{:S(2)}) collective-permute-start(bf16[256,256]{1,0:T(8,128)(2,1)S(1)} %get-tuple-element.36), channel_id=1, source_target_pairs={{0,3},{1,2},{2,1},{3,0},{4,7},{5,6},{6,5},{7,4},{8,11},{9,10},{10,... | collective-permute-start | bytes 393224 | tf_op jit(solution)/shard_map/ppermute | solution.py:42
  16.7 52.9 %collective-permute-start.1 = (bf16[256,256]{1,0:T(8,128)(2,1)S(1)}, bf16[256,256]{1,0:T(8,128)(2,1)S(1)}, u32[]{:S(2)}, u32[]{:S(2)}) collective-permute-start(bf16[256,256]{1,0:T(8,128)(2,1)S(1)} %get-tuple-element.36), channel_id=1, source_target_pairs={{0,1},{1,0},{2,3},{3,2},{4,5},{5,4},{6,7},{7,6},{8,9},{9,8},{10,11... | collective-permute-start | bytes 393224 | tf_op jit(solution)/shard_map/ppermute | solution.py:42
  72.8 18.2 %collective-permute-start.6 = (bf16[4,256,128]{2,1,0:T(8,128)(2,1)S(1)}, bf16[4,256,128]{2,1,0:T(8,128)(2,1)S(1)}, u32[]{:S(2)}, u32[]{:S(2)}) collective-permute-start(bf16[4,256,128]{2,1,0:T(8,128)(2,1)S(1)} %shard_map.72.refs_0_), channel_id=1, source_target_pairs={{0,4},{4,0},{1,5},{5,1},{2,6},{6,2},{3,7},{7,3},{8,12},{12,8},{9,1... | collective-permute-start | bytes 786440 | tf_op jit(solution)/shard_map/ppermute | solution.py:42
  78.3 19.8 %collective-permute-start.8 = (bf16[4,256,128]{2,1,0:T(8,128)(2,1)S(1)}, bf16[4,256,128]{2,1,0:T(8,128)(2,1)S(1)}, u32[]{:S(2)}, u32[]{:S(2)}) collective-permute-start(bf16[4,256,128]{2,1,0:T(8,128)(2,1)S(1)} %shard_map.73.refs_2_.refs_0_), channel_id=1, source_target_pairs={{0,4},{4,0},{1,5},{5,1},{2,6},{6,2},{3,7},{7,3},{8,12},{12,8},{9,1... | collective-permute-start | bytes 786440 | tf_op jit(solution)/shard_map/ppermute | solution.py:42
  93.9 13.0 %collective-permute-start.7 = (bf16[2,256,128]{2,1,0:T(8,128)(2,1)S(1)}, bf16[2,256,128]{2,1,0:T(8,128)(2,1)S(1)}, u32[]{:S(2)}, u32[]{:S(2)}) collective-permute-start(bf16[2,256,128]{2,1,0:T(8,128)(2,1)S(1)} %get-tuple-element.45), channel_id=1, source_target_pairs={{0,4},{4,0},{8,12},{12,8},{16,20},{20,16},{24,28},{28,24},{1,5},{5... | collective-permute-start | bytes 393224 | tf_op jit(solution)/shard_map/ppermute | solution.py:295
  94.0 14.7 %collective-permute-start.10 = (bf16[2,256,128]{2,1,0:T(8,128)(2,1)S(1)}, bf16[2,256,128]{2,1,0:T(8,128)(2,1)S(1)}, u32[]{:S(2)}, u32[]{:S(2)}) collective-permute-start(bf16[2,256,128]{2,1,0:T(8,128)(2,1)S(1)} %get-tuple-element.47), channel_id=1, source_target_pairs={{0,12},{4,8},{8,4},{12,0},{16,28},{20,24},{24,20},{28,16},{1,13},{... | collective-permute-start | bytes 393224 | tf_op jit(solution)/shard_map/ppermute | solution.py:295
  96.2 12.5 %collective-permute-start.12 = (bf16[2,256,128]{2,1,0:T(8,128)(2,1)S(1)}, bf16[2,256,128]{2,1,0:T(8,128)(2,1)S(1)}, u32[]{:S(2)}, u32[]{:S(2)}) collective-permute-start(bf16[2,256,128]{2,1,0:T(8,128)(2,1)S(1)} %get-tuple-element.51), channel_id=1, source_target_pairs={{0,8},{8,0},{16,24},{24,16},{1,9},{9,1},{17,25},{25,17},{2,10},{10... | collective-permute-start | bytes 393224 | tf_op jit(solution)/shard_map/ppermute | solution.py:42
  100.9 15.8 %collective-permute-start.9 = (bf16[2,256,128]{2,1,0:T(8,128)(2,1)S(1)}, bf16[2,256,128]{2,1,0:T(8,128)(2,1)S(1)}, u32[]{:S(2)}, u32[]{:S(2)}) collective-permute-start(bf16[2,256,128]{2,1,0:T(8,128)(2,1)S(1)} %get-tuple-element.46), channel_id=1, source_target_pairs={{0,4},{4,0},{8,12},{12,8},{16,20},{20,16},{24,28},{28,24},{1,5},{5... | collective-permute-start | bytes 393224 | tf_op jit(solution)/shard_map/ppermute | solution.py:295
  101.0 17.5 %collective-permute-start.11 = (bf16[2,256,128]{2,1,0:T(8,128)(2,1)S(1)}, bf16[2,256,128]{2,1,0:T(8,128)(2,1)S(1)}, u32[]{:S(2)}, u32[]{:S(2)}) collective-permute-start(bf16[2,256,128]{2,1,0:T(8,128)(2,1)S(1)} %get-tuple-element.48), channel_id=1, source_target_pairs={{0,12},{4,8},{8,4},{12,0},{16,28},{20,24},{24,20},{28,16},{1,13},{... | collective-permute-start | bytes 393224 | tf_op jit(solution)/shard_map/ppermute | solution.py:295
  106.9 11.6 %collective-permute-start.13 = (bf16[2,256,128]{2,1,0:T(8,128)(2,1)S(1)}, bf16[2,256,128]{2,1,0:T(8,128)(2,1)S(1)}, u32[]{:S(2)}, u32[]{:S(2)}) collective-permute-start(bf16[2,256,128]{2,1,0:T(8,128)(2,1)S(1)} %get-tuple-element.52), channel_id=1, source_target_pairs={{0,8},{8,0},{16,24},{24,16},{1,9},{9,1},{17,25},{25,17},{2,10},{10... | collective-permute-start | bytes 393224 | tf_op jit(solution)/shard_map/ppermute | solution.py:42
  118.8 4.3 %collective-permute-start.14 = (bf16[2,256,256]{2,1,0:T(8,128)(2,1)S(1)}, bf16[2,256,256]{2,1,0:T(8,128)(2,1)S(1)}, u32[]{:S(2)}, u32[]{:S(2)}) collective-permute-start(bf16[2,256,256]{2,1,0:T(8,128)(2,1)S(1)} %get-tuple-element.55), channel_id=1, source_target_pairs={{0,8},{8,0},{16,24},{24,16},{1,9},{9,1},{17,25},{25,17},{2,10},{10... | collective-permute-start | bytes 786440 | tf_op jit(solution)/shard_map/ppermute | solution.py:42
  119.2 11.0 %collective-permute-start.21 = (bf16[2,256,256]{2,1,0:T(8,128)(2,1)S(1)}, bf16[2,256,256]{2,1,0:T(8,128)(2,1)S(1)}, u32[]{:S(2)}, u32[]{:S(2)}) collective-permute-start(bf16[2,256,256]{2,1,0:T(8,128)(2,1)S(1)} %get-tuple-element.54.refs_1_), channel_id=1, source_target_pairs={{0,19},{1,18},{2,17},{3,16},{8,27},{9,26},{10,25},{11,24},{16,3},{... | collective-permute-start | bytes 786440 | tf_op jit(solution)/shard_map/ppermute | solution.py:42
  120.6 15.3 %collective-permute-start.20 = (bf16[2,256,256]{2,1,0:T(8,128)(2,1)S(1)}, bf16[2,256,256]{2,1,0:T(8,128)(2,1)S(1)}, u32[]{:S(2)}, u32[]{:S(2)}) collective-permute-start(bf16[2,256,256]{2,1,0:T(8,128)(2,1)S(1)} %get-tuple-element.54.refs_1_), channel_id=1, source_target_pairs={{0,18},{1,19},{2,16},{3,17},{8,26},{9,27},{10,24},{11,25},{16,2},{... | collective-permute-start | bytes 786440 | tf_op jit(solution)/shard_map/ppermute | solution.py:42
  125.3 26.6 %collective-permute-start.15 = (bf16[3,256,256]{2,1,0:T(8,128)(2,1)S(1)}, bf16[3,256,256]{2,1,0:T(8,128)(2,1)S(1)}, u32[]{:S(2)}, u32[]{:S(2)}) collective-permute-start(bf16[3,256,256]{2,1,0:T(8,128)(2,1)S(1)} %get-tuple-element.61), channel_id=1, source_target_pairs={{0,1},{1,0},{2,3},{3,2},{8,9},{9,8},{10,11},{11,10},{16,17},{17,16... | collective-permute-start | bytes 1179656 | tf_op jit(solution)/shard_map/ppermute | solution.py:42
  125.9 26.0 %collective-permute-start.16 = (bf16[3,256,256]{2,1,0:T(8,128)(2,1)S(1)}, bf16[3,256,256]{2,1,0:T(8,128)(2,1)S(1)}, u32[]{:S(2)}, u32[]{:S(2)}) collective-permute-start(bf16[3,256,256]{2,1,0:T(8,128)(2,1)S(1)} %get-tuple-element.62), channel_id=1, source_target_pairs={{0,2},{1,3},{2,0},{3,1},{8,10},{9,11},{10,8},{11,9},{16,18},{17,19... | collective-permute-start | bytes 1179656 | tf_op jit(solution)/shard_map/ppermute | solution.py:42
  125.9 25.9 %collective-permute-start.17 = (bf16[3,256,256]{2,1,0:T(8,128)(2,1)S(1)}, bf16[3,256,256]{2,1,0:T(8,128)(2,1)S(1)}, u32[]{:S(2)}, u32[]{:S(2)}) collective-permute-start(bf16[3,256,256]{2,1,0:T(8,128)(2,1)S(1)} %get-tuple-element.63), channel_id=1, source_target_pairs={{0,3},{1,2},{2,1},{3,0},{8,11},{9,10},{10,9},{11,8},{16,19},{17,18... | collective-permute-start | bytes 1179656 | tf_op jit(solution)/shard_map/ppermute | solution.py:42
  130.2 10.7 %collective-permute-start.19 = (bf16[2,256,256]{2,1,0:T(8,128)(2,1)S(1)}, bf16[2,256,256]{2,1,0:T(8,128)(2,1)S(1)}, u32[]{:S(2)}, u32[]{:S(2)}) collective-permute-start(bf16[2,256,256]{2,1,0:T(8,128)(2,1)S(1)} %get-tuple-element.54.refs_1_), channel_id=1, source_target_pairs={{0,17},{1,16},{2,19},{3,18},{8,25},{9,24},{10,27},{11,26},{16,1},{... | collective-permute-start | bytes 786440 | tf_op jit(solution)/shard_map/ppermute | solution.py:42
  135.9 10.5 %collective-permute-start.18 = (bf16[2,256,256]{2,1,0:T(8,128)(2,1)S(1)}, bf16[2,256,256]{2,1,0:T(8,128)(2,1)S(1)}, u32[]{:S(2)}, u32[]{:S(2)}) collective-permute-start(bf16[2,256,256]{2,1,0:T(8,128)(2,1)S(1)} %get-tuple-element.54.refs_1_), channel_id=1, source_target_pairs={{0,16},{1,17},{2,18},{3,19},{8,24},{9,25},{10,26},{11,27},{16,0},{... | collective-permute-start | bytes 786440 | tf_op jit(solution)/shard_map/ppermute | solution.py:42

commit v13 on v12

--- a/solution.py
+++ b/solution.py
@@ -76,24 +76,45 @@
         outs[d][sensors:, :] = tail
 
 
+def pack_diagonal(block, out_ref, at):
+    half = block.shape[0] // 2
+    out_ref[at:at + half, :] = block[:half]
+    corner = block[half:, half:]
+    out_ref[at + half:at + half + half // 2, :] = jnp.concatenate([corner[:half // 2], corner[half // 2:]], 1)
+
+
+def unpack_diagonal(came_ref, at):
+    half = came_ref.shape[1] // 2
+    upper = came_ref[at:at + half, :]
+    corner = came_ref[at + half:at + half + half // 2, :]
+    corner = jnp.concatenate([corner[:, :half], corner[:, half:]], 0)
+    return jnp.concatenate([upper, jnp.concatenate([upper[:, half:].T, corner], 1)], 0)
+
+
 def prior_kernel(scale_ref, own_ref, after_ref, full_ref, diagonal_ref, wide_ref):
     cells = own_ref.shape[0]
-    full_ref[...] = own_ref[...]
+    quad = my_place()[1]
+    on, off = (pl.ds(pl.multiple_of(p * cells, cells), cells) for p in (quad & 1, 1 - (quad & 1)))
+    diagonal = own_ref[:, on]
+    pack_diagonal(diagonal, diagonal_ref, 0)
+    full_ref[:cells, :] = own_ref[:, off]
+    pack_diagonal(diagonal, full_ref, cells)
     wide_ref[...] = jnp.full(wide_ref.shape, scale_ref[0], f32)
-    diagonal_ref[...] = own_ref[:, pl.ds(pl.multiple_of((my_place()[1] & 1) * cells, cells), cells)]
 
 
 def gather_kernel(groups, quads, own_ref, *refs):
     came, data = refs[:quads - 1], refs[quads - 1:quads - 1 + groups]
     prior_ref, noise_ref, *streams = refs[quads + groups:]
-    me, quad = my_place()[0] * CORES + my_place()[2], my_place()[1]
+    me, quad = lax.axis_index("sensor"), my_place()[1]
     sensors, cells = streams[0].shape[1], own_ref.shape[0]
     on, off = (pl.ds(pl.multiple_of(p * cells, cells), cells) for p in (quad & 1, 1 - (quad & 1)))
     for d in range(0, quads, 2):
-        rows = own_ref if d == 0 else came[d - 1]
-        prior_ref[quad ^ d] = rows[...]
-        prior_ref[quad ^ d ^ 1, :, on] = rows[:, off].T
-        prior_ref[quad ^ d ^ 1, :, off] = came[d][...]
+        diagonal = own_ref[:, on] if d == 0 else unpack_diagonal(came[d - 1], cells)
+        beside = own_ref[:, off] if d == 0 else came[d - 1][:cells, :]
+        prior_ref[quad ^ d, :, on] = diagonal
+        prior_ref[quad ^ d, :, off] = beside
+        prior_ref[quad ^ d ^ 1, :, on] = beside.T
+        prior_ref[quad ^ d ^ 1, :, off] = unpack_diagonal(came[d], 0)
     row = lax.broadcasted_iota(jnp.int32, (sensors, sensors), 0)
     col = lax.broadcasted_iota(jnp.int32, (sensors, sensors), 1)
     for d in range(groups):
@@ -205,23 +226,25 @@
         out[...] = held_ref[my_place()[1] ^ d]
 
 
-def end_kernel(chips, quads, *refs):
-    came, (dual_out, post_out, dual_ref, post_ref, sems) = refs[:chips], refs[chips:]
-    pair, quad = my_place()[0], my_place()[1]
-    cells = post_ref.shape[1] // 2
+def end_kernel(e, quads, follows, *refs):
+    came, refs = refs[:quads], refs[quads + follows:]
+    count = 1 + (e == 0)
+    outs, (dual_ref, sems, *post) = refs[:count], refs[count:]
+    pair, quad, _ = my_place()
     sends = []
-    for chip in reversed(range(chips)):
-        e, d = divmod(chip, quads)
+    for d in range(quads):
         for core in range(CORES):
             freq = (CORES * (pair ^ e) + core) * quads + (quad ^ d)
             for part in range(2):
-                dual_ref[chip, core, part] = came[chip][core, :, part * LANES:(part + 1) * LANES].astype(f32)
-            sends.append(pltpu.make_async_copy(dual_ref.at[chip, core], dual_out.at[freq], sems.at[chip, core]))
+                dual_ref[d, core, part] = came[d][core, :, part * LANES:(part + 1) * LANES].astype(f32)
+            sends.append(pltpu.make_async_copy(dual_ref.at[d, core], outs[0].at[freq], sems.at[d, core]))
             sends[-1].start()
         if e == 0:
-            post_ref[d, pl.ds(0, cells, stride=2), :] = came[chip][CORES, :, :LANES].astype(f32)
-            post_ref[d, pl.ds(1, cells, stride=2), :] = came[chip][CORES, :, LANES:].astype(f32)
-            sends.append(pltpu.make_async_copy(post_ref.at[d], post_out.at[quad ^ d], sems.at[chip, CORES]))
+            post_ref = post[0]
+            cells = post_ref.shape[1] // 2
+            post_ref[d, pl.ds(0, cells, stride=2), :] = came[d][CORES, :, :LANES].astype(f32)
+            post_ref[d, pl.ds(1, cells, stride=2), :] = came[d][CORES, :, LANES:].astype(f32)
+            sends.append(pltpu.make_async_copy(post_ref.at[d], outs[1].at[quad ^ d], sems.at[d, CORES]))
             sends[-1].start()
     for copy in sends:
         copy.wait()
@@ -247,10 +270,11 @@
         moved=groups * sensors * LANES * 12,
     )(observed, noise_var.reshape(1, sensors))
     data = [data[0]] + [swap(data[d], "sensor", d) for d in range(1, groups)]
+    packed = cells // 2 + cells // 4
     rows, diagonal, scale = call(
         prior_kernel,
         [SMEM, VMEM, ANY],
-        [shape((cells, width), bf16), shape((cells, cells), bf16), shape((8, LANES), f32)],
+        [shape((cells + packed, cells), bf16), shape((packed, cells), bf16), shape((8, LANES), f32)],
     )(scale, prior_rows, data[1])
     came = [swap(diagonal if d % 2 else rows, "quad", d) for d in range(1, quads)]
     near = call(bring_kernel, [ANY], [shape(held.shape, bf16)], [pltpu.SemaphoreType.DMA], moved=8 * 2**20)(held)[0]
@@ -328,19 +352,28 @@
         for d in reversed(range(quads)):
             out = near_ones[d] if e == 0 else finals[e]
             duals[e * quads + d] = swap(out, both, CORES * e * quads + d) if e + d else out
-    dual, posterior = call(
-        functools.partial(end_kernel, pairs * quads, quads),
-        [VMEM] * (pairs * quads),
-        [shape((frequencies, halves, sensors, LANES), f32), shape((quads, cells * 2, LANES), f32)],
-        [
-            pltpu.VMEM((pairs * quads, CORES, halves, sensors, LANES), f32),
-            pltpu.VMEM((quads, cells * 2, LANES), f32),
-            pltpu.SemaphoreType.DMA((pairs * quads, CORES + 1)),
-        ],
-        [ANY, ANY],
-        moved=8 * 2**20,
-    )(*[duals[i] for i in range(pairs * quads)])
-    return dual, posterior.reshape(quads, cells, 2, LANES)
+    dual, posterior = [], []
+    for e in reversed(range(pairs)):
+        out = [shape((frequencies, halves, sensors, LANES), f32)]
+        scratch = [
+            pltpu.VMEM((quads, CORES, halves, sensors, LANES), f32),
+            pltpu.SemaphoreType.DMA((quads, CORES + 1)),
+        ]
+        if e == 0:
+            out.append(shape((quads, cells * 2, LANES), f32))
+            scratch.append(pltpu.VMEM((quads, cells * 2, LANES), f32))
+        *dual, last = call(
+            functools.partial(end_kernel, e, quads, len(dual)),
+            [VMEM] * quads + [ANY] * len(dual),
+            out,
+            scratch,
+            [ANY] * len(out),
+            moved=4 * 2**20,
+            aliases={quads: 0} if dual else None,
+        )(*[duals[e * quads + d] for d in range(quads)], *dual)
+        if e:
+            dual = [last]
+    return dual[0], last.reshape(quads, cells, 2, LANES)
 
 
 def solution(mesh):

time: 155 us -> 153 us (0.987)
  waiting for transfers between devices: 99.4 us -> 94.7 us
  starting transfers between devices: 31.4 us -> 33.7 us
    ppermute x4, waiting for transfers between devices: 15.3 us -> 12.3 us  [to_other_sides(): lax.ppermute(x, ('sensor', 'side'), [(i, i ^ 1 + CORES * cross) for i in...]
    ppermute x18, starting transfers between devices: 20.5 us -> 22.8 us  [swap(): return lax.ppermute(x, axes, [(i, i ^ distance) for i in range(count)])]
    ppermute x18, waiting for transfers between devices: 39.8 us -> 38.2 us  [swap(): return lax.ppermute(x, axes, [(i, i ^ distance) for i in range(count)])]
    pallas_call x2 -> x3, Pallas kernels: 3.22 us -> 3.88 us  [the longest x2 3.2 us: on_device(): call(functools.partial(end_kernel, e, quads, len(dual)), [VMEM] * quads +...]
  transfers between devices with their start and end apart: 23 -> 23, of which waited for: 16 -> 14; matrix products, arithmetic and copies ran while one was open for 0% -> 0% of each run, Pallas kernels for 9% -> 10%
where the time goes in v13:
time: 153 us
  waiting for transfers between devices  94.7 us (62%)
  starting transfers between devices  33.7 us (22%)
  Pallas kernels  20.7 us (14%)
  local copies, waits for them, and re-layouts  2.78 us (2%)
    all_to_all x1, waiting for transfers between devices, on_device(): lax.all_to_all(forward_map.reshape(frequencies, halves * sensors, cells),...  44.2 us
    ppermute x18, waiting for transfers between devices, swap(): return lax.ppermute(x, axes, [(i, i ^ distance) for i in range(count)])  38.2 us
    ppermute x18, starting transfers between devices, swap(): return lax.ppermute(x, axes, [(i, i ^ distance) for i in range(count)])  22.8 us
    ppermute x4, waiting for transfers between devices, to_other_sides(): lax.ppermute(x, ('sensor', 'side'), [(i, i ^ 1 + CORES * cross) for i in...  12.3 us
    pallas_call x4, Pallas kernels, step(): call(functools.partial(step_kernel, stage, len(preds), len(after)), [VMEM...  11.3 us
    all_to_all x1, starting transfers between devices, on_device(): lax.all_to_all(forward_map.reshape(frequencies, halves * sensors, cells),...  6.35 us
    ppermute x4, starting transfers between devices, to_other_sides(): lax.ppermute(x, ('sensor', 'side'), [(i, i ^ 1 + CORES * cross) for i in...  4.61 us
    pallas_call x2, Pallas kernels, on_device(): call(functools.partial(end_kernel, e, quads, len(dual)), [VMEM] * quads +...  3.2 us
  transfers between devices with their start and end apart: 23, of which 14 were waited for; matrix products, arithmetic and copies ran while one was open for 0% of the time, Pallas kernels for 10%

profile of v13, /device:TPU:0, one launch (start us, length us, event | category | flops | bytes accessed | tf_op | source)
XLA Modules:
  0.0 152.7 jit_solution(8082795178599777146)
XLA Ops:
  0.6 6.4 %all-to-all-start = ((bf16[16,512,256]{2,1,0:T(8,128)(2,1)}), bf16[16,512,256]{2,1,0:T(8,128)(2,1)}, u32[]{:S(2)}, u32[]{:S(2)}) async-start(bf16[16,512,256]{2,1,0:T(8,128)(2,1)} %bitcast.5), calls=%async_computation | async-start | bytes 8388608 | tf_op jit(solution)/shard_map/all_to_all | solution.py:261
  7.0 2.2 %copy-done = f32[16,2,256,128]{3,2,1,0:T(8,128)S(1)} copy-done((f32[16,2,256,128]{3,2,1,0:T(8,128)S(1)}, f32[16,2,256,128]{3,2,1,0:T(8,128)}, u32[]{:S(2)}) %copy-start) | copy-done | bytes 4194328
  11.9 1.9 %collective-permute-start.2 = (bf16[448,256]{1,0:T(8,128)(2,1)S(1)}, bf16[448,256]{1,0:T(8,128)(2,1)S(1)}, u32[]{:S(2)}, u32[]{:S(2)}) collective-permute-start(bf16[448,256]{1,0:T(8,128)(2,1)S(1)} %get-tuple-element.37), channel_id=1, source_target_pairs={{0,2},{1,3},{2,0},{3,1},{4,6},{5,7},{6,4},{7,5},{8,10},{9,11},{10,... | collective-permute-start | bytes 688136 | tf_op jit(solution)/shard_map/ppermute | solution.py:42
  13.8 1.5 collective-permute-start.4
  15.3 1.5 collective-permute-start.3
  17.3 44.2 %all-to-all-done = bf16[16,512,256]{2,1,0:T(8,128)(2,1)} async-done(((bf16[16,512,256]{2,1,0:T(8,128)(2,1)}), bf16[16,512,256]{2,1,0:T(8,128)(2,1)}, u32[]{:S(2)}, u32[]{:S(2)}) %all-to-all-start) | async-done | bytes 4194336 | tf_op jit(solution)/shard_map/all_to_all | solution.py:261
  61.5 2.2 %shard_map.70.refs_7_.map_ref = bf16[4,4,512,256]{3,2,1,0:T(8,128)(2,1)S(1)} custom-call(bf16[4,4,512,256]{3,2,1,0:T(8,128)(2,1)} %bitcast.2.map_ref), custom_call_target="tpu_custom_call" | custom-call | bytes 8388608 | tf_op jit(solution)/shard_map/pallas_call | solution.py:280
  63.7 2.4 %collective-permute-done.4.refs_5_ = bf16[272,256]{1,0:T(8,128)(2,1)S(1)} collective-permute-done((bf16[272,256]{1,0:T(8,128)(2,1)S(1)}, bf16[272,256]{1,0:T(8,128)(2,1)S(1)}, u32[]{:S(2)}, u32[]{:S(2)}) %collective-permute-start.4) | collective-permute-done | bytes 139296 | tf_op jit(solution)/shard_map/ppermute | solution.py:42
  66.2 2.0 %collective-permute-done.5.refs_6_ = bf16[272,256]{1,0:T(8,128)(2,1)S(1)} collective-permute-done((bf16[272,256]{1,0:T(8,128)(2,1)S(1)}, bf16[272,256]{1,0:T(8,128)(2,1)S(1)}, u32[]{:S(2)}, u32[]{:S(2)}) %collective-permute-start.5) | collective-permute-done | bytes 139296 | tf_op jit(solution)/shard_map/ppermute | solution.py:42
  68.6 2.8 %shard_map.72.refs_0_ = bf16[4,256,128]{2,1,0:T(8,128)(2,1)S(1)} custom-call(f32[8,128]{1,0:T(8,128)S(1)} %get-tuple-element.35.scale_ref, bf16[4,4,512,256]{3,2,1,0:T(8,128)(2,1)S(1)} %shard_map.70.refs_7_.map_ref, bf16[4,256,512]{2,1,0:T(8,128)(2,1)S(1)} %get-tuple-element.41.prior_ref, bf16[4,256,128]{2,1,0:T(8,128)(2,1)S(1)} %get-tuple-element.42.obs_ref, ...), custom_call_target="tpu_custom_call" | custom-call | flops 2147483648 | bytes 8388608 | tf_op jit(solution)/shard_map/pallas_call | solution.py:302
  71.4 2.7 %collective-permute-start.6 = (bf16[4,256,128]{2,1,0:T(8,128)(2,1)S(1)}, bf16[4,256,128]{2,1,0:T(8,128)(2,1)S(1)}, u32[]{:S(2)}, u32[]{:S(2)}) collective-permute-start(bf16[4,256,128]{2,1,0:T(8,128)(2,1)S(1)} %shard_map.72.refs_0_), channel_id=1, source_target_pairs={{0,4},{4,0},{1,5},{5,1},{2,6},{6,2},{3,7},{7,3},{8,12},{12,8},{9,1... | collective-permute-start | bytes 786440 | tf_op jit(solution)/shard_map/ppermute | solution.py:42
  74.1 2.8 %shard_map.73.refs_2_.refs_0_ = bf16[4,256,128]{2,1,0:T(8,128)(2,1)S(1)} custom-call(f32[8,128]{1,0:T(8,128)S(1)} %get-tuple-element.35.scale_ref, bf16[4,4,512,256]{3,2,1,0:T(8,128)(2,1)S(1)} %shard_map.70.refs_7_.map_ref, bf16[4,256,512]{2,1,0:T(8,128)(2,1)S(1)} %get-tuple-element.41.prior_ref, bf16[4,256,128]{2,1,0:T(8,128)(2,1)S(1)} %get-tuple-element.44.obs_ref, ...), custom_call_target="tpu_custom_call" | custom-call | flops 2147483648 | bytes 8388608 | tf_op jit(solution)/shard_map/pallas_call | solution.py:302
  77.3 13.3 %collective-permute-done.6.refs_1_ = bf16[4,256,128]{2,1,0:T(8,128)(2,1)S(1)} collective-permute-done((bf16[4,256,128]{2,1,0:T(8,128)(2,1)S(1)}, bf16[4,256,128]{2,1,0:T(8,128)(2,1)S(1)}, u32[]{:S(2)}, u32[]{:S(2)}) %collective-permute-start.6) | collective-permute-done | bytes 262176 | tf_op jit(solution)/shard_map/ppermute | solution.py:42
  90.5 2.9 %shard_map.74 = (bf16[2,256,128]{2,1,0:T(8,128)(2,1)S(1)}, bf16[2,256,128]{2,1,0:T(8,128)(2,1)S(1)}, f32[2,256,128]{2,1,0:T(8,128)S(1)}, bf16[2,256,128]{2,1,0:T(8,128)(2,1)S(1)}) custom-call(f32[8,128]{1,0:T(8,128)S(1)} %get-tuple-element.35.scale_ref, bf16[4,4,512,256]{3,2,1,0:T(8,128)(2,1)S(1)} %shard_map.70.refs_7_.map_ref, ...), custom_call_target="tpu_custom_call" | custom-call | flops 2147483648 | bytes 8388608 | tf_op jit(solution)/shard_map/pallas_call | solution.py:302
  93.5 2.2 %collective-permute-start.10 = (bf16[2,256,128]{2,1,0:T(8,128)(2,1)S(1)}, bf16[2,256,128]{2,1,0:T(8,128)(2,1)S(1)}, u32[]{:S(2)}, u32[]{:S(2)}) collective-permute-start(bf16[2,256,128]{2,1,0:T(8,128)(2,1)S(1)} %get-tuple-element.47), channel_id=1, source_target_pairs={{0,12},{4,8},{8,4},{12,0},{16,28},{20,24},{24,20},{28,16},{1,13},{... | collective-permute-start | bytes 393224 | tf_op jit(solution)/shard_map/ppermute | solution.py:319
  96.5 2.9 %shard_map.75 = (bf16[2,256,128]{2,1,0:T(8,128)(2,1)S(1)}, bf16[2,256,128]{2,1,0:T(8,128)(2,1)S(1)}, f32[2,256,128]{2,1,0:T(8,128)S(1)}, bf16[2,256,128]{2,1,0:T(8,128)(2,1)S(1)}) custom-call(f32[8,128]{1,0:T(8,128)S(1)} %get-tuple-element.35.scale_ref, bf16[4,4,512,256]{3,2,1,0:T(8,128)(2,1)S(1)} %shard_map.70.refs_7_.map_ref, ...), custom_call_target="tpu_custom_call" | custom-call | flops 2147483648 | bytes 8388608 | tf_op jit(solution)/shard_map/pallas_call | solution.py:302
  99.5 2.2 %collective-permute-start.11 = (bf16[2,256,128]{2,1,0:T(8,128)(2,1)S(1)}, bf16[2,256,128]{2,1,0:T(8,128)(2,1)S(1)}, u32[]{:S(2)}, u32[]{:S(2)}) collective-permute-start(bf16[2,256,128]{2,1,0:T(8,128)(2,1)S(1)} %get-tuple-element.48), channel_id=1, source_target_pairs={{0,12},{4,8},{8,4},{12,0},{16,28},{20,24},{24,20},{28,16},{1,13},{... | collective-permute-start | bytes 393224 | tf_op jit(solution)/shard_map/ppermute | solution.py:319
  101.7 4.7 %collective-permute-done.7.refs_0_ = bf16[2,256,128]{2,1,0:T(8,128)(2,1)S(1)} collective-permute-done((bf16[2,256,128]{2,1,0:T(8,128)(2,1)S(1)}, bf16[2,256,128]{2,1,0:T(8,128)(2,1)S(1)}, u32[]{:S(2)}, u32[]{:S(2)}) %collective-permute-start.7) | collective-permute-done | bytes 131104 | tf_op jit(solution)/shard_map/ppermute | solution.py:319
  106.3 2.0 %collective-permute-done.10.refs_2_ = bf16[2,256,128]{2,1,0:T(8,128)(2,1)S(1)} collective-permute-done((bf16[2,256,128]{2,1,0:T(8,128)(2,1)S(1)}, bf16[2,256,128]{2,1,0:T(8,128)(2,1)S(1)}, u32[]{:S(2)}, u32[]{:S(2)}) %collective-permute-start.10) | collective-permute-done | bytes 131104 | tf_op jit(solution)/shard_map/ppermute | solution.py:319
  108.4 3.6 %collective-permute-done.9.refs_1_ = bf16[2,256,128]{2,1,0:T(8,128)(2,1)S(1)} collective-permute-done((bf16[2,256,128]{2,1,0:T(8,128)(2,1)S(1)}, bf16[2,256,128]{2,1,0:T(8,128)(2,1)S(1)}, u32[]{:S(2)}, u32[]{:S(2)}) %collective-permute-start.9) | collective-permute-done | bytes 131104 | tf_op jit(solution)/shard_map/ppermute | solution.py:319
  112.0 2.0 %collective-permute-done.11.refs_3_ = bf16[2,256,128]{2,1,0:T(8,128)(2,1)S(1)} collective-permute-done((bf16[2,256,128]{2,1,0:T(8,128)(2,1)S(1)}, bf16[2,256,128]{2,1,0:T(8,128)(2,1)S(1)}, u32[]{:S(2)}, u32[]{:S(2)}) %collective-permute-start.11) | collective-permute-done | bytes 131104 | tf_op jit(solution)/shard_map/ppermute | solution.py:319
  114.5 7.0 %collective-permute-start.21 = (bf16[2,256,256]{2,1,0:T(8,128)(2,1)S(1)}, bf16[2,256,256]{2,1,0:T(8,128)(2,1)S(1)}, u32[]{:S(2)}, u32[]{:S(2)}) collective-permute-start(bf16[2,256,256]{2,1,0:T(8,128)(2,1)S(1)} %get-tuple-element.54.refs_1_), channel_id=1, source_target_pairs={{0,19},{1,18},{2,17},{3,16},{8,27},{9,26},{10,25},{11,24},{16,3},{... | collective-permute-start | bytes 786440 | tf_op jit(solution)/shard_map/ppermute | solution.py:42
  121.5 2.1 %shard_map.77 = (bf16[256,256]{1,0:T(8,128)(2,1)S(1)}, bf16[256,256]{1,0:T(8,128)(2,1)S(1)}, bf16[256,256]{1,0:T(8,128)(2,1)S(1)}, bf16[256,256]{1,0:T(8,128)(2,1)S(1)}) custom-call(f32[8,128]{1,0:T(8,128)S(1)} %get-tuple-element.35.scale_ref, bf16[4,4,512,256]{3,2,1,0:T(8,128)(2,1)S(1)} %shard_map.70.refs_7_.map_ref, ...), custom_call_target="tpu_custom_call" | custom-call | flops 2147483648 | bytes 8388608 | tf_op jit(solution)/shard_map/pallas_call | solution.py:336
  124.4 2.2 %collective-permute-start.16 = (bf16[3,256,256]{2,1,0:T(8,128)(2,1)S(1)}, bf16[3,256,256]{2,1,0:T(8,128)(2,1)S(1)}, u32[]{:S(2)}, u32[]{:S(2)}) collective-permute-start(bf16[3,256,256]{2,1,0:T(8,128)(2,1)S(1)} %get-tuple-element.62), channel_id=1, source_target_pairs={{0,2},{1,3},{2,0},{3,1},{8,10},{9,11},{10,8},{11,9},{16,18},{17,19... | collective-permute-start | bytes 1179656 | tf_op jit(solution)/shard_map/ppermute | solution.py:42
  126.6 1.1 collective-permute-start.17
  129.5 4.4 %collective-permute-done.20.refs_2_ = bf16[2,256,256]{2,1,0:T(8,128)(2,1)S(1)} collective-permute-done((bf16[2,256,256]{2,1,0:T(8,128)(2,1)S(1)}, bf16[2,256,256]{2,1,0:T(8,128)(2,1)S(1)}, u32[]{:S(2)}, u32[]{:S(2)}) %collective-permute-start.20) | collective-permute-done | bytes 262176 | tf_op jit(solution)/shard_map/ppermute | solution.py:42
  133.9 1.0 collective-permute-start.18
  134.8 5.0 %collective-permute-done.19.refs_1_ = bf16[2,256,256]{2,1,0:T(8,128)(2,1)S(1)} collective-permute-done((bf16[2,256,256]{2,1,0:T(8,128)(2,1)S(1)}, bf16[2,256,256]{2,1,0:T(8,128)(2,1)S(1)}, u32[]{:S(2)}, u32[]{:S(2)}) %collective-permute-start.19) | collective-permute-done | bytes 262176 | tf_op jit(solution)/shard_map/ppermute | solution.py:42
  139.8 4.4 %collective-permute-done.18.refs_0_ = bf16[2,256,256]{2,1,0:T(8,128)(2,1)S(1)} collective-permute-done((bf16[2,256,256]{2,1,0:T(8,128)(2,1)S(1)}, bf16[2,256,256]{2,1,0:T(8,128)(2,1)S(1)}, u32[]{:S(2)}, u32[]{:S(2)}) %collective-permute-start.18) | collective-permute-done | bytes 262176 | tf_op jit(solution)/shard_map/ppermute | solution.py:42
  144.2 1.4 shard_map.79.refs_4_
  145.6 5.3 %collective-permute-done.15.refs_1_ = bf16[3,256,256]{2,1,0:T(8,128)(2,1)S(1)} collective-permute-done((bf16[3,256,256]{2,1,0:T(8,128)(2,1)S(1)}, bf16[3,256,256]{2,1,0:T(8,128)(2,1)S(1)}, u32[]{:S(2)}, u32[]{:S(2)}) %collective-permute-start.15) | collective-permute-done | bytes 393248 | tf_op jit(solution)/shard_map/ppermute | solution.py:42
  150.9 1.8 %shard_map.80 = (f32[16,2,256,128]{3,2,1,0:T(8,128)}, f32[4,512,128]{2,1,0:T(8,128)}) custom-call(bf16[3,256,256]{2,1,0:T(8,128)(2,1)S(1)} %get-tuple-element.60.refs_0_, bf16[3,256,256]{2,1,0:T(8,128)(2,1)S(1)} %collective-permute-done.15.refs_1_, bf16[3,256,256]{2,1,0:T(8,128)(2,1)S(1)} %collective-permute-done.16.refs_2_, ...), custom_call_target="tpu_custom_call", output_to_operand_aliasing={{0}: (4, {})} | custom-call | bytes 4194304 | tf_op jit(solution)/shard_map/pallas_call | solution.py:365
  (36 shorter events, 8.2 us)
Async XLA Ops:
  0.6 6.4 %copy-start.2 = (f32[256]{0:T(256)S(1)}, f32[256]{0:T(256)}, u32[]{:S(2)}) copy-start(f32[256]{0:T(256)} %param.7) | copy-start | bytes 3076
  0.6 60.9 %all-to-all-start = ((bf16[16,512,256]{2,1,0:T(8,128)(2,1)}), bf16[16,512,256]{2,1,0:T(8,128)(2,1)}, u32[]{:S(2)}, u32[]{:S(2)}) async-start(bf16[16,512,256]{2,1,0:T(8,128)(2,1)} %bitcast.5), calls=%async_computation | async-start | bytes 8388608 | tf_op jit(solution)/shard_map/all_to_all | solution.py:261
  7.0 3.2 %copy-start.3 = (f32[16]{0:T(128)S(1)}, f32[16]{0:T(128)}, u32[]{:S(2)}) copy-start(f32[16]{0:T(128)} %param.9) | copy-start | bytes 196
  7.0 2.2 %copy-start = (f32[16,2,256,128]{3,2,1,0:T(8,128)S(1)}, f32[16,2,256,128]{3,2,1,0:T(8,128)}, u32[]{:S(2)}) copy-start(f32[16,2,256,128]{3,2,1,0:T(8,128)} %obs_ref.1) | copy-start | bytes 12582916
  9.2 2.0 %copy-start.1 = (bf16[256,512]{1,0:T(8,128)(2,1)S(1)}, bf16[256,512]{1,0:T(8,128)(2,1)}, u32[]{:S(2)}) copy-start(bf16[256,512]{1,0:T(8,128)(2,1)} %own_ref.3) | copy-start | bytes 786436
  9.8 1.4 collective-permute-start
  11.9 56.4 %collective-permute-start.2 = (bf16[448,256]{1,0:T(8,128)(2,1)S(1)}, bf16[448,256]{1,0:T(8,128)(2,1)S(1)}, u32[]{:S(2)}, u32[]{:S(2)}) collective-permute-start(bf16[448,256]{1,0:T(8,128)(2,1)S(1)} %get-tuple-element.37), channel_id=1, source_target_pairs={{0,2},{1,3},{2,0},{3,1},{4,6},{5,7},{6,4},{7,5},{8,10},{9,11},{10,... | collective-permute-start | bytes 688136 | tf_op jit(solution)/shard_map/ppermute | solution.py:42
  13.8 52.3 %collective-permute-start.4 = (bf16[272,256]{1,0:T(8,128)(2,1)S(1)}, bf16[272,256]{1,0:T(8,128)(2,1)S(1)}, u32[]{:S(2)}, u32[]{:S(2)}) collective-permute-start(bf16[272,256]{1,0:T(8,128)(2,1)S(1)} %get-tuple-element.39), channel_id=1, source_target_pairs={{0,16},{8,24},{16,0},{24,8},{1,17},{9,25},{17,1},{25,9},{2,18},{10... | collective-permute-start | bytes 417800 | tf_op jit(solution)/shard_map/ppermute | solution.py:42
  15.3 52.9 %collective-permute-start.5 = (bf16[272,256]{1,0:T(8,128)(2,1)S(1)}, bf16[272,256]{1,0:T(8,128)(2,1)S(1)}, u32[]{:S(2)}, u32[]{:S(2)}) collective-permute-start(bf16[272,256]{1,0:T(8,128)(2,1)S(1)} %get-tuple-element.40), channel_id=1, source_target_pairs={{0,24},{8,16},{16,8},{24,0},{1,25},{9,17},{17,9},{25,1},{2,26},{10... | collective-permute-start | bytes 417800 | tf_op jit(solution)/shard_map/ppermute | solution.py:42
  15.3 53.0 %collective-permute-start.3 = (bf16[192,256]{1,0:T(8,128)(2,1)S(1)}, bf16[192,256]{1,0:T(8,128)(2,1)S(1)}, u32[]{:S(2)}, u32[]{:S(2)}) collective-permute-start(bf16[192,256]{1,0:T(8,128)(2,1)S(1)} %get-tuple-element.36), channel_id=1, source_target_pairs={{0,3},{1,2},{2,1},{3,0},{4,7},{5,6},{6,5},{7,4},{8,11},{9,10},{10,... | collective-permute-start | bytes 294920 | tf_op jit(solution)/shard_map/ppermute | solution.py:42
  16.7 51.5 %collective-permute-start.1 = (bf16[192,256]{1,0:T(8,128)(2,1)S(1)}, bf16[192,256]{1,0:T(8,128)(2,1)S(1)}, u32[]{:S(2)}, u32[]{:S(2)}) collective-permute-start(bf16[192,256]{1,0:T(8,128)(2,1)S(1)} %get-tuple-element.36), channel_id=1, source_target_pairs={{0,1},{1,0},{2,3},{3,2},{4,5},{5,4},{6,7},{7,6},{8,9},{9,8},{10,11... | collective-permute-start | bytes 294920 | tf_op jit(solution)/shard_map/ppermute | solution.py:42
  71.4 19.1 %collective-permute-start.6 = (bf16[4,256,128]{2,1,0:T(8,128)(2,1)S(1)}, bf16[4,256,128]{2,1,0:T(8,128)(2,1)S(1)}, u32[]{:S(2)}, u32[]{:S(2)}) collective-permute-start(bf16[4,256,128]{2,1,0:T(8,128)(2,1)S(1)} %shard_map.72.refs_0_), channel_id=1, source_target_pairs={{0,4},{4,0},{1,5},{5,1},{2,6},{6,2},{3,7},{7,3},{8,12},{12,8},{9,1... | collective-permute-start | bytes 786440 | tf_op jit(solution)/shard_map/ppermute | solution.py:42
  76.9 19.6 %collective-permute-start.8 = (bf16[4,256,128]{2,1,0:T(8,128)(2,1)S(1)}, bf16[4,256,128]{2,1,0:T(8,128)(2,1)S(1)}, u32[]{:S(2)}, u32[]{:S(2)}) collective-permute-start(bf16[4,256,128]{2,1,0:T(8,128)(2,1)S(1)} %shard_map.73.refs_2_.refs_0_), channel_id=1, source_target_pairs={{0,4},{4,0},{1,5},{5,1},{2,6},{6,2},{3,7},{7,3},{8,12},{12,8},{9,1... | collective-permute-start | bytes 786440 | tf_op jit(solution)/shard_map/ppermute | solution.py:42
  93.4 12.9 %collective-permute-start.7 = (bf16[2,256,128]{2,1,0:T(8,128)(2,1)S(1)}, bf16[2,256,128]{2,1,0:T(8,128)(2,1)S(1)}, u32[]{:S(2)}, u32[]{:S(2)}) collective-permute-start(bf16[2,256,128]{2,1,0:T(8,128)(2,1)S(1)} %get-tuple-element.45), channel_id=1, source_target_pairs={{0,4},{4,0},{8,12},{12,8},{16,20},{20,16},{24,28},{28,24},{1,5},{5... | collective-permute-start | bytes 393224 | tf_op jit(solution)/shard_map/ppermute | solution.py:319
  93.5 14.9 %collective-permute-start.10 = (bf16[2,256,128]{2,1,0:T(8,128)(2,1)S(1)}, bf16[2,256,128]{2,1,0:T(8,128)(2,1)S(1)}, u32[]{:S(2)}, u32[]{:S(2)}) collective-permute-start(bf16[2,256,128]{2,1,0:T(8,128)(2,1)S(1)} %get-tuple-element.47), channel_id=1, source_target_pairs={{0,12},{4,8},{8,4},{12,0},{16,28},{20,24},{24,20},{28,16},{1,13},{... | collective-permute-start | bytes 393224 | tf_op jit(solution)/shard_map/ppermute | solution.py:319
  95.7 12.7 %collective-permute-start.12 = (bf16[2,256,128]{2,1,0:T(8,128)(2,1)S(1)}, bf16[2,256,128]{2,1,0:T(8,128)(2,1)S(1)}, u32[]{:S(2)}, u32[]{:S(2)}) collective-permute-start(bf16[2,256,128]{2,1,0:T(8,128)(2,1)S(1)} %get-tuple-element.51), channel_id=1, source_target_pairs={{0,8},{8,0},{16,24},{24,16},{1,9},{9,1},{17,25},{25,17},{2,10},{10... | collective-permute-start | bytes 393224 | tf_op jit(solution)/shard_map/ppermute | solution.py:42
  99.4 12.6 %collective-permute-start.9 = (bf16[2,256,128]{2,1,0:T(8,128)(2,1)S(1)}, bf16[2,256,128]{2,1,0:T(8,128)(2,1)S(1)}, u32[]{:S(2)}, u32[]{:S(2)}) collective-permute-start(bf16[2,256,128]{2,1,0:T(8,128)(2,1)S(1)} %get-tuple-element.46), channel_id=1, source_target_pairs={{0,4},{4,0},{8,12},{12,8},{16,20},{20,16},{24,28},{28,24},{1,5},{5... | collective-permute-start | bytes 393224 | tf_op jit(solution)/shard_map/ppermute | solution.py:319
  99.5 14.5 %collective-permute-start.11 = (bf16[2,256,128]{2,1,0:T(8,128)(2,1)S(1)}, bf16[2,256,128]{2,1,0:T(8,128)(2,1)S(1)}, u32[]{:S(2)}, u32[]{:S(2)}) collective-permute-start(bf16[2,256,128]{2,1,0:T(8,128)(2,1)S(1)} %get-tuple-element.48), channel_id=1, source_target_pairs={{0,12},{4,8},{8,4},{12,0},{16,28},{20,24},{24,20},{28,16},{1,13},{... | collective-permute-start | bytes 393224 | tf_op jit(solution)/shard_map/ppermute | solution.py:319
  106.3 7.6 %collective-permute-start.13 = (bf16[2,256,128]{2,1,0:T(8,128)(2,1)S(1)}, bf16[2,256,128]{2,1,0:T(8,128)(2,1)S(1)}, u32[]{:S(2)}, u32[]{:S(2)}) collective-permute-start(bf16[2,256,128]{2,1,0:T(8,128)(2,1)S(1)} %get-tuple-element.52), channel_id=1, source_target_pairs={{0,8},{8,0},{16,24},{24,16},{1,9},{9,1},{17,25},{25,17},{2,10},{10... | collective-permute-start | bytes 393224 | tf_op jit(solution)/shard_map/ppermute | solution.py:42
  114.2 7.3 %collective-permute-start.14 = (bf16[2,256,256]{2,1,0:T(8,128)(2,1)S(1)}, bf16[2,256,256]{2,1,0:T(8,128)(2,1)S(1)}, u32[]{:S(2)}, u32[]{:S(2)}) collective-permute-start(bf16[2,256,256]{2,1,0:T(8,128)(2,1)S(1)} %get-tuple-element.55), channel_id=1, source_target_pairs={{0,8},{8,0},{16,24},{24,16},{1,9},{9,1},{17,25},{25,17},{2,10},{10... | collective-permute-start | bytes 786440 | tf_op jit(solution)/shard_map/ppermute | solution.py:42
  114.5 14.2 %collective-permute-start.21 = (bf16[2,256,256]{2,1,0:T(8,128)(2,1)S(1)}, bf16[2,256,256]{2,1,0:T(8,128)(2,1)S(1)}, u32[]{:S(2)}, u32[]{:S(2)}) collective-permute-start(bf16[2,256,256]{2,1,0:T(8,128)(2,1)S(1)} %get-tuple-element.54.refs_1_), channel_id=1, source_target_pairs={{0,19},{1,18},{2,17},{3,16},{8,27},{9,26},{10,25},{11,24},{16,3},{... | collective-permute-start | bytes 786440 | tf_op jit(solution)/shard_map/ppermute | solution.py:42
  121.5 12.3 %collective-permute-start.20 = (bf16[2,256,256]{2,1,0:T(8,128)(2,1)S(1)}, bf16[2,256,256]{2,1,0:T(8,128)(2,1)S(1)}, u32[]{:S(2)}, u32[]{:S(2)}) collective-permute-start(bf16[2,256,256]{2,1,0:T(8,128)(2,1)S(1)} %get-tuple-element.54.refs_1_), channel_id=1, source_target_pairs={{0,18},{1,19},{2,16},{3,17},{8,26},{9,27},{10,24},{11,25},{16,2},{... | collective-permute-start | bytes 786440 | tf_op jit(solution)/shard_map/ppermute | solution.py:42
  123.7 27.2 %collective-permute-start.15 = (bf16[3,256,256]{2,1,0:T(8,128)(2,1)S(1)}, bf16[3,256,256]{2,1,0:T(8,128)(2,1)S(1)}, u32[]{:S(2)}, u32[]{:S(2)}) collective-permute-start(bf16[3,256,256]{2,1,0:T(8,128)(2,1)S(1)} %get-tuple-element.61), channel_id=1, source_target_pairs={{0,1},{1,0},{2,3},{3,2},{8,9},{9,8},{10,11},{11,10},{16,17},{17,16... | collective-permute-start | bytes 1179656 | tf_op jit(solution)/shard_map/ppermute | solution.py:42
  124.4 26.4 %collective-permute-start.16 = (bf16[3,256,256]{2,1,0:T(8,128)(2,1)S(1)}, bf16[3,256,256]{2,1,0:T(8,128)(2,1)S(1)}, u32[]{:S(2)}, u32[]{:S(2)}) collective-permute-start(bf16[3,256,256]{2,1,0:T(8,128)(2,1)S(1)} %get-tuple-element.62), channel_id=1, source_target_pairs={{0,2},{1,3},{2,0},{3,1},{8,10},{9,11},{10,8},{11,9},{16,18},{17,19... | collective-permute-start | bytes 1179656 | tf_op jit(solution)/shard_map/ppermute | solution.py:42
  126.6 24.3 %collective-permute-start.17 = (bf16[3,256,256]{2,1,0:T(8,128)(2,1)S(1)}, bf16[3,256,256]{2,1,0:T(8,128)(2,1)S(1)}, u32[]{:S(2)}, u32[]{:S(2)}) collective-permute-start(bf16[3,256,256]{2,1,0:T(8,128)(2,1)S(1)} %get-tuple-element.63), channel_id=1, source_target_pairs={{0,3},{1,2},{2,1},{3,0},{8,11},{9,10},{10,9},{11,8},{16,19},{17,18... | collective-permute-start | bytes 1179656 | tf_op jit(solution)/shard_map/ppermute | solution.py:42
  128.7 11.1 %collective-permute-start.19 = (bf16[2,256,256]{2,1,0:T(8,128)(2,1)S(1)}, bf16[2,256,256]{2,1,0:T(8,128)(2,1)S(1)}, u32[]{:S(2)}, u32[]{:S(2)}) collective-permute-start(bf16[2,256,256]{2,1,0:T(8,128)(2,1)S(1)} %get-tuple-element.54.refs_1_), channel_id=1, source_target_pairs={{0,17},{1,16},{2,19},{3,18},{8,25},{9,24},{10,27},{11,26},{16,1},{... | collective-permute-start | bytes 786440 | tf_op jit(solution)/shard_map/ppermute | solution.py:42
  133.9 10.4 %collective-permute-start.18 = (bf16[2,256,256]{2,1,0:T(8,128)(2,1)S(1)}, bf16[2,256,256]{2,1,0:T(8,128)(2,1)S(1)}, u32[]{:S(2)}, u32[]{:S(2)}) collective-permute-start(bf16[2,256,256]{2,1,0:T(8,128)(2,1)S(1)} %get-tuple-element.54.refs_1_), channel_id=1, source_target_pairs={{0,16},{1,17},{2,18},{3,19},{8,24},{9,25},{10,26},{11,27},{16,0},{... | collective-permute-start | bytes 786440 | tf_op jit(solution)/shard_map/ppermute | solution.py:42

commit v14 on v13

--- a/solution.py
+++ b/solution.py
@@ -226,25 +226,25 @@
         out[...] = held_ref[my_place()[1] ^ d]
 
 
-def end_kernel(e, quads, follows, *refs):
-    came, refs = refs[:quads], refs[quads + follows:]
+def end_kernel(e, quads, members, follows, *refs):
+    came, refs = refs[:len(members)], refs[len(members) + follows:]
     count = 1 + (e == 0)
     outs, (dual_ref, sems, *post) = refs[:count], refs[count:]
     pair, quad, _ = my_place()
     sends = []
-    for d in range(quads):
+    for i, d in enumerate(members):
         for core in range(CORES):
             freq = (CORES * (pair ^ e) + core) * quads + (quad ^ d)
             for part in range(2):
-                dual_ref[d, core, part] = came[d][core, :, part * LANES:(part + 1) * LANES].astype(f32)
-            sends.append(pltpu.make_async_copy(dual_ref.at[d, core], outs[0].at[freq], sems.at[d, core]))
+                dual_ref[i, core, part] = came[i][core, :, part * LANES:(part + 1) * LANES].astype(f32)
+            sends.append(pltpu.make_async_copy(dual_ref.at[i, core], outs[0].at[freq], sems.at[i, core]))
             sends[-1].start()
         if e == 0:
             post_ref = post[0]
             cells = post_ref.shape[1] // 2
-            post_ref[d, pl.ds(0, cells, stride=2), :] = came[d][CORES, :, :LANES].astype(f32)
-            post_ref[d, pl.ds(1, cells, stride=2), :] = came[d][CORES, :, LANES:].astype(f32)
-            sends.append(pltpu.make_async_copy(post_ref.at[d], outs[1].at[quad ^ d], sems.at[d, CORES]))
+            post_ref[i, pl.ds(0, cells, stride=2), :] = came[i][CORES, :, :LANES].astype(f32)
+            post_ref[i, pl.ds(1, cells, stride=2), :] = came[i][CORES, :, LANES:].astype(f32)
+            sends.append(pltpu.make_async_copy(post_ref.at[i], outs[1].at[quad ^ d], sems.at[i, CORES]))
             sends[-1].start()
     for copy in sends:
         copy.wait()
@@ -352,28 +352,29 @@
         for d in reversed(range(quads)):
             out = near_ones[d] if e == 0 else finals[e]
             duals[e * quads + d] = swap(out, both, CORES * e * quads + d) if e + d else out
-    dual, posterior = [], []
-    for e in reversed(range(pairs)):
+    far = [(e, list(range(quads))) for e in reversed(range(1, pairs))]
+    done = []
+    for e, members in far + [(0, list(range(0, quads, 2))), (0, list(range(1, quads, 2)))]:
+        count = len(members)
         out = [shape((frequencies, halves, sensors, LANES), f32)]
         scratch = [
-            pltpu.VMEM((quads, CORES, halves, sensors, LANES), f32),
-            pltpu.SemaphoreType.DMA((quads, CORES + 1)),
+            pltpu.VMEM((count, CORES, halves, sensors, LANES), f32),
+            pltpu.SemaphoreType.DMA((count, CORES + 1)),
         ]
         if e == 0:
             out.append(shape((quads, cells * 2, LANES), f32))
-            scratch.append(pltpu.VMEM((quads, cells * 2, LANES), f32))
-        *dual, last = call(
-            functools.partial(end_kernel, e, quads, len(dual)),
-            [VMEM] * quads + [ANY] * len(dual),
+            scratch.append(pltpu.VMEM((count, cells * 2, LANES), f32))
+        done = call(
+            functools.partial(end_kernel, e, quads, members, len(done)),
+            [VMEM] * count + [ANY] * len(done),
             out,
             scratch,
             [ANY] * len(out),
             moved=4 * 2**20,
-            aliases={quads: 0} if dual else None,
-        )(*[duals[e * quads + d] for d in range(quads)], *dual)
-        if e:
-            dual = [last]
-    return dual[0], last.reshape(quads, cells, 2, LANES)
+            aliases={count + i: i for i in range(len(done))},
+        )(*[duals[e * quads + d] for d in members], *done)
+    dual, posterior = done
+    return dual, posterior.reshape(quads, cells, 2, LANES)
 
 
 def solution(mesh):

time: 153 us -> 152 us (level)
    pallas_call x2 -> x3, Pallas kernels: 3.2 us -> 3.84 us  [on_device(): call(functools.partial(end_kernel, e, quads, members, len(done)), [VMEM]...]
  transfers between devices with their start and end apart: 23 -> 23, of which waited for: 14 -> 14; matrix products, arithmetic and copies ran while one was open for 0% -> 0% of each run, Pallas kernels for 10% -> 11%
where the time goes in v14:
time: 152 us
  waiting for transfers between devices  93.5 us (62%)
  starting transfers between devices  33.9 us (22%)
  Pallas kernels  21.2 us (14%)
  local copies, waits for them, and re-layouts  2.78 us (2%)
    all_to_all x1, waiting for transfers between devices, on_device(): lax.all_to_all(forward_map.reshape(frequencies, halves * sensors, cells),...  44.2 us
    ppermute x18, waiting for transfers between devices, swap(): return lax.ppermute(x, axes, [(i, i ^ distance) for i in range(count)])  37 us
    ppermute x18, starting transfers between devices, swap(): return lax.ppermute(x, axes, [(i, i ^ distance) for i in range(count)])  22.9 us
    ppermute x4, waiting for transfers between devices, to_other_sides(): lax.ppermute(x, ('sensor', 'side'), [(i, i ^ 1 + CORES * cross) for i in...  12.4 us
    pallas_call x4, Pallas kernels, step(): call(functools.partial(step_kernel, stage, len(preds), len(after)), [VMEM...  11.1 us
    all_to_all x1, starting transfers between devices, on_device(): lax.all_to_all(forward_map.reshape(frequencies, halves * sensors, cells),...  6.35 us
    ppermute x4, starting transfers between devices, to_other_sides(): lax.ppermute(x, ('sensor', 'side'), [(i, i ^ 1 + CORES * cross) for i in...  4.62 us
    pallas_call x3, Pallas kernels, on_device(): call(functools.partial(end_kernel, e, quads, members, len(done)), [VMEM]...  3.84 us
  transfers between devices with their start and end apart: 23, of which 14 were waited for; matrix products, arithmetic and copies ran while one was open for 0% of the time, Pallas kernels for 11%

profile of v14, /device:TPU:0, one launch (start us, length us, event | category | flops | bytes accessed | tf_op | source)
XLA Modules:
  0.0 152.2 jit_solution(15431338396594174099)
XLA Ops:
  0.6 6.4 %all-to-all-start = ((bf16[16,512,256]{2,1,0:T(8,128)(2,1)}), bf16[16,512,256]{2,1,0:T(8,128)(2,1)}, u32[]{:S(2)}, u32[]{:S(2)}) async-start(bf16[16,512,256]{2,1,0:T(8,128)(2,1)} %bitcast.5), calls=%async_computation | async-start | bytes 8388608 | tf_op jit(solution)/shard_map/all_to_all | solution.py:261
  7.0 2.2 %copy-done = f32[16,2,256,128]{3,2,1,0:T(8,128)S(1)} copy-done((f32[16,2,256,128]{3,2,1,0:T(8,128)S(1)}, f32[16,2,256,128]{3,2,1,0:T(8,128)}, u32[]{:S(2)}) %copy-start) | copy-done | bytes 4194328
  11.9 1.9 %collective-permute-start.2 = (bf16[448,256]{1,0:T(8,128)(2,1)S(1)}, bf16[448,256]{1,0:T(8,128)(2,1)S(1)}, u32[]{:S(2)}, u32[]{:S(2)}) collective-permute-start(bf16[448,256]{1,0:T(8,128)(2,1)S(1)} %get-tuple-element.39), channel_id=1, source_target_pairs={{0,2},{1,3},{2,0},{3,1},{4,6},{5,7},{6,4},{7,5},{8,10},{9,11},{10,... | collective-permute-start | bytes 688136 | tf_op jit(solution)/shard_map/ppermute | solution.py:42
  13.8 1.5 collective-permute-start.4
  15.3 1.5 collective-permute-start.3
  17.3 44.2 %all-to-all-done = bf16[16,512,256]{2,1,0:T(8,128)(2,1)} async-done(((bf16[16,512,256]{2,1,0:T(8,128)(2,1)}), bf16[16,512,256]{2,1,0:T(8,128)(2,1)}, u32[]{:S(2)}, u32[]{:S(2)}) %all-to-all-start) | async-done | bytes 4194336 | tf_op jit(solution)/shard_map/all_to_all | solution.py:261
  61.5 2.2 %shard_map.70.refs_7_.map_ref = bf16[4,4,512,256]{3,2,1,0:T(8,128)(2,1)S(1)} custom-call(bf16[4,4,512,256]{3,2,1,0:T(8,128)(2,1)} %bitcast.2.map_ref), custom_call_target="tpu_custom_call" | custom-call | bytes 8388608 | tf_op jit(solution)/shard_map/pallas_call | solution.py:280
  63.7 2.4 %collective-permute-done.4.refs_5_ = bf16[272,256]{1,0:T(8,128)(2,1)S(1)} collective-permute-done((bf16[272,256]{1,0:T(8,128)(2,1)S(1)}, bf16[272,256]{1,0:T(8,128)(2,1)S(1)}, u32[]{:S(2)}, u32[]{:S(2)}) %collective-permute-start.4) | collective-permute-done | bytes 139296 | tf_op jit(solution)/shard_map/ppermute | solution.py:42
  66.2 2.0 %collective-permute-done.5.refs_6_ = bf16[272,256]{1,0:T(8,128)(2,1)S(1)} collective-permute-done((bf16[272,256]{1,0:T(8,128)(2,1)S(1)}, bf16[272,256]{1,0:T(8,128)(2,1)S(1)}, u32[]{:S(2)}, u32[]{:S(2)}) %collective-permute-start.5) | collective-permute-done | bytes 139296 | tf_op jit(solution)/shard_map/ppermute | solution.py:42
  68.6 2.7 %shard_map.72.refs_0_ = bf16[4,256,128]{2,1,0:T(8,128)(2,1)S(1)} custom-call(f32[8,128]{1,0:T(8,128)S(1)} %get-tuple-element.37.scale_ref, bf16[4,4,512,256]{3,2,1,0:T(8,128)(2,1)S(1)} %shard_map.70.refs_7_.map_ref, bf16[4,256,512]{2,1,0:T(8,128)(2,1)S(1)} %get-tuple-element.43.prior_ref, bf16[4,256,128]{2,1,0:T(8,128)(2,1)S(1)} %get-tuple-element.44.obs_ref, ...), custom_call_target="tpu_custom_call" | custom-call | flops 2147483648 | bytes 8388608 | tf_op jit(solution)/shard_map/pallas_call | solution.py:302
  71.4 2.7 %collective-permute-start.6 = (bf16[4,256,128]{2,1,0:T(8,128)(2,1)S(1)}, bf16[4,256,128]{2,1,0:T(8,128)(2,1)S(1)}, u32[]{:S(2)}, u32[]{:S(2)}) collective-permute-start(bf16[4,256,128]{2,1,0:T(8,128)(2,1)S(1)} %shard_map.72.refs_0_), channel_id=1, source_target_pairs={{0,4},{4,0},{1,5},{5,1},{2,6},{6,2},{3,7},{7,3},{8,12},{12,8},{9,1... | collective-permute-start | bytes 786440 | tf_op jit(solution)/shard_map/ppermute | solution.py:42
  74.0 2.8 %shard_map.73.refs_2_.refs_0_ = bf16[4,256,128]{2,1,0:T(8,128)(2,1)S(1)} custom-call(f32[8,128]{1,0:T(8,128)S(1)} %get-tuple-element.37.scale_ref, bf16[4,4,512,256]{3,2,1,0:T(8,128)(2,1)S(1)} %shard_map.70.refs_7_.map_ref, bf16[4,256,512]{2,1,0:T(8,128)(2,1)S(1)} %get-tuple-element.43.prior_ref, bf16[4,256,128]{2,1,0:T(8,128)(2,1)S(1)} %get-tuple-element.46.obs_ref, ...), custom_call_target="tpu_custom_call" | custom-call | flops 2147483648 | bytes 8388608 | tf_op jit(solution)/shard_map/pallas_call | solution.py:302
  77.2 13.3 %collective-permute-done.6.refs_1_ = bf16[4,256,128]{2,1,0:T(8,128)(2,1)S(1)} collective-permute-done((bf16[4,256,128]{2,1,0:T(8,128)(2,1)S(1)}, bf16[4,256,128]{2,1,0:T(8,128)(2,1)S(1)}, u32[]{:S(2)}, u32[]{:S(2)}) %collective-permute-start.6) | collective-permute-done | bytes 262176 | tf_op jit(solution)/shard_map/ppermute | solution.py:42
  90.5 2.8 %shard_map.74 = (bf16[2,256,128]{2,1,0:T(8,128)(2,1)S(1)}, bf16[2,256,128]{2,1,0:T(8,128)(2,1)S(1)}, f32[2,256,128]{2,1,0:T(8,128)S(1)}, bf16[2,256,128]{2,1,0:T(8,128)(2,1)S(1)}) custom-call(f32[8,128]{1,0:T(8,128)S(1)} %get-tuple-element.37.scale_ref, bf16[4,4,512,256]{3,2,1,0:T(8,128)(2,1)S(1)} %shard_map.70.refs_7_.map_ref, ...), custom_call_target="tpu_custom_call" | custom-call | flops 2147483648 | bytes 8388608 | tf_op jit(solution)/shard_map/pallas_call | solution.py:302
  93.4 2.2 %collective-permute-start.10 = (bf16[2,256,128]{2,1,0:T(8,128)(2,1)S(1)}, bf16[2,256,128]{2,1,0:T(8,128)(2,1)S(1)}, u32[]{:S(2)}, u32[]{:S(2)}) collective-permute-start(bf16[2,256,128]{2,1,0:T(8,128)(2,1)S(1)} %get-tuple-element.49), channel_id=1, source_target_pairs={{0,12},{4,8},{8,4},{12,0},{16,28},{20,24},{24,20},{28,16},{1,13},{... | collective-permute-start | bytes 393224 | tf_op jit(solution)/shard_map/ppermute | solution.py:319
  96.4 2.8 %shard_map.75 = (bf16[2,256,128]{2,1,0:T(8,128)(2,1)S(1)}, bf16[2,256,128]{2,1,0:T(8,128)(2,1)S(1)}, f32[2,256,128]{2,1,0:T(8,128)S(1)}, bf16[2,256,128]{2,1,0:T(8,128)(2,1)S(1)}) custom-call(f32[8,128]{1,0:T(8,128)S(1)} %get-tuple-element.37.scale_ref, bf16[4,4,512,256]{3,2,1,0:T(8,128)(2,1)S(1)} %shard_map.70.refs_7_.map_ref, ...), custom_call_target="tpu_custom_call" | custom-call | flops 2147483648 | bytes 8388608 | tf_op jit(solution)/shard_map/pallas_call | solution.py:302
  99.4 2.2 %collective-permute-start.11 = (bf16[2,256,128]{2,1,0:T(8,128)(2,1)S(1)}, bf16[2,256,128]{2,1,0:T(8,128)(2,1)S(1)}, u32[]{:S(2)}, u32[]{:S(2)}) collective-permute-start(bf16[2,256,128]{2,1,0:T(8,128)(2,1)S(1)} %get-tuple-element.50), channel_id=1, source_target_pairs={{0,12},{4,8},{8,4},{12,0},{16,28},{20,24},{24,20},{28,16},{1,13},{... | collective-permute-start | bytes 393224 | tf_op jit(solution)/shard_map/ppermute | solution.py:319
  101.5 4.7 %collective-permute-done.7.refs_0_ = bf16[2,256,128]{2,1,0:T(8,128)(2,1)S(1)} collective-permute-done((bf16[2,256,128]{2,1,0:T(8,128)(2,1)S(1)}, bf16[2,256,128]{2,1,0:T(8,128)(2,1)S(1)}, u32[]{:S(2)}, u32[]{:S(2)}) %collective-permute-start.7) | collective-permute-done | bytes 131104 | tf_op jit(solution)/shard_map/ppermute | solution.py:319
  106.2 2.1 %collective-permute-done.10.refs_2_ = bf16[2,256,128]{2,1,0:T(8,128)(2,1)S(1)} collective-permute-done((bf16[2,256,128]{2,1,0:T(8,128)(2,1)S(1)}, bf16[2,256,128]{2,1,0:T(8,128)(2,1)S(1)}, u32[]{:S(2)}, u32[]{:S(2)}) %collective-permute-start.10) | collective-permute-done | bytes 131104 | tf_op jit(solution)/shard_map/ppermute | solution.py:319
  108.3 3.6 %collective-permute-done.9.refs_1_ = bf16[2,256,128]{2,1,0:T(8,128)(2,1)S(1)} collective-permute-done((bf16[2,256,128]{2,1,0:T(8,128)(2,1)S(1)}, bf16[2,256,128]{2,1,0:T(8,128)(2,1)S(1)}, u32[]{:S(2)}, u32[]{:S(2)}) %collective-permute-start.9) | collective-permute-done | bytes 131104 | tf_op jit(solution)/shard_map/ppermute | solution.py:319
  111.9 2.1 %collective-permute-done.11.refs_3_ = bf16[2,256,128]{2,1,0:T(8,128)(2,1)S(1)} collective-permute-done((bf16[2,256,128]{2,1,0:T(8,128)(2,1)S(1)}, bf16[2,256,128]{2,1,0:T(8,128)(2,1)S(1)}, u32[]{:S(2)}, u32[]{:S(2)}) %collective-permute-start.11) | collective-permute-done | bytes 131104 | tf_op jit(solution)/shard_map/ppermute | solution.py:319
  114.4 7.0 %collective-permute-start.21 = (bf16[2,256,256]{2,1,0:T(8,128)(2,1)S(1)}, bf16[2,256,256]{2,1,0:T(8,128)(2,1)S(1)}, u32[]{:S(2)}, u32[]{:S(2)}) collective-permute-start(bf16[2,256,256]{2,1,0:T(8,128)(2,1)S(1)} %get-tuple-element.56.refs_1_), channel_id=1, source_target_pairs={{0,19},{1,18},{2,17},{3,16},{8,27},{9,26},{10,25},{11,24},{16,3},{... | collective-permute-start | bytes 786440 | tf_op jit(solution)/shard_map/ppermute | solution.py:42
  121.5 2.1 %shard_map.77 = (bf16[256,256]{1,0:T(8,128)(2,1)S(1)}, bf16[256,256]{1,0:T(8,128)(2,1)S(1)}, bf16[256,256]{1,0:T(8,128)(2,1)S(1)}, bf16[256,256]{1,0:T(8,128)(2,1)S(1)}) custom-call(f32[8,128]{1,0:T(8,128)S(1)} %get-tuple-element.37.scale_ref, bf16[4,4,512,256]{3,2,1,0:T(8,128)(2,1)S(1)} %shard_map.70.refs_7_.map_ref, ...), custom_call_target="tpu_custom_call" | custom-call | flops 2147483648 | bytes 8388608 | tf_op jit(solution)/shard_map/pallas_call | solution.py:336
  123.7 2.5 %collective-permute-start.17 = (bf16[3,256,256]{2,1,0:T(8,128)(2,1)S(1)}, bf16[3,256,256]{2,1,0:T(8,128)(2,1)S(1)}, u32[]{:S(2)}, u32[]{:S(2)}) collective-permute-start(bf16[3,256,256]{2,1,0:T(8,128)(2,1)S(1)} %get-tuple-element.65), channel_id=1, source_target_pairs={{0,2},{1,3},{2,0},{3,1},{8,10},{9,11},{10,8},{11,9},{16,18},{17,19... | collective-permute-start | bytes 1179656 | tf_op jit(solution)/shard_map/ppermute | solution.py:42
  126.6 1.2 collective-permute-start.16
  129.5 4.3 %collective-permute-done.20.refs_2_ = bf16[2,256,256]{2,1,0:T(8,128)(2,1)S(1)} collective-permute-done((bf16[2,256,256]{2,1,0:T(8,128)(2,1)S(1)}, bf16[2,256,256]{2,1,0:T(8,128)(2,1)S(1)}, u32[]{:S(2)}, u32[]{:S(2)}) %collective-permute-start.20) | collective-permute-done | bytes 262176 | tf_op jit(solution)/shard_map/ppermute | solution.py:42
  134.8 4.9 %collective-permute-done.19.refs_1_ = bf16[2,256,256]{2,1,0:T(8,128)(2,1)S(1)} collective-permute-done((bf16[2,256,256]{2,1,0:T(8,128)(2,1)S(1)}, bf16[2,256,256]{2,1,0:T(8,128)(2,1)S(1)}, u32[]{:S(2)}, u32[]{:S(2)}) %collective-permute-start.19) | collective-permute-done | bytes 262176 | tf_op jit(solution)/shard_map/ppermute | solution.py:42
  139.7 4.4 %collective-permute-done.18.refs_0_ = bf16[2,256,256]{2,1,0:T(8,128)(2,1)S(1)} collective-permute-done((bf16[2,256,256]{2,1,0:T(8,128)(2,1)S(1)}, bf16[2,256,256]{2,1,0:T(8,128)(2,1)S(1)}, u32[]{:S(2)}, u32[]{:S(2)}) %collective-permute-start.18) | collective-permute-done | bytes 262176 | tf_op jit(solution)/shard_map/ppermute | solution.py:42
  144.2 1.4 shard_map.79.refs_2_
  145.6 1.2 shard_map.80
  146.8 4.2 %collective-permute-done.15.refs_0_ = bf16[3,256,256]{2,1,0:T(8,128)(2,1)S(1)} collective-permute-done((bf16[3,256,256]{2,1,0:T(8,128)(2,1)S(1)}, bf16[3,256,256]{2,1,0:T(8,128)(2,1)S(1)}, u32[]{:S(2)}, u32[]{:S(2)}) %collective-permute-start.15) | collective-permute-done | bytes 393248 | tf_op jit(solution)/shard_map/ppermute | solution.py:42
  151.0 1.2 shard_map.81
  (37 shorter events, 8.8 us)
Async XLA Ops:
  0.6 6.4 %copy-start.2 = (f32[256]{0:T(256)S(1)}, f32[256]{0:T(256)}, u32[]{:S(2)}) copy-start(f32[256]{0:T(256)} %param.7) | copy-start | bytes 3076
  0.6 60.9 %all-to-all-start = ((bf16[16,512,256]{2,1,0:T(8,128)(2,1)}), bf16[16,512,256]{2,1,0:T(8,128)(2,1)}, u32[]{:S(2)}, u32[]{:S(2)}) async-start(bf16[16,512,256]{2,1,0:T(8,128)(2,1)} %bitcast.5), calls=%async_computation | async-start | bytes 8388608 | tf_op jit(solution)/shard_map/all_to_all | solution.py:261
  7.0 3.2 %copy-start.3 = (f32[16]{0:T(128)S(1)}, f32[16]{0:T(128)}, u32[]{:S(2)}) copy-start(f32[16]{0:T(128)} %param.9) | copy-start | bytes 196
  7.0 2.2 %copy-start = (f32[16,2,256,128]{3,2,1,0:T(8,128)S(1)}, f32[16,2,256,128]{3,2,1,0:T(8,128)}, u32[]{:S(2)}) copy-start(f32[16,2,256,128]{3,2,1,0:T(8,128)} %obs_ref.1) | copy-start | bytes 12582916
  9.2 2.0 %copy-start.1 = (bf16[256,512]{1,0:T(8,128)(2,1)S(1)}, bf16[256,512]{1,0:T(8,128)(2,1)}, u32[]{:S(2)}) copy-start(bf16[256,512]{1,0:T(8,128)(2,1)} %own_ref.3) | copy-start | bytes 786436
  9.8 1.4 collective-permute-start
  11.9 56.4 %collective-permute-start.2 = (bf16[448,256]{1,0:T(8,128)(2,1)S(1)}, bf16[448,256]{1,0:T(8,128)(2,1)S(1)}, u32[]{:S(2)}, u32[]{:S(2)}) collective-permute-start(bf16[448,256]{1,0:T(8,128)(2,1)S(1)} %get-tuple-element.39), channel_id=1, source_target_pairs={{0,2},{1,3},{2,0},{3,1},{4,6},{5,7},{6,4},{7,5},{8,10},{9,11},{10,... | collective-permute-start | bytes 688136 | tf_op jit(solution)/shard_map/ppermute | solution.py:42
  13.8 52.3 %collective-permute-start.4 = (bf16[272,256]{1,0:T(8,128)(2,1)S(1)}, bf16[272,256]{1,0:T(8,128)(2,1)S(1)}, u32[]{:S(2)}, u32[]{:S(2)}) collective-permute-start(bf16[272,256]{1,0:T(8,128)(2,1)S(1)} %get-tuple-element.41), channel_id=1, source_target_pairs={{0,16},{8,24},{16,0},{24,8},{1,17},{9,25},{17,1},{25,9},{2,18},{10... | collective-permute-start | bytes 417800 | tf_op jit(solution)/shard_map/ppermute | solution.py:42
  15.3 52.9 %collective-permute-start.5 = (bf16[272,256]{1,0:T(8,128)(2,1)S(1)}, bf16[272,256]{1,0:T(8,128)(2,1)S(1)}, u32[]{:S(2)}, u32[]{:S(2)}) collective-permute-start(bf16[272,256]{1,0:T(8,128)(2,1)S(1)} %get-tuple-element.42), channel_id=1, source_target_pairs={{0,24},{8,16},{16,8},{24,0},{1,25},{9,17},{17,9},{25,1},{2,26},{10... | collective-permute-start | bytes 417800 | tf_op jit(solution)/shard_map/ppermute | solution.py:42
  15.3 53.0 %collective-permute-start.3 = (bf16[192,256]{1,0:T(8,128)(2,1)S(1)}, bf16[192,256]{1,0:T(8,128)(2,1)S(1)}, u32[]{:S(2)}, u32[]{:S(2)}) collective-permute-start(bf16[192,256]{1,0:T(8,128)(2,1)S(1)} %get-tuple-element.38), channel_id=1, source_target_pairs={{0,3},{1,2},{2,1},{3,0},{4,7},{5,6},{6,5},{7,4},{8,11},{9,10},{10,... | collective-permute-start | bytes 294920 | tf_op jit(solution)/shard_map/ppermute | solution.py:42
  16.7 51.5 %collective-permute-start.1 = (bf16[192,256]{1,0:T(8,128)(2,1)S(1)}, bf16[192,256]{1,0:T(8,128)(2,1)S(1)}, u32[]{:S(2)}, u32[]{:S(2)}) collective-permute-start(bf16[192,256]{1,0:T(8,128)(2,1)S(1)} %get-tuple-element.38), channel_id=1, source_target_pairs={{0,1},{1,0},{2,3},{3,2},{4,5},{5,4},{6,7},{7,6},{8,9},{9,8},{10,11... | collective-permute-start | bytes 294920 | tf_op jit(solution)/shard_map/ppermute | solution.py:42
  71.4 19.1 %collective-permute-start.6 = (bf16[4,256,128]{2,1,0:T(8,128)(2,1)S(1)}, bf16[4,256,128]{2,1,0:T(8,128)(2,1)S(1)}, u32[]{:S(2)}, u32[]{:S(2)}) collective-permute-start(bf16[4,256,128]{2,1,0:T(8,128)(2,1)S(1)} %shard_map.72.refs_0_), channel_id=1, source_target_pairs={{0,4},{4,0},{1,5},{5,1},{2,6},{6,2},{3,7},{7,3},{8,12},{12,8},{9,1... | collective-permute-start | bytes 786440 | tf_op jit(solution)/shard_map/ppermute | solution.py:42
  76.8 19.6 %collective-permute-start.8 = (bf16[4,256,128]{2,1,0:T(8,128)(2,1)S(1)}, bf16[4,256,128]{2,1,0:T(8,128)(2,1)S(1)}, u32[]{:S(2)}, u32[]{:S(2)}) collective-permute-start(bf16[4,256,128]{2,1,0:T(8,128)(2,1)S(1)} %shard_map.73.refs_2_.refs_0_), channel_id=1, source_target_pairs={{0,4},{4,0},{1,5},{5,1},{2,6},{6,2},{3,7},{7,3},{8,12},{12,8},{9,1... | collective-permute-start | bytes 786440 | tf_op jit(solution)/shard_map/ppermute | solution.py:42
  93.3 12.9 %collective-permute-start.7 = (bf16[2,256,128]{2,1,0:T(8,128)(2,1)S(1)}, bf16[2,256,128]{2,1,0:T(8,128)(2,1)S(1)}, u32[]{:S(2)}, u32[]{:S(2)}) collective-permute-start(bf16[2,256,128]{2,1,0:T(8,128)(2,1)S(1)} %get-tuple-element.47), channel_id=1, source_target_pairs={{0,4},{4,0},{8,12},{12,8},{16,20},{20,16},{24,28},{28,24},{1,5},{5... | collective-permute-start | bytes 393224 | tf_op jit(solution)/shard_map/ppermute | solution.py:319
  93.4 14.9 %collective-permute-start.10 = (bf16[2,256,128]{2,1,0:T(8,128)(2,1)S(1)}, bf16[2,256,128]{2,1,0:T(8,128)(2,1)S(1)}, u32[]{:S(2)}, u32[]{:S(2)}) collective-permute-start(bf16[2,256,128]{2,1,0:T(8,128)(2,1)S(1)} %get-tuple-element.49), channel_id=1, source_target_pairs={{0,12},{4,8},{8,4},{12,0},{16,28},{20,24},{24,20},{28,16},{1,13},{... | collective-permute-start | bytes 393224 | tf_op jit(solution)/shard_map/ppermute | solution.py:319
  95.6 12.7 %collective-permute-start.12 = (bf16[2,256,128]{2,1,0:T(8,128)(2,1)S(1)}, bf16[2,256,128]{2,1,0:T(8,128)(2,1)S(1)}, u32[]{:S(2)}, u32[]{:S(2)}) collective-permute-start(bf16[2,256,128]{2,1,0:T(8,128)(2,1)S(1)} %get-tuple-element.53), channel_id=1, source_target_pairs={{0,8},{8,0},{16,24},{24,16},{1,9},{9,1},{17,25},{25,17},{2,10},{10... | collective-permute-start | bytes 393224 | tf_op jit(solution)/shard_map/ppermute | solution.py:42
  99.2 12.6 %collective-permute-start.9 = (bf16[2,256,128]{2,1,0:T(8,128)(2,1)S(1)}, bf16[2,256,128]{2,1,0:T(8,128)(2,1)S(1)}, u32[]{:S(2)}, u32[]{:S(2)}) collective-permute-start(bf16[2,256,128]{2,1,0:T(8,128)(2,1)S(1)} %get-tuple-element.48), channel_id=1, source_target_pairs={{0,4},{4,0},{8,12},{12,8},{16,20},{20,16},{24,28},{28,24},{1,5},{5... | collective-permute-start | bytes 393224 | tf_op jit(solution)/shard_map/ppermute | solution.py:319
  99.4 14.5 %collective-permute-start.11 = (bf16[2,256,128]{2,1,0:T(8,128)(2,1)S(1)}, bf16[2,256,128]{2,1,0:T(8,128)(2,1)S(1)}, u32[]{:S(2)}, u32[]{:S(2)}) collective-permute-start(bf16[2,256,128]{2,1,0:T(8,128)(2,1)S(1)} %get-tuple-element.50), channel_id=1, source_target_pairs={{0,12},{4,8},{8,4},{12,0},{16,28},{20,24},{24,20},{28,16},{1,13},{... | collective-permute-start | bytes 393224 | tf_op jit(solution)/shard_map/ppermute | solution.py:319
  106.2 7.7 %collective-permute-start.13 = (bf16[2,256,128]{2,1,0:T(8,128)(2,1)S(1)}, bf16[2,256,128]{2,1,0:T(8,128)(2,1)S(1)}, u32[]{:S(2)}, u32[]{:S(2)}) collective-permute-start(bf16[2,256,128]{2,1,0:T(8,128)(2,1)S(1)} %get-tuple-element.54), channel_id=1, source_target_pairs={{0,8},{8,0},{16,24},{24,16},{1,9},{9,1},{17,25},{25,17},{2,10},{10... | collective-permute-start | bytes 393224 | tf_op jit(solution)/shard_map/ppermute | solution.py:42
  114.2 7.3 %collective-permute-start.14 = (bf16[2,256,256]{2,1,0:T(8,128)(2,1)S(1)}, bf16[2,256,256]{2,1,0:T(8,128)(2,1)S(1)}, u32[]{:S(2)}, u32[]{:S(2)}) collective-permute-start(bf16[2,256,256]{2,1,0:T(8,128)(2,1)S(1)} %get-tuple-element.57), channel_id=1, source_target_pairs={{0,8},{8,0},{16,24},{24,16},{1,9},{9,1},{17,25},{25,17},{2,10},{10... | collective-permute-start | bytes 786440 | tf_op jit(solution)/shard_map/ppermute | solution.py:42
  114.4 14.2 %collective-permute-start.21 = (bf16[2,256,256]{2,1,0:T(8,128)(2,1)S(1)}, bf16[2,256,256]{2,1,0:T(8,128)(2,1)S(1)}, u32[]{:S(2)}, u32[]{:S(2)}) collective-permute-start(bf16[2,256,256]{2,1,0:T(8,128)(2,1)S(1)} %get-tuple-element.56.refs_1_), channel_id=1, source_target_pairs={{0,19},{1,18},{2,17},{3,16},{8,27},{9,26},{10,25},{11,24},{16,3},{... | collective-permute-start | bytes 786440 | tf_op jit(solution)/shard_map/ppermute | solution.py:42
  121.5 12.3 %collective-permute-start.20 = (bf16[2,256,256]{2,1,0:T(8,128)(2,1)S(1)}, bf16[2,256,256]{2,1,0:T(8,128)(2,1)S(1)}, u32[]{:S(2)}, u32[]{:S(2)}) collective-permute-start(bf16[2,256,256]{2,1,0:T(8,128)(2,1)S(1)} %get-tuple-element.56.refs_1_), channel_id=1, source_target_pairs={{0,18},{1,19},{2,16},{3,17},{8,26},{9,27},{10,24},{11,25},{16,2},{... | collective-permute-start | bytes 786440 | tf_op jit(solution)/shard_map/ppermute | solution.py:42
  123.7 21.9 %collective-permute-start.17 = (bf16[3,256,256]{2,1,0:T(8,128)(2,1)S(1)}, bf16[3,256,256]{2,1,0:T(8,128)(2,1)S(1)}, u32[]{:S(2)}, u32[]{:S(2)}) collective-permute-start(bf16[3,256,256]{2,1,0:T(8,128)(2,1)S(1)} %get-tuple-element.65), channel_id=1, source_target_pairs={{0,2},{1,3},{2,0},{3,1},{8,10},{9,11},{10,8},{11,9},{16,18},{17,19... | collective-permute-start | bytes 1179656 | tf_op jit(solution)/shard_map/ppermute | solution.py:42
  126.2 24.8 %collective-permute-start.15 = (bf16[3,256,256]{2,1,0:T(8,128)(2,1)S(1)}, bf16[3,256,256]{2,1,0:T(8,128)(2,1)S(1)}, u32[]{:S(2)}, u32[]{:S(2)}) collective-permute-start(bf16[3,256,256]{2,1,0:T(8,128)(2,1)S(1)} %get-tuple-element.62), channel_id=1, source_target_pairs={{0,1},{1,0},{2,3},{3,2},{8,9},{9,8},{10,11},{11,10},{16,17},{17,16... | collective-permute-start | bytes 1179656 | tf_op jit(solution)/shard_map/ppermute | solution.py:42
  126.6 24.4 %collective-permute-start.16 = (bf16[3,256,256]{2,1,0:T(8,128)(2,1)S(1)}, bf16[3,256,256]{2,1,0:T(8,128)(2,1)S(1)}, u32[]{:S(2)}, u32[]{:S(2)}) collective-permute-start(bf16[3,256,256]{2,1,0:T(8,128)(2,1)S(1)} %get-tuple-element.63), channel_id=1, source_target_pairs={{0,3},{1,2},{2,1},{3,0},{8,11},{9,10},{10,9},{11,8},{16,19},{17,18... | collective-permute-start | bytes 1179656 | tf_op jit(solution)/shard_map/ppermute | solution.py:42
  128.6 11.1 %collective-permute-start.19 = (bf16[2,256,256]{2,1,0:T(8,128)(2,1)S(1)}, bf16[2,256,256]{2,1,0:T(8,128)(2,1)S(1)}, u32[]{:S(2)}, u32[]{:S(2)}) collective-permute-start(bf16[2,256,256]{2,1,0:T(8,128)(2,1)S(1)} %get-tuple-element.56.refs_1_), channel_id=1, source_target_pairs={{0,17},{1,16},{2,19},{3,18},{8,25},{9,24},{10,27},{11,26},{16,1},{... | collective-permute-start | bytes 786440 | tf_op jit(solution)/shard_map/ppermute | solution.py:42
  133.8 10.4 %collective-permute-start.18 = (bf16[2,256,256]{2,1,0:T(8,128)(2,1)S(1)}, bf16[2,256,256]{2,1,0:T(8,128)(2,1)S(1)}, u32[]{:S(2)}, u32[]{:S(2)}) collective-permute-start(bf16[2,256,256]{2,1,0:T(8,128)(2,1)S(1)} %get-tuple-element.56.refs_1_), channel_id=1, source_target_pairs={{0,16},{1,17},{2,18},{3,19},{8,24},{9,25},{10,26},{11,27},{16,0},{... | collective-permute-start | bytes 786440 | tf_op jit(solution)/shard_map/ppermute | solution.py:42

commit v15 on v14

--- a/solution.py
+++ b/solution.py
@@ -205,13 +205,6 @@
     return jnp.concatenate([x[:, :HALF] for x in streams] + [x[:, HALF:] for x in streams], 1)
 
 
-def send_kernel(dual_ref, *refs):
-    posts, outs = refs[:len(refs) // 2], refs[len(refs) // 2:]
-    for post, out in zip(posts, outs):
-        out[:CORES] = dual_ref[...]
-        out[CORES] = post[...]
-
-
 def post_kernel(pairs, scale_ref, map_ref, prior_ref, *refs):
     duals, got_ref, refs = refs[:pairs], refs[pairs], refs[pairs + 1:]
     outs, (sides_ref, held_ref) = refs[:-2], refs[-2:]
@@ -227,8 +220,8 @@
 
 
 def end_kernel(e, quads, members, follows, *refs):
-    came, refs = refs[:len(members)], refs[len(members) + follows:]
     count = 1 + (e == 0)
+    came, refs = refs[:len(members) * count], refs[len(members) * count + follows:]
     outs, (dual_ref, sems, *post) = refs[:count], refs[count:]
     pair, quad, _ = my_place()
     sends = []
@@ -242,8 +235,8 @@
         if e == 0:
             post_ref = post[0]
             cells = post_ref.shape[1] // 2
-            post_ref[i, pl.ds(0, cells, stride=2), :] = came[i][CORES, :, :LANES].astype(f32)
-            post_ref[i, pl.ds(1, cells, stride=2), :] = came[i][CORES, :, LANES:].astype(f32)
+            post_ref[i, pl.ds(0, cells, stride=2), :] = came[len(members) + i][:, :LANES].astype(f32)
+            post_ref[i, pl.ds(1, cells, stride=2), :] = came[len(members) + i][:, LANES:].astype(f32)
             sends.append(pltpu.make_async_copy(post_ref.at[i], outs[1].at[quad ^ d], sems.at[i, CORES]))
             sends[-1].start()
     for copy in sends:
@@ -341,20 +334,19 @@
         flops=2**31,
         moved=8 * 2**20,
     )(scale, near, prior, *finals, got)
-    near_ones = call(
-        send_kernel,
-        [VMEM] * (1 + quads),
-        [shape((CORES + 1, sensors, 2 * LANES), bf16)] * quads,
-        moved=2**20,
-    )(finals[0], *posts)
     duals = {}
     for e in reversed(range(pairs)):
-        for d in reversed(range(quads)):
-            out = near_ones[d] if e == 0 else finals[e]
-            duals[e * quads + d] = swap(out, both, CORES * e * quads + d) if e + d else out
+        for d in range(quads):
+            low, high = d & 1, d & ~1
+            if low and high:
+                first, second = (high, low) if e == 0 else (low, high)
+                duals[e * quads + d] = swap(duals[e * quads + first], "quad", second)
+            else:
+                duals[e * quads + d] = swap(finals[e], both, CORES * e * quads + d) if e + d else finals[e]
+    posts = [posts[0]] + [swap(posts[d], "quad", d) for d in range(1, quads)]
     far = [(e, list(range(quads))) for e in reversed(range(1, pairs))]
     done = []
-    for e, members in far + [(0, list(range(0, quads, 2))), (0, list(range(1, quads, 2)))]:
+    for e, members in far + [(0, list(range(quads - 1))), (0, [quads - 1])]:
         count = len(members)
         out = [shape((frequencies, halves, sensors, LANES), f32)]
         scratch = [
@@ -366,13 +358,13 @@
             scratch.append(pltpu.VMEM((count, cells * 2, LANES), f32))
         done = call(
             functools.partial(end_kernel, e, quads, members, len(done)),
-            [VMEM] * count + [ANY] * len(done),
+            [VMEM] * (count * len(out)) + [ANY] * len(done),
             out,
             scratch,
             [ANY] * len(out),
             moved=4 * 2**20,
-            aliases={count + i: i for i in range(len(done))},
-        )(*[duals[e * quads + d] for d in members], *done)
+            aliases={count * len(out) + i: i for i in range(len(done))},
+        )(*[duals[e * quads + d] for d in members], *[posts[d] for d in members if e == 0], *done)
     dual, posterior = done
     return dual, posterior.reshape(quads, cells, 2, LANES)
 

time: 152 us -> 149 us (0.980); the launches traced: 152 us -> 147 us
  waiting for transfers between devices: 93.5 us -> 79.8 us
  starting transfers between devices: 33.9 us -> 42.8 us
    ppermute x18 -> x21, waiting for transfers between devices: 37 us -> 23.3 us  [swap(): return lax.ppermute(x, axes, [(i, i ^ distance) for i in range(count)])]
    ppermute x18 -> x21, starting transfers between devices: 22.9 us -> 31.9 us  [swap(): return lax.ppermute(x, axes, [(i, i ^ distance) for i in range(count)])]
  transfers between devices with their start and end apart: 23 -> 26, of which waited for: 14 -> 14; matrix products, arithmetic and copies ran while one was open for 0% -> 0% of each run, Pallas kernels for 11% -> 11%
where the time goes in v15:
time: 149 us; the launch traced here: 147 us
  waiting for transfers between devices  79.8 us (54%)
  starting transfers between devices  42.8 us (29%)
  Pallas kernels  21.1 us (14%)
  local copies, waits for them, and re-layouts  2.78 us (2%)
    all_to_all x1, waiting for transfers between devices, on_device(): lax.all_to_all(forward_map.reshape(frequencies, halves * sensors, cells),...  44.2 us
    ppermute x21, starting transfers between devices, swap(): return lax.ppermute(x, axes, [(i, i ^ distance) for i in range(count)])  31.9 us
    ppermute x21, waiting for transfers between devices, swap(): return lax.ppermute(x, axes, [(i, i ^ distance) for i in range(count)])  23.3 us
    ppermute x4, waiting for transfers between devices, to_other_sides(): lax.ppermute(x, ('sensor', 'side'), [(i, i ^ 1 + CORES * cross) for i in...  12.4 us
    pallas_call x4, Pallas kernels, step(): call(functools.partial(step_kernel, stage, len(preds), len(after)), [VMEM...  11.1 us
    all_to_all x1, starting transfers between devices, on_device(): lax.all_to_all(forward_map.reshape(frequencies, halves * sensors, cells),...  6.35 us
    ppermute x4, starting transfers between devices, to_other_sides(): lax.ppermute(x, ('sensor', 'side'), [(i, i ^ 1 + CORES * cross) for i in...  4.62 us
    pallas_call x3, Pallas kernels, on_device(): call(functools.partial(end_kernel, e, quads, members, len(done)), [VMEM]...  3.84 us
  transfers between devices with their start and end apart: 26, of which 14 were waited for; matrix products, arithmetic and copies ran while one was open for 0% of the time, Pallas kernels for 11%

profile of v15, /device:TPU:0, one launch (start us, length us, event | category | flops | bytes accessed | tf_op | source)
XLA Modules:
  0.0 147.4 jit_solution(13363843610191218980)
XLA Ops:
  0.6 6.4 %all-to-all-start = ((bf16[16,512,256]{2,1,0:T(8,128)(2,1)}), bf16[16,512,256]{2,1,0:T(8,128)(2,1)}, u32[]{:S(2)}, u32[]{:S(2)}) async-start(bf16[16,512,256]{2,1,0:T(8,128)(2,1)} %bitcast.5), calls=%async_computation | async-start | bytes 8388608 | tf_op jit(solution)/shard_map/all_to_all | solution.py:254
  7.0 2.2 %copy-done = f32[16,2,256,128]{3,2,1,0:T(8,128)S(1)} copy-done((f32[16,2,256,128]{3,2,1,0:T(8,128)S(1)}, f32[16,2,256,128]{3,2,1,0:T(8,128)}, u32[]{:S(2)}) %copy-start) | copy-done | bytes 4194328
  11.9 1.9 %collective-permute-start.2 = (bf16[448,256]{1,0:T(8,128)(2,1)S(1)}, bf16[448,256]{1,0:T(8,128)(2,1)S(1)}, u32[]{:S(2)}, u32[]{:S(2)}) collective-permute-start(bf16[448,256]{1,0:T(8,128)(2,1)S(1)} %get-tuple-element.35), channel_id=1, source_target_pairs={{0,2},{1,3},{2,0},{3,1},{4,6},{5,7},{6,4},{7,5},{8,10},{9,11},{10,... | collective-permute-start | bytes 688136 | tf_op jit(solution)/shard_map/ppermute | solution.py:42
  13.8 1.5 collective-permute-start.4
  15.3 1.5 collective-permute-start.3
  17.3 44.2 %all-to-all-done = bf16[16,512,256]{2,1,0:T(8,128)(2,1)} async-done(((bf16[16,512,256]{2,1,0:T(8,128)(2,1)}), bf16[16,512,256]{2,1,0:T(8,128)(2,1)}, u32[]{:S(2)}, u32[]{:S(2)}) %all-to-all-start) | async-done | bytes 4194336 | tf_op jit(solution)/shard_map/all_to_all | solution.py:254
  61.5 2.2 %shard_map.70.refs_7_.map_ref = bf16[4,4,512,256]{3,2,1,0:T(8,128)(2,1)S(1)} custom-call(bf16[4,4,512,256]{3,2,1,0:T(8,128)(2,1)} %bitcast.2.map_ref), custom_call_target="tpu_custom_call" | custom-call | bytes 8388608 | tf_op jit(solution)/shard_map/pallas_call | solution.py:273
  63.7 2.4 %collective-permute-done.4.refs_5_ = bf16[272,256]{1,0:T(8,128)(2,1)S(1)} collective-permute-done((bf16[272,256]{1,0:T(8,128)(2,1)S(1)}, bf16[272,256]{1,0:T(8,128)(2,1)S(1)}, u32[]{:S(2)}, u32[]{:S(2)}) %collective-permute-start.4) | collective-permute-done | bytes 139296 | tf_op jit(solution)/shard_map/ppermute | solution.py:42
  66.2 2.0 %collective-permute-done.5.refs_6_ = bf16[272,256]{1,0:T(8,128)(2,1)S(1)} collective-permute-done((bf16[272,256]{1,0:T(8,128)(2,1)S(1)}, bf16[272,256]{1,0:T(8,128)(2,1)S(1)}, u32[]{:S(2)}, u32[]{:S(2)}) %collective-permute-start.5) | collective-permute-done | bytes 139296 | tf_op jit(solution)/shard_map/ppermute | solution.py:42
  68.6 2.7 %shard_map.72.refs_0_ = bf16[4,256,128]{2,1,0:T(8,128)(2,1)S(1)} custom-call(f32[8,128]{1,0:T(8,128)S(1)} %get-tuple-element.33.scale_ref, bf16[4,4,512,256]{3,2,1,0:T(8,128)(2,1)S(1)} %shard_map.70.refs_7_.map_ref, bf16[4,256,512]{2,1,0:T(8,128)(2,1)S(1)} %get-tuple-element.39.prior_ref, bf16[4,256,128]{2,1,0:T(8,128)(2,1)S(1)} %get-tuple-element.40.obs_ref, ...), custom_call_target="tpu_custom_call" | custom-call | flops 2147483648 | bytes 8388608 | tf_op jit(solution)/shard_map/pallas_call | solution.py:295
  71.4 2.7 %collective-permute-start.6 = (bf16[4,256,128]{2,1,0:T(8,128)(2,1)S(1)}, bf16[4,256,128]{2,1,0:T(8,128)(2,1)S(1)}, u32[]{:S(2)}, u32[]{:S(2)}) collective-permute-start(bf16[4,256,128]{2,1,0:T(8,128)(2,1)S(1)} %shard_map.72.refs_0_), channel_id=1, source_target_pairs={{0,4},{4,0},{1,5},{5,1},{2,6},{6,2},{3,7},{7,3},{8,12},{12,8},{9,1... | collective-permute-start | bytes 786440 | tf_op jit(solution)/shard_map/ppermute | solution.py:42
  74.0 2.8 %shard_map.73.refs_2_.refs_0_ = bf16[4,256,128]{2,1,0:T(8,128)(2,1)S(1)} custom-call(f32[8,128]{1,0:T(8,128)S(1)} %get-tuple-element.33.scale_ref, bf16[4,4,512,256]{3,2,1,0:T(8,128)(2,1)S(1)} %shard_map.70.refs_7_.map_ref, bf16[4,256,512]{2,1,0:T(8,128)(2,1)S(1)} %get-tuple-element.39.prior_ref, bf16[4,256,128]{2,1,0:T(8,128)(2,1)S(1)} %get-tuple-element.42.obs_ref, ...), custom_call_target="tpu_custom_call" | custom-call | flops 2147483648 | bytes 8388608 | tf_op jit(solution)/shard_map/pallas_call | solution.py:295
  77.2 13.3 %collective-permute-done.6.refs_1_ = bf16[4,256,128]{2,1,0:T(8,128)(2,1)S(1)} collective-permute-done((bf16[4,256,128]{2,1,0:T(8,128)(2,1)S(1)}, bf16[4,256,128]{2,1,0:T(8,128)(2,1)S(1)}, u32[]{:S(2)}, u32[]{:S(2)}) %collective-permute-start.6) | collective-permute-done | bytes 262176 | tf_op jit(solution)/shard_map/ppermute | solution.py:42
  90.5 2.8 %shard_map.74 = (bf16[2,256,128]{2,1,0:T(8,128)(2,1)S(1)}, bf16[2,256,128]{2,1,0:T(8,128)(2,1)S(1)}, f32[2,256,128]{2,1,0:T(8,128)S(1)}, bf16[2,256,128]{2,1,0:T(8,128)(2,1)S(1)}) custom-call(f32[8,128]{1,0:T(8,128)S(1)} %get-tuple-element.33.scale_ref, bf16[4,4,512,256]{3,2,1,0:T(8,128)(2,1)S(1)} %shard_map.70.refs_7_.map_ref, ...), custom_call_target="tpu_custom_call" | custom-call | flops 2147483648 | bytes 8388608 | tf_op jit(solution)/shard_map/pallas_call | solution.py:295
  93.4 2.2 %collective-permute-start.10 = (bf16[2,256,128]{2,1,0:T(8,128)(2,1)S(1)}, bf16[2,256,128]{2,1,0:T(8,128)(2,1)S(1)}, u32[]{:S(2)}, u32[]{:S(2)}) collective-permute-start(bf16[2,256,128]{2,1,0:T(8,128)(2,1)S(1)} %get-tuple-element.45), channel_id=1, source_target_pairs={{0,12},{4,8},{8,4},{12,0},{16,28},{20,24},{24,20},{28,16},{1,13},{... | collective-permute-start | bytes 393224 | tf_op jit(solution)/shard_map/ppermute | solution.py:312
  96.4 2.8 %shard_map.75 = (bf16[2,256,128]{2,1,0:T(8,128)(2,1)S(1)}, bf16[2,256,128]{2,1,0:T(8,128)(2,1)S(1)}, f32[2,256,128]{2,1,0:T(8,128)S(1)}, bf16[2,256,128]{2,1,0:T(8,128)(2,1)S(1)}) custom-call(f32[8,128]{1,0:T(8,128)S(1)} %get-tuple-element.33.scale_ref, bf16[4,4,512,256]{3,2,1,0:T(8,128)(2,1)S(1)} %shard_map.70.refs_7_.map_ref, ...), custom_call_target="tpu_custom_call" | custom-call | flops 2147483648 | bytes 8388608 | tf_op jit(solution)/shard_map/pallas_call | solution.py:295
  99.4 2.2 %collective-permute-start.11 = (bf16[2,256,128]{2,1,0:T(8,128)(2,1)S(1)}, bf16[2,256,128]{2,1,0:T(8,128)(2,1)S(1)}, u32[]{:S(2)}, u32[]{:S(2)}) collective-permute-start(bf16[2,256,128]{2,1,0:T(8,128)(2,1)S(1)} %get-tuple-element.46), channel_id=1, source_target_pairs={{0,12},{4,8},{8,4},{12,0},{16,28},{20,24},{24,20},{28,16},{1,13},{... | collective-permute-start | bytes 393224 | tf_op jit(solution)/shard_map/ppermute | solution.py:312
  101.5 4.7 %collective-permute-done.7.refs_0_ = bf16[2,256,128]{2,1,0:T(8,128)(2,1)S(1)} collective-permute-done((bf16[2,256,128]{2,1,0:T(8,128)(2,1)S(1)}, bf16[2,256,128]{2,1,0:T(8,128)(2,1)S(1)}, u32[]{:S(2)}, u32[]{:S(2)}) %collective-permute-start.7) | collective-permute-done | bytes 131104 | tf_op jit(solution)/shard_map/ppermute | solution.py:312
  106.2 2.1 %collective-permute-done.10.refs_2_ = bf16[2,256,128]{2,1,0:T(8,128)(2,1)S(1)} collective-permute-done((bf16[2,256,128]{2,1,0:T(8,128)(2,1)S(1)}, bf16[2,256,128]{2,1,0:T(8,128)(2,1)S(1)}, u32[]{:S(2)}, u32[]{:S(2)}) %collective-permute-start.10) | collective-permute-done | bytes 131104 | tf_op jit(solution)/shard_map/ppermute | solution.py:312
  108.3 3.6 %collective-permute-done.9.refs_1_ = bf16[2,256,128]{2,1,0:T(8,128)(2,1)S(1)} collective-permute-done((bf16[2,256,128]{2,1,0:T(8,128)(2,1)S(1)}, bf16[2,256,128]{2,1,0:T(8,128)(2,1)S(1)}, u32[]{:S(2)}, u32[]{:S(2)}) %collective-permute-start.9) | collective-permute-done | bytes 131104 | tf_op jit(solution)/shard_map/ppermute | solution.py:312
  111.9 2.1 %collective-permute-done.11.refs_3_ = bf16[2,256,128]{2,1,0:T(8,128)(2,1)S(1)} collective-permute-done((bf16[2,256,128]{2,1,0:T(8,128)(2,1)S(1)}, bf16[2,256,128]{2,1,0:T(8,128)(2,1)S(1)}, u32[]{:S(2)}, u32[]{:S(2)}) %collective-permute-start.11) | collective-permute-done | bytes 131104 | tf_op jit(solution)/shard_map/ppermute | solution.py:312
  114.2 2.2 %collective-permute-start.22 = (bf16[2,256,256]{2,1,0:T(8,128)(2,1)S(1)}, bf16[2,256,256]{2,1,0:T(8,128)(2,1)S(1)}, u32[]{:S(2)}, u32[]{:S(2)}) collective-permute-start(bf16[2,256,256]{2,1,0:T(8,128)(2,1)S(1)} %get-tuple-element.52.refs_1_), channel_id=1, source_target_pairs={{0,17},{1,16},{2,19},{3,18},{8,25},{9,24},{10,27},{11,26},{16,1},{... | collective-permute-start | bytes 786440 | tf_op jit(solution)/shard_map/ppermute | solution.py:42
  116.4 5.6 %collective-permute-start.14 = (bf16[2,256,256]{2,1,0:T(8,128)(2,1)S(1)}, bf16[2,256,256]{2,1,0:T(8,128)(2,1)S(1)}, u32[]{:S(2)}, u32[]{:S(2)}) collective-permute-start(bf16[2,256,256]{2,1,0:T(8,128)(2,1)S(1)} %get-tuple-element.51.refs_0_), channel_id=1, source_target_pairs={{0,2},{1,3},{2,0},{3,1},{8,10},{9,11},{10,8},{11,9},{16,18},{17,19... | collective-permute-start | bytes 786440 | tf_op jit(solution)/shard_map/ppermute | solution.py:42
  123.6 5.7 %collective-permute-start.24 = (bf16[2,256,256]{2,1,0:T(8,128)(2,1)S(1)}, bf16[2,256,256]{2,1,0:T(8,128)(2,1)S(1)}, u32[]{:S(2)}, u32[]{:S(2)}) collective-permute-start(bf16[2,256,256]{2,1,0:T(8,128)(2,1)S(1)} %collective-permute-done.22.refs_1_), channel_id=1, source_target_pairs={{0,2},{1,3},{2,0},{3,1},{4,6},{5,7},{6,4},{7,5},{8,10},{9,11},{10,... | collective-permute-start | bytes 786440 | tf_op jit(solution)/shard_map/ppermute | solution.py:42
  129.3 1.6 %collective-permute-start.18 = (bf16[2,256,256]{2,1,0:T(8,128)(2,1)S(1)}, bf16[2,256,256]{2,1,0:T(8,128)(2,1)S(1)}, u32[]{:S(2)}, u32[]{:S(2)}) collective-permute-start(bf16[2,256,256]{2,1,0:T(8,128)(2,1)S(1)} %get-tuple-element.51.refs_0_), channel_id=1, source_target_pairs={{0,1},{1,0},{2,3},{3,2},{8,9},{9,8},{10,11},{11,10},{16,17},{17,16... | collective-permute-start | bytes 786440 | tf_op jit(solution)/shard_map/ppermute | solution.py:42
  131.3 2.1 %shard_map.77 = (bf16[256,256]{1,0:T(8,128)(2,1)S(1)}, bf16[256,256]{1,0:T(8,128)(2,1)S(1)}, bf16[256,256]{1,0:T(8,128)(2,1)S(1)}, bf16[256,256]{1,0:T(8,128)(2,1)S(1)}) custom-call(f32[8,128]{1,0:T(8,128)S(1)} %get-tuple-element.33.scale_ref, bf16[4,4,512,256]{3,2,1,0:T(8,128)(2,1)S(1)} %shard_map.70.refs_7_.map_ref, ...), custom_call_target="tpu_custom_call" | custom-call | flops 2147483648 | bytes 8388608 | tf_op jit(solution)/shard_map/pallas_call | solution.py:329
  133.4 1.8 %collective-permute-done.23.refs_2_ = bf16[2,256,256]{2,1,0:T(8,128)(2,1)S(1)} collective-permute-done((bf16[2,256,256]{2,1,0:T(8,128)(2,1)S(1)}, bf16[2,256,256]{2,1,0:T(8,128)(2,1)S(1)}, u32[]{:S(2)}, u32[]{:S(2)}) %collective-permute-start.23) | collective-permute-done | bytes 262176 | tf_op jit(solution)/shard_map/ppermute | solution.py:42
  136.5 3.0 %collective-permute-start.20 = (bf16[256,256]{1,0:T(8,128)(2,1)S(1)}, bf16[256,256]{1,0:T(8,128)(2,1)S(1)}, u32[]{:S(2)}, u32[]{:S(2)}) collective-permute-start(bf16[256,256]{1,0:T(8,128)(2,1)S(1)} %get-tuple-element.57), channel_id=1, source_target_pairs={{0,2},{1,3},{2,0},{3,1},{4,6},{5,7},{6,4},{7,5},{8,10},{9,11},{10,... | collective-permute-start | bytes 393224 | tf_op jit(solution)/shard_map/ppermute | solution.py:42
  140.4 1.7 %collective-permute-start.17 = (bf16[256,256]{1,0:T(8,128)(2,1)S(1)}, bf16[256,256]{1,0:T(8,128)(2,1)S(1)}, u32[]{:S(2)}, u32[]{:S(2)}) collective-permute-start(bf16[256,256]{1,0:T(8,128)(2,1)S(1)} %get-tuple-element.54), channel_id=1, source_target_pairs={{0,3},{1,2},{2,1},{3,0},{4,7},{5,6},{6,5},{7,4},{8,11},{9,10},{10,... | collective-permute-start | bytes 393224 | tf_op jit(solution)/shard_map/ppermute | solution.py:42
  142.1 1.4 shard_map.78.refs_6_
  143.6 1.5 %shard_map.79 = (f32[16,2,256,128]{3,2,1,0:T(8,128)}, f32[4,512,128]{2,1,0:T(8,128)}) custom-call(bf16[2,256,256]{2,1,0:T(8,128)(2,1)S(1)} %get-tuple-element.51.refs_0_, bf16[2,256,256]{2,1,0:T(8,128)(2,1)S(1)} %collective-permute-done.18.refs_1_, bf16[2,256,256]{2,1,0:T(8,128)(2,1)S(1)} %collective-permute-done.14.refs_2_, ...), custom_call_target="tpu_custom_call", output_to_operand_aliasing={{0}: (6, {})} | custom-call | bytes 4194304 | tf_op jit(solution)/shard_map/pallas_call | solution.py:359
  145.1 1.3 collective-permute-done.17.refs_1_
  (42 shorter events, 10.4 us)
Async XLA Ops:
  0.6 6.4 %copy-start.2 = (f32[256]{0:T(256)S(1)}, f32[256]{0:T(256)}, u32[]{:S(2)}) copy-start(f32[256]{0:T(256)} %param.7) | copy-start | bytes 3076
  0.6 60.9 %all-to-all-start = ((bf16[16,512,256]{2,1,0:T(8,128)(2,1)}), bf16[16,512,256]{2,1,0:T(8,128)(2,1)}, u32[]{:S(2)}, u32[]{:S(2)}) async-start(bf16[16,512,256]{2,1,0:T(8,128)(2,1)} %bitcast.5), calls=%async_computation | async-start | bytes 8388608 | tf_op jit(solution)/shard_map/all_to_all | solution.py:254
  7.0 3.2 %copy-start.3 = (f32[16]{0:T(128)S(1)}, f32[16]{0:T(128)}, u32[]{:S(2)}) copy-start(f32[16]{0:T(128)} %param.9) | copy-start | bytes 196
  7.0 2.2 %copy-start = (f32[16,2,256,128]{3,2,1,0:T(8,128)S(1)}, f32[16,2,256,128]{3,2,1,0:T(8,128)}, u32[]{:S(2)}) copy-start(f32[16,2,256,128]{3,2,1,0:T(8,128)} %obs_ref.1) | copy-start | bytes 12582916
  9.2 2.0 %copy-start.1 = (bf16[256,512]{1,0:T(8,128)(2,1)S(1)}, bf16[256,512]{1,0:T(8,128)(2,1)}, u32[]{:S(2)}) copy-start(bf16[256,512]{1,0:T(8,128)(2,1)} %own_ref.3) | copy-start | bytes 786436
  9.8 1.4 collective-permute-start
  11.9 56.4 %collective-permute-start.2 = (bf16[448,256]{1,0:T(8,128)(2,1)S(1)}, bf16[448,256]{1,0:T(8,128)(2,1)S(1)}, u32[]{:S(2)}, u32[]{:S(2)}) collective-permute-start(bf16[448,256]{1,0:T(8,128)(2,1)S(1)} %get-tuple-element.35), channel_id=1, source_target_pairs={{0,2},{1,3},{2,0},{3,1},{4,6},{5,7},{6,4},{7,5},{8,10},{9,11},{10,... | collective-permute-start | bytes 688136 | tf_op jit(solution)/shard_map/ppermute | solution.py:42
  13.8 52.3 %collective-permute-start.4 = (bf16[272,256]{1,0:T(8,128)(2,1)S(1)}, bf16[272,256]{1,0:T(8,128)(2,1)S(1)}, u32[]{:S(2)}, u32[]{:S(2)}) collective-permute-start(bf16[272,256]{1,0:T(8,128)(2,1)S(1)} %get-tuple-element.37), channel_id=1, source_target_pairs={{0,16},{8,24},{16,0},{24,8},{1,17},{9,25},{17,1},{25,9},{2,18},{10... | collective-permute-start | bytes 417800 | tf_op jit(solution)/shard_map/ppermute | solution.py:42
  15.3 52.9 %collective-permute-start.5 = (bf16[272,256]{1,0:T(8,128)(2,1)S(1)}, bf16[272,256]{1,0:T(8,128)(2,1)S(1)}, u32[]{:S(2)}, u32[]{:S(2)}) collective-permute-start(bf16[272,256]{1,0:T(8,128)(2,1)S(1)} %get-tuple-element.38), channel_id=1, source_target_pairs={{0,24},{8,16},{16,8},{24,0},{1,25},{9,17},{17,9},{25,1},{2,26},{10... | collective-permute-start | bytes 417800 | tf_op jit(solution)/shard_map/ppermute | solution.py:42
  15.3 53.0 %collective-permute-start.3 = (bf16[192,256]{1,0:T(8,128)(2,1)S(1)}, bf16[192,256]{1,0:T(8,128)(2,1)S(1)}, u32[]{:S(2)}, u32[]{:S(2)}) collective-permute-start(bf16[192,256]{1,0:T(8,128)(2,1)S(1)} %get-tuple-element.34), channel_id=1, source_target_pairs={{0,3},{1,2},{2,1},{3,0},{4,7},{5,6},{6,5},{7,4},{8,11},{9,10},{10,... | collective-permute-start | bytes 294920 | tf_op jit(solution)/shard_map/ppermute | solution.py:42
  16.7 51.5 %collective-permute-start.1 = (bf16[192,256]{1,0:T(8,128)(2,1)S(1)}, bf16[192,256]{1,0:T(8,128)(2,1)S(1)}, u32[]{:S(2)}, u32[]{:S(2)}) collective-permute-start(bf16[192,256]{1,0:T(8,128)(2,1)S(1)} %get-tuple-element.34), channel_id=1, source_target_pairs={{0,1},{1,0},{2,3},{3,2},{4,5},{5,4},{6,7},{7,6},{8,9},{9,8},{10,11... | collective-permute-start | bytes 294920 | tf_op jit(solution)/shard_map/ppermute | solution.py:42
  71.4 19.1 %collective-permute-start.6 = (bf16[4,256,128]{2,1,0:T(8,128)(2,1)S(1)}, bf16[4,256,128]{2,1,0:T(8,128)(2,1)S(1)}, u32[]{:S(2)}, u32[]{:S(2)}) collective-permute-start(bf16[4,256,128]{2,1,0:T(8,128)(2,1)S(1)} %shard_map.72.refs_0_), channel_id=1, source_target_pairs={{0,4},{4,0},{1,5},{5,1},{2,6},{6,2},{3,7},{7,3},{8,12},{12,8},{9,1... | collective-permute-start | bytes 786440 | tf_op jit(solution)/shard_map/ppermute | solution.py:42
  76.8 19.6 %collective-permute-start.8 = (bf16[4,256,128]{2,1,0:T(8,128)(2,1)S(1)}, bf16[4,256,128]{2,1,0:T(8,128)(2,1)S(1)}, u32[]{:S(2)}, u32[]{:S(2)}) collective-permute-start(bf16[4,256,128]{2,1,0:T(8,128)(2,1)S(1)} %shard_map.73.refs_2_.refs_0_), channel_id=1, source_target_pairs={{0,4},{4,0},{1,5},{5,1},{2,6},{6,2},{3,7},{7,3},{8,12},{12,8},{9,1... | collective-permute-start | bytes 786440 | tf_op jit(solution)/shard_map/ppermute | solution.py:42
  93.3 12.9 %collective-permute-start.7 = (bf16[2,256,128]{2,1,0:T(8,128)(2,1)S(1)}, bf16[2,256,128]{2,1,0:T(8,128)(2,1)S(1)}, u32[]{:S(2)}, u32[]{:S(2)}) collective-permute-start(bf16[2,256,128]{2,1,0:T(8,128)(2,1)S(1)} %get-tuple-element.43), channel_id=1, source_target_pairs={{0,4},{4,0},{8,12},{12,8},{16,20},{20,16},{24,28},{28,24},{1,5},{5... | collective-permute-start | bytes 393224 | tf_op jit(solution)/shard_map/ppermute | solution.py:312
  93.4 14.9 %collective-permute-start.10 = (bf16[2,256,128]{2,1,0:T(8,128)(2,1)S(1)}, bf16[2,256,128]{2,1,0:T(8,128)(2,1)S(1)}, u32[]{:S(2)}, u32[]{:S(2)}) collective-permute-start(bf16[2,256,128]{2,1,0:T(8,128)(2,1)S(1)} %get-tuple-element.45), channel_id=1, source_target_pairs={{0,12},{4,8},{8,4},{12,0},{16,28},{20,24},{24,20},{28,16},{1,13},{... | collective-permute-start | bytes 393224 | tf_op jit(solution)/shard_map/ppermute | solution.py:312
  95.6 12.7 %collective-permute-start.12 = (bf16[2,256,128]{2,1,0:T(8,128)(2,1)S(1)}, bf16[2,256,128]{2,1,0:T(8,128)(2,1)S(1)}, u32[]{:S(2)}, u32[]{:S(2)}) collective-permute-start(bf16[2,256,128]{2,1,0:T(8,128)(2,1)S(1)} %get-tuple-element.49), channel_id=1, source_target_pairs={{0,8},{8,0},{16,24},{24,16},{1,9},{9,1},{17,25},{25,17},{2,10},{10... | collective-permute-start | bytes 393224 | tf_op jit(solution)/shard_map/ppermute | solution.py:42
  99.2 12.6 %collective-permute-start.9 = (bf16[2,256,128]{2,1,0:T(8,128)(2,1)S(1)}, bf16[2,256,128]{2,1,0:T(8,128)(2,1)S(1)}, u32[]{:S(2)}, u32[]{:S(2)}) collective-permute-start(bf16[2,256,128]{2,1,0:T(8,128)(2,1)S(1)} %get-tuple-element.44), channel_id=1, source_target_pairs={{0,4},{4,0},{8,12},{12,8},{16,20},{20,16},{24,28},{28,24},{1,5},{5... | collective-permute-start | bytes 393224 | tf_op jit(solution)/shard_map/ppermute | solution.py:312
  99.4 14.5 %collective-permute-start.11 = (bf16[2,256,128]{2,1,0:T(8,128)(2,1)S(1)}, bf16[2,256,128]{2,1,0:T(8,128)(2,1)S(1)}, u32[]{:S(2)}, u32[]{:S(2)}) collective-permute-start(bf16[2,256,128]{2,1,0:T(8,128)(2,1)S(1)} %get-tuple-element.46), channel_id=1, source_target_pairs={{0,12},{4,8},{8,4},{12,0},{16,28},{20,24},{24,20},{28,16},{1,13},{... | collective-permute-start | bytes 393224 | tf_op jit(solution)/shard_map/ppermute | solution.py:312
  106.2 7.7 %collective-permute-start.13 = (bf16[2,256,128]{2,1,0:T(8,128)(2,1)S(1)}, bf16[2,256,128]{2,1,0:T(8,128)(2,1)S(1)}, u32[]{:S(2)}, u32[]{:S(2)}) collective-permute-start(bf16[2,256,128]{2,1,0:T(8,128)(2,1)S(1)} %get-tuple-element.50), channel_id=1, source_target_pairs={{0,8},{8,0},{16,24},{24,16},{1,9},{9,1},{17,25},{25,17},{2,10},{10... | collective-permute-start | bytes 393224 | tf_op jit(solution)/shard_map/ppermute | solution.py:42
  114.2 9.4 %collective-permute-start.22 = (bf16[2,256,256]{2,1,0:T(8,128)(2,1)S(1)}, bf16[2,256,256]{2,1,0:T(8,128)(2,1)S(1)}, u32[]{:S(2)}, u32[]{:S(2)}) collective-permute-start(bf16[2,256,256]{2,1,0:T(8,128)(2,1)S(1)} %get-tuple-element.52.refs_1_), channel_id=1, source_target_pairs={{0,17},{1,16},{2,19},{3,18},{8,25},{9,24},{10,27},{11,26},{16,1},{... | collective-permute-start | bytes 786440 | tf_op jit(solution)/shard_map/ppermute | solution.py:42
  116.4 12.9 %collective-permute-start.16 = (bf16[2,256,256]{2,1,0:T(8,128)(2,1)S(1)}, bf16[2,256,256]{2,1,0:T(8,128)(2,1)S(1)}, u32[]{:S(2)}, u32[]{:S(2)}) collective-permute-start(bf16[2,256,256]{2,1,0:T(8,128)(2,1)S(1)} %get-tuple-element.53), channel_id=1, source_target_pairs={{0,8},{8,0},{16,24},{24,16},{1,9},{9,1},{17,25},{25,17},{2,10},{10... | collective-permute-start | bytes 786440 | tf_op jit(solution)/shard_map/ppermute | solution.py:42
  116.4 14.6 %collective-permute-start.14 = (bf16[2,256,256]{2,1,0:T(8,128)(2,1)S(1)}, bf16[2,256,256]{2,1,0:T(8,128)(2,1)S(1)}, u32[]{:S(2)}, u32[]{:S(2)}) collective-permute-start(bf16[2,256,256]{2,1,0:T(8,128)(2,1)S(1)} %get-tuple-element.51.refs_0_), channel_id=1, source_target_pairs={{0,2},{1,3},{2,0},{3,1},{8,10},{9,11},{10,8},{11,9},{16,18},{17,19... | collective-permute-start | bytes 786440 | tf_op jit(solution)/shard_map/ppermute | solution.py:42
  122.0 13.3 %collective-permute-start.23 = (bf16[2,256,256]{2,1,0:T(8,128)(2,1)S(1)}, bf16[2,256,256]{2,1,0:T(8,128)(2,1)S(1)}, u32[]{:S(2)}, u32[]{:S(2)}) collective-permute-start(bf16[2,256,256]{2,1,0:T(8,128)(2,1)S(1)} %get-tuple-element.52.refs_1_), channel_id=1, source_target_pairs={{0,18},{1,19},{2,16},{3,17},{8,26},{9,27},{10,24},{11,25},{16,2},{... | collective-permute-start | bytes 786440 | tf_op jit(solution)/shard_map/ppermute | solution.py:42
  122.4 14.1 %collective-permute-start.21 = (bf16[2,256,256]{2,1,0:T(8,128)(2,1)S(1)}, bf16[2,256,256]{2,1,0:T(8,128)(2,1)S(1)}, u32[]{:S(2)}, u32[]{:S(2)}) collective-permute-start(bf16[2,256,256]{2,1,0:T(8,128)(2,1)S(1)} %get-tuple-element.52.refs_1_), channel_id=1, source_target_pairs={{0,16},{1,17},{2,18},{3,19},{8,24},{9,25},{10,26},{11,27},{16,0},{... | collective-permute-start | bytes 786440 | tf_op jit(solution)/shard_map/ppermute | solution.py:42
  123.6 16.8 %collective-permute-start.24 = (bf16[2,256,256]{2,1,0:T(8,128)(2,1)S(1)}, bf16[2,256,256]{2,1,0:T(8,128)(2,1)S(1)}, u32[]{:S(2)}, u32[]{:S(2)}) collective-permute-start(bf16[2,256,256]{2,1,0:T(8,128)(2,1)S(1)} %collective-permute-done.22.refs_1_), channel_id=1, source_target_pairs={{0,2},{1,3},{2,0},{3,1},{4,6},{5,7},{6,4},{7,5},{8,10},{9,11},{10,... | collective-permute-start | bytes 786440 | tf_op jit(solution)/shard_map/ppermute | solution.py:42
  129.3 14.3 %collective-permute-start.18 = (bf16[2,256,256]{2,1,0:T(8,128)(2,1)S(1)}, bf16[2,256,256]{2,1,0:T(8,128)(2,1)S(1)}, u32[]{:S(2)}, u32[]{:S(2)}) collective-permute-start(bf16[2,256,256]{2,1,0:T(8,128)(2,1)S(1)} %get-tuple-element.51.refs_0_), channel_id=1, source_target_pairs={{0,1},{1,0},{2,3},{3,2},{8,9},{9,8},{10,11},{11,10},{16,17},{17,16... | collective-permute-start | bytes 786440 | tf_op jit(solution)/shard_map/ppermute | solution.py:42
  130.9 15.5 %collective-permute-start.15 = (bf16[2,256,256]{2,1,0:T(8,128)(2,1)S(1)}, bf16[2,256,256]{2,1,0:T(8,128)(2,1)S(1)}, u32[]{:S(2)}, u32[]{:S(2)}) collective-permute-start(bf16[2,256,256]{2,1,0:T(8,128)(2,1)S(1)} %collective-permute-done.14.refs_2_), channel_id=1, source_target_pairs={{0,1},{1,0},{2,3},{3,2},{4,5},{5,4},{6,7},{7,6},{8,9},{9,8},{10,11... | collective-permute-start | bytes 786440 | tf_op jit(solution)/shard_map/ppermute | solution.py:42
  135.2 8.4 %collective-permute-start.19 = (bf16[256,256]{1,0:T(8,128)(2,1)S(1)}, bf16[256,256]{1,0:T(8,128)(2,1)S(1)}, u32[]{:S(2)}, u32[]{:S(2)}) collective-permute-start(bf16[256,256]{1,0:T(8,128)(2,1)S(1)} %get-tuple-element.56), channel_id=1, source_target_pairs={{0,1},{1,0},{2,3},{3,2},{4,5},{5,4},{6,7},{7,6},{8,9},{9,8},{10,11... | collective-permute-start | bytes 393224 | tf_op jit(solution)/shard_map/ppermute | solution.py:42
  136.5 7.1 %collective-permute-start.20 = (bf16[256,256]{1,0:T(8,128)(2,1)S(1)}, bf16[256,256]{1,0:T(8,128)(2,1)S(1)}, u32[]{:S(2)}, u32[]{:S(2)}) collective-permute-start(bf16[256,256]{1,0:T(8,128)(2,1)S(1)} %get-tuple-element.57), channel_id=1, source_target_pairs={{0,2},{1,3},{2,0},{3,1},{4,6},{5,7},{6,4},{7,5},{8,10},{9,11},{10,... | collective-permute-start | bytes 393224 | tf_op jit(solution)/shard_map/ppermute | solution.py:42
  140.4 6.0 %collective-permute-start.17 = (bf16[256,256]{1,0:T(8,128)(2,1)S(1)}, bf16[256,256]{1,0:T(8,128)(2,1)S(1)}, u32[]{:S(2)}, u32[]{:S(2)}) collective-permute-start(bf16[256,256]{1,0:T(8,128)(2,1)S(1)} %get-tuple-element.54), channel_id=1, source_target_pairs={{0,3},{1,2},{2,1},{3,0},{4,7},{5,6},{6,5},{7,4},{8,11},{9,10},{10,... | collective-permute-start | bytes 393224 | tf_op jit(solution)/shard_map/ppermute | solution.py:42

commit v16 on v15

--- a/solution.py
+++ b/solution.py
@@ -335,7 +335,7 @@
         moved=8 * 2**20,
     )(scale, near, prior, *finals, got)
     duals = {}
-    for e in reversed(range(pairs)):
+    for e in range(pairs):
         for d in range(quads):
             low, high = d & 1, d & ~1
             if low and high:
@@ -346,7 +346,7 @@
     posts = [posts[0]] + [swap(posts[d], "quad", d) for d in range(1, quads)]
     far = [(e, list(range(quads))) for e in reversed(range(1, pairs))]
     done = []
-    for e, members in far + [(0, list(range(quads - 1))), (0, [quads - 1])]:
+    for e, members in far + [(0, [0, 1]), (0, list(range(2, quads)))]:
         count = len(members)
         out = [shape((frequencies, halves, sensors, LANES), f32)]
         scratch = [

time: 149 us -> 149 us (level)
  no operation moved by 1% of the time
where the time goes in v16:
time: 149 us; the launch traced here: 148 us
  waiting for transfers between devices  80.1 us (54%)
  starting transfers between devices  42.8 us (29%)
  Pallas kernels  21.1 us (14%)
  local copies, waits for them, and re-layouts  2.78 us (2%)
    all_to_all x1, waiting for transfers between devices, on_device(): lax.all_to_all(forward_map.reshape(frequencies, halves * sensors, cells),...  44.2 us
    ppermute x21, starting transfers between devices, swap(): return lax.ppermute(x, axes, [(i, i ^ distance) for i in range(count)])  31.9 us
    ppermute x21, waiting for transfers between devices, swap(): return lax.ppermute(x, axes, [(i, i ^ distance) for i in range(count)])  23.6 us
    ppermute x4, waiting for transfers between devices, to_other_sides(): lax.ppermute(x, ('sensor', 'side'), [(i, i ^ 1 + CORES * cross) for i in...  12.4 us
    pallas_call x4, Pallas kernels, step(): call(functools.partial(step_kernel, stage, len(preds), len(after)), [VMEM...  11.1 us
    all_to_all x1, starting transfers between devices, on_device(): lax.all_to_all(forward_map.reshape(frequencies, halves * sensors, cells),...  6.35 us
    ppermute x4, starting transfers between devices, to_other_sides(): lax.ppermute(x, ('sensor', 'side'), [(i, i ^ 1 + CORES * cross) for i in...  4.62 us
    pallas_call x3, Pallas kernels, on_device(): call(functools.partial(end_kernel, e, quads, members, len(done)), [VMEM]...  3.84 us
  transfers between devices with their start and end apart: 26, of which 14 were waited for; matrix products, arithmetic and copies ran while one was open for 0% of the time, Pallas kernels for 11%

profile of v16, /device:TPU:0, one launch (start us, length us, event | category | flops | bytes accessed | tf_op | source)
XLA Modules:
  0.0 147.7 jit_solution(6542177436999951806)
XLA Ops:
  0.6 6.4 %all-to-all-start = ((bf16[16,512,256]{2,1,0:T(8,128)(2,1)}), bf16[16,512,256]{2,1,0:T(8,128)(2,1)}, u32[]{:S(2)}, u32[]{:S(2)}) async-start(bf16[16,512,256]{2,1,0:T(8,128)(2,1)} %bitcast.5), calls=%async_computation | async-start | bytes 8388608 | tf_op jit(solution)/shard_map/all_to_all | solution.py:254
  7.0 2.2 %copy-done = f32[16,2,256,128]{3,2,1,0:T(8,128)S(1)} copy-done((f32[16,2,256,128]{3,2,1,0:T(8,128)S(1)}, f32[16,2,256,128]{3,2,1,0:T(8,128)}, u32[]{:S(2)}) %copy-start) | copy-done | bytes 4194328
  11.9 1.9 %collective-permute-start.2 = (bf16[448,256]{1,0:T(8,128)(2,1)S(1)}, bf16[448,256]{1,0:T(8,128)(2,1)S(1)}, u32[]{:S(2)}, u32[]{:S(2)}) collective-permute-start(bf16[448,256]{1,0:T(8,128)(2,1)S(1)} %get-tuple-element.35), channel_id=1, source_target_pairs={{0,2},{1,3},{2,0},{3,1},{4,6},{5,7},{6,4},{7,5},{8,10},{9,11},{10,... | collective-permute-start | bytes 688136 | tf_op jit(solution)/shard_map/ppermute | solution.py:42
  13.8 1.5 collective-permute-start.4
  15.3 1.5 collective-permute-start.3
  17.3 44.2 %all-to-all-done = bf16[16,512,256]{2,1,0:T(8,128)(2,1)} async-done(((bf16[16,512,256]{2,1,0:T(8,128)(2,1)}), bf16[16,512,256]{2,1,0:T(8,128)(2,1)}, u32[]{:S(2)}, u32[]{:S(2)}) %all-to-all-start) | async-done | bytes 4194336 | tf_op jit(solution)/shard_map/all_to_all | solution.py:254
  61.5 2.2 %shard_map.70.refs_7_.map_ref = bf16[4,4,512,256]{3,2,1,0:T(8,128)(2,1)S(1)} custom-call(bf16[4,4,512,256]{3,2,1,0:T(8,128)(2,1)} %bitcast.2.map_ref), custom_call_target="tpu_custom_call" | custom-call | bytes 8388608 | tf_op jit(solution)/shard_map/pallas_call | solution.py:273
  63.7 2.4 %collective-permute-done.4.refs_5_ = bf16[272,256]{1,0:T(8,128)(2,1)S(1)} collective-permute-done((bf16[272,256]{1,0:T(8,128)(2,1)S(1)}, bf16[272,256]{1,0:T(8,128)(2,1)S(1)}, u32[]{:S(2)}, u32[]{:S(2)}) %collective-permute-start.4) | collective-permute-done | bytes 139296 | tf_op jit(solution)/shard_map/ppermute | solution.py:42
  66.2 2.0 %collective-permute-done.5.refs_6_ = bf16[272,256]{1,0:T(8,128)(2,1)S(1)} collective-permute-done((bf16[272,256]{1,0:T(8,128)(2,1)S(1)}, bf16[272,256]{1,0:T(8,128)(2,1)S(1)}, u32[]{:S(2)}, u32[]{:S(2)}) %collective-permute-start.5) | collective-permute-done | bytes 139296 | tf_op jit(solution)/shard_map/ppermute | solution.py:42
  68.6 2.7 %shard_map.72.refs_0_ = bf16[4,256,128]{2,1,0:T(8,128)(2,1)S(1)} custom-call(f32[8,128]{1,0:T(8,128)S(1)} %get-tuple-element.33.scale_ref, bf16[4,4,512,256]{3,2,1,0:T(8,128)(2,1)S(1)} %shard_map.70.refs_7_.map_ref, bf16[4,256,512]{2,1,0:T(8,128)(2,1)S(1)} %get-tuple-element.39.prior_ref, bf16[4,256,128]{2,1,0:T(8,128)(2,1)S(1)} %get-tuple-element.40.obs_ref, ...), custom_call_target="tpu_custom_call" | custom-call | flops 2147483648 | bytes 8388608 | tf_op jit(solution)/shard_map/pallas_call | solution.py:295
  71.4 2.7 %collective-permute-start.6 = (bf16[4,256,128]{2,1,0:T(8,128)(2,1)S(1)}, bf16[4,256,128]{2,1,0:T(8,128)(2,1)S(1)}, u32[]{:S(2)}, u32[]{:S(2)}) collective-permute-start(bf16[4,256,128]{2,1,0:T(8,128)(2,1)S(1)} %shard_map.72.refs_0_), channel_id=1, source_target_pairs={{0,4},{4,0},{1,5},{5,1},{2,6},{6,2},{3,7},{7,3},{8,12},{12,8},{9,1... | collective-permute-start | bytes 786440 | tf_op jit(solution)/shard_map/ppermute | solution.py:42
  74.0 2.8 %shard_map.73.refs_2_.refs_0_ = bf16[4,256,128]{2,1,0:T(8,128)(2,1)S(1)} custom-call(f32[8,128]{1,0:T(8,128)S(1)} %get-tuple-element.33.scale_ref, bf16[4,4,512,256]{3,2,1,0:T(8,128)(2,1)S(1)} %shard_map.70.refs_7_.map_ref, bf16[4,256,512]{2,1,0:T(8,128)(2,1)S(1)} %get-tuple-element.39.prior_ref, bf16[4,256,128]{2,1,0:T(8,128)(2,1)S(1)} %get-tuple-element.42.obs_ref, ...), custom_call_target="tpu_custom_call" | custom-call | flops 2147483648 | bytes 8388608 | tf_op jit(solution)/shard_map/pallas_call | solution.py:295
  77.2 13.3 %collective-permute-done.6.refs_1_ = bf16[4,256,128]{2,1,0:T(8,128)(2,1)S(1)} collective-permute-done((bf16[4,256,128]{2,1,0:T(8,128)(2,1)S(1)}, bf16[4,256,128]{2,1,0:T(8,128)(2,1)S(1)}, u32[]{:S(2)}, u32[]{:S(2)}) %collective-permute-start.6) | collective-permute-done | bytes 262176 | tf_op jit(solution)/shard_map/ppermute | solution.py:42
  90.5 2.8 %shard_map.74 = (bf16[2,256,128]{2,1,0:T(8,128)(2,1)S(1)}, bf16[2,256,128]{2,1,0:T(8,128)(2,1)S(1)}, f32[2,256,128]{2,1,0:T(8,128)S(1)}, bf16[2,256,128]{2,1,0:T(8,128)(2,1)S(1)}) custom-call(f32[8,128]{1,0:T(8,128)S(1)} %get-tuple-element.33.scale_ref, bf16[4,4,512,256]{3,2,1,0:T(8,128)(2,1)S(1)} %shard_map.70.refs_7_.map_ref, ...), custom_call_target="tpu_custom_call" | custom-call | flops 2147483648 | bytes 8388608 | tf_op jit(solution)/shard_map/pallas_call | solution.py:295
  93.4 2.2 %collective-permute-start.10 = (bf16[2,256,128]{2,1,0:T(8,128)(2,1)S(1)}, bf16[2,256,128]{2,1,0:T(8,128)(2,1)S(1)}, u32[]{:S(2)}, u32[]{:S(2)}) collective-permute-start(bf16[2,256,128]{2,1,0:T(8,128)(2,1)S(1)} %get-tuple-element.45), channel_id=1, source_target_pairs={{0,12},{4,8},{8,4},{12,0},{16,28},{20,24},{24,20},{28,16},{1,13},{... | collective-permute-start | bytes 393224 | tf_op jit(solution)/shard_map/ppermute | solution.py:312
  96.4 2.8 %shard_map.75 = (bf16[2,256,128]{2,1,0:T(8,128)(2,1)S(1)}, bf16[2,256,128]{2,1,0:T(8,128)(2,1)S(1)}, f32[2,256,128]{2,1,0:T(8,128)S(1)}, bf16[2,256,128]{2,1,0:T(8,128)(2,1)S(1)}) custom-call(f32[8,128]{1,0:T(8,128)S(1)} %get-tuple-element.33.scale_ref, bf16[4,4,512,256]{3,2,1,0:T(8,128)(2,1)S(1)} %shard_map.70.refs_7_.map_ref, ...), custom_call_target="tpu_custom_call" | custom-call | flops 2147483648 | bytes 8388608 | tf_op jit(solution)/shard_map/pallas_call | solution.py:295
  99.4 2.2 %collective-permute-start.11 = (bf16[2,256,128]{2,1,0:T(8,128)(2,1)S(1)}, bf16[2,256,128]{2,1,0:T(8,128)(2,1)S(1)}, u32[]{:S(2)}, u32[]{:S(2)}) collective-permute-start(bf16[2,256,128]{2,1,0:T(8,128)(2,1)S(1)} %get-tuple-element.46), channel_id=1, source_target_pairs={{0,12},{4,8},{8,4},{12,0},{16,28},{20,24},{24,20},{28,16},{1,13},{... | collective-permute-start | bytes 393224 | tf_op jit(solution)/shard_map/ppermute | solution.py:312
  101.5 4.7 %collective-permute-done.7.refs_0_ = bf16[2,256,128]{2,1,0:T(8,128)(2,1)S(1)} collective-permute-done((bf16[2,256,128]{2,1,0:T(8,128)(2,1)S(1)}, bf16[2,256,128]{2,1,0:T(8,128)(2,1)S(1)}, u32[]{:S(2)}, u32[]{:S(2)}) %collective-permute-start.7) | collective-permute-done | bytes 131104 | tf_op jit(solution)/shard_map/ppermute | solution.py:312
  106.2 2.1 %collective-permute-done.10.refs_2_ = bf16[2,256,128]{2,1,0:T(8,128)(2,1)S(1)} collective-permute-done((bf16[2,256,128]{2,1,0:T(8,128)(2,1)S(1)}, bf16[2,256,128]{2,1,0:T(8,128)(2,1)S(1)}, u32[]{:S(2)}, u32[]{:S(2)}) %collective-permute-start.10) | collective-permute-done | bytes 131104 | tf_op jit(solution)/shard_map/ppermute | solution.py:312
  108.3 3.6 %collective-permute-done.9.refs_1_ = bf16[2,256,128]{2,1,0:T(8,128)(2,1)S(1)} collective-permute-done((bf16[2,256,128]{2,1,0:T(8,128)(2,1)S(1)}, bf16[2,256,128]{2,1,0:T(8,128)(2,1)S(1)}, u32[]{:S(2)}, u32[]{:S(2)}) %collective-permute-start.9) | collective-permute-done | bytes 131104 | tf_op jit(solution)/shard_map/ppermute | solution.py:312
  111.9 2.1 %collective-permute-done.11.refs_3_ = bf16[2,256,128]{2,1,0:T(8,128)(2,1)S(1)} collective-permute-done((bf16[2,256,128]{2,1,0:T(8,128)(2,1)S(1)}, bf16[2,256,128]{2,1,0:T(8,128)(2,1)S(1)}, u32[]{:S(2)}, u32[]{:S(2)}) %collective-permute-start.11) | collective-permute-done | bytes 131104 | tf_op jit(solution)/shard_map/ppermute | solution.py:312
  114.2 2.2 %collective-permute-start.22 = (bf16[2,256,256]{2,1,0:T(8,128)(2,1)S(1)}, bf16[2,256,256]{2,1,0:T(8,128)(2,1)S(1)}, u32[]{:S(2)}, u32[]{:S(2)}) collective-permute-start(bf16[2,256,256]{2,1,0:T(8,128)(2,1)S(1)} %get-tuple-element.52.refs_1_), channel_id=1, source_target_pairs={{0,17},{1,16},{2,19},{3,18},{8,25},{9,24},{10,27},{11,26},{16,1},{... | collective-permute-start | bytes 786440 | tf_op jit(solution)/shard_map/ppermute | solution.py:42
  116.4 5.6 %collective-permute-start.14 = (bf16[2,256,256]{2,1,0:T(8,128)(2,1)S(1)}, bf16[2,256,256]{2,1,0:T(8,128)(2,1)S(1)}, u32[]{:S(2)}, u32[]{:S(2)}) collective-permute-start(bf16[2,256,256]{2,1,0:T(8,128)(2,1)S(1)} %get-tuple-element.51.refs_0_), channel_id=1, source_target_pairs={{0,2},{1,3},{2,0},{3,1},{8,10},{9,11},{10,8},{11,9},{16,18},{17,19... | collective-permute-start | bytes 786440 | tf_op jit(solution)/shard_map/ppermute | solution.py:42
  123.6 5.7 %collective-permute-start.24 = (bf16[2,256,256]{2,1,0:T(8,128)(2,1)S(1)}, bf16[2,256,256]{2,1,0:T(8,128)(2,1)S(1)}, u32[]{:S(2)}, u32[]{:S(2)}) collective-permute-start(bf16[2,256,256]{2,1,0:T(8,128)(2,1)S(1)} %collective-permute-done.22.refs_1_), channel_id=1, source_target_pairs={{0,2},{1,3},{2,0},{3,1},{4,6},{5,7},{6,4},{7,5},{8,10},{9,11},{10,... | collective-permute-start | bytes 786440 | tf_op jit(solution)/shard_map/ppermute | solution.py:42
  129.3 1.6 %collective-permute-start.19 = (bf16[2,256,256]{2,1,0:T(8,128)(2,1)S(1)}, bf16[2,256,256]{2,1,0:T(8,128)(2,1)S(1)}, u32[]{:S(2)}, u32[]{:S(2)}) collective-permute-start(bf16[2,256,256]{2,1,0:T(8,128)(2,1)S(1)} %get-tuple-element.51.refs_0_), channel_id=1, source_target_pairs={{0,1},{1,0},{2,3},{3,2},{8,9},{9,8},{10,11},{11,10},{16,17},{17,16... | collective-permute-start | bytes 786440 | tf_op jit(solution)/shard_map/ppermute | solution.py:42
  131.3 2.1 %shard_map.77 = (bf16[256,256]{1,0:T(8,128)(2,1)S(1)}, bf16[256,256]{1,0:T(8,128)(2,1)S(1)}, bf16[256,256]{1,0:T(8,128)(2,1)S(1)}, bf16[256,256]{1,0:T(8,128)(2,1)S(1)}) custom-call(f32[8,128]{1,0:T(8,128)S(1)} %get-tuple-element.33.scale_ref, bf16[4,4,512,256]{3,2,1,0:T(8,128)(2,1)S(1)} %shard_map.70.refs_7_.map_ref, ...), custom_call_target="tpu_custom_call" | custom-call | flops 2147483648 | bytes 8388608 | tf_op jit(solution)/shard_map/pallas_call | solution.py:329
  133.4 1.8 %collective-permute-done.23.refs_2_ = bf16[2,256,256]{2,1,0:T(8,128)(2,1)S(1)} collective-permute-done((bf16[2,256,256]{2,1,0:T(8,128)(2,1)S(1)}, bf16[2,256,256]{2,1,0:T(8,128)(2,1)S(1)}, u32[]{:S(2)}, u32[]{:S(2)}) %collective-permute-start.23) | collective-permute-done | bytes 262176 | tf_op jit(solution)/shard_map/ppermute | solution.py:42
  136.5 3.0 %collective-permute-start.17 = (bf16[256,256]{1,0:T(8,128)(2,1)S(1)}, bf16[256,256]{1,0:T(8,128)(2,1)S(1)}, u32[]{:S(2)}, u32[]{:S(2)}) collective-permute-start(bf16[256,256]{1,0:T(8,128)(2,1)S(1)} %get-tuple-element.54), channel_id=1, source_target_pairs={{0,2},{1,3},{2,0},{3,1},{4,6},{5,7},{6,4},{7,5},{8,10},{9,11},{10,... | collective-permute-start | bytes 393224 | tf_op jit(solution)/shard_map/ppermute | solution.py:42
  140.4 1.7 %collective-permute-start.18 = (bf16[256,256]{1,0:T(8,128)(2,1)S(1)}, bf16[256,256]{1,0:T(8,128)(2,1)S(1)}, u32[]{:S(2)}, u32[]{:S(2)}) collective-permute-start(bf16[256,256]{1,0:T(8,128)(2,1)S(1)} %get-tuple-element.55), channel_id=1, source_target_pairs={{0,3},{1,2},{2,1},{3,0},{4,7},{5,6},{6,5},{7,4},{8,11},{9,10},{10,... | collective-permute-start | bytes 393224 | tf_op jit(solution)/shard_map/ppermute | solution.py:42
  142.1 1.4 shard_map.78.refs_4_
  143.6 1.2 shard_map.79
  144.8 1.6 %collective-permute-done.18.refs_3_ = bf16[256,256]{1,0:T(8,128)(2,1)S(1)} collective-permute-done((bf16[256,256]{1,0:T(8,128)(2,1)S(1)}, bf16[256,256]{1,0:T(8,128)(2,1)S(1)}, u32[]{:S(2)}, u32[]{:S(2)}) %collective-permute-start.18) | collective-permute-done | bytes 131104 | tf_op jit(solution)/shard_map/ppermute | solution.py:42
  (42 shorter events, 10.7 us)
Async XLA Ops:
  0.6 6.4 %copy-start.2 = (f32[256]{0:T(256)S(1)}, f32[256]{0:T(256)}, u32[]{:S(2)}) copy-start(f32[256]{0:T(256)} %param.7) | copy-start | bytes 3076
  0.6 60.9 %all-to-all-start = ((bf16[16,512,256]{2,1,0:T(8,128)(2,1)}), bf16[16,512,256]{2,1,0:T(8,128)(2,1)}, u32[]{:S(2)}, u32[]{:S(2)}) async-start(bf16[16,512,256]{2,1,0:T(8,128)(2,1)} %bitcast.5), calls=%async_computation | async-start | bytes 8388608 | tf_op jit(solution)/shard_map/all_to_all | solution.py:254
  7.0 3.2 %copy-start.3 = (f32[16]{0:T(128)S(1)}, f32[16]{0:T(128)}, u32[]{:S(2)}) copy-start(f32[16]{0:T(128)} %param.9) | copy-start | bytes 196
  7.0 2.2 %copy-start = (f32[16,2,256,128]{3,2,1,0:T(8,128)S(1)}, f32[16,2,256,128]{3,2,1,0:T(8,128)}, u32[]{:S(2)}) copy-start(f32[16,2,256,128]{3,2,1,0:T(8,128)} %obs_ref.1) | copy-start | bytes 12582916
  9.2 2.0 %copy-start.1 = (bf16[256,512]{1,0:T(8,128)(2,1)S(1)}, bf16[256,512]{1,0:T(8,128)(2,1)}, u32[]{:S(2)}) copy-start(bf16[256,512]{1,0:T(8,128)(2,1)} %own_ref.3) | copy-start | bytes 786436
  9.8 1.4 collective-permute-start
  11.9 56.4 %collective-permute-start.2 = (bf16[448,256]{1,0:T(8,128)(2,1)S(1)}, bf16[448,256]{1,0:T(8,128)(2,1)S(1)}, u32[]{:S(2)}, u32[]{:S(2)}) collective-permute-start(bf16[448,256]{1,0:T(8,128)(2,1)S(1)} %get-tuple-element.35), channel_id=1, source_target_pairs={{0,2},{1,3},{2,0},{3,1},{4,6},{5,7},{6,4},{7,5},{8,10},{9,11},{10,... | collective-permute-start | bytes 688136 | tf_op jit(solution)/shard_map/ppermute | solution.py:42
  13.8 52.3 %collective-permute-start.4 = (bf16[272,256]{1,0:T(8,128)(2,1)S(1)}, bf16[272,256]{1,0:T(8,128)(2,1)S(1)}, u32[]{:S(2)}, u32[]{:S(2)}) collective-permute-start(bf16[272,256]{1,0:T(8,128)(2,1)S(1)} %get-tuple-element.37), channel_id=1, source_target_pairs={{0,16},{8,24},{16,0},{24,8},{1,17},{9,25},{17,1},{25,9},{2,18},{10... | collective-permute-start | bytes 417800 | tf_op jit(solution)/shard_map/ppermute | solution.py:42
  15.3 52.9 %collective-permute-start.5 = (bf16[272,256]{1,0:T(8,128)(2,1)S(1)}, bf16[272,256]{1,0:T(8,128)(2,1)S(1)}, u32[]{:S(2)}, u32[]{:S(2)}) collective-permute-start(bf16[272,256]{1,0:T(8,128)(2,1)S(1)} %get-tuple-element.38), channel_id=1, source_target_pairs={{0,24},{8,16},{16,8},{24,0},{1,25},{9,17},{17,9},{25,1},{2,26},{10... | collective-permute-start | bytes 417800 | tf_op jit(solution)/shard_map/ppermute | solution.py:42
  15.3 53.0 %collective-permute-start.3 = (bf16[192,256]{1,0:T(8,128)(2,1)S(1)}, bf16[192,256]{1,0:T(8,128)(2,1)S(1)}, u32[]{:S(2)}, u32[]{:S(2)}) collective-permute-start(bf16[192,256]{1,0:T(8,128)(2,1)S(1)} %get-tuple-element.34), channel_id=1, source_target_pairs={{0,3},{1,2},{2,1},{3,0},{4,7},{5,6},{6,5},{7,4},{8,11},{9,10},{10,... | collective-permute-start | bytes 294920 | tf_op jit(solution)/shard_map/ppermute | solution.py:42
  16.7 51.5 %collective-permute-start.1 = (bf16[192,256]{1,0:T(8,128)(2,1)S(1)}, bf16[192,256]{1,0:T(8,128)(2,1)S(1)}, u32[]{:S(2)}, u32[]{:S(2)}) collective-permute-start(bf16[192,256]{1,0:T(8,128)(2,1)S(1)} %get-tuple-element.34), channel_id=1, source_target_pairs={{0,1},{1,0},{2,3},{3,2},{4,5},{5,4},{6,7},{7,6},{8,9},{9,8},{10,11... | collective-permute-start | bytes 294920 | tf_op jit(solution)/shard_map/ppermute | solution.py:42
  71.4 19.1 %collective-permute-start.6 = (bf16[4,256,128]{2,1,0:T(8,128)(2,1)S(1)}, bf16[4,256,128]{2,1,0:T(8,128)(2,1)S(1)}, u32[]{:S(2)}, u32[]{:S(2)}) collective-permute-start(bf16[4,256,128]{2,1,0:T(8,128)(2,1)S(1)} %shard_map.72.refs_0_), channel_id=1, source_target_pairs={{0,4},{4,0},{1,5},{5,1},{2,6},{6,2},{3,7},{7,3},{8,12},{12,8},{9,1... | collective-permute-start | bytes 786440 | tf_op jit(solution)/shard_map/ppermute | solution.py:42
  76.8 19.6 %collective-permute-start.8 = (bf16[4,256,128]{2,1,0:T(8,128)(2,1)S(1)}, bf16[4,256,128]{2,1,0:T(8,128)(2,1)S(1)}, u32[]{:S(2)}, u32[]{:S(2)}) collective-permute-start(bf16[4,256,128]{2,1,0:T(8,128)(2,1)S(1)} %shard_map.73.refs_2_.refs_0_), channel_id=1, source_target_pairs={{0,4},{4,0},{1,5},{5,1},{2,6},{6,2},{3,7},{7,3},{8,12},{12,8},{9,1... | collective-permute-start | bytes 786440 | tf_op jit(solution)/shard_map/ppermute | solution.py:42
  93.3 12.9 %collective-permute-start.7 = (bf16[2,256,128]{2,1,0:T(8,128)(2,1)S(1)}, bf16[2,256,128]{2,1,0:T(8,128)(2,1)S(1)}, u32[]{:S(2)}, u32[]{:S(2)}) collective-permute-start(bf16[2,256,128]{2,1,0:T(8,128)(2,1)S(1)} %get-tuple-element.43), channel_id=1, source_target_pairs={{0,4},{4,0},{8,12},{12,8},{16,20},{20,16},{24,28},{28,24},{1,5},{5... | collective-permute-start | bytes 393224 | tf_op jit(solution)/shard_map/ppermute | solution.py:312
  93.4 14.9 %collective-permute-start.10 = (bf16[2,256,128]{2,1,0:T(8,128)(2,1)S(1)}, bf16[2,256,128]{2,1,0:T(8,128)(2,1)S(1)}, u32[]{:S(2)}, u32[]{:S(2)}) collective-permute-start(bf16[2,256,128]{2,1,0:T(8,128)(2,1)S(1)} %get-tuple-element.45), channel_id=1, source_target_pairs={{0,12},{4,8},{8,4},{12,0},{16,28},{20,24},{24,20},{28,16},{1,13},{... | collective-permute-start | bytes 393224 | tf_op jit(solution)/shard_map/ppermute | solution.py:312
  95.6 12.7 %collective-permute-start.12 = (bf16[2,256,128]{2,1,0:T(8,128)(2,1)S(1)}, bf16[2,256,128]{2,1,0:T(8,128)(2,1)S(1)}, u32[]{:S(2)}, u32[]{:S(2)}) collective-permute-start(bf16[2,256,128]{2,1,0:T(8,128)(2,1)S(1)} %get-tuple-element.49), channel_id=1, source_target_pairs={{0,8},{8,0},{16,24},{24,16},{1,9},{9,1},{17,25},{25,17},{2,10},{10... | collective-permute-start | bytes 393224 | tf_op jit(solution)/shard_map/ppermute | solution.py:42
  99.2 12.6 %collective-permute-start.9 = (bf16[2,256,128]{2,1,0:T(8,128)(2,1)S(1)}, bf16[2,256,128]{2,1,0:T(8,128)(2,1)S(1)}, u32[]{:S(2)}, u32[]{:S(2)}) collective-permute-start(bf16[2,256,128]{2,1,0:T(8,128)(2,1)S(1)} %get-tuple-element.44), channel_id=1, source_target_pairs={{0,4},{4,0},{8,12},{12,8},{16,20},{20,16},{24,28},{28,24},{1,5},{5... | collective-permute-start | bytes 393224 | tf_op jit(solution)/shard_map/ppermute | solution.py:312
  99.4 14.5 %collective-permute-start.11 = (bf16[2,256,128]{2,1,0:T(8,128)(2,1)S(1)}, bf16[2,256,128]{2,1,0:T(8,128)(2,1)S(1)}, u32[]{:S(2)}, u32[]{:S(2)}) collective-permute-start(bf16[2,256,128]{2,1,0:T(8,128)(2,1)S(1)} %get-tuple-element.46), channel_id=1, source_target_pairs={{0,12},{4,8},{8,4},{12,0},{16,28},{20,24},{24,20},{28,16},{1,13},{... | collective-permute-start | bytes 393224 | tf_op jit(solution)/shard_map/ppermute | solution.py:312
  106.2 7.7 %collective-permute-start.13 = (bf16[2,256,128]{2,1,0:T(8,128)(2,1)S(1)}, bf16[2,256,128]{2,1,0:T(8,128)(2,1)S(1)}, u32[]{:S(2)}, u32[]{:S(2)}) collective-permute-start(bf16[2,256,128]{2,1,0:T(8,128)(2,1)S(1)} %get-tuple-element.50), channel_id=1, source_target_pairs={{0,8},{8,0},{16,24},{24,16},{1,9},{9,1},{17,25},{25,17},{2,10},{10... | collective-permute-start | bytes 393224 | tf_op jit(solution)/shard_map/ppermute | solution.py:42
  114.2 9.4 %collective-permute-start.22 = (bf16[2,256,256]{2,1,0:T(8,128)(2,1)S(1)}, bf16[2,256,256]{2,1,0:T(8,128)(2,1)S(1)}, u32[]{:S(2)}, u32[]{:S(2)}) collective-permute-start(bf16[2,256,256]{2,1,0:T(8,128)(2,1)S(1)} %get-tuple-element.52.refs_1_), channel_id=1, source_target_pairs={{0,17},{1,16},{2,19},{3,18},{8,25},{9,24},{10,27},{11,26},{16,1},{... | collective-permute-start | bytes 786440 | tf_op jit(solution)/shard_map/ppermute | solution.py:42
  116.4 12.9 %collective-permute-start.16 = (bf16[2,256,256]{2,1,0:T(8,128)(2,1)S(1)}, bf16[2,256,256]{2,1,0:T(8,128)(2,1)S(1)}, u32[]{:S(2)}, u32[]{:S(2)}) collective-permute-start(bf16[2,256,256]{2,1,0:T(8,128)(2,1)S(1)} %get-tuple-element.53), channel_id=1, source_target_pairs={{0,8},{8,0},{16,24},{24,16},{1,9},{9,1},{17,25},{25,17},{2,10},{10... | collective-permute-start | bytes 786440 | tf_op jit(solution)/shard_map/ppermute | solution.py:42
  116.4 14.6 %collective-permute-start.14 = (bf16[2,256,256]{2,1,0:T(8,128)(2,1)S(1)}, bf16[2,256,256]{2,1,0:T(8,128)(2,1)S(1)}, u32[]{:S(2)}, u32[]{:S(2)}) collective-permute-start(bf16[2,256,256]{2,1,0:T(8,128)(2,1)S(1)} %get-tuple-element.51.refs_0_), channel_id=1, source_target_pairs={{0,2},{1,3},{2,0},{3,1},{8,10},{9,11},{10,8},{11,9},{16,18},{17,19... | collective-permute-start | bytes 786440 | tf_op jit(solution)/shard_map/ppermute | solution.py:42
  122.0 13.3 %collective-permute-start.23 = (bf16[2,256,256]{2,1,0:T(8,128)(2,1)S(1)}, bf16[2,256,256]{2,1,0:T(8,128)(2,1)S(1)}, u32[]{:S(2)}, u32[]{:S(2)}) collective-permute-start(bf16[2,256,256]{2,1,0:T(8,128)(2,1)S(1)} %get-tuple-element.52.refs_1_), channel_id=1, source_target_pairs={{0,18},{1,19},{2,16},{3,17},{8,26},{9,27},{10,24},{11,25},{16,2},{... | collective-permute-start | bytes 786440 | tf_op jit(solution)/shard_map/ppermute | solution.py:42
  122.4 14.1 %collective-permute-start.21 = (bf16[2,256,256]{2,1,0:T(8,128)(2,1)S(1)}, bf16[2,256,256]{2,1,0:T(8,128)(2,1)S(1)}, u32[]{:S(2)}, u32[]{:S(2)}) collective-permute-start(bf16[2,256,256]{2,1,0:T(8,128)(2,1)S(1)} %get-tuple-element.52.refs_1_), channel_id=1, source_target_pairs={{0,16},{1,17},{2,18},{3,19},{8,24},{9,25},{10,26},{11,27},{16,0},{... | collective-permute-start | bytes 786440 | tf_op jit(solution)/shard_map/ppermute | solution.py:42
  123.6 16.8 %collective-permute-start.24 = (bf16[2,256,256]{2,1,0:T(8,128)(2,1)S(1)}, bf16[2,256,256]{2,1,0:T(8,128)(2,1)S(1)}, u32[]{:S(2)}, u32[]{:S(2)}) collective-permute-start(bf16[2,256,256]{2,1,0:T(8,128)(2,1)S(1)} %collective-permute-done.22.refs_1_), channel_id=1, source_target_pairs={{0,2},{1,3},{2,0},{3,1},{4,6},{5,7},{6,4},{7,5},{8,10},{9,11},{10,... | collective-permute-start | bytes 786440 | tf_op jit(solution)/shard_map/ppermute | solution.py:42
  129.3 14.3 %collective-permute-start.19 = (bf16[2,256,256]{2,1,0:T(8,128)(2,1)S(1)}, bf16[2,256,256]{2,1,0:T(8,128)(2,1)S(1)}, u32[]{:S(2)}, u32[]{:S(2)}) collective-permute-start(bf16[2,256,256]{2,1,0:T(8,128)(2,1)S(1)} %get-tuple-element.51.refs_0_), channel_id=1, source_target_pairs={{0,1},{1,0},{2,3},{3,2},{8,9},{9,8},{10,11},{11,10},{16,17},{17,16... | collective-permute-start | bytes 786440 | tf_op jit(solution)/shard_map/ppermute | solution.py:42
  130.9 15.5 %collective-permute-start.15 = (bf16[2,256,256]{2,1,0:T(8,128)(2,1)S(1)}, bf16[2,256,256]{2,1,0:T(8,128)(2,1)S(1)}, u32[]{:S(2)}, u32[]{:S(2)}) collective-permute-start(bf16[2,256,256]{2,1,0:T(8,128)(2,1)S(1)} %collective-permute-done.14.refs_0_), channel_id=1, source_target_pairs={{0,1},{1,0},{2,3},{3,2},{4,5},{5,4},{6,7},{7,6},{8,9},{9,8},{10,11... | collective-permute-start | bytes 786440 | tf_op jit(solution)/shard_map/ppermute | solution.py:42
  135.2 8.4 %collective-permute-start.20 = (bf16[256,256]{1,0:T(8,128)(2,1)S(1)}, bf16[256,256]{1,0:T(8,128)(2,1)S(1)}, u32[]{:S(2)}, u32[]{:S(2)}) collective-permute-start(bf16[256,256]{1,0:T(8,128)(2,1)S(1)} %get-tuple-element.57), channel_id=1, source_target_pairs={{0,1},{1,0},{2,3},{3,2},{4,5},{5,4},{6,7},{7,6},{8,9},{9,8},{10,11... | collective-permute-start | bytes 393224 | tf_op jit(solution)/shard_map/ppermute | solution.py:42
  136.5 8.4 %collective-permute-start.17 = (bf16[256,256]{1,0:T(8,128)(2,1)S(1)}, bf16[256,256]{1,0:T(8,128)(2,1)S(1)}, u32[]{:S(2)}, u32[]{:S(2)}) collective-permute-start(bf16[256,256]{1,0:T(8,128)(2,1)S(1)} %get-tuple-element.54), channel_id=1, source_target_pairs={{0,2},{1,3},{2,0},{3,1},{4,6},{5,7},{6,4},{7,5},{8,10},{9,11},{10,... | collective-permute-start | bytes 393224 | tf_op jit(solution)/shard_map/ppermute | solution.py:42
  140.4 6.0 %collective-permute-start.18 = (bf16[256,256]{1,0:T(8,128)(2,1)S(1)}, bf16[256,256]{1,0:T(8,128)(2,1)S(1)}, u32[]{:S(2)}, u32[]{:S(2)}) collective-permute-start(bf16[256,256]{1,0:T(8,128)(2,1)S(1)} %get-tuple-element.55), channel_id=1, source_target_pairs={{0,3},{1,2},{2,1},{3,0},{4,7},{5,6},{6,5},{7,4},{8,11},{9,10},{10,... | collective-permute-start | bytes 393224 | tf_op jit(solution)/shard_map/ppermute | solution.py:42
